TPU v7x, 128 devices: a whole 4x4x4 slice. The times are simulated.
128 devices in a mesh: dp: 32 (over y, x, core), mp: 4 (over z).
Axes of the slice: x: 4, y: 4, z: 4, core: 2. Of those that a mesh axis runs over, the one named last changes fastest.
Arguments:
- residual: float32 [32, 512, 2048], P('dp', 'mp'), may hold values from -6 to 6
- cotangent: float32 [32, 512, 2048], P('dp', 'mp'), may hold values from -6 to 6
- document_lengths: int32 [32, 4], P('dp'), may hold values from 1 to 448, 512 in all within a row
- norm_gains: float32 [2, 2048], P(None, 'dp'), may hold values from 0.5 to 1.5
- query_weight: float32 [2048, 2048], P('dp', 'mp'), may hold values from -0.125 to 0.125
- keyvalue_weight: float32 [2, 2048, 256], P(None, 'dp', 'mp'), may hold values from -0.125 to 0.125
- output_weight: float32 [2048, 2048], P('mp', 'dp'), may hold values from -1.5 to 1.5
- gateup_weight: float32 [2, 2048, 5632], P(None, 'dp', 'mp'), may hold values from -0.125 to 0.125
- down_weight: float32 [5632, 2048], P('mp', 'dp'), may hold values from -0.078125 to 0.078125
- moment_gains: float32 [2, 2048], P(None, 'dp'), may hold values from -80 to 80
- moment_query: float32 [2048, 2048], P('dp', 'mp'), may hold values from -80 to 80
- moment_keyvalue: float32 [2, 2048, 256], P(None, 'dp', 'mp'), may hold values from -80 to 80
- moment_output: float32 [2048, 2048], P('mp', 'dp'), may hold values from -10 to 10
- moment_gateup: float32 [2, 2048, 5632], P(None, 'dp', 'mp'), may hold values from -24 to 24
- moment_down: float32 [5632, 2048], P('mp', 'dp'), may hold values from -48 to 48
- square_gains: float32 [2, 2048], P(None, 'dp'), may hold values from 868.352 to 3440.64
- square_query: float32 [2048, 2048], P('dp', 'mp'), may hold values from 868.352 to 3440.64
- square_keyvalue: float32 [2, 2048, 256], P(None, 'dp', 'mp'), may hold values from 868.352 to 3440.64
- square_output: float32 [2048, 2048], P('mp', 'dp'), may hold values from 13.1072 to 52.4288
- square_gateup: float32 [2, 2048, 5632], P(None, 'dp', 'mp'), may hold values from 78.6432 to 311.296
- square_down: float32 [5632, 2048], P('mp', 'dp'), may hold values from 311.296 to 1245.184
Outputs:
- block_output: float32 [32, 512, 2048], P('dp', 'mp')
- input_gradient: float32 [32, 512, 2048], P('dp', 'mp')
- gradient_gains: float32 [2, 2048], P(None, 'dp')
- gradient_query: float32 [2048, 2048], P('dp', 'mp')
- gradient_keyvalue: float32 [2, 2048, 256], P(None, 'dp', 'mp')
- gradient_output: float32 [2048, 2048], P('mp', 'dp')
- gradient_gateup: float32 [2, 2048, 5632], P(None, 'dp', 'mp')
- gradient_down: float32 [5632, 2048], P('mp', 'dp')
- momentum_gains: float32 [2, 2048], P(None, 'dp')
- momentum_query: float32 [2048, 2048], P('dp', 'mp')
- momentum_keyvalue: float32 [2, 2048, 256], P(None, 'dp', 'mp')
- momentum_output: float32 [2048, 2048], P('mp', 'dp')
- momentum_gateup: float32 [2, 2048, 5632], P(None, 'dp', 'mp')
- momentum_down: float32 [5632, 2048], P('mp', 'dp')
- variance_gains: float32 [2, 2048], P(None, 'dp')
- variance_query: float32 [2048, 2048], P('dp', 'mp')
- variance_keyvalue: float32 [2, 2048, 256], P(None, 'dp', 'mp')
- variance_output: float32 [2048, 2048], P('mp', 'dp')
- variance_gateup: float32 [2, 2048, 5632], P(None, 'dp', 'mp')
- variance_down: float32 [5632, 2048], P('mp', 'dp')
- updated_gains: float32 [2, 2048], P(None, 'dp')
- updated_query: float32 [2048, 2048], P('dp', 'mp')
- updated_keyvalue: float32 [2, 2048, 256], P(None, 'dp', 'mp')
- updated_output: float32 [2048, 2048], P('mp', 'dp')
- updated_gateup: float32 [2, 2048, 5632], P(None, 'dp', 'mp')
- updated_down: float32 [5632, 2048], P('mp', 'dp')
Inputs may be any that keep to these rules, and one draw needn't show every extreme that they name: `document_lengths`: the 4 lengths of a row sum to 512; every row has one document of exactly 448 tokens.
All inputs are finite; a program needn't handle non-finite values.
Results may differ from a plain program's by a relative error of at most 0.025.
Values may be sent and summed in bfloat16 or wider, within the bound.
No kernel may reach another device: no remote copies, remote signals or barrier semaphores. Data moves between devices by JAX's collectives and lax.ppermute only.
A program may use at most 192 MiB of HBM per device.

v0:
```python
import jax
import jax.numpy as jnp
from jax import lax
from jax.sharding import PartitionSpec as P

HEAD_DIM = 64
STEP = 10


EPS = 1e-05
THETA = 10000.0
BETA_ONE = 0.9
BETA_TWO = 0.95
ADAM_EPS = 1e-08
RATES = (1.0, 0.05, 0.05, 0.5, 0.05, 0.025)
DECAYS = (0.0, 0.1, 0.1, 0.1, 0.1, 0.1)


def rows_first(arrays, axis, dims):
    turned = [jnp.moveaxis(a, dim, 0) for a, dim in zip(arrays, dims)]
    widths = [t[0].size for t in turned]
    both = jnp.concatenate([t.reshape(-1, w) for t, w in zip(turned, widths)], axis=1)
    out = lax.all_gather(both, axis, axis=0, tiled=True)
    pieces = jnp.split(out, [sum(widths[:k]) for k in range(1, len(widths))], axis=1)
    return tuple(
        (
            jnp.moveaxis(b.reshape(-1, *t.shape[1:]), 0, dim)
            for b, t, dim in zip(pieces, turned, dims)
        )
    )


def in_order(pieces, dim):
    lengths = list(pieces.shape[1:])
    lengths[dim] *= pieces.shape[0]
    return jnp.moveaxis(pieces, 0, dim).reshape(lengths)


def copy_for_each(x, axis):
    copies = jnp.broadcast_to(x, (lax.axis_size(axis), *x.shape))
    return lax.all_to_all(copies, axis, split_axis=0, concat_axis=0, tiled=True)


def gather_directly(x, axis, dim):
    return in_order(copy_for_each(x, axis), dim)


def cut_along(x, dim, peers):
    before, after = (x.shape[:dim], x.shape[dim + 1 :])
    return jnp.moveaxis(x.reshape(*before, peers, -1, *after), dim, 0)


def summed_on_arrival(x, axis, dim):
    pieces = cut_along(x, dim, lax.axis_size(axis))
    arrived = lax.all_to_all(pieces, axis, split_axis=0, concat_axis=0, tiled=True)
    return arrived.sum(axis=0)


def summed_on_arrival_2(x, axis, dim):
    pieces = cut_along(x, dim, lax.axis_size(axis))
    arrived = lax.all_to_all(pieces, axis, split_axis=0, concat_axis=0, tiled=True)
    return arrived.astype(jnp.float32).sum(axis=0)


def sum_together(arrays, axis, dims):
    peers = lax.axis_size(axis)
    pieces = [cut_along(a, dim, peers) for a, dim in zip(arrays, dims)]
    lines = jnp.concatenate([b.reshape(peers, -1) for b in pieces], axis=1)
    extent = max(16, -(-lines.shape[1] // 1024) * 8)
    lines = jnp.pad(lines, ((0, 0), (0, extent * 128 - lines.shape[1]))).reshape(-1, 128)
    vector, at, outs = (lax.psum_scatter(lines, axis, tiled=True).reshape(-1), 0, [])
    for b in pieces:
        part = b[0]
        outs.append(vector[at : at + part.size].reshape(part.shape))
        at += part.size
    return tuple(outs)


def taken_together(x, axis):
    return copy_for_each(x, axis).sum(axis=0)


def rope_angles(position, head_size):
    half_size = head_size // 2
    indices = jnp.arange(half_size).astype(jnp.float32)
    frequency = 1.0 / THETA ** (2.0 * indices / head_size)
    angles = position.astype(jnp.float32)[..., None] * frequency
    return (jnp.cos(angles), jnp.sin(angles))


def rotate(tensor, cosine, sine_table):
    half_size = tensor.shape[-1] // 2
    leading = tensor[..., :half_size]
    trailing = tensor[..., half_size:]
    cosine = cosine[..., None, :]
    sine_table = sine_table[..., None, :]
    return jnp.concatenate(
        [leading * cosine - trailing * sine_table, trailing * cosine + leading * sine_table],
        axis=-1,
    )


def rotate_back(tensor, cosine, sine_table):
    half_size = tensor.shape[-1] // 2
    leading = tensor[..., :half_size]
    trailing = tensor[..., half_size:]
    cosine = cosine[..., None, :]
    sine_table = sine_table[..., None, :]
    return jnp.concatenate(
        [leading * cosine + trailing * sine_table, trailing * cosine - leading * sine_table],
        axis=-1,
    )


def doc_layout(lengths_row, length):
    boundary = jnp.cumsum(lengths_row)
    starts = boundary - lengths_row
    positions = jnp.arange(length)
    segment = jnp.sum((positions[:, None] >= boundary[None, :]).astype(jnp.int32), axis=1)
    leading = jnp.max(jnp.where(starts[None, :] <= positions[:, None], starts[None, :], 0), axis=1)
    return (segment, positions - leading)


def norm_forward(tensor, gain):
    inverse = lax.rsqrt(jnp.mean(tensor * tensor, axis=-1, keepdims=True) + EPS)
    return (tensor * inverse * gain, inverse)


def norm_backward(tensor, inverse, gain, upstream):
    weighted = upstream * gain
    inner = jnp.mean(weighted * tensor, axis=-1, keepdims=True)
    grad_tensor = inverse * weighted - tensor * inverse * inverse * inverse * inner
    grad_gain = jnp.sum(upstream * tensor * inverse, axis=(0, 1))
    return (grad_tensor, grad_gain)


def allowed_pairs(segment):
    length = segment.shape[0]
    positions = jnp.arange(length)
    return (segment[:, None] == segment[None, :]) & (positions[None, :] <= positions[:, None])


def score_block(grouped, key_rows, segment):
    head_size = grouped.shape[-1]
    scores = jnp.einsum(
        "qkgd,skd->kgqs", grouped, key_rows, preferred_element_type=jnp.float32
    ) * head_size ** (-0.5)
    return jnp.where(allowed_pairs(segment), scores, -1e30)


def attend_forward(element):
    queries, key_rows, value_rows, segment = element
    length, heads, head_size = queries.shape
    groups = key_rows.shape[1]
    grouped = queries.reshape(length, groups, heads // groups, head_size)
    scores = score_block(grouped, key_rows, segment)
    maximum = jnp.max(scores, axis=-1, keepdims=True)
    exponent = jnp.exp(scores - maximum)
    total = jnp.sum(exponent, axis=-1, keepdims=True)
    probability = (exponent / total).astype(jnp.bfloat16)
    result = jnp.einsum(
        "kgqs,skd->qkgd", probability, value_rows, preferred_element_type=jnp.float32
    )
    return (result.reshape(length, heads * head_size), maximum + jnp.log(total))


def attend_backward(element):
    queries, key_rows, value_rows, segment, logsum, upstream = element
    length, heads, head_size = queries.shape
    groups = key_rows.shape[1]
    grouped = queries.reshape(length, groups, heads // groups, head_size)
    upstream_grouped = upstream.reshape(length, groups, heads // groups, head_size)
    scores = score_block(grouped, key_rows, segment)
    probability = jnp.exp(scores - logsum)
    grad_values = jnp.einsum(
        "kgqs,qkgd->skd",
        probability.astype(jnp.bfloat16),
        upstream_grouped,
        preferred_element_type=jnp.float32,
    )
    grad_probs = jnp.einsum(
        "qkgd,skd->kgqs", upstream_grouped, value_rows, preferred_element_type=jnp.float32
    )
    inner = jnp.sum(probability * grad_probs, axis=-1, keepdims=True)
    grad_scores = (probability * (grad_probs - inner)).astype(jnp.bfloat16)
    scale = head_size ** (-0.5)
    grad_queries = (
        jnp.einsum("kgqs,skd->qkgd", grad_scores, key_rows, preferred_element_type=jnp.float32)
        * scale
    )
    grad_keys = (
        jnp.einsum("kgqs,qkgd->skd", grad_scores, grouped, preferred_element_type=jnp.float32)
        * scale
    )
    return (grad_queries.reshape(length, heads, head_size), grad_keys, grad_values)


def adamw(weight, gradient, moment, square, rate, decay):
    momentum = BETA_ONE * moment + (1.0 - BETA_ONE) * gradient
    variance = BETA_TWO * square + (1.0 - BETA_TWO) * gradient * gradient
    moment_hat = momentum / (1.0 - BETA_ONE**STEP)
    square_hat = variance / (1.0 - BETA_TWO**STEP)
    updated = weight - rate * (moment_hat / (jnp.sqrt(square_hat) + ADAM_EPS) + decay * weight)
    return (momentum, variance, updated)


def on_device(
    residual,
    cotangent,
    document_lengths,
    norm_gains,
    query_weight,
    keyvalue_weight,
    output_weight,
    gateup_weight,
    down_weight,
    moment_gains,
    moment_query,
    moment_keyvalue,
    moment_output,
    moment_gateup,
    moment_down,
    square_gains,
    square_query,
    square_keyvalue,
    square_output,
    square_gateup,
    square_down,
):
    row_count, local_len, features = residual.shape
    length = local_len * lax.axis_size("mp")
    segment, position = jax.vmap(lambda lengths_row: doc_layout(lengths_row, length))(
        document_lengths
    )
    cosine, sine_table = rope_angles(position, HEAD_DIM)
    low_gains = norm_gains.astype(jnp.bfloat16)
    low_query = query_weight.astype(jnp.bfloat16)
    low_keyvalue = keyvalue_weight.astype(jnp.bfloat16)
    low_output = output_weight.astype(jnp.bfloat16)
    low_gateup = gateup_weight.astype(jnp.bfloat16)
    low_down = down_weight.astype(jnp.bfloat16)
    gathered = rows_first(
        (low_gains, low_query, low_keyvalue, low_output, low_gateup, low_down),
        "dp",
        (1, 0, 1, 1, 1, 1),
    )
    gain_full, query_full, keyvalue_full, output_full, gateup_full, down_full = gathered
    gain_values = gain_full.astype(jnp.float32)
    qkv_full = jnp.concatenate((query_full, keyvalue_full[0], keyvalue_full[1]), axis=1)
    query_cols = query_full.shape[1]
    pair_cols = keyvalue_full.shape[2]
    heads_local = query_cols // HEAD_DIM
    groups_local = pair_cols // HEAD_DIM
    normed_one, inverse_one = norm_forward(residual, gain_values[0])
    rows_one = gather_directly(normed_one.astype(jnp.bfloat16), "mp", 1)
    projected = jnp.einsum("rsd,dc->rsc", rows_one, qkv_full, preferred_element_type=jnp.float32)
    query_raw = projected[..., :query_cols].reshape(row_count, length, heads_local, HEAD_DIM)
    key_raw = projected[..., query_cols : query_cols + pair_cols].reshape(
        row_count, length, groups_local, HEAD_DIM
    )
    value_raw = projected[..., query_cols + pair_cols :].reshape(
        row_count, length, groups_local, HEAD_DIM
    )
    queries = rotate(query_raw, cosine, sine_table).astype(jnp.bfloat16)
    key_rows = rotate(key_raw, cosine, sine_table).astype(jnp.bfloat16)
    value_rows = value_raw.astype(jnp.bfloat16)
    mixed, logsum = lax.map(attend_forward, (queries, key_rows, value_rows, segment))
    attended = mixed.astype(jnp.bfloat16)
    attended_seq = jnp.swapaxes(attended, 0, 1)
    block = attended_seq
    attention = summed_on_arrival(
        jnp.einsum("nrc,cd->nrd", block, output_full, preferred_element_type=jnp.float32), "mp", 0
    )
    middle = residual + jnp.swapaxes(attention, 0, 1)
    normed_two, inverse_two = norm_forward(middle, gain_values[1])
    rows_two = gather_directly(normed_two.astype(jnp.bfloat16), "mp", 1)
    gate_up = jnp.einsum("rsd,edf->rsef", rows_two, gateup_full, preferred_element_type=jnp.float32)
    gate_act = gate_up[:, :, 0]
    up_act = gate_up[:, :, 1]
    sigmoid = jax.nn.sigmoid(gate_act)
    activated = gate_act * sigmoid
    hidden = (activated * up_act).astype(jnp.bfloat16)
    hidden_seq = jnp.swapaxes(hidden, 0, 1)
    block = hidden_seq
    feedfwd = summed_on_arrival_2(
        jnp.einsum("nrf,fd->nrd", block, down_full, preferred_element_type=jnp.float32).astype(
            jnp.bfloat16
        ),
        "mp",
        0,
    )
    block_output = middle + jnp.swapaxes(feedfwd, 0, 1)
    grad_rows = gather_directly(cotangent.astype(jnp.bfloat16), "mp", 1)
    grad_hidden = jnp.einsum(
        "rsd,fd->rsf", grad_rows, down_full, preferred_element_type=jnp.float32
    )
    grad_down = jnp.einsum("rsf,rsd->fd", hidden, grad_rows, preferred_element_type=jnp.float32)
    slope = sigmoid * (1.0 + gate_act * (1.0 - sigmoid))
    grad_gateup = jnp.stack((grad_hidden * up_act * slope, grad_hidden * activated), axis=2).astype(
        jnp.bfloat16
    )
    grad_gateup_weight = jnp.einsum(
        "rsd,rsef->edf", rows_two, grad_gateup, preferred_element_type=jnp.float32
    )
    gateup_seq = jnp.swapaxes(grad_gateup, 0, 1)
    block = gateup_seq
    grad_normed_two = jnp.swapaxes(
        summed_on_arrival_2(
            jnp.einsum(
                "nref,edf->nrd", block, gateup_full, preferred_element_type=jnp.float32
            ).astype(jnp.bfloat16),
            "mp",
            0,
        ),
        0,
        1,
    )
    grad_middle_norm, gain_two = norm_backward(middle, inverse_two, gain_values[1], grad_normed_two)
    grad_middle = cotangent + grad_middle_norm
    reduced_gateup, reduced_down = (
        lax.psum_scatter(
            grad_gateup_weight.astype(jnp.bfloat16), "dp", scatter_dimension=1, tiled=True
        ).astype(jnp.float32),
        lax.psum_scatter(
            grad_down.astype(jnp.bfloat16), "dp", scatter_dimension=1, tiled=True
        ).astype(jnp.float32),
    )
    attention_rows = gather_directly(grad_middle.astype(jnp.bfloat16), "mp", 1)
    grad_attended = jnp.einsum(
        "rsd,cd->rsc", attention_rows, output_full, preferred_element_type=jnp.float32
    ).astype(jnp.bfloat16)
    grad_output = jnp.einsum(
        "rsc,rsd->cd", attended, attention_rows, preferred_element_type=jnp.float32
    )
    grad_attended_heads = grad_attended.reshape(row_count, length, heads_local, HEAD_DIM)
    grad_queries, grad_keys, grad_values = lax.map(
        attend_backward, (queries, key_rows, value_rows, segment, logsum, grad_attended_heads)
    )
    grad_queries = rotate_back(grad_queries, cosine, sine_table)
    grad_keys = rotate_back(grad_keys, cosine, sine_table)
    grad_projected = jnp.concatenate(
        (
            grad_queries.reshape(row_count, length, query_cols),
            grad_keys.reshape(row_count, length, pair_cols),
            grad_values.reshape(row_count, length, pair_cols),
        ),
        axis=-1,
    ).astype(jnp.bfloat16)
    grad_qkv_weight = jnp.einsum(
        "rsd,rsc->dc", rows_one, grad_projected, preferred_element_type=jnp.float32
    )
    grad_query = grad_qkv_weight[:, :query_cols]
    grad_keyvalue = jnp.stack(
        (
            grad_qkv_weight[:, query_cols : query_cols + pair_cols],
            grad_qkv_weight[:, query_cols + pair_cols :],
        )
    )
    projected_seq = jnp.swapaxes(grad_projected, 0, 1)
    block = projected_seq
    grad_normed_one = jnp.swapaxes(
        summed_on_arrival_2(
            jnp.einsum("nrc,dc->nrd", block, qkv_full, preferred_element_type=jnp.float32).astype(
                jnp.bfloat16
            ),
            "mp",
            0,
        ),
        0,
        1,
    )
    grad_input_norm, gain_one = norm_backward(
        residual, inverse_one, gain_values[0], grad_normed_one
    )
    input_gradient = grad_middle + grad_input_norm
    gain_part = jnp.stack((gain_one, gain_two))
    reduced_gains, reduced_query, reduced_keyvalue, reduced_output = tuple(
        (
            part.astype(jnp.float32)
            for part in sum_together(
                (
                    gain_part.astype(jnp.bfloat16),
                    grad_query.astype(jnp.bfloat16),
                    grad_keyvalue.astype(jnp.bfloat16),
                    grad_output.astype(jnp.bfloat16),
                ),
                "dp",
                (1, 0, 1, 1),
            )
        )
    )
    reduced_gains = taken_together(reduced_gains, "mp")
    masters = (norm_gains, query_weight, keyvalue_weight, output_weight, gateup_weight, down_weight)
    reduced = (
        reduced_gains,
        reduced_query,
        reduced_keyvalue,
        reduced_output,
        reduced_gateup,
        reduced_down,
    )
    moments = (
        moment_gains,
        moment_query,
        moment_keyvalue,
        moment_output,
        moment_gateup,
        moment_down,
    )
    squares = (
        square_gains,
        square_query,
        square_keyvalue,
        square_output,
        square_gateup,
        square_down,
    )
    results = [
        adamw(masters[i], reduced[i], moments[i], squares[i], RATES[i], DECAYS[i]) for i in range(6)
    ]
    return (
        block_output,
        input_gradient,
        reduced[0],
        reduced[1],
        reduced[2],
        reduced[3],
        reduced[4],
        reduced[5],
        results[0][0],
        results[1][0],
        results[2][0],
        results[3][0],
        results[4][0],
        results[5][0],
        results[0][1],
        results[1][1],
        results[2][1],
        results[3][1],
        results[4][1],
        results[5][1],
        results[0][2],
        results[1][2],
        results[2][2],
        results[3][2],
        results[4][2],
        results[5][2],
    )


def solution(mesh):
    placed = (
        P("dp", "mp", None),
        P("dp", "mp", None),
        P("dp", None),
        P(None, "dp"),
        P("dp", "mp"),
        P(None, "dp", "mp"),
        P("mp", "dp"),
        P(None, "dp", "mp"),
        P("mp", "dp"),
        P(None, "dp"),
        P("dp", "mp"),
        P(None, "dp", "mp"),
        P("mp", "dp"),
        P(None, "dp", "mp"),
        P("mp", "dp"),
        P(None, "dp"),
        P("dp", "mp"),
        P(None, "dp", "mp"),
        P("mp", "dp"),
        P(None, "dp", "mp"),
        P("mp", "dp"),
    )
    return jax.shard_map(
        on_device,
        mesh=mesh,
        in_specs=placed,
        out_specs=(
            P("dp", "mp", None),
            P("dp", "mp", None),
            P(None, "dp"),
            P("dp", "mp"),
            P(None, "dp", "mp"),
            P("mp", "dp"),
            P(None, "dp", "mp"),
            P("mp", "dp"),
            P(None, "dp"),
            P("dp", "mp"),
            P(None, "dp", "mp"),
            P("mp", "dp"),
            P(None, "dp", "mp"),
            P("mp", "dp"),
            P(None, "dp"),
            P("dp", "mp"),
            P(None, "dp", "mp"),
            P("mp", "dp"),
            P(None, "dp", "mp"),
            P("mp", "dp"),
            P(None, "dp"),
            P("dp", "mp"),
            P(None, "dp", "mp"),
            P("mp", "dp"),
            P(None, "dp", "mp"),
            P("mp", "dp"),
        ),
        check_vma=False,
    )
```

profile of v0, /device:TPU:0, one launch (start us, length us, event | category | flops | bytes accessed | tf_op | source)
XLA Modules:
  0.0 739.9 jit_solution(279391699796707430)
XLA Ops:
  14.9 88.1 %all-gather.2.cloned.1.call-done = bf16[2048,5378]{1,0:T(8,128)(2,1)} async-done(((bf16[64,5378]{1,0:T(8,128)(2,1)}), bf16[2048,5378]{1,0:T(8,128)(2,1)}) %all-gather.2.cloned.1.call-update) | async-done | bytes 22028304 | tf_op jit(solution)/shard_map/all_gather | solution.py:23
  107.4 4.5 all-to-all-start
  115.4 4.1 split.25
  119.6 19.3 %all-to-all-done = bf16[4,1,128,2048]{3,2,1,0:T(8,128)(2,1)} async-done(((bf16[4,1,128,2048]{3,2,1,0:T(8,128)(2,1)}), bf16[4,1,128,2048]{3,2,1,0:T(8,128)(2,1)}, u32[]{:S(2)}, u32[]{:S(2)}) %all-to-all-start) | async-done | bytes 2097184 | tf_op jit(solution)/shard_map/all_to_all | solution.py:41
  139.0 4.0 convolution_bitcast_fusion.1
  150.7 3.8 convolution_bitcast_fusion
  154.5 52.1 %all_to_all.45 = f32[4,128,1,2048]{3,1,2,0:T(8,128)} all-to-all(f32[4,128,1,2048]{3,1,2,0:T(8,128)S(1)} %convolution_bitcast_fusion), channel_id=1, replica_groups=mesh['dp'=32,'mp'=4] {'mp'}, dimensions={0} | all-to-all | bytes 8388608 | tf_op jit(solution)/shard_map/all_to_all | solution.py:55
  206.6 2.6 reduce_sum.135
  211.2 4.7 all-to-all-start.2
  216.8 24.5 %all-to-all-done.2 = bf16[4,1,128,2048]{3,2,1,0:T(8,128)(2,1)} async-done(((bf16[4,1,128,2048]{3,2,1,0:T(8,128)(2,1)}), bf16[4,1,128,2048]{3,2,1,0:T(8,128)(2,1)}, u32[]{:S(2)}, u32[]{:S(2)}) %all-to-all-start.2) | async-done | bytes 2097184 | tf_op jit(solution)/shard_map/all_to_all | solution.py:41
  241.3 2.7 broadcast_in_dim.105
  243.9 4.5 all-to-all-start.4
  248.4 8.0 %split.28 = bf16[2048,2816]{1,0:T(8,128)(2,1)S(1)} slice(bf16[2048,5378]{1,0:T(8,128)(2,1)} %all-gather.2.cloned.1.call-done), slice={[0:2048], [1154:3970]} | slice | bytes 23068672 | tf_op jit(solution)/shard_map/split | solution.py:24
  256.4 4.2 copy-done.2
  260.6 9.1 %fusion.20 = f32[1,512,2,1408]{3,1,2,0:T(8,128)} fusion(bf16[512,2048,1]{1,0,2:T(8,128)(2,1)} %bitcast.35, bf16[256,2,8,1408]{3,2,1,0:T(8,128)(2,1)S(1)} %bitcast.282), kind=kOutput, calls=%fused_computation.30 | convolution fusion | flops 5905580032 | bytes 19398656 | tf_op jit(solution)/shard_map/rsd,edf->rsef/dot_general | solution.py:277
  269.7 3.2 all-to-all-done.4
  272.8 9.6 %fusion.49 = (bf16[512,1,1408]{2,0,1:T(8,128)(2,1)S(1)}, bf16[512,1,1408]{2,0,1:T(8,128)(2,1)S(1)}) fusion(f32[1,512,2,1408]{3,1,2,0:T(8,128)} %fusion.20, bf16[512,2048]{1,0:T(8,128)(2,1)} %bitcast.44, bf16[2048,5378]{1,0:T(8,128)(2,1)} %all-gather.2.cloned.1.call-done), kind=kOutput, calls=%fused_computation.70 | convolution fusion | flops 2962161664 | bytes 16515072 | tf_op jit(solution)/shard_map/rsd,fd->rsf/dot_general | solution.py:294
  282.5 7.4 %bitcast_convert_fusion = bf16[512,2048]{1,0:T(8,128)(2,1)} fusion(bf16[256,2,8,1408]{3,2,1,0:T(8,128)(2,1)S(1)} %bitcast.283, bf16[512,1,1408]{2,0,1:T(8,128)(2,1)S(1)} %get-tuple-element.292, bf16[512,1,1408]{2,0,1:T(8,128)(2,1)S(1)} %get-tuple-element.291), kind=kOutput, calls=%fused_computation.34 | convolution fusion | flops 5908070400 | bytes 16515072 | tf_op jit(solution)/shard_map/nref,edf->nrd/dot_general | solution.py:309
  289.9 15.0 %all-to-all-start.5 = ((bf16[4,128,1,2048]{3,1,2,0:T(8,128)(2,1)}), bf16[4,128,1,2048]{3,1,2,0:T(8,128)(2,1)}, u32[]{:S(2)}, u32[]{:S(2)}) async-start(bf16[4,128,1,2048]{3,1,2,0:T(8,128)(2,1)} %bitcast.294), calls=%async_computation.5 | async-start | bytes 4194304 | tf_op jit(solution)/shard_map/all_to_all | solution.py:61
  304.9 9.7 %fusion.31 = bf16[512,2048]{1,0:T(8,128)(2,1)} fusion(bf16[2048,5378]{1,0:T(8,128)(2,1)} %all-gather.2.cloned.1.call-done, f32[1,512,2,1408]{3,1,2,0:T(8,128)} %fusion.20), kind=kOutput, calls=%fused_computation.45 | convolution fusion | flops 2958163968 | bytes 13631488 | tf_op jit(solution)/shard_map/nrf,fd->nrd/dot_general | solution.py:286
  314.6 13.6 %all-to-all-done.5 = bf16[4,128,1,2048]{3,1,2,0:T(8,128)(2,1)} async-done(((bf16[4,128,1,2048]{3,1,2,0:T(8,128)(2,1)}), bf16[4,128,1,2048]{3,1,2,0:T(8,128)(2,1)}, u32[]{:S(2)}, u32[]{:S(2)}) %all-to-all-start.5) | async-done | bytes 2097184 | tf_op jit(solution)/shard_map/all_to_all | solution.py:61
  328.1 4.4 all-to-all-start.3
  335.5 19.6 %all-to-all-done.3 = bf16[4,128,1,2048]{3,1,2,0:T(8,128)(2,1)} async-done(((bf16[4,128,1,2048]{3,1,2,0:T(8,128)(2,1)}), bf16[4,128,1,2048]{3,1,2,0:T(8,128)(2,1)}, u32[]{:S(2)}, u32[]{:S(2)}) %all-to-all-start.3) | async-done | bytes 2097184 | tf_op jit(solution)/shard_map/all_to_all | solution.py:61
  360.8 3.6 all-to-all-start.6
  365.2 11.1 %convert_bitcast_fusion = bf16[2,2048,1408]{1,2,0:T(8,128)(2,1)} fusion(bf16[512,2048,1]{1,0,2:T(8,128)(2,1)} %bitcast.35, bf16[512,1,1408]{2,0,1:T(8,128)(2,1)} %copy-done.61, bf16[512,1,1408]{2,0,1:T(8,128)(2,1)} %copy-done.60), kind=kOutput, calls=%fused_computation.3 | convolution fusion | flops 5912788992 | bytes 16515072 | tf_op jit(solution)/shard_map/rsd,rsef->edf/dot_general | solution.py:302
  376.3 9.7 %all-to-all-done.6 = bf16[4,1,128,2048]{3,2,1,0:T(8,128)(2,1)S(1)} async-done(((bf16[4,1,128,2048]{3,2,1,0:T(8,128)(2,1)}), bf16[4,1,128,2048]{3,2,1,0:T(8,128)(2,1)S(1)}, u32[]{:S(2)}, u32[]{:S(2)}) %all-to-all-start.6) | async-done | bytes 2097184 | tf_op jit(solution)/shard_map/all_to_all | solution.py:41
  386.0 3.8 fusion.51
  389.8 4.9 fusion.65
  394.8 2.6 fusion.8
  397.4 2.8 fusion.24
  403.5 3.3 convolution_convert_fusion.3
  406.8 4.5 all-to-all-start.7
  411.3 9.3 %convolution_convert_fusion = bf16[1408,2048]{0,1:T(8,128)(2,1)} fusion(bf16[512,2048]{1,0:T(8,128)(2,1)} %bitcast.44, f32[1,512,2,1408]{3,1,2,0:T(8,128)} %fusion.20), kind=kOutput, calls=%fused_computation.20 | convolution fusion | flops 2959998976 | bytes 13631488 | tf_op jit(solution)/shard_map/rsf,rsd->fd/dot_general | solution.py:297
  420.6 28.9 %copy.325 = bf16[2,2048,1408]{2,0,1:T(2,128)(2,1)} copy(bf16[2,2048,1408]{1,2,0:T(8,128)(2,1)} %convert_bitcast_fusion) | data formatting | bytes 23068672 | tf_op jit(solution)/shard_map/convert_element_type | solution.py:322
  450.3 3.7 convolution_convert_fusion.2
  454.0 3.1 copy.321
  457.1 3.2 copy.322
  460.3 6.1 reshape.925
  466.4 3.2 convolution_convert_fusion.1
  475.0 2.4 maximum_bitcast_fusion
  477.5 2.7 reshape.923
  480.2 2.6 copy.318
  482.8 4.2 reshape_reshape.3
  489.7 3.8 fusion.19
  493.5 6.3 reshape.926
  503.6 31.2 %reduce-scatter.2.cloned.1.call-done = bf16[1408,64]{0,1:T(8,128)(2,1)} async-done(((bf16[1408,2048]{0,1:T(8,128)(2,1)}), bf16[1408,64]{0,1:T(8,128)(2,1)}) %reduce-scatter.2.cloned.1.call-update) | async-done | bytes 180240 | tf_op jit(solution)/shard_map/reduce_scatter | solution.py:324
  537.1 180.4 %all-reduce.6.cloned.1.call-done = (bf16[18688,128]{1,0:T(8,128)(2,1)}, bf16[2,2048,1408]{2,0,1:T(2,128)(2,1)}) async-done(((bf16[18688,128]{1,0:T(8,128)(2,1)}, bf16[2,2048,1408]{2,0,1:T(2,128)(2,1)}), (bf16[18688,128]{1,0:T(8,128)(2,1)}, bf16[2,2048,1408]{2,0,1:T(2,128)(2,1)})) %all-reduce.6.cloned.1.call-update) | async-done | bytes 16318480
  718.9 4.4 all-to-all-start.8
  (227 shorter events, 62.9 us)
Async XLA Ops:
  7.2 7.4 copy-start.58
  7.2 7.5 %copy-start.1 = (f32[1,128,2048]{2,1,0:T(8,128)S(1)}, f32[1,128,2048]{2,1,0:T(8,128)}, u32[]{:S(2)}) copy-start(f32[1,128,2048]{2,1,0:T(8,128)} %param.21) | copy-start | bytes 3145732
  7.2 95.8 %all-gather.2.cloned.1.call-start = ((), (), s32[]{:S(2)}) async-start(), calls=%async_computation.10 | async-start | bytes 23248896 | tf_op jit(solution)/shard_map/all_gather | solution.py:23
  14.8 128.4 %copy-start.50 = (f32[32]{0:T(128)}, f32[32]{0:T(128)S(1)}, u32[]{:S(2)}) copy-start(f32[32]{0:T(128)S(1)} %negate_power_fusion) | copy-start | bytes 388
  14.9 92.5 %copy-start.52 = (f32[128]{0:T(128)}, f32[128]{0:T(128)S(1)}, u32[]{:S(2)}) copy-start(f32[128]{0:T(128)S(1)} %add_rsqrt_fusion.1) | copy-start | bytes 1540
  107.4 31.6 %all-to-all-start = ((bf16[4,1,128,2048]{3,2,1,0:T(8,128)(2,1)}), bf16[4,1,128,2048]{3,2,1,0:T(8,128)(2,1)}, u32[]{:S(2)}, u32[]{:S(2)}) async-start(bf16[4,1,128,2048]{3,2,1,0:T(8,128)(2,1)} %broadcast_in_dim.100), calls=%async_computation | async-start | bytes 4194304 | tf_op jit(solution)/shard_map/all_to_all | solution.py:41
  112.1 31.1 %copy-start.47 = (f32[512]{0:T(512)}, f32[512]{0:T(512)S(1)}, u32[]{:S(2)}) copy-start(f32[512]{0:T(512)S(1)} %subtract_convert_fusion.2) | copy-start | bytes 6148
  119.6 23.4 %copy-start.24 = (bf16[2048,64]{1,0:T(8,128)(2,1)}, bf16[2048,64]{1,0:T(8,128)(2,1)S(1)}, u32[]{:S(2)}) copy-start(bf16[2048,64]{1,0:T(8,128)(2,1)S(1)} %get-tuple-element.302) | copy-start | bytes 786436
  119.6 23.3 %copy-start.26 = (bf16[2048,64]{1,0:T(8,128)(2,1)}, bf16[2048,64]{1,0:T(8,128)(2,1)S(1)}, u32[]{:S(2)}) copy-start(bf16[2048,64]{1,0:T(8,128)(2,1)S(1)} %get-tuple-element.303) | copy-start | bytes 786436
  143.0 3.8 copy-start.12
  145.6 3.4 copy-start.43
  150.5 3.9 copy-start.21
  209.6 6.4 copy-start.6
  211.2 30.1 %all-to-all-start.2 = ((bf16[4,1,128,2048]{3,2,1,0:T(8,128)(2,1)}), bf16[4,1,128,2048]{3,2,1,0:T(8,128)(2,1)}, u32[]{:S(2)}, u32[]{:S(2)}) async-start(bf16[4,1,128,2048]{3,2,1,0:T(8,128)(2,1)} %broadcast_in_dim.104), calls=%async_computation.2 | async-start | bytes 4194304 | tf_op jit(solution)/shard_map/all_to_all | solution.py:41
  243.9 28.9 %all-to-all-start.4 = ((bf16[4,1,128,2048]{3,2,1,0:T(8,128)(2,1)}), bf16[4,1,128,2048]{3,2,1,0:T(8,128)(2,1)}, u32[]{:S(2)}, u32[]{:S(2)}) async-start(bf16[4,1,128,2048]{3,2,1,0:T(8,128)(2,1)} %broadcast_in_dim.105), calls=%async_computation.4 | async-start | bytes 4194304 | tf_op jit(solution)/shard_map/all_to_all | solution.py:41
  256.4 4.2 copy-start.2
  272.8 9.6 %copy-start.3 = (bf16[2048,2816]{1,0:T(8,128)(2,1)S(1)}, bf16[2048,2816]{1,0:T(8,128)(2,1)}, u32[]{:S(2)}) copy-start(bf16[2048,2816]{1,0:T(8,128)(2,1)} %copy-done.2) | copy-start | bytes 34603012
  282.4 7.4 %copy-start.60 = (bf16[512,1,1408]{2,0,1:T(8,128)(2,1)}, bf16[512,1,1408]{2,0,1:T(8,128)(2,1)S(1)}, u32[]{:S(2)}) copy-start(bf16[512,1,1408]{2,0,1:T(8,128)(2,1)S(1)} %get-tuple-element.291) | copy-start | bytes 4325380
  282.4 7.4 %copy-start.61 = (bf16[512,1,1408]{2,0,1:T(8,128)(2,1)}, bf16[512,1,1408]{2,0,1:T(8,128)(2,1)S(1)}, u32[]{:S(2)}) copy-start(bf16[512,1,1408]{2,0,1:T(8,128)(2,1)S(1)} %get-tuple-element.292) | copy-start | bytes 4325380
  289.9 38.3 %all-to-all-start.5 = ((bf16[4,128,1,2048]{3,1,2,0:T(8,128)(2,1)}), bf16[4,128,1,2048]{3,1,2,0:T(8,128)(2,1)}, u32[]{:S(2)}, u32[]{:S(2)}) async-start(bf16[4,128,1,2048]{3,1,2,0:T(8,128)(2,1)} %bitcast.294), calls=%async_computation.5 | async-start | bytes 4194304 | tf_op jit(solution)/shard_map/all_to_all | solution.py:61
  328.1 27.0 %all-to-all-start.3 = ((bf16[4,128,1,2048]{3,1,2,0:T(8,128)(2,1)}), bf16[4,128,1,2048]{3,1,2,0:T(8,128)(2,1)}, u32[]{:S(2)}, u32[]{:S(2)}) async-start(bf16[4,128,1,2048]{3,1,2,0:T(8,128)(2,1)} %bitcast.293), calls=%async_computation.3 | async-start | bytes 4194304 | tf_op jit(solution)/shard_map/all_to_all | solution.py:61
  360.8 25.2 %all-to-all-start.6 = ((bf16[4,1,128,2048]{3,2,1,0:T(8,128)(2,1)}), bf16[4,1,128,2048]{3,2,1,0:T(8,128)(2,1)S(1)}, u32[]{:S(2)}, u32[]{:S(2)}) async-start(bf16[4,1,128,2048]{3,2,1,0:T(8,128)(2,1)} %broadcast_in_dim.106), calls=%async_computation.6 | async-start | bytes 4194304 | tf_op jit(solution)/shard_map/all_to_all | solution.py:41
  386.0 8.8 %slice-start = ((s8[8388608]{0:T(1024)(128)(4,1)}), s8[4194304]{0:T(1024)(128)(4,1)S(1)}, s32[]{:S(2)}) async-start(s8[8388608]{0:T(1024)(128)(4,1)} %bitcast.280), calls=%async_computation.13 | async-start | bytes 8388608
  389.8 5.0 slice-start.1
  394.8 8.3 %copy-start.41 = (bf16[512,64]{0,1:T(8,128)(2,1)}, bf16[512,64]{0,1:T(8,128)(2,1)S(1)}, u32[]{:S(2)}) copy-start(bf16[512,64]{0,1:T(8,128)(2,1)S(1)} %fusion.65) | copy-start | bytes 196612
  403.1 3.7 copy-start.22
  406.8 80.3 %all-to-all-start.7 = ((bf16[4,128,1,2048]{3,1,2,0:T(8,128)(2,1)}), bf16[4,128,1,2048]{3,1,2,0:T(8,128)(2,1)}, u32[]{:S(2)}, u32[]{:S(2)}) async-start(bf16[4,128,1,2048]{3,1,2,0:T(8,128)(2,1)} %bitcast.292), calls=%async_computation.7 | async-start | bytes 4194304 | tf_op jit(solution)/shard_map/all_to_all | solution.py:61
  411.2 123.5 %reduce-scatter.2.cloned.1.call-start = ((), (), s32[]{:S(2)}) async-start(), calls=%async_computation.11 | async-start | bytes 5947392 | tf_op jit(solution)/shard_map/reduce_scatter | solution.py:324
  449.6 267.9 %all-reduce.6.cloned.1.call-start = ((), (), s32[]{:S(2)}) async-start(), calls=%async_computation.12 | async-start | bytes 32636928
  460.3 6.1 copy-start.23
  460.3 6.1 copy-start.42
  471.9 8.3 %slice-start.2 = ((bf16[2048,640]{0,1:T(8,128)(2,1)}), bf16[2048,512]{0,1:T(8,128)(2,1)S(1)}, s32[]{:S(2)}) async-start(bf16[2048,640]{0,1:T(8,128)(2,1)} %copy-done.4), calls=%async_computation.15 | async-start | bytes 4194304 | tf_op jit(solution)/shard_map/slice | solution.py:352
  482.8 6.4 copy-start.32
  482.8 6.4 copy-start.53
  499.8 35.0 %copy-start.11 = (f32[1408,64]{0,1:T(8,128)S(1)}, f32[1408,64]{0,1:T(8,128)}, u32[]{:S(2)}) copy-start(f32[1408,64]{0,1:T(8,128)} %param.29) | copy-start | bytes 1081348
  503.6 223.1 %copy-start.8 = (f32[2,64,1408]{2,1,0:T(8,128)S(1)}, f32[2,64,1408]{2,1,0:T(8,128)}, u32[]{:S(2)}) copy-start(f32[2,64,1408]{2,1,0:T(8,128)} %param.28) | copy-start | bytes 2162692
  503.6 223.2 %copy-start.15 = (f32[2,64,1408]{2,1,0:T(8,128)S(1)}, f32[2,64,1408]{2,1,0:T(8,128)}, u32[]{:S(2)}) copy-start(f32[2,64,1408]{2,1,0:T(8,128)} %param.40) | copy-start | bytes 2162692
  503.6 223.2 %copy-start.16 = (f32[2,64,1408]{2,1,0:T(8,128)S(1)}, f32[2,64,1408]{2,1,0:T(8,128)}, u32[]{:S(2)}) copy-start(f32[2,64,1408]{2,1,0:T(8,128)} %param.34) | copy-start | bytes 2162692
  718.9 12.1 %all-to-all-start.8 = ((f32[4,1,128]{2,1,0:T(1,128)}), f32[4,1,128]{2,1,0:T(1,128)S(1)}, u32[]{:S(2)}, u32[]{:S(2)}) async-start(f32[4,1,128]{2,1,0:T(1,128)} %reshape.949), calls=%async_computation.8 | async-start | bytes 4096 | tf_op jit(solution)/shard_map/all_to_all | solution.py:41
  724.3 4.3 copy-start.20
  725.2 5.1 copy-start.29
  725.5 4.0 copy-start.17
  726.9 3.4 copy-start.28
  726.9 3.4 copy-start.45
  726.9 3.4 copy-start.46
  726.9 5.4 copy-start.55
  726.9 5.4 copy-start.56
  726.9 5.4 copy-start.57
  (28 other events, 49.7 us)
Sparse Core Ops, SparseCore 0:
  14.7 88.2 all-gather.1
  449.7 85.0 reduce-scatter.1
  539.2 178.2 all-reduce.5
where the time goes:
time: 753 us; the launch traced here: 740 us
  waiting for transfers between devices  390 us (52%)
  local copies, waits for them, and re-layouts  100 us (13%)
  matrix products  90.6 us (12%)
  blocking collectives  52.1 us (7%)
  starting transfers between devices  45.7 us (6%)
  other arithmetic  45.1 us (6%)
  between operations  16.6 us (2%)
    unnamed x4, waiting for transfers between devices  180 us
    all_gather x1, waiting for transfers between devices, rows_first(): out = lax.all_gather(both, axis, axis=0, tiled=True)  88.1 us
    all_to_all x5, waiting for transfers between devices, copy_for_each(): return lax.all_to_all(copies, axis, split_axis=0, concat_axis=0, tiled=True)  56.7 us
    all_to_all x1, blocking collectives, summed_on_arrival(): lax.all_to_all(pieces, axis, split_axis=0, concat_axis=0, tiled=True)  52.1 us
    all_to_all x3, waiting for transfers between devices, summed_on_arrival_2(): lax.all_to_all(pieces, axis, split_axis=0, concat_axis=0, tiled=True)  33.2 us
    reduce_scatter x1, waiting for transfers between devices, on_device(): lax.psum_scatter(grad_down.astype(jnp.bfloat16), 'dp', scatter_dimension=...  31.2 us
    convert_element_type x1, local copies, waits for them, and re-layouts, on_device(): grad_gateup_weight.astype(jnp.bfloat16)  28.9 us
    all_to_all x3, starting transfers between devices, summed_on_arrival_2(): lax.all_to_all(pieces, axis, split_axis=0, concat_axis=0, tiled=True)  23.9 us
  transfers between devices with their start and end apart: 11, of which 9 were waited for; matrix products, arithmetic and copies ran while one was open for 20% of the time, Pallas kernels for 0%

commit v1 on v0

v1 whole, which is shorter than its diff:
```python
import functools

import jax
import jax.numpy as jnp
from jax import lax
from jax.experimental import pallas as pl
from jax.experimental.pallas import tpu as pltpu
from jax.sharding import PartitionSpec as P

HEAD_DIM = 64
HEADS_LOCAL = 8
QUERY_COLS = 512
QKV_COLS = 640
HIDDEN = 1408
SEQ = 512
PART = 128
D = 2048
STEP = 10

EPS = 1e-05
THETA = 10000.0
BETA_ONE = 0.9
BETA_TWO = 0.95
ADAM_EPS = 1e-08
RATES = (1.0, 0.05, 0.05, 0.5, 0.05, 0.025)
DECAYS = (0.0, 0.1, 0.1, 0.1, 0.1, 0.1)
SIDE = 4
BF16 = jnp.bfloat16
F32 = jnp.float32


def shift_z(x, by):
    return lax.ppermute(x, "mp", [(i, (i + by) % SIDE) for i in range(SIDE)])


def dp_index(y, x, core):
    return (y * SIDE + x) * 2 + core


def shift_x(a, by):
    pairs = [
        (dp_index(y, x, c), dp_index(y, (x + by) % SIDE, c))
        for y in range(SIDE)
        for x in range(SIDE)
        for c in range(2)
    ]
    return lax.ppermute(a, "dp", pairs)


def shift_y(a, by):
    pairs = [
        (dp_index(y, x, c), dp_index((y + by) % SIDE, x, c))
        for y in range(SIDE)
        for x in range(SIDE)
        for c in range(2)
    ]
    return lax.ppermute(a, "dp", pairs)


def swap_core(a):
    return lax.ppermute(a, "dp", [(i, i ^ 1) for i in range(32)])


def place():
    i = lax.axis_index("dp")
    return i // (2 * SIDE), (i // 2) % SIDE, i % 2


def gather_z(x):
    half = x.shape[0] // 2
    before = shift_z(x, 1)
    after = shift_z(x, -1)
    far_top = shift_z(before[:half], 1)
    far_bottom = shift_z(after[half:], -1)
    return jnp.concatenate([x, before, after, far_top, far_bottom], axis=0)


def scatter_z(parts):
    own, before, after, far = (parts[k * PART : (k + 1) * PART] for k in range(4))
    half = PART // 2
    far_low = far.astype(BF16)
    got_top = shift_z(far_low[:half], 1)
    got_bottom = shift_z(far_low[half:], -1)
    to_after = jnp.concatenate([after[:half] + got_top.astype(F32), after[half:]], axis=0)
    to_before = jnp.concatenate([before[:half], before[half:] + got_bottom.astype(F32)], axis=0)
    from_before = shift_z(to_after.astype(BF16), 1)
    from_after = shift_z(to_before.astype(BF16), -1)
    return own + from_before.astype(F32) + from_after.astype(F32)


def spread(x, move, at):
    out = jnp.zeros((SIDE, *x.shape), x.dtype)
    out = lax.dynamic_update_index_in_dim(out, x, at, 0)
    for by in (1, -1, 2):
        out = lax.dynamic_update_index_in_dim(out, move(x, by), (at - by) % SIDE, 0)
    return out


def gather_dp(x, first):
    y, xx, core = place()
    if first == "x":
        blocks = spread(spread(x, shift_x, xx), shift_y, y)
    else:
        blocks = jnp.swapaxes(spread(spread(x, shift_y, y), shift_x, xx), 0, 1)
    blocks = blocks.reshape(SIDE * SIDE, *x.shape)
    other = swap_core(blocks)
    pair = jnp.zeros((SIDE * SIDE, 2, *x.shape), x.dtype)
    pair = lax.dynamic_update_index_in_dim(pair, blocks, core, 1)
    pair = lax.dynamic_update_index_in_dim(pair, other, 1 - core, 1)
    return pair.reshape(-1, x.shape[1])


def collect(x, move, at, dim):
    total = lax.dynamic_index_in_dim(x, at, dim, keepdims=False).astype(F32)
    for by in (1, -1, 2):
        piece = lax.dynamic_index_in_dim(x, (at + by) % SIDE, dim, keepdims=False)
        total = total + move(piece, by).astype(F32)
    return total


def scatter_dp(g, first):
    y, xx, core = place()
    n = g.shape[1]
    blocks = g.reshape(SIDE, SIDE, 2, 64, n)
    mine = lax.dynamic_index_in_dim(blocks, core, 2, keepdims=False)
    other = lax.dynamic_index_in_dim(blocks, 1 - core, 2, keepdims=False)
    both = (mine.astype(F32) + swap_core(other).astype(F32)).astype(BF16)
    if first == "x":
        line = collect(both, shift_x, xx, 1).astype(BF16)
        return collect(line, shift_y, y, 0)
    line = collect(both, shift_y, y, 0).astype(BF16)
    return collect(line, shift_x, xx, 0)


def turn(x, cosine, sine):
    lane = lax.broadcasted_iota(jnp.int32, x.shape, 1)
    ahead = pltpu.roll(x, 96, 1)
    behind = pltpu.roll(x, 32, 1)
    return x * cosine + jnp.where(lane % HEAD_DIM < HEAD_DIM // 2, ahead, behind) * sine


def nt(a, b):
    return lax.dot_general(a, b, (((1,), (1,)), ((), ())), preferred_element_type=F32)


def tn(a, b):
    return lax.dot_general(a, b, (((0,), (0,)), ((), ())), preferred_element_type=F32)


def nn(a, b):
    return lax.dot_general(a, b, (((1,), (0,)), ((), ())), preferred_element_type=F32)


def make_bias(tok_q, tok_k, seg_q, seg_k):
    allowed = (seg_q == seg_k) & (tok_k <= tok_q)
    return jnp.where(allowed, 0.0, -1e30)


def forward_kernel(
    qkv_ref, cos_ref, sin_ref, tokq_ref, tokk_ref, segq_ref, segk_ref,
    att_ref, q_ref, kv_ref, lse_ref, bias_ref,
):
    cosine, sine = cos_ref[...], sin_ref[...]
    for pair in range(HEADS_LOCAL // 2):
        cols = slice(pair * 128, pair * 128 + 128)
        q_ref[:, cols] = (turn(qkv_ref[:, cols], cosine, sine).astype(BF16)) * BF16(0.125)
    kv = qkv_ref[:, QUERY_COLS:QKV_COLS]
    lane = lax.broadcasted_iota(jnp.int32, kv.shape, 1)
    kv = jnp.where(lane < HEAD_DIM, turn(kv, cosine, sine), kv).astype(BF16)
    kv_ref[...] = kv
    keys, values = kv[:, :HEAD_DIM], kv[:, HEAD_DIM:]
    bias_ref[...] = make_bias(tokq_ref[...], tokk_ref[...], segq_ref[...], segk_ref[...])
    for block in range(SEQ // PART):
        rows = slice(block * PART, block * PART + PART)
        bias = bias_ref[rows, :]
        outs, sums = [], []
        for h in range(HEADS_LOCAL):
            q = q_ref[rows, h * HEAD_DIM : (h + 1) * HEAD_DIM]
            s = nt(q, keys) + bias
            top = jnp.max(s, axis=1, keepdims=True)
            e = jnp.exp(s - top)
            total = jnp.sum(e, axis=1, keepdims=True)
            p = (e * (1.0 / total)).astype(BF16)
            outs.append(nn(p, values).astype(BF16))
            sums.append(top + jnp.log(total))
        att_ref[rows, :] = jnp.concatenate(outs, axis=1)
        lse_ref[rows, :] = jnp.concatenate(sums, axis=1)


def backward_kernel(
    q_ref, kv_ref, lse_ref, up_ref, cos_ref, sin_ref, tokq_ref, tokk_ref, segq_ref, segk_ref,
    out_ref, bias_ref, dkv_ref,
):
    cosine, sine = cos_ref[...], -sin_ref[...]
    kv = kv_ref[...]
    keys, values = kv[:, :HEAD_DIM], kv[:, HEAD_DIM:]
    bias_ref[...] = make_bias(tokq_ref[...], tokk_ref[...], segq_ref[...], segk_ref[...])
    dkv_ref[...] = jnp.zeros_like(dkv_ref)
    for block in range(SEQ // PART):
        rows = slice(block * PART, block * PART + PART)
        bias = bias_ref[rows, :]
        dqs = []
        dk = jnp.zeros((SEQ, HEAD_DIM), F32)
        dv = jnp.zeros((SEQ, HEAD_DIM), F32)
        for h in range(HEADS_LOCAL):
            cols = slice(h * HEAD_DIM, (h + 1) * HEAD_DIM)
            q, up = q_ref[rows, cols], up_ref[rows, cols]
            s = nt(q, keys) + bias
            p = jnp.exp(s - lse_ref[rows, h : h + 1])
            dp = nt(up, values)
            inner = jnp.sum(p * dp, axis=1, keepdims=True)
            ds = (p * (dp - inner)).astype(BF16)
            dqs.append(nn(ds, keys) * 0.125)
            dk = dk + tn(ds, q)
            dv = dv + tn(p.astype(BF16), up)
        dkv_ref[...] += jnp.concatenate([dk, dv], axis=1)
        for pair in range(HEADS_LOCAL // 2):
            dq = jnp.concatenate(dqs[2 * pair : 2 * pair + 2], axis=1)
            dq = turn(dq, cosine[rows], sine[rows])
            out_ref[rows, pair * 128 : pair * 128 + 128] = dq.astype(BF16)
    dkv = dkv_ref[...]
    lane = lax.broadcasted_iota(jnp.int32, dkv.shape, 1)
    dkv = jnp.where(lane < HEAD_DIM, turn(dkv, cosine, sine), dkv)
    out_ref[:, QUERY_COLS:QKV_COLS] = dkv.astype(BF16)


def whole(n):
    return [pl.BlockSpec(memory_space=pltpu.VMEM)] * n


def attend_forward(qkv, tables):
    return pl.pallas_call(
        forward_kernel,
        out_shape=(
            jax.ShapeDtypeStruct((SEQ, QUERY_COLS), BF16),
            jax.ShapeDtypeStruct((SEQ, QUERY_COLS), BF16),
            jax.ShapeDtypeStruct((SEQ, 128), BF16),
            jax.ShapeDtypeStruct((SEQ, HEADS_LOCAL), F32),
        ),
        in_specs=whole(7),
        out_specs=whole(4),
        scratch_shapes=[pltpu.VMEM((SEQ, SEQ), F32)],
        compiler_params=pltpu.CompilerParams(vmem_limit_bytes=24 * 2**20),
        cost_estimate=pl.CostEstimate(
            flops=4 * HEADS_LOCAL * SEQ * SEQ * HEAD_DIM,
            bytes_accessed=4 * 2**20,
            transcendentals=HEADS_LOCAL * SEQ * SEQ,
        ),
    )(qkv, *tables)


def attend_backward(q, kv, lse, upstream, tables):
    return pl.pallas_call(
        backward_kernel,
        out_shape=jax.ShapeDtypeStruct((SEQ, QKV_COLS), BF16),
        in_specs=whole(10),
        out_specs=pl.BlockSpec(memory_space=pltpu.VMEM),
        scratch_shapes=[pltpu.VMEM((SEQ, SEQ), F32), pltpu.VMEM((SEQ, 128), F32)],
        compiler_params=pltpu.CompilerParams(vmem_limit_bytes=24 * 2**20),
        cost_estimate=pl.CostEstimate(
            flops=10 * HEADS_LOCAL * SEQ * SEQ * HEAD_DIM,
            bytes_accessed=4 * 2**20,
            transcendentals=HEADS_LOCAL * SEQ * SEQ,
        ),
    )(q, kv, lse, upstream, *tables)


def attention_tables(lengths):
    z = lax.axis_index("mp")
    block = jnp.stack([z, (z + 3) % SIDE, (z + 1) % SIDE, (z + 2) % SIDE])
    token = (block[:, None] * PART + jnp.arange(PART)[None, :]).reshape(SEQ)
    boundary = jnp.cumsum(lengths)
    starts = boundary - lengths
    segment = jnp.sum((token[:, None] >= boundary[None, :]).astype(jnp.int32), axis=1)
    leading = jnp.max(jnp.where(starts[None, :] <= token[:, None], starts[None, :], 0), axis=1)
    indices = jnp.arange(HEAD_DIM // 2).astype(F32)
    frequency = 1.0 / THETA ** (2.0 * indices / HEAD_DIM)
    angles = (token - leading).astype(F32)[:, None] * frequency[None, :]
    cosine, sine = jnp.cos(angles), jnp.sin(angles)
    cosine = jnp.concatenate([cosine] * 4, axis=1)
    sine = jnp.concatenate([-sine, sine, -sine, sine], axis=1)
    return (cosine, sine, token[:, None], token[None, :], segment[:, None], segment[None, :])


def adamw(weight, gradient, moment, square, rate, decay):
    momentum = BETA_ONE * moment + (1.0 - BETA_ONE) * gradient
    variance = BETA_TWO * square + (1.0 - BETA_TWO) * gradient * gradient
    moment_hat = momentum / (1.0 - BETA_ONE**STEP)
    square_hat = variance / (1.0 - BETA_TWO**STEP)
    updated = weight - rate * (moment_hat / (jnp.sqrt(square_hat) + ADAM_EPS) + decay * weight)
    return (momentum, variance, updated)


def inverse_rms(v):
    return lax.rsqrt(jnp.mean(v * v, axis=-1, keepdims=True) + EPS)


def norm_backward(v, inverse, upstream):
    inner = jnp.mean(upstream * v, axis=-1, keepdims=True)
    return inverse * upstream - v * (inverse * inverse * inverse * inner)


def after(x, *others):
    return lax.optimization_barrier((x, *others))[0]


def on_device(
    residual, cotangent, document_lengths,
    norm_gains, query_weight, keyvalue_weight, output_weight, gateup_weight, down_weight,
    moment_gains, moment_query, moment_keyvalue, moment_output, moment_gateup, moment_down,
    square_gains, square_query, square_keyvalue, square_output, square_gateup, square_down,
):
    residual, cotangent = residual[0], cotangent[0]
    low_gains = norm_gains.astype(BF16).astype(F32)
    gain_one, gain_two = low_gains[0][:, None], low_gains[1][:, None]
    low_qkv = jnp.concatenate(
        (query_weight, keyvalue_weight[0], keyvalue_weight[1]), axis=1
    ).astype(BF16)
    low_gateup = jnp.concatenate((gateup_weight[0], gateup_weight[1]), axis=1).astype(BF16)
    low_output = output_weight.astype(BF16).T
    low_down = down_weight.astype(BF16).T

    scaled_qkv = (low_qkv.astype(F32) * gain_one).astype(BF16)
    scaled_gateup = (low_gateup.astype(F32) * gain_two).astype(BF16)

    ffn_full = lax.all_gather(
        jnp.concatenate((scaled_gateup, low_down), axis=1), "dp", axis=0, tiled=True
    )
    gateup_full = ffn_full[:, : 2 * HIDDEN]
    down_full = ffn_full[:, 2 * HIDDEN :]
    qkv_full = gather_dp(scaled_qkv, "x")
    output_full = gather_dp(low_output, "y")

    inverse_one = inverse_rms(residual)
    rows_one = gather_z((residual * inverse_one).astype(BF16))
    tables = attention_tables(document_lengths[0])
    attended, q, kv, lse = attend_forward(nn(rows_one, qkv_full), tables)
    attention = scatter_z(nt(attended, output_full))
    middle = residual + attention
    inverse_two = inverse_rms(middle)
    rows_two = gather_z((middle * inverse_two).astype(BF16))
    cot_rows = gather_z(after(cotangent.astype(BF16), rows_one))

    gate_up = nn(rows_two, gateup_full)
    gate, up = gate_up[:, :HIDDEN], gate_up[:, HIDDEN:]
    sigmoid = jax.nn.sigmoid(gate)
    activated = gate * sigmoid
    hidden = (activated * up).astype(BF16)
    grad_hidden = nn(cot_rows, down_full)
    slope = sigmoid * (1.0 + gate * (1.0 - sigmoid))
    grad_gate = (grad_hidden * up * slope).astype(BF16)
    grad_up = (grad_hidden * activated).astype(BF16)
    grad_gateup = jnp.concatenate((grad_gate, grad_up), axis=1)

    grad_normed_two = scatter_z(nt(grad_gateup, gateup_full))
    grad_down = lax.psum_scatter(
        tn(cot_rows, hidden).astype(BF16), "dp", scatter_dimension=0, tiled=True
    ).astype(F32)
    grad_ffn = lax.psum_scatter(
        tn(rows_two, grad_gateup).astype(BF16), "dp", scatter_dimension=0, tiled=True
    ).astype(F32)
    feedfwd = scatter_z(nt(hidden, down_full))
    block_output = middle + feedfwd

    grad_middle = cotangent + norm_backward(middle, inverse_two, grad_normed_two)
    attention_rows = gather_z(grad_middle.astype(BF16))
    grad_attended = nn(attention_rows, output_full).astype(BF16)
    grad_output = scatter_dp(tn(attention_rows, attended).astype(BF16), "y")
    grad_projected = attend_backward(q, kv, lse, grad_attended, tables)
    grad_qkv = scatter_dp(tn(rows_one, grad_projected).astype(BF16), "x")
    grad_normed_one = scatter_z(nt(grad_projected, qkv_full))
    input_gradient = grad_middle + norm_backward(residual, inverse_one, grad_normed_one)

    gain_parts = jnp.stack(
        (
            jnp.sum(low_qkv.astype(F32) * grad_qkv, axis=1),
            jnp.sum(low_gateup.astype(F32) * grad_ffn, axis=1),
        )
    )
    gains = gain_parts + shift_z(gain_parts, 1) + shift_z(gain_parts, -1) + shift_z(gain_parts, 2)
    grad_qkv = grad_qkv * gain_one
    grad_ffn = grad_ffn * gain_two
    reduced = (
        gains,
        grad_qkv[:, :QUERY_COLS],
        jnp.stack((grad_qkv[:, QUERY_COLS : QUERY_COLS + 64], grad_qkv[:, QUERY_COLS + 64 :])),
        grad_output.T,
        jnp.stack((grad_ffn[:, :HIDDEN], grad_ffn[:, HIDDEN:])),
        grad_down.T,
    )
    masters = (norm_gains, query_weight, keyvalue_weight, output_weight, gateup_weight, down_weight)
    moments = (
        moment_gains, moment_query, moment_keyvalue, moment_output, moment_gateup, moment_down,
    )
    squares = (
        square_gains, square_query, square_keyvalue, square_output, square_gateup, square_down,
    )
    results = [
        adamw(masters[i], reduced[i], moments[i], squares[i], RATES[i], DECAYS[i]) for i in range(6)
    ]
    return (
        block_output[None],
        input_gradient[None],
        *reduced,
        *(r[0] for r in results),
        *(r[1] for r in results),
        *(r[2] for r in results),
    )


def solution(mesh):
    rows = P("dp", "mp", None)
    weights = (
        P(None, "dp"),
        P("dp", "mp"),
        P(None, "dp", "mp"),
        P("mp", "dp"),
        P(None, "dp", "mp"),
        P("mp", "dp"),
    )
    return jax.shard_map(
        on_device,
        mesh=mesh,
        in_specs=(rows, rows, P("dp", None), *weights, *weights, *weights),
        out_specs=(rows, rows, *weights, *weights, *weights, *weights),
        check_vma=False,
    )
```

time: 753 us -> 416 us (0.55)
  waiting for transfers between devices: 390 us -> 174 us
  local copies, waits for them, and re-layouts: 100 us -> 17.9 us
  blocking collectives: 52.1 us -> 0 us
  starting transfers between devices: 45.7 us -> 89.5 us
  matrix products: 90.6 us -> 62.1 us
  Pallas kernels: 0 us -> 26.1 us
  other arithmetic: 45.1 us -> 22.8 us
    unnamed x4 -> x3, waiting for transfers between devices: 180 us -> 0.05 us
    ppermute x0 -> x63, waiting for transfers between devices: none -> 155 us  [the longest x35 88.6 us: shift_z(): return lax.ppermute(x, 'mp', [(i, (i + by) % SIDE) for i in range(SIDE)])]
    all_to_all x8 -> x0, waiting for transfers between devices: 89.9 us -> none  [the longest x5 56.7 us: copy_for_each(): return lax.all_to_all(copies, axis, split_axis=0, concat_axis=0, tiled=True)]
    ppermute x0 -> x63, starting transfers between devices: none -> 89.2 us  [the longest x35 58.4 us: shift_z(): return lax.ppermute(x, 'mp', [(i, (i + by) % SIDE) for i in range(SIDE)])]
    all_gather x1, waiting for transfers between devices: 88.1 us -> 0.01 us  [on_device(): lax.all_gather(jnp.concatenate((scaled_gateup, low_down), axis=1), 'dp',...]
    all_to_all x1 -> x0, blocking collectives: 52.1 us -> none  [summed_on_arrival(): lax.all_to_all(pieces, axis, split_axis=0, concat_axis=0, tiled=True)]
    all_to_all x8 -> x0, starting transfers between devices: 45.6 us -> none  [the longest x3 23.9 us: summed_on_arrival_2(): lax.all_to_all(pieces, axis, split_axis=0, concat_axis=0, tiled=True)]
    convert_element_type x8 -> x0, local copies, waits for them, and re-layouts: 32.5 us -> none  [the longest x1 28.9 us: on_device(): grad_gateup_weight.astype(jnp.bfloat16)]
  transfers between devices with their start and end apart: 11 -> 66, of which waited for: 9 -> 34; matrix products, arithmetic and copies ran while one was open for 20% -> 17% of each run, Pallas kernels for 0% -> 6%
where the time goes in v1:
time: 416 us; the launch traced here: 408 us
  waiting for transfers between devices  174 us (42%)
  starting transfers between devices  89.5 us (22%)
  matrix products  62.1 us (15%)
  Pallas kernels  26.1 us (6%)
  other arithmetic  22.8 us (5%)
  local copies, waits for them, and re-layouts  17.9 us (4%)
  between operations  15.6 us (4%)
    ppermute x35, waiting for transfers between devices, shift_z(): return lax.ppermute(x, 'mp', [(i, (i + by) % SIDE) for i in range(SIDE)])  88.6 us
    ppermute x35, starting transfers between devices, shift_z(): return lax.ppermute(x, 'mp', [(i, (i + by) % SIDE) for i in range(SIDE)])  58.4 us
    ppermute x12, waiting for transfers between devices, shift_x(): return lax.ppermute(a, 'dp', pairs)  34.4 us
    ppermute x12, waiting for transfers between devices, shift_y(): return lax.ppermute(a, 'dp', pairs)  32.4 us
    dot_general x4, matrix products, nn(): lax.dot_general(a, b, (((1,), (0,)), ((), ())), preferred_element_type=F32)  23.5 us
    ppermute x12, starting transfers between devices, shift_y(): return lax.ppermute(a, 'dp', pairs)  19.9 us
    dot_general x4, matrix products, tn(): lax.dot_general(a, b, (((0,), (0,)), ((), ())), preferred_element_type=F32)  19.5 us
    dot_general x4, matrix products, nt(): lax.dot_general(a, b, (((1,), (1,)), ((), ())), preferred_element_type=F32)  19.1 us
  transfers between devices with their start and end apart: 66, of which 34 were waited for; matrix products, arithmetic and copies ran while one was open for 17% of the time, Pallas kernels for 6%

profile of v1, /device:TPU:0, one launch (start us, length us, event | category | flops | bytes accessed | tf_op | source)
XLA Modules:
  0.0 407.9 jit_solution(9827012866256522634)
XLA Ops:
  12.0 3.2 collective-permute-start.12
  17.6 3.1 collective-permute-start.6
  26.2 4.1 %collective-permute-start.1 = (bf16[128,2048]{1,0:T(8,128)(2,1)S(1)}, bf16[128,2048]{1,0:T(8,128)(2,1)S(1)}, u32[]{:S(2)}, u32[]{:S(2)}) collective-permute-start(bf16[128,2048]{1,0:T(8,128)(2,1)S(1)} %get-tuple-element.70), channel_id=1, source_target_pairs={{0,3},{1,0},{2,1},{3,2},{4,7},{5,4},{6,5},{7,6},{8,11},{9,8},{10,9... | collective-permute-start | bytes 1572872 | tf_op jit(solution)/shard_map/ppermute | solution.py:33
  35.2 14.2 %collective-permute-done.14 = bf16[4,64,512]{2,1,0:T(8,128)(2,1)S(1)} collective-permute-done((bf16[4,64,512]{2,1,0:T(8,128)(2,1)S(1)}, bf16[4,64,512]{2,1,0:T(8,128)(2,1)S(1)}, u32[]{:S(2)}, u32[]{:S(2)}) %collective-permute-start.14) | collective-permute-done | bytes 262176 | tf_op jit(solution)/shard_map/ppermute | solution.py:47
  49.4 2.9 collective-permute-start.9
  54.9 22.3 %collective-permute-done.7 = bf16[4,64,640]{2,1,0:T(8,128)(2,1)S(1)} collective-permute-done((bf16[4,64,640]{2,1,0:T(8,128)(2,1)S(1)}, bf16[4,64,640]{2,1,0:T(8,128)(2,1)S(1)}, u32[]{:S(2)}, u32[]{:S(2)}) %collective-permute-start.7) | collective-permute-done | bytes 327712 | tf_op jit(solution)/shard_map/ppermute | solution.py:57
  78.5 3.1 collective-permute-start.3
  82.0 9.1 %collective-permute-done.2 = bf16[64,2048]{1,0:T(8,128)(2,1)S(1)} collective-permute-done((bf16[64,2048]{1,0:T(8,128)(2,1)S(1)}, bf16[64,2048]{1,0:T(8,128)(2,1)S(1)}, u32[]{:S(2)}, u32[]{:S(2)}) %collective-permute-start.2) | collective-permute-done | bytes 262176 | tf_op jit(solution)/shard_map/ppermute | solution.py:33
  94.6 11.9 %shard_map.404 = (bf16[512,512]{1,0:T(8,128)(2,1)S(1)}, bf16[512,512]{1,0:T(8,128)(2,1)S(1)}, bf16[512,128]{1,0:T(8,128)(2,1)S(1)}, f32[512,8]{1,0:T(8,128)S(1)}) custom-call(f32[512,640]{1,0:T(8,128)S(1)} %fusion.79.qkv_ref, f32[512,128]{1,0:T(8,128)S(1)} %get-tuple-element.141.cos_ref, f32[512,128]{1,0:T(8,128)S(1)} %get-tuple-element.142.sin_ref, ...), custom_call_target="tpu_custom_call" | custom-call | flops 536870912 | bytes 4194304 | tf_op jit(solution)/shard_map/pallas_call | solution.py:232
  108.0 3.2 collective-permute-start.20
  113.3 5.0 %collective-permute-done.18 = bf16[64,2048]{1,0:T(8,128)(2,1)S(1)} collective-permute-done((bf16[64,2048]{1,0:T(8,128)(2,1)S(1)}, bf16[64,2048]{1,0:T(8,128)(2,1)S(1)}, u32[]{:S(2)}, u32[]{:S(2)}) %collective-permute-start.18) | collective-permute-done | bytes 262176 | tf_op jit(solution)/shard_map/ppermute | solution.py:33
  118.6 3.3 collective-permute-start.21
  122.1 7.1 %collective-permute-done.31 = bf16[128,2048]{1,0:T(8,128)(2,1)S(1)} collective-permute-done((bf16[128,2048]{1,0:T(8,128)(2,1)S(1)}, bf16[128,2048]{1,0:T(8,128)(2,1)S(1)}, u32[]{:S(2)}, u32[]{:S(2)}) %collective-permute-start.31) | collective-permute-done | bytes 524320 | tf_op jit(solution)/shard_map/ppermute | solution.py:33
  129.2 4.2 %collective-permute-start.33 = (bf16[64,2048]{1,0:T(8,128)(2,1)S(1)}, bf16[64,2048]{1,0:T(8,128)(2,1)S(1)}, u32[]{:S(2)}, u32[]{:S(2)}) collective-permute-start(bf16[64,2048]{1,0:T(8,128)(2,1)S(1)} %slice.282), channel_id=1, source_target_pairs={{0,3},{1,0},{2,1},{3,2},{4,7},{5,4},{6,5},{7,6},{8,11},{9,8},{10,9... | collective-permute-start | bytes 786440 | tf_op jit(solution)/shard_map/ppermute | solution.py:33
  133.5 6.9 %collective-permute-done.21 = bf16[128,2048]{1,0:T(8,128)(2,1)S(1)} collective-permute-done((bf16[128,2048]{1,0:T(8,128)(2,1)S(1)}, bf16[128,2048]{1,0:T(8,128)(2,1)S(1)}, u32[]{:S(2)}, u32[]{:S(2)}) %collective-permute-start.21) | collective-permute-done | bytes 524320 | tf_op jit(solution)/shard_map/ppermute | solution.py:33
  142.4 3.2 collective-permute-start.23
  146.1 9.2 %collective-permute-done.23 = bf16[128,2048]{1,0:T(8,128)(2,1)S(1)} collective-permute-done((bf16[128,2048]{1,0:T(8,128)(2,1)S(1)}, bf16[128,2048]{1,0:T(8,128)(2,1)S(1)}, u32[]{:S(2)}, u32[]{:S(2)}) %collective-permute-start.23) | collective-permute-done | bytes 524320 | tf_op jit(solution)/shard_map/ppermute | solution.py:33
  155.3 3.8 collective-permute-start.25
  160.8 5.9 %collective-permute-done.24 = bf16[64,2048]{1,0:T(8,128)(2,1)S(1)} collective-permute-done((bf16[64,2048]{1,0:T(8,128)(2,1)S(1)}, bf16[64,2048]{1,0:T(8,128)(2,1)S(1)}, u32[]{:S(2)}, u32[]{:S(2)}) %collective-permute-start.24) | collective-permute-done | bytes 262176 | tf_op jit(solution)/shard_map/ppermute | solution.py:33
  168.2 10.3 %fusion.2 = f32[512,2816]{1,0:T(8,128)S(1)} fusion(bf16[512,2048]{1,0:T(8,128)(2,1)} %constant_dynamic-update-slice_fusion.5, bf16[2048,4224]{1,0:T(8,128)(2,1)} %all-gather.2.cloned.1.call-done), kind=kOutput, calls=%fused_computation.3 | convolution fusion | flops 5905580032 | bytes 19398656 | tf_op jit(solution)/shard_map/dot_general | solution.py:151
  178.5 8.6 %multiply_convert_fusion.1 = (bf16[512,1408]{1,0:T(8,128)(2,1)}, bf16[512,1408]{1,0:T(8,128)(2,1)}, bf16[512,1408]{1,0:T(8,128)(2,1)S(1)}) fusion(f32[512,2816]{1,0:T(8,128)S(1)} %fusion.2, bf16[512,2048]{1,0:T(8,128)(2,1)S(1)} %copy-done.37, bf16[2048,4224]{1,0:T(8,128)(2,1)} %all-gather.2.cloned.1.call-done), kind=kOutput, calls=%fused_computation.14 | convolution fusion | flops 2963603456 | bytes 17956864 | tf_op jit(solution)/shard_map/dot_general | solution.py:151
  188.2 5.3 %convolution_convert_fusion.1 = bf16[2048,1408]{1,0:T(8,128)(2,1)} fusion(bf16[512,2048]{1,0:T(8,128)(2,1)S(1)} %copy-done.37, bf16[512,1408]{1,0:T(8,128)(2,1)S(1)} %get-tuple-element.73), kind=kOutput, calls=%fused_computation.5 | convolution fusion | flops 2955673600 | bytes 9306112 | tf_op jit(solution)/shard_map/dot_general | solution.py:147
  193.7 11.1 %convolution_convert_fusion = bf16[2048,2816]{1,0:T(8,128)(2,1)} fusion(bf16[512,2048]{1,0:T(8,128)(2,1)} %constant_dynamic-update-slice_fusion.5, bf16[512,1408]{1,0:T(8,128)(2,1)} %get-tuple-element.72, bf16[512,1408]{1,0:T(8,128)(2,1)} %get-tuple-element.71), kind=kOutput, calls=%fused_computation | convolution fusion | flops 5917114368 | bytes 16515072 | tf_op jit(solution)/shard_map/dot_general | solution.py:147
  204.9 6.1 %fusion.77 = (bf16[512,2048]{1,0:T(8,128)(2,1)S(1)}, f32[512,2048]{1,0:T(8,128)S(1)}) fusion(bf16[512,1408]{1,0:T(8,128)(2,1)} %copy-done.55, bf16[2048,4224]{1,0:T(8,128)(2,1)} %all-gather.2.cloned.1.call-done), kind=kOutput, calls=%fused_computation.230 | convolution fusion | flops 2953838592 | bytes 13500416 | tf_op jit(solution)/shard_map/dot_general | solution.py:143
  211.2 3.2 collective-permute-start.28
  214.4 9.7 %fusion.76 = (bf16[512,2048]{1,0:T(8,128)(2,1)S(1)}, f32[512,2048]{1,0:T(8,128)S(1)}) fusion(bf16[2048,4224]{1,0:T(8,128)(2,1)} %all-gather.2.cloned.1.call-done, bf16[512,1408]{1,0:T(8,128)(2,1)} %get-tuple-element.72, bf16[512,1408]{1,0:T(8,128)(2,1)S(1)} %copy-done.56), kind=kOutput, calls=%fused_computation.229 | convolution fusion | flops 5912395776 | bytes 20709376 | tf_op jit(solution)/shard_map/dot_general | solution.py:143
  224.3 3.2 collective-permute-start.36
  229.9 4.8 %collective-permute-done.34 = bf16[64,2048]{1,0:T(8,128)(2,1)S(1)} collective-permute-done((bf16[64,2048]{1,0:T(8,128)(2,1)S(1)}, bf16[64,2048]{1,0:T(8,128)(2,1)S(1)}, u32[]{:S(2)}, u32[]{:S(2)}) %collective-permute-start.34) | collective-permute-done | bytes 262176 | tf_op jit(solution)/shard_map/ppermute | solution.py:33
  234.9 3.3 collective-permute-start.37
  238.4 6.8 %collective-permute-done.29 = bf16[128,2048]{1,0:T(8,128)(2,1)S(1)} collective-permute-done((bf16[128,2048]{1,0:T(8,128)(2,1)S(1)}, bf16[128,2048]{1,0:T(8,128)(2,1)S(1)}, u32[]{:S(2)}, u32[]{:S(2)}) %collective-permute-start.29) | collective-permute-done | bytes 524320 | tf_op jit(solution)/shard_map/ppermute | solution.py:33
  246.0 4.8 %collective-permute-done.37 = bf16[128,2048]{1,0:T(8,128)(2,1)S(1)} collective-permute-done((bf16[128,2048]{1,0:T(8,128)(2,1)S(1)}, bf16[128,2048]{1,0:T(8,128)(2,1)S(1)}, u32[]{:S(2)}, u32[]{:S(2)}) %collective-permute-start.37) | collective-permute-done | bytes 524320 | tf_op jit(solution)/shard_map/ppermute | solution.py:33
  257.7 9.0 %collective-permute-done.39 = bf16[128,2048]{1,0:T(8,128)(2,1)} collective-permute-done((bf16[128,2048]{1,0:T(8,128)(2,1)}, bf16[128,2048]{1,0:T(8,128)(2,1)}, u32[]{:S(2)}, u32[]{:S(2)}) %collective-permute-start.39) | collective-permute-done | bytes 524320 | tf_op jit(solution)/shard_map/ppermute | solution.py:33
  267.7 3.8 collective-permute-start.41
  276.7 3.8 collective-permute-done.40
  284.8 14.2 %shard_map.405 = bf16[512,640]{1,0:T(8,128)(2,1)S(1)} custom-call(bf16[512,512]{1,0:T(8,128)(2,1)S(1)} %get-tuple-element.33.q_ref, bf16[512,128]{1,0:T(8,128)(2,1)S(1)} %get-tuple-element.34.kv_ref, f32[512,8]{1,0:T(8,128)S(1)} %get-tuple-element.35.lse_ref, bf16[512,512]{1,0:T(8,128)(2,1)S(1)} %convolution_convert_fusion.4.up_ref, ...), custom_call_target="tpu_custom_call" | custom-call | flops 1342177280 | bytes 4194304 | tf_op jit(solution)/shard_map/pallas_call | solution.py:253
  301.2 3.2 collective-permute-start.44
  305.9 2.9 collective-permute-done.42
  309.7 3.8 collective-permute-start.45
  316.0 4.5 %collective-permute-done.45 = bf16[128,2048]{1,0:T(8,128)(2,1)S(1)} collective-permute-done((bf16[128,2048]{1,0:T(8,128)(2,1)S(1)}, bf16[128,2048]{1,0:T(8,128)(2,1)S(1)}, u32[]{:S(2)}, u32[]{:S(2)}) %collective-permute-start.45) | collective-permute-done | bytes 524320 | tf_op jit(solution)/shard_map/ppermute | solution.py:33
  320.5 3.4 collective-permute-done.43
  336.0 3.4 collective-permute-done.59
  339.4 3.1 collective-permute-done.58
  343.0 8.6 %collective-permute-done.47 = bf16[4,64,640]{2,1,0:T(8,128)(2,1)S(1)} collective-permute-done((bf16[4,64,640]{2,1,0:T(8,128)(2,1)S(1)}, bf16[4,64,640]{2,1,0:T(8,128)(2,1)S(1)}, u32[]{:S(2)}, u32[]{:S(2)}) %collective-permute-start.47) | collective-permute-done | bytes 327712 | tf_op jit(solution)/shard_map/ppermute | solution.py:47
  351.6 3.3 collective-permute-done.49
  354.9 5.8 %collective-permute-done.48 = bf16[4,64,640]{2,1,0:T(8,128)(2,1)S(1)} collective-permute-done((bf16[4,64,640]{2,1,0:T(8,128)(2,1)S(1)}, bf16[4,64,640]{2,1,0:T(8,128)(2,1)S(1)}, u32[]{:S(2)}, u32[]{:S(2)}) %collective-permute-start.48) | collective-permute-done | bytes 327712 | tf_op jit(solution)/shard_map/ppermute | solution.py:47
  361.6 2.9 collective-permute-start.51
  372.4 18.4 %reduce-scatter.3.cloned.1.call-done = bf16[64,2816]{1,0:T(8,128)(2,1)} async-done(((bf16[2048,2816]{1,0:T(8,128)(2,1)}), bf16[64,2816]{1,0:T(8,128)(2,1)}) %reduce-scatter.3.cloned.1.call-update) | async-done | bytes 360464 | tf_op jit(solution)/shard_map/reduce_scatter | solution.py:359
  392.1 3.0 collective-permute-start.54
  (340 shorter events, 92.3 us)
Async XLA Ops:
  7.2 161.0 %all-gather.2.cloned.1.call-start = ((), (), s32[]{:S(2)}) async-start(), calls=%async_computation.2 | async-start | bytes 17842176 | tf_op jit(solution)/shard_map/all_gather | solution.py:326
  12.0 358.4 %reduce-scatter.5.cloned.1.call-start = ((), (), s32[]{:S(2)}) async-start(), calls=%async_computation.4 | async-start | bytes 5947392 | tf_op jit(solution)/shard_map/reduce_scatter | solution.py:356
  12.0 14.2 %collective-permute-start.12 = (bf16[64,512]{1,0:T(8,128)(2,1)S(1)}, bf16[64,512]{1,0:T(8,128)(2,1)S(1)}, u32[]{:S(2)}, u32[]{:S(2)}) collective-permute-start(bf16[64,512]{1,0:T(8,128)(2,1)S(1)} %convert_bitcast_fusion.2), channel_id=1, source_target_pairs={{0,96},{4,100},{8,104},{12,108},{16,112},{20,116},{24,120},{28,124... | collective-permute-start | bytes 196616 | tf_op jit(solution)/shard_map/ppermute | solution.py:57
  15.2 15.1 %collective-permute-start.13 = (bf16[64,512]{1,0:T(8,128)(2,1)S(1)}, bf16[64,512]{1,0:T(8,128)(2,1)S(1)}, u32[]{:S(2)}, u32[]{:S(2)}) collective-permute-start(bf16[64,512]{1,0:T(8,128)(2,1)S(1)} %convert_bitcast_fusion.2), channel_id=1, source_target_pairs={{0,64},{4,68},{8,72},{12,76},{16,80},{20,84},{24,88},{28,92},{32,9... | collective-permute-start | bytes 196616 | tf_op jit(solution)/shard_map/ppermute | solution.py:57
  17.6 17.1 %collective-permute-start.6 = (bf16[64,640]{1,0:T(8,128)(2,1)S(1)}, bf16[64,640]{1,0:T(8,128)(2,1)S(1)}, u32[]{:S(2)}, u32[]{:S(2)}) collective-permute-start(bf16[64,640]{1,0:T(8,128)(2,1)S(1)} %fusion.42), channel_id=1, source_target_pairs={{0,16},{4,20},{8,24},{12,28},{16,0},{20,4},{24,8},{28,12},{32,48},... | collective-permute-start | bytes 245768 | tf_op jit(solution)/shard_map/ppermute | solution.py:47
  20.7 12.1 %collective-permute-start.5 = (bf16[64,640]{1,0:T(8,128)(2,1)S(1)}, bf16[64,640]{1,0:T(8,128)(2,1)S(1)}, u32[]{:S(2)}, u32[]{:S(2)}) collective-permute-start(bf16[64,640]{1,0:T(8,128)(2,1)S(1)} %fusion.42), channel_id=1, source_target_pairs={{0,24},{4,28},{8,0},{12,4},{16,8},{20,12},{24,16},{28,20},{32,56},... | collective-permute-start | bytes 245768 | tf_op jit(solution)/shard_map/ppermute | solution.py:47
  26.2 52.2 %collective-permute-start.1 = (bf16[128,2048]{1,0:T(8,128)(2,1)S(1)}, bf16[128,2048]{1,0:T(8,128)(2,1)S(1)}, u32[]{:S(2)}, u32[]{:S(2)}) collective-permute-start(bf16[128,2048]{1,0:T(8,128)(2,1)S(1)} %get-tuple-element.70), channel_id=1, source_target_pairs={{0,3},{1,0},{2,1},{3,2},{4,7},{5,4},{6,5},{7,6},{8,11},{9,8},{10,9... | collective-permute-start | bytes 1572872 | tf_op jit(solution)/shard_map/ppermute | solution.py:33
  30.4 51.2 %collective-permute-start = (bf16[128,2048]{1,0:T(8,128)(2,1)S(1)}, bf16[128,2048]{1,0:T(8,128)(2,1)S(1)}, u32[]{:S(2)}, u32[]{:S(2)}) collective-permute-start(bf16[128,2048]{1,0:T(8,128)(2,1)S(1)} %get-tuple-element.70), channel_id=1, source_target_pairs={{0,1},{1,2},{2,3},{3,0},{4,5},{5,6},{6,7},{7,4},{8,9},{9,10},{10,1... | collective-permute-start | bytes 1572872 | tf_op jit(solution)/shard_map/ppermute | solution.py:33
  32.6 21.4 %collective-permute-start.16 = (bf16[4,64,512]{2,1,0:T(8,128)(2,1)S(1)}, bf16[4,64,512]{2,1,0:T(8,128)(2,1)S(1)}, u32[]{:S(2)}, u32[]{:S(2)}) collective-permute-start(bf16[4,64,512]{2,1,0:T(8,128)(2,1)S(1)} %bitcast_dynamic-update-slice_fusion.14), channel_id=1, source_target_pairs={{0,16},{4,20},{8,24},{12,28},{16,0},{20,4},{24,8},{28,12},{32,48},... | collective-permute-start | bytes 786440 | tf_op jit(solution)/shard_map/ppermute | solution.py:47
  32.8 19.5 %collective-permute-start.15 = (bf16[4,64,512]{2,1,0:T(8,128)(2,1)S(1)}, bf16[4,64,512]{2,1,0:T(8,128)(2,1)S(1)}, u32[]{:S(2)}, u32[]{:S(2)}) collective-permute-start(bf16[4,64,512]{2,1,0:T(8,128)(2,1)S(1)} %bitcast_dynamic-update-slice_fusion.14), channel_id=1, source_target_pairs={{0,24},{4,28},{8,0},{12,4},{16,8},{20,12},{24,16},{28,20},{32,56},... | collective-permute-start | bytes 786440 | tf_op jit(solution)/shard_map/ppermute | solution.py:47
  34.7 14.7 %collective-permute-start.14 = (bf16[4,64,512]{2,1,0:T(8,128)(2,1)S(1)}, bf16[4,64,512]{2,1,0:T(8,128)(2,1)S(1)}, u32[]{:S(2)}, u32[]{:S(2)}) collective-permute-start(bf16[4,64,512]{2,1,0:T(8,128)(2,1)S(1)} %bitcast_dynamic-update-slice_fusion.14), channel_id=1, source_target_pairs={{0,8},{4,12},{8,16},{12,20},{16,24},{20,28},{24,0},{28,4},{32,40},... | collective-permute-start | bytes 786440 | tf_op jit(solution)/shard_map/ppermute | solution.py:47
  49.4 27.9 %collective-permute-start.9 = (bf16[4,64,640]{2,1,0:T(8,128)(2,1)S(1)}, bf16[4,64,640]{2,1,0:T(8,128)(2,1)S(1)}, u32[]{:S(2)}, u32[]{:S(2)}) collective-permute-start(bf16[4,64,640]{2,1,0:T(8,128)(2,1)S(1)} %bitcast_dynamic-update-slice_fusion.10), channel_id=1, source_target_pairs={{0,64},{4,68},{8,72},{12,76},{16,80},{20,84},{24,88},{28,92},{32,9... | collective-permute-start | bytes 983048 | tf_op jit(solution)/shard_map/ppermute | solution.py:57
  52.3 24.9 %collective-permute-start.8 = (bf16[4,64,640]{2,1,0:T(8,128)(2,1)S(1)}, bf16[4,64,640]{2,1,0:T(8,128)(2,1)S(1)}, u32[]{:S(2)}, u32[]{:S(2)}) collective-permute-start(bf16[4,64,640]{2,1,0:T(8,128)(2,1)S(1)} %bitcast_dynamic-update-slice_fusion.10), channel_id=1, source_target_pairs={{0,96},{4,100},{8,104},{12,108},{16,112},{20,116},{24,120},{28,124... | collective-permute-start | bytes 983048 | tf_op jit(solution)/shard_map/ppermute | solution.py:57
  53.9 23.2 %collective-permute-start.7 = (bf16[4,64,640]{2,1,0:T(8,128)(2,1)S(1)}, bf16[4,64,640]{2,1,0:T(8,128)(2,1)S(1)}, u32[]{:S(2)}, u32[]{:S(2)}) collective-permute-start(bf16[4,64,640]{2,1,0:T(8,128)(2,1)S(1)} %bitcast_dynamic-update-slice_fusion.10), channel_id=1, source_target_pairs={{0,32},{4,36},{8,40},{12,44},{16,48},{20,52},{24,56},{28,60},{32,6... | collective-permute-start | bytes 983048 | tf_op jit(solution)/shard_map/ppermute | solution.py:57
  77.1 14.1 %collective-permute-start.17 = (bf16[16,64,512]{2,1,0:T(8,128)(2,1)S(1)}, bf16[16,64,512]{2,1,0:T(8,128)(2,1)S(1)}, u32[]{:S(2)}, u32[]{:S(2)}) collective-permute-start(bf16[16,64,512]{2,1,0:T(8,128)(2,1)S(1)} %bitcast.223), channel_id=1, source_target_pairs={{0,4},{4,0},{8,12},{12,8},{16,20},{20,16},{24,28},{28,24},{32,36},... | collective-permute-start | bytes 3145736 | tf_op jit(solution)/shard_map/ppermute | solution.py:61
  77.3 14.0 %collective-permute-start.10 = (bf16[16,64,640]{2,1,0:T(8,128)(2,1)S(1)}, bf16[16,64,640]{2,1,0:T(8,128)(2,1)S(1)}, u32[]{:S(2)}, u32[]{:S(2)}) collective-permute-start(bf16[16,64,640]{2,1,0:T(8,128)(2,1)S(1)} %bitcast.220), channel_id=1, source_target_pairs={{0,4},{4,0},{8,12},{12,8},{16,20},{20,16},{24,28},{28,24},{32,36},... | collective-permute-start | bytes 3932168 | tf_op jit(solution)/shard_map/ppermute | solution.py:61
  78.5 12.6 %collective-permute-start.3 = (bf16[64,2048]{1,0:T(8,128)(2,1)S(1)}, bf16[64,2048]{1,0:T(8,128)(2,1)S(1)}, u32[]{:S(2)}, u32[]{:S(2)}) collective-permute-start(bf16[64,2048]{1,0:T(8,128)(2,1)S(1)} %slice.258), channel_id=1, source_target_pairs={{0,3},{1,0},{2,1},{3,2},{4,7},{5,4},{6,5},{7,6},{8,11},{9,8},{10,9... | collective-permute-start | bytes 786440 | tf_op jit(solution)/shard_map/ppermute | solution.py:33
  107.9 10.5 %collective-permute-start.18 = (bf16[64,2048]{1,0:T(8,128)(2,1)S(1)}, bf16[64,2048]{1,0:T(8,128)(2,1)S(1)}, u32[]{:S(2)}, u32[]{:S(2)}) collective-permute-start(bf16[64,2048]{1,0:T(8,128)(2,1)S(1)} %get-tuple-element.96), channel_id=1, source_target_pairs={{0,1},{1,2},{2,3},{3,0},{4,5},{5,6},{6,7},{7,4},{8,9},{9,10},{10,1... | collective-permute-start | bytes 786440 | tf_op jit(solution)/shard_map/ppermute | solution.py:33
  111.3 17.9 %collective-permute-start.31 = (bf16[128,2048]{1,0:T(8,128)(2,1)S(1)}, bf16[128,2048]{1,0:T(8,128)(2,1)S(1)}, u32[]{:S(2)}, u32[]{:S(2)}) collective-permute-start(bf16[128,2048]{1,0:T(8,128)(2,1)S(1)} %bitcast_convert_fusion), channel_id=1, source_target_pairs={{0,3},{1,0},{2,1},{3,2},{4,7},{5,4},{6,5},{7,6},{8,11},{9,8},{10,9... | collective-permute-start | bytes 1572872 | tf_op jit(solution)/shard_map/ppermute | solution.py:33
  111.3 22.0 %collective-permute-start.30 = (bf16[128,2048]{1,0:T(8,128)(2,1)S(1)}, bf16[128,2048]{1,0:T(8,128)(2,1)S(1)}, u32[]{:S(2)}, u32[]{:S(2)}) collective-permute-start(bf16[128,2048]{1,0:T(8,128)(2,1)S(1)} %bitcast_convert_fusion), channel_id=1, source_target_pairs={{0,1},{1,2},{2,3},{3,0},{4,5},{5,6},{6,7},{7,4},{8,9},{9,10},{10,1... | collective-permute-start | bytes 1572872 | tf_op jit(solution)/shard_map/ppermute | solution.py:33
  118.6 21.8 %collective-permute-start.21 = (bf16[128,2048]{1,0:T(8,128)(2,1)S(1)}, bf16[128,2048]{1,0:T(8,128)(2,1)S(1)}, u32[]{:S(2)}, u32[]{:S(2)}) collective-permute-start(bf16[128,2048]{1,0:T(8,128)(2,1)S(1)} %pad_maximum_fusion.6), channel_id=1, source_target_pairs={{0,3},{1,0},{2,1},{3,2},{4,7},{5,4},{6,5},{7,6},{8,11},{9,8},{10,9... | collective-permute-start | bytes 1572872 | tf_op jit(solution)/shard_map/ppermute | solution.py:33
  121.9 18.9 %collective-permute-start.19 = (bf16[128,2048]{1,0:T(8,128)(2,1)S(1)}, bf16[128,2048]{1,0:T(8,128)(2,1)S(1)}, u32[]{:S(2)}, u32[]{:S(2)}) collective-permute-start(bf16[128,2048]{1,0:T(8,128)(2,1)S(1)} %pad_maximum_fusion.5), channel_id=1, source_target_pairs={{0,1},{1,2},{2,3},{3,0},{4,5},{5,6},{6,7},{7,4},{8,9},{9,10},{10,1... | collective-permute-start | bytes 1572872 | tf_op jit(solution)/shard_map/ppermute | solution.py:33
  129.2 16.8 %collective-permute-start.33 = (bf16[64,2048]{1,0:T(8,128)(2,1)S(1)}, bf16[64,2048]{1,0:T(8,128)(2,1)S(1)}, u32[]{:S(2)}, u32[]{:S(2)}) collective-permute-start(bf16[64,2048]{1,0:T(8,128)(2,1)S(1)} %slice.282), channel_id=1, source_target_pairs={{0,3},{1,0},{2,1},{3,2},{4,7},{5,4},{6,5},{7,6},{8,11},{9,8},{10,9... | collective-permute-start | bytes 786440 | tf_op jit(solution)/shard_map/ppermute | solution.py:33
  133.4 12.3 %collective-permute-start.32 = (bf16[64,2048]{1,0:T(8,128)(2,1)S(1)}, bf16[64,2048]{1,0:T(8,128)(2,1)S(1)}, u32[]{:S(2)}, u32[]{:S(2)}) collective-permute-start(bf16[64,2048]{1,0:T(8,128)(2,1)S(1)} %slice.281), channel_id=1, source_target_pairs={{0,1},{1,2},{2,3},{3,0},{4,5},{5,6},{6,7},{7,4},{8,9},{9,10},{10,1... | collective-permute-start | bytes 786440 | tf_op jit(solution)/shard_map/ppermute | solution.py:33
  142.4 12.8 %collective-permute-start.23 = (bf16[128,2048]{1,0:T(8,128)(2,1)S(1)}, bf16[128,2048]{1,0:T(8,128)(2,1)S(1)}, u32[]{:S(2)}, u32[]{:S(2)}) collective-permute-start(bf16[128,2048]{1,0:T(8,128)(2,1)S(1)} %get-tuple-element.66), channel_id=1, source_target_pairs={{0,3},{1,0},{2,1},{3,2},{4,7},{5,4},{6,5},{7,6},{8,11},{9,8},{10,9... | collective-permute-start | bytes 1572872 | tf_op jit(solution)/shard_map/ppermute | solution.py:33
  145.7 13.4 %collective-permute-start.22 = (bf16[128,2048]{1,0:T(8,128)(2,1)S(1)}, bf16[128,2048]{1,0:T(8,128)(2,1)S(1)}, u32[]{:S(2)}, u32[]{:S(2)}) collective-permute-start(bf16[128,2048]{1,0:T(8,128)(2,1)S(1)} %get-tuple-element.66), channel_id=1, source_target_pairs={{0,1},{1,2},{2,3},{3,0},{4,5},{5,6},{6,7},{7,4},{8,9},{9,10},{10,1... | collective-permute-start | bytes 1572872 | tf_op jit(solution)/shard_map/ppermute | solution.py:33
  155.3 12.2 %collective-permute-start.25 = (bf16[64,2048]{1,0:T(8,128)(2,1)S(1)}, bf16[64,2048]{1,0:T(8,128)(2,1)S(1)}, u32[]{:S(2)}, u32[]{:S(2)}) collective-permute-start(bf16[64,2048]{1,0:T(8,128)(2,1)S(1)} %slice.267), channel_id=1, source_target_pairs={{0,3},{1,0},{2,1},{3,2},{4,7},{5,4},{6,5},{7,6},{8,11},{9,8},{10,9... | collective-permute-start | bytes 786440 | tf_op jit(solution)/shard_map/ppermute | solution.py:33
  193.5 197.3 %reduce-scatter.3.cloned.1.call-start = ((), (), s32[]{:S(2)}) async-start(), calls=%async_computation.3 | async-start | bytes 11894784 | tf_op jit(solution)/shard_map/reduce_scatter | solution.py:359
  211.1 16.4 %collective-permute-start.26 = (bf16[64,2048]{1,0:T(8,128)(2,1)S(1)}, bf16[64,2048]{1,0:T(8,128)(2,1)S(1)}, u32[]{:S(2)}, u32[]{:S(2)}) collective-permute-start(bf16[64,2048]{1,0:T(8,128)(2,1)S(1)} %get-tuple-element.92), channel_id=1, source_target_pairs={{0,1},{1,2},{2,3},{3,0},{4,5},{5,6},{6,7},{7,4},{8,9},{9,10},{10,1... | collective-permute-start | bytes 786440 | tf_op jit(solution)/shard_map/ppermute | solution.py:33
  211.2 16.4 %collective-permute-start.28 = (bf16[64,2048]{1,0:T(8,128)(2,1)S(1)}, bf16[64,2048]{1,0:T(8,128)(2,1)S(1)}, u32[]{:S(2)}, u32[]{:S(2)}) collective-permute-start(bf16[64,2048]{1,0:T(8,128)(2,1)S(1)} %get-tuple-element.93), channel_id=1, source_target_pairs={{0,3},{1,0},{2,1},{3,2},{4,7},{5,4},{6,5},{7,6},{8,11},{9,8},{10,9... | collective-permute-start | bytes 786440 | tf_op jit(solution)/shard_map/ppermute | solution.py:33
  227.7 17.4 %collective-permute-start.29 = (bf16[128,2048]{1,0:T(8,128)(2,1)S(1)}, bf16[128,2048]{1,0:T(8,128)(2,1)S(1)}, u32[]{:S(2)}, u32[]{:S(2)}) collective-permute-start(bf16[128,2048]{1,0:T(8,128)(2,1)S(1)} %pad_maximum_fusion.8), channel_id=1, source_target_pairs={{0,3},{1,0},{2,1},{3,2},{4,7},{5,4},{6,5},{7,6},{8,11},{9,8},{10,9... | collective-permute-start | bytes 1572872 | tf_op jit(solution)/shard_map/ppermute | solution.py:33
  227.9 18.2 %collective-permute-start.27 = (bf16[128,2048]{1,0:T(8,128)(2,1)S(1)}, bf16[128,2048]{1,0:T(8,128)(2,1)S(1)}, u32[]{:S(2)}, u32[]{:S(2)}) collective-permute-start(bf16[128,2048]{1,0:T(8,128)(2,1)S(1)} %pad_maximum_fusion.7), channel_id=1, source_target_pairs={{0,1},{1,2},{2,3},{3,0},{4,5},{5,6},{6,7},{7,4},{8,9},{9,10},{10,1... | collective-permute-start | bytes 1572872 | tf_op jit(solution)/shard_map/ppermute | solution.py:33
  234.9 15.8 %collective-permute-start.37 = (bf16[128,2048]{1,0:T(8,128)(2,1)S(1)}, bf16[128,2048]{1,0:T(8,128)(2,1)S(1)}, u32[]{:S(2)}, u32[]{:S(2)}) collective-permute-start(bf16[128,2048]{1,0:T(8,128)(2,1)S(1)} %pad_maximum_fusion.10), channel_id=1, source_target_pairs={{0,3},{1,0},{2,1},{3,2},{4,7},{5,4},{6,5},{7,6},{8,11},{9,8},{10,9... | collective-permute-start | bytes 1572872 | tf_op jit(solution)/shard_map/ppermute | solution.py:33
  238.3 13.4 %collective-permute-start.35 = (bf16[128,2048]{1,0:T(8,128)(2,1)S(1)}, bf16[128,2048]{1,0:T(8,128)(2,1)S(1)}, u32[]{:S(2)}, u32[]{:S(2)}) collective-permute-start(bf16[128,2048]{1,0:T(8,128)(2,1)S(1)} %pad_maximum_fusion.9), channel_id=1, source_target_pairs={{0,1},{1,2},{2,3},{3,0},{4,5},{5,6},{6,7},{7,4},{8,9},{9,10},{10,1... | collective-permute-start | bytes 1572872 | tf_op jit(solution)/shard_map/ppermute | solution.py:33
  254.9 11.8 %collective-permute-start.39 = (bf16[128,2048]{1,0:T(8,128)(2,1)}, bf16[128,2048]{1,0:T(8,128)(2,1)}, u32[]{:S(2)}, u32[]{:S(2)}) collective-permute-start(bf16[128,2048]{1,0:T(8,128)(2,1)} %get-tuple-element.63), channel_id=1, source_target_pairs={{0,3},{1,0},{2,1},{3,2},{4,7},{5,4},{6,5},{7,6},{8,11},{9,8},{10,9... | collective-permute-start | bytes 1572872 | tf_op jit(solution)/shard_map/ppermute | solution.py:33
  257.6 13.8 %collective-permute-start.38 = (bf16[128,2048]{1,0:T(8,128)(2,1)}, bf16[128,2048]{1,0:T(8,128)(2,1)}, u32[]{:S(2)}, u32[]{:S(2)}) collective-permute-start(bf16[128,2048]{1,0:T(8,128)(2,1)} %get-tuple-element.63), channel_id=1, source_target_pairs={{0,1},{1,2},{2,3},{3,0},{4,5},{5,6},{6,7},{7,4},{8,9},{9,10},{10,1... | collective-permute-start | bytes 1572872 | tf_op jit(solution)/shard_map/ppermute | solution.py:33
  267.7 13.5 %collective-permute-start.41 = (bf16[64,2048]{1,0:T(8,128)(2,1)S(1)}, bf16[64,2048]{1,0:T(8,128)(2,1)S(1)}, u32[]{:S(2)}, u32[]{:S(2)}) collective-permute-start(bf16[64,2048]{1,0:T(8,128)(2,1)S(1)} %slice.291), channel_id=1, source_target_pairs={{0,3},{1,0},{2,1},{3,2},{4,7},{5,4},{6,5},{7,6},{8,11},{9,8},{10,9... | collective-permute-start | bytes 786440 | tf_op jit(solution)/shard_map/ppermute | solution.py:33
  305.8 19.8 %collective-permute-start.56 = (bf16[4,4,64,512]{3,2,1,0:T(8,128)(2,1)S(1)}, bf16[4,4,64,512]{3,2,1,0:T(8,128)(2,1)S(1)}, u32[]{:S(2)}, u32[]{:S(2)}) collective-permute-start(bf16[4,4,64,512]{3,2,1,0:T(8,128)(2,1)S(1)} %dynamic-slice_bitcast_fusion), channel_id=1, source_target_pairs={{0,4},{4,0},{8,12},{12,8},{16,20},{20,16},{24,28},{28,24},{32,36},... | collective-permute-start | bytes 3145736 | tf_op jit(solution)/shard_map/ppermute | solution.py:61
  309.7 10.8 %collective-permute-start.45 = (bf16[128,2048]{1,0:T(8,128)(2,1)S(1)}, bf16[128,2048]{1,0:T(8,128)(2,1)S(1)}, u32[]{:S(2)}, u32[]{:S(2)}) collective-permute-start(bf16[128,2048]{1,0:T(8,128)(2,1)S(1)} %pad_maximum_fusion.12), channel_id=1, source_target_pairs={{0,3},{1,0},{2,1},{3,2},{4,7},{5,4},{6,5},{7,6},{8,11},{9,8},{10,9... | collective-permute-start | bytes 1572872 | tf_op jit(solution)/shard_map/ppermute | solution.py:33
  315.9 16.2 %collective-permute-start.46 = (bf16[4,4,64,640]{3,2,0,1:T(8,128)(2,1)S(1)}, bf16[4,4,64,640]{3,2,0,1:T(8,128)(2,1)S(1)}, u32[]{:S(2)}, u32[]{:S(2)}) collective-permute-start(bf16[4,4,64,640]{3,2,0,1:T(8,128)(2,1)S(1)} %bitcast.227), channel_id=1, source_target_pairs={{0,4},{4,0},{8,12},{12,8},{16,20},{20,16},{24,28},{28,24},{32,36},... | collective-permute-start | bytes 3932168 | tf_op jit(solution)/shard_map/ppermute | solution.py:61
  328.2 11.2 %collective-permute-start.59 = (bf16[4,64,512]{2,1,0:T(8,128)(2,1)S(1)}, bf16[4,64,512]{2,1,0:T(8,128)(2,1)S(1)}, u32[]{:S(2)}, u32[]{:S(2)}) collective-permute-start(bf16[4,64,512]{2,1,0:T(8,128)(2,1)S(1)} %get-tuple-element.104), channel_id=1, source_target_pairs={{0,64},{4,68},{8,72},{12,76},{16,80},{20,84},{24,88},{28,92},{32,9... | collective-permute-start | bytes 786440 | tf_op jit(solution)/shard_map/ppermute | solution.py:57
  329.6 13.0 %collective-permute-start.58 = (bf16[4,64,512]{2,1,0:T(8,128)(2,1)S(1)}, bf16[4,64,512]{2,1,0:T(8,128)(2,1)S(1)}, u32[]{:S(2)}, u32[]{:S(2)}) collective-permute-start(bf16[4,64,512]{2,1,0:T(8,128)(2,1)S(1)} %get-tuple-element.105), channel_id=1, source_target_pairs={{0,96},{4,100},{8,104},{12,108},{16,112},{20,116},{24,120},{28,124... | collective-permute-start | bytes 786440 | tf_op jit(solution)/shard_map/ppermute | solution.py:57
  332.7 18.9 %collective-permute-start.47 = (bf16[4,64,640]{2,1,0:T(8,128)(2,1)S(1)}, bf16[4,64,640]{2,1,0:T(8,128)(2,1)S(1)}, u32[]{:S(2)}, u32[]{:S(2)}) collective-permute-start(bf16[4,64,640]{2,1,0:T(8,128)(2,1)S(1)} %get-tuple-element.100), channel_id=1, source_target_pairs={{0,8},{4,12},{8,16},{12,20},{16,24},{20,28},{24,0},{28,4},{32,40},... | collective-permute-start | bytes 983048 | tf_op jit(solution)/shard_map/ppermute | solution.py:47
  332.8 22.2 %collective-permute-start.49 = (bf16[4,64,640]{2,1,0:T(8,128)(2,1)S(1)}, bf16[4,64,640]{2,1,0:T(8,128)(2,1)S(1)}, u32[]{:S(2)}, u32[]{:S(2)}) collective-permute-start(bf16[4,64,640]{2,1,0:T(8,128)(2,1)S(1)} %get-tuple-element.101), channel_id=1, source_target_pairs={{0,16},{4,20},{8,24},{12,28},{16,0},{20,4},{24,8},{28,12},{32,48},... | collective-permute-start | bytes 983048 | tf_op jit(solution)/shard_map/ppermute | solution.py:47
  333.7 27.0 %collective-permute-start.48 = (bf16[4,64,640]{2,1,0:T(8,128)(2,1)S(1)}, bf16[4,64,640]{2,1,0:T(8,128)(2,1)S(1)}, u32[]{:S(2)}, u32[]{:S(2)}) collective-permute-start(bf16[4,64,640]{2,1,0:T(8,128)(2,1)S(1)} %get-tuple-element.102), channel_id=1, source_target_pairs={{0,24},{4,28},{8,0},{12,4},{16,8},{20,12},{24,16},{28,20},{32,56},... | collective-permute-start | bytes 983048 | tf_op jit(solution)/shard_map/ppermute | solution.py:47
  342.8 18.8 %collective-permute-start.60 = (bf16[64,512]{1,0:T(8,128)(2,1)S(1)}, bf16[64,512]{1,0:T(8,128)(2,1)S(1)}, u32[]{:S(2)}, u32[]{:S(2)}) collective-permute-start(bf16[64,512]{1,0:T(8,128)(2,1)S(1)} %get-tuple-element.119), channel_id=1, source_target_pairs={{0,8},{4,12},{8,16},{12,20},{16,24},{20,28},{24,0},{28,4},{32,40},... | collective-permute-start | bytes 196616 | tf_op jit(solution)/shard_map/ppermute | solution.py:47
  342.9 21.6 %collective-permute-start.62 = (bf16[64,512]{1,0:T(8,128)(2,1)S(1)}, bf16[64,512]{1,0:T(8,128)(2,1)S(1)}, u32[]{:S(2)}, u32[]{:S(2)}) collective-permute-start(bf16[64,512]{1,0:T(8,128)(2,1)S(1)} %get-tuple-element.120), channel_id=1, source_target_pairs={{0,16},{4,20},{8,24},{12,28},{16,0},{20,4},{24,8},{28,12},{32,48},... | collective-permute-start | bytes 196616 | tf_op jit(solution)/shard_map/ppermute | solution.py:47
  351.6 13.4 %collective-permute-start.61 = (bf16[64,512]{1,0:T(8,128)(2,1)S(1)}, bf16[64,512]{1,0:T(8,128)(2,1)S(1)}, u32[]{:S(2)}, u32[]{:S(2)}) collective-permute-start(bf16[64,512]{1,0:T(8,128)(2,1)S(1)} %get-tuple-element.121), channel_id=1, source_target_pairs={{0,24},{4,28},{8,0},{12,4},{16,8},{20,12},{24,16},{28,20},{32,56},... | collective-permute-start | bytes 196616 | tf_op jit(solution)/shard_map/ppermute | solution.py:47
  (75 other events, 877.8 us)
Sparse Core Ops, SparseCore 0:
  12.1 91.7 all-gather.1
  193.6 81.9 reduce-scatter.4
  279.9 110.9 reduce-scatter.2

commit v2 on v1

v2 whole, which is shorter than its diff:
```python
import functools

import jax
import jax.numpy as jnp
from jax import lax
from jax.experimental import pallas as pl
from jax.experimental.pallas import tpu as pltpu
from jax.sharding import PartitionSpec as P

HEAD_DIM = 64
HEADS_LOCAL = 8
QUERY_COLS = 512
QKV_COLS = 640
HIDDEN = 1408
SEQ = 512
PART = 128
D = 2048
STEP = 10

EPS = 1e-05
THETA = 10000.0
BETA_ONE = 0.9
BETA_TWO = 0.95
ADAM_EPS = 1e-08
RATES = (1.0, 0.05, 0.05, 0.5, 0.05, 0.025)
DECAYS = (0.0, 0.1, 0.1, 0.1, 0.1, 0.1)
SIDE = 4
BF16 = jnp.bfloat16
F32 = jnp.float32
SPLIT = 768


def cost(us):
    return pl.CostEstimate(
        flops=int(us * 1.1e9), bytes_accessed=int(us * 3.0e6), transcendentals=0
    )


def pair_mask(core, step):
    return (1, 3)[step] if core == 0 else (3, 1)[step]


def dp_index(y, x, core):
    return (y * SIDE + x) * 2 + core


def chips():
    return [(y, x, c) for y in range(SIDE) for x in range(SIDE) for c in range(2)]


def pair_z(a, step):
    pairs = [
        (dp * SIDE + z, dp * SIDE + (z ^ pair_mask(dp % 2, step)))
        for dp in range(2 * SIDE * SIDE)
        for z in range(SIDE)
    ]
    return lax.ppermute(a, ("dp", "mp"), pairs)


def pair_x(a, step):
    pairs = [(dp_index(y, x, c), dp_index(y, x ^ pair_mask(c, step), c)) for y, x, c in chips()]
    return lax.ppermute(a, "dp", pairs)


def pair_y(a, step):
    pairs = [(dp_index(y, x, c), dp_index(y ^ pair_mask(c, step), x, c)) for y, x, c in chips()]
    return lax.ppermute(a, "dp", pairs)


def shift_z(x, by):
    return lax.ppermute(x, "mp", [(i, (i + by) % SIDE) for i in range(SIDE)])


def shift_first(a, by):
    pairs = [
        (dp_index(y, x, c), dp_index((y + by) % SIDE, x, c) if c else dp_index(y, (x + by) % SIDE, c))
        for y, x, c in chips()
    ]
    return lax.ppermute(a, "dp", pairs)


def shift_second(a, by):
    pairs = [
        (dp_index(y, x, c), dp_index(y, (x + by) % SIDE, c) if c else dp_index((y + by) % SIDE, x, c))
        for y, x, c in chips()
    ]
    return lax.ppermute(a, "dp", pairs)


def swap_core(a):
    return lax.ppermute(a, "dp", [(i, i ^ 1) for i in range(2 * SIDE * SIDE)])


def place():
    i = lax.axis_index("dp")
    return i // (2 * SIDE), (i // 2) % SIDE, i % 2


def here():
    return jnp.stack(place()).astype(jnp.int32)


def pick(k, values):
    out = jnp.int32(values[0])
    for i in range(1, len(values)):
        out = jnp.where(k == i, values[i], out)
    return out


def pair_steps(core):
    return jnp.where(core == 0, jnp.array([0, 1, 3, 2]), jnp.array([0, 3, 1, 2])).astype(jnp.int32)


def split_sum(near, got):
    k = near.shape[0] // 2
    keep = near[:k].astype(F32) + got[:k].astype(F32)
    return keep, (near[k:].astype(F32) + got[k:].astype(F32)).astype(BF16)


def place_kernel(here_ref, mine_ref, other_ref, qkv_ref, output_ref):
    y, x, core = here_ref[0], here_ref[1], here_ref[2]

    @pl.loop(0, SIDE * SIDE)
    def _(k):
        first, second = pick(k // SIDE, (0, 3, 1, 2)), pick(k % SIDE, (0, 3, 1, 2))
        for own, blocks_ref in ((True, mine_ref), (False, other_ref)):
            c = core if own else 1 - core
            along_x, along_y = jnp.where(c == 0, first, second), jnp.where(c == 0, second, first)
            chip = ((y + along_y) % SIDE) * SIDE + (x + along_x) % SIDE
            qkv_ref[chip, c] = blocks_ref[k, :, :QKV_COLS]
            output_ref[chip, c] = blocks_ref[k, :, QKV_COLS:]


def place_attention(mine, other):
    parts = pl.pallas_call(
        place_kernel,
        out_shape=[
            jax.ShapeDtypeStruct((SIDE * SIDE, 2, 64, n), mine.dtype)
            for n in (QKV_COLS, QUERY_COLS)
        ],
        in_specs=[pl.BlockSpec(memory_space=pltpu.SMEM)] + whole(2),
        out_specs=whole(2),
        compiler_params=pltpu.CompilerParams(vmem_limit_bytes=32 * 2**20),
        cost_estimate=cost(3),
    )(here(), mine, other)
    return [p.reshape(D, -1) for p in parts]


def fold_kernel(x_first, here_ref, mine_ref, got_ref, near_ref, far_ref):
    y, x, core = here_ref[0], here_ref[1], here_ref[2]
    steps = lambda k: pick(k, (0, jnp.where(core == 0, 1, 3), jnp.where(core == 0, 3, 1), 2))

    def chip(k):
        first, second = steps(k // SIDE), steps(k % SIDE)
        if x_first:
            return (y ^ second) * SIDE + (x ^ first)
        return (y ^ first) * SIDE + (x ^ second)

    @pl.loop(0, 2 * SIDE)
    def _(k):
        i, j = chip(k), chip(2 * SIDE + k)
        near_ref[k] = (mine_ref[i].astype(F32) + got_ref[i].astype(F32)).astype(BF16)
        far_ref[k] = (mine_ref[j].astype(F32) + got_ref[j].astype(F32)).astype(BF16)


def fold(mine, got, x_first, us):
    n = mine.shape[2]
    return pl.pallas_call(
        functools.partial(fold_kernel, x_first),
        out_shape=[jax.ShapeDtypeStruct((2 * SIDE, 64, n), BF16)] * 2,
        in_specs=[pl.BlockSpec(memory_space=pltpu.SMEM)] + whole(2),
        out_specs=whole(2),
        compiler_params=pltpu.CompilerParams(vmem_limit_bytes=32 * 2**20),
        cost_estimate=cost(us),
    )(here(), mine, got)


def pair_first(a, step, x_first):
    return (pair_x if x_first else pair_y)(a, step)


def pair_second(a, step, x_first):
    return (pair_y if x_first else pair_x)(a, step)


def scatter_second(line, x_first):
    keep, sent = split_sum(line[:2], pair_second(line[2:], 1, x_first))
    return keep[0] + pair_second(sent, 0, x_first)[0].astype(F32)


def nt(a, b):
    return lax.dot_general(a, b, (((1,), (1,)), ((), ())), preferred_element_type=F32)


def tn(a, b):
    return lax.dot_general(a, b, (((0,), (0,)), ((), ())), preferred_element_type=F32)


def nn(a, b):
    return lax.dot_general(a, b, (((1,), (0,)), ((), ())), preferred_element_type=F32)


def whole(n):
    return [pl.BlockSpec(memory_space=pltpu.VMEM)] * n


def prepare_kernel(
    gains_ref, query_ref, keyvalue_ref, output_ref, gateup_ref, down_ref, part_ref, ffn_ref
):
    gains = gains_ref[...].astype(BF16).astype(F32)
    scaled = lambda k, w: (w.astype(BF16).astype(F32) * gains[:, k : k + 1]).astype(BF16)
    part_ref[:, :QUERY_COLS] = scaled(0, query_ref[...])
    part_ref[:, QUERY_COLS:QKV_COLS] = scaled(
        0, jnp.concatenate([keyvalue_ref[0], keyvalue_ref[1]], axis=1)
    )
    part_ref[:, QKV_COLS:] = output_ref[...].astype(BF16)
    ffn_ref[:, :HIDDEN] = scaled(1, gateup_ref[0])
    ffn_ref[:, HIDDEN : 2 * HIDDEN] = scaled(1, gateup_ref[1])
    ffn_ref[:, 2 * HIDDEN :] = down_ref[...].astype(BF16)


def prepare(norm_gains, query, keyvalue, output, gateup, down):
    return pl.pallas_call(
        prepare_kernel,
        out_shape=[
            jax.ShapeDtypeStruct((64, QKV_COLS + QUERY_COLS), BF16),
            jax.ShapeDtypeStruct((64, 3 * HIDDEN), BF16),
        ],
        in_specs=whole(6),
        out_specs=whole(2),
        compiler_params=pltpu.CompilerParams(vmem_limit_bytes=16 * 2**20),
        cost_estimate=cost(2),
    )(norm_gains.T, query, keyvalue, output.T, gateup, down.T)


def back_kernel(gate_ref, up_ref, gate_w_ref, up_w_ref, near_ref, far_ref):
    out = nt(gate_ref[...], gate_w_ref[...]) + nt(up_ref[...], up_w_ref[...])
    near_ref[...] = out[: SEQ // 2]
    far_ref[...] = out[SEQ // 2 :].astype(BF16)


def back_to_rows(grad_gate, grad_up, weights):
    tile = 512
    grad = pl.BlockSpec((SEQ, HIDDEN), lambda i: (0, 0))
    weight = lambda at: pl.BlockSpec((tile, HIDDEN), lambda i: (i, at))
    out = pl.BlockSpec((SEQ // 2, tile), lambda i: (0, i))
    return pl.pallas_call(
        back_kernel,
        out_shape=[jax.ShapeDtypeStruct((SEQ // 2, D), t) for t in (F32, BF16)],
        grid=(D // tile,),
        in_specs=[grad, grad, weight(0), weight(1)],
        out_specs=[out, out],
        compiler_params=pltpu.CompilerParams(vmem_limit_bytes=32 * 2**20),
        cost_estimate=cost(10),
    )(grad_gate, grad_up, weights, weights)


def turn_kernel(a_ref, turned_ref):
    turned_ref[...] = a_ref[...].T


def turned(a):
    return pl.pallas_call(
        turn_kernel,
        out_shape=jax.ShapeDtypeStruct((D, SEQ), BF16),
        in_specs=whole(1),
        out_specs=whole(1)[0],
        compiler_params=pltpu.CompilerParams(vmem_limit_bytes=16 * 2**20),
        cost_estimate=cost(1),
    )(a)


def weights_kernel(at, core_ref, a_ref, b_ref, c_ref, d_ref, mine_ref, other_ref):
    first = core_ref[0] == 0
    n = b_ref.shape[1]

    @pl.loop(0, D // 256)
    def _(chunk):
        rows = pl.ds(pl.multiple_of(chunk * 256, 256), 256)
        out = nn(a_ref[rows, :], b_ref[...]).astype(BF16)
        more = nn(c_ref[rows, :], d_ref[:, at]).astype(BF16)
        for k in range(2):
            for cols, full in ((slice(0, n), out), (slice(n, None), more)):
                low, high = full[k * 128 : k * 128 + 64], full[k * 128 + 64 : k * 128 + 128]
                mine_ref[chunk * 2 + k, :, cols] = jnp.where(first, low, high)
                other_ref[chunk * 2 + k, :, cols] = jnp.where(first, high, low)


def weight_gradients(a, b, c, d, at):
    n = b.shape[1] + at.stop - at.start
    _, _, core = place()
    return pl.pallas_call(
        functools.partial(weights_kernel, at),
        out_shape=[jax.ShapeDtypeStruct((SIDE * SIDE, 64, n), BF16)] * 2,
        in_specs=[pl.BlockSpec(memory_space=pltpu.SMEM)] + whole(4),
        out_specs=whole(2),
        compiler_params=pltpu.CompilerParams(vmem_limit_bytes=40 * 2**20),
        cost_estimate=cost(8),
    )(core[None], a, b, c, d)


def by_chip(g):
    _, _, core = place()
    g = g.reshape(SIDE * SIDE, 2, 64, g.shape[1])
    pick = lambda c: lax.dynamic_index_in_dim(g, c, 1, keepdims=False)
    return pick(core), pick(1 - core)


def hidden_kernel(
    near_ref, far_ref, gate_w_ref, up_w_ref, grad_hidden_ref,
    hidden_ref, grad_gate_ref, grad_up_ref, rows_ref,
):
    @pl.when(pl.program_id(0) == 0)
    def _():
        rows_ref[: SEQ // 2, :] = near_ref[...]
        rows_ref[SEQ // 2 :, :] = far_ref[...]

    gate_up = nn(rows_ref[...], jnp.concatenate([gate_w_ref[...], up_w_ref[...]], axis=1))
    grad_hidden = grad_hidden_ref[...]
    gate, up = gate_up[:, :128], gate_up[:, 128:]
    sigmoid = 1.0 / (1.0 + jnp.exp(-gate))
    activated = gate * sigmoid
    slope = sigmoid * (1.0 + gate * (1.0 - sigmoid))
    hidden_ref[...] = (activated * up).astype(BF16)
    grad_gate_ref[...] = (grad_hidden * up * slope).astype(BF16)
    grad_up_ref[...] = (grad_hidden * activated).astype(BF16)


def hidden_units(near, far, grad_hidden, weights):
    steps = HIDDEN // 128
    weight = lambda at: pl.BlockSpec((D, 128), lambda j: (0, at * steps + j))
    return pl.pallas_call(
        hidden_kernel,
        out_shape=[jax.ShapeDtypeStruct((SEQ, HIDDEN), BF16)] * 3,
        grid=(steps,),
        in_specs=[pl.BlockSpec((SEQ // 2, D), lambda j: (0, 0))] * 2
        + [weight(0), weight(1), pl.BlockSpec((SEQ, 128), lambda j: (0, j))],
        out_specs=[pl.BlockSpec((SEQ, 128), lambda j: (0, j))] * 3,
        scratch_shapes=[pltpu.VMEM((SEQ, D), BF16)],
        compiler_params=pltpu.CompilerParams(vmem_limit_bytes=24 * 2**20),
        cost_estimate=cost(10),
    )(near, far, weights, weights, grad_hidden)


def turn(x, cosine, sine):
    lane = lax.broadcasted_iota(jnp.int32, x.shape, 1)
    ahead = pltpu.roll(x, 96, 1)
    behind = pltpu.roll(x, 32, 1)
    return x * cosine + jnp.where(lane % HEAD_DIM < HEAD_DIM // 2, ahead, behind) * sine


def mask_bias(ends_ref, block):
    shape = ((block + 1) * PART, PART)
    key = lax.broadcasted_iota(jnp.int32, shape, 0)
    query = lax.broadcasted_iota(jnp.int32, shape, 1) + block * PART
    key_segment = jnp.zeros(shape, jnp.int32)
    query_segment = jnp.zeros(shape, jnp.int32)
    for d in range(4):
        key_segment += (key >= ends_ref[d]).astype(jnp.int32)
        query_segment += (query >= ends_ref[d]).astype(jnp.int32)
    return jnp.where((key_segment == query_segment) & (key <= query), 0.0, -1e30)


def halves(x):
    none = jnp.zeros_like(x)
    return jnp.concatenate([x, none], axis=1), jnp.concatenate([none, x], axis=1)


def in_token_order(slot_ref, kv_ref, ordered_ref):
    for block in range(SIDE):
        rows = pl.ds(pl.multiple_of(slot_ref[block] * PART, PART), PART)
        ordered_ref[block * PART : (block + 1) * PART, :] = kv_ref[rows, :]


def forward_kernel(
    slot_ref, ends_ref, qkv_ref, cos_ref, sin_ref, att_ref, q_ref, kv_ref, lse_ref, ordered_ref
):
    cosine, sine = cos_ref[...], sin_ref[...]
    for pair in range(HEADS_LOCAL // 2):
        cols = slice(pair * 128, pair * 128 + 128)
        q_ref[:, cols] = (turn(qkv_ref[:, cols], cosine, sine).astype(BF16)) * BF16(0.125)
    kv = qkv_ref[:, QUERY_COLS:QKV_COLS]
    lane = lax.broadcasted_iota(jnp.int32, kv.shape, 1)
    kv_ref[...] = jnp.where(lane < HEAD_DIM, turn(kv, cosine, sine), kv).astype(BF16)
    in_token_order(slot_ref, kv_ref, ordered_ref)
    kv = ordered_ref[...]
    keys_both = halves(kv[:, :HEAD_DIM])
    values_turned = kv.astype(F32).T[HEAD_DIM:].astype(BF16)
    for block in range(SIDE):
        seen = (block + 1) * PART
        rows = pl.ds(pl.multiple_of(slot_ref[block] * PART, PART), PART)
        bias = mask_bias(ends_ref, block)
        for pair in range(HEADS_LOCAL // 2):
            cols = slice(pair * 128, pair * 128 + 128)
            q = q_ref[rows, cols]
            outs = []
            for h in range(2):
                s = nt(keys_both[h][:seen], q) + bias
                top = jnp.max(s, axis=0, keepdims=True)
                e = jnp.exp(s - top)
                total = jnp.sum(e, axis=0, keepdims=True)
                p = (e * (1.0 / total)).astype(BF16)
                outs.append(nn(values_turned[:, :seen], p))
                lse_ref[2 * pair + h : 2 * pair + h + 1, block * PART : seen] = top + jnp.log(total)
            att_ref[rows, cols] = jnp.concatenate(outs, axis=0).T.astype(BF16)


def backward_kernel(
    slot_ref, ends_ref, q_ref, kv_ref, lse_ref, up_ref, cos_ref, sin_ref,
    out_ref, ordered_ref, dk_ref, dv_ref,
):
    in_token_order(slot_ref, kv_ref, ordered_ref)
    kv = ordered_ref[...]
    keys_both, values_both = halves(kv[:, :HEAD_DIM]), halves(kv[:, HEAD_DIM:])
    keys_turned = kv.astype(F32).T[:HEAD_DIM].astype(BF16)
    dk_ref[...] = jnp.zeros_like(dk_ref)
    dv_ref[...] = jnp.zeros_like(dv_ref)
    lane = lax.broadcasted_iota(jnp.int32, (PART, 128), 1)
    for block in range(SIDE):
        seen = (block + 1) * PART
        rows = pl.ds(pl.multiple_of(slot_ref[block] * PART, PART), PART)
        bias = mask_bias(ends_ref, block)
        cosine, sine = cos_ref[rows, :], -sin_ref[rows, :]
        for pair in range(HEADS_LOCAL // 2):
            cols = slice(pair * 128, pair * 128 + 128)
            q, up = q_ref[rows, cols], up_ref[rows, cols]
            dqs, ps, dss = [], [], []
            for h in range(2):
                s = nt(keys_both[h][:seen], q) + bias
                p = jnp.exp(s - lse_ref[2 * pair + h : 2 * pair + h + 1, block * PART : seen])
                dp = nt(values_both[h][:seen], up)
                inner = jnp.sum(p * dp, axis=0, keepdims=True)
                ds = (p * (dp - inner)).astype(BF16)
                dqs.append(nn(keys_turned[:, :seen], ds))
                ps.append(p.astype(BF16))
                dss.append(ds)
            none = jnp.zeros_like(q)
            q_apart = jnp.concatenate(
                [jnp.where(lane < HEAD_DIM, q, none), jnp.where(lane < HEAD_DIM, none, q)], axis=0
            )
            up_apart = jnp.concatenate(
                [jnp.where(lane < HEAD_DIM, up, none), jnp.where(lane < HEAD_DIM, none, up)], axis=0
            )
            dk_ref[:seen, :] += nn(jnp.concatenate(dss, axis=1), q_apart)
            dv_ref[:seen, :] += nn(jnp.concatenate(ps, axis=1), up_apart)
            dq = jnp.concatenate(dqs, axis=0).T * 0.125
            out_ref[rows, cols] = turn(dq, cosine, sine).astype(BF16)
    lane = lax.broadcasted_iota(jnp.int32, (SEQ, 128), 1)
    dk, dv = dk_ref[...], dv_ref[...]
    dk, dv = dk + pltpu.roll(dk, HEAD_DIM, 1), dv + pltpu.roll(dv, HEAD_DIM, 1)
    dk_ref[...] = jnp.where(lane < HEAD_DIM, dk, dv)
    for block in range(SIDE):
        rows = pl.ds(pl.multiple_of(slot_ref[block] * PART, PART), PART)
        dkv = dk_ref[block * PART : (block + 1) * PART, :]
        turned = turn(dkv, cos_ref[rows, :], -sin_ref[rows, :])
        dkv = jnp.where(lane[:PART] < HEAD_DIM, turned, dkv)
        out_ref[rows, QUERY_COLS:QKV_COLS] = dkv.astype(BF16)


def small(n):
    return [pl.BlockSpec(memory_space=pltpu.SMEM)] * n


def attend_forward(qkv, tables):
    slot, ends, cosine, sine = tables
    return pl.pallas_call(
        forward_kernel,
        out_shape=(
            jax.ShapeDtypeStruct((SEQ, QUERY_COLS), BF16),
            jax.ShapeDtypeStruct((SEQ, QUERY_COLS), BF16),
            jax.ShapeDtypeStruct((SEQ, 128), BF16),
            jax.ShapeDtypeStruct((HEADS_LOCAL, SEQ), F32),
        ),
        in_specs=small(2) + whole(3),
        out_specs=whole(4),
        scratch_shapes=[pltpu.VMEM((SEQ, 128), BF16)],
        compiler_params=pltpu.CompilerParams(vmem_limit_bytes=24 * 2**20),
        cost_estimate=cost(8),
    )(slot, ends, qkv, cosine, sine)


def attend_backward(q, kv, lse, upstream, tables):
    slot, ends, cosine, sine = tables
    return pl.pallas_call(
        backward_kernel,
        out_shape=jax.ShapeDtypeStruct((SEQ, QKV_COLS), BF16),
        in_specs=small(2) + whole(6),
        out_specs=pl.BlockSpec(memory_space=pltpu.VMEM),
        scratch_shapes=[
            pltpu.VMEM((SEQ, 128), BF16),
            pltpu.VMEM((SEQ, 128), F32),
            pltpu.VMEM((SEQ, 128), F32),
        ],
        compiler_params=pltpu.CompilerParams(vmem_limit_bytes=24 * 2**20),
        cost_estimate=cost(10),
    )(slot, ends, q, kv, lse, upstream, cosine, sine)


def attention_tables(lengths):
    block = lax.axis_index("mp") ^ pair_steps(place()[2])
    slot = jnp.sum(
        jnp.where(block[None, :] == jnp.arange(SIDE)[:, None], jnp.arange(SIDE)[None, :], 0), axis=1
    ).astype(jnp.int32)
    token = (block[:, None] * PART + jnp.arange(PART)[None, :]).reshape(SEQ)
    ends = jnp.cumsum(lengths).astype(jnp.int32)
    starts = ends - lengths
    leading = jnp.max(jnp.where(starts[None, :] <= token[:, None], starts[None, :], 0), axis=1)
    indices = jnp.arange(HEAD_DIM // 2).astype(F32)
    frequency = 1.0 / THETA ** (2.0 * indices / HEAD_DIM)
    angles = (token - leading).astype(F32)[:, None] * frequency[None, :]
    cosine, sine = jnp.cos(angles), jnp.sin(angles)
    cosine = jnp.concatenate([cosine] * 4, axis=1)
    sine = jnp.concatenate([-sine, sine, -sine, sine], axis=1)
    return slot, ends, cosine, sine


def adamw(weight, gradient, moment, square, rate, decay):
    momentum = BETA_ONE * moment + (1.0 - BETA_ONE) * gradient
    variance = BETA_TWO * square + (1.0 - BETA_TWO) * gradient * gradient
    moment_hat = momentum / (1.0 - BETA_ONE**STEP)
    square_hat = variance / (1.0 - BETA_TWO**STEP)
    updated = weight - rate * (moment_hat / (jnp.sqrt(square_hat) + ADAM_EPS) + decay * weight)
    return (momentum, variance, updated)


def inverse_rms(v):
    return lax.rsqrt(jnp.mean(v * v, axis=-1, keepdims=True) + EPS)


def norm_backward(v, inverse, upstream):
    inner = jnp.mean(upstream * v, axis=-1, keepdims=True)
    return inverse * upstream - v * (inverse * inverse * inverse * inner)


def after(x, *others):
    return lax.optimization_barrier((x, *others))[0]


def on_device(
    residual, cotangent, document_lengths,
    norm_gains, query_weight, keyvalue_weight, output_weight, gateup_weight, down_weight,
    moment_gains, moment_query, moment_keyvalue, moment_output, moment_gateup, moment_down,
    square_gains, square_query, square_keyvalue, square_output, square_gateup, square_down,
):
    residual, cotangent = residual[0], cotangent[0]
    half = SEQ // 2

    inverse_one = inverse_rms(residual)
    normed_one = (residual * inverse_one).astype(BF16)
    one_near = jnp.concatenate([normed_one, pair_z(normed_one, 0)])
    part, ffn_part = prepare(
        norm_gains, after(query_weight, normed_one),
        keyvalue_weight, output_weight, gateup_weight, down_weight,
    )
    line = jnp.stack([part, shift_first(part, 1), shift_first(part, -1), shift_first(part, 2)])
    ffn_full = lax.all_gather(ffn_part, "dp", axis=0, tiled=True)
    tables = attention_tables(document_lengths[0])
    line = after(line, one_near, *tables)
    plane = [line, shift_second(line, 1), shift_second(line, -1), shift_second(line, 2)]
    one_far = pair_z(one_near, 1)
    low_cotangent = after(cotangent.astype(BF16), one_near)
    cot_near = jnp.concatenate([low_cotangent, pair_z(low_cotangent, 0)])
    mine = jnp.stack(plane, axis=1).reshape(SIDE * SIDE, *part.shape)
    mine = after(mine, one_far, cot_near)
    other = swap_core(mine)
    cot_far = pair_z(cot_near, 1)
    qkv_full, output_full = place_attention(mine, other)
    qkv = nn(one_near, qkv_full), nn(one_far, qkv_full)
    attended, q, kv, lse = attend_forward(jnp.concatenate(qkv), tables)

    far = nt(after(attended, cot_far)[half:], output_full).astype(BF16)
    got = pair_z(far, 1)
    near = nt(after(attended, far)[:half], output_full)
    cot_rows = jnp.concatenate([cot_near, cot_far])
    cot_turned = turned(after(cot_rows, near))
    keep, sent = split_sum(near, after(got, cot_turned))
    middle = residual + (keep + pair_z(sent, 0).astype(F32))
    inverse_two = inverse_rms(middle)
    normed_two = (middle * inverse_two).astype(BF16)
    got = pair_z(normed_two, 0)
    down_full = ffn_full[:, 2 * HIDDEN :]
    grad_hidden = nn(after(cot_rows, normed_two), down_full)
    two_near = jnp.concatenate([normed_two, after(got, grad_hidden)])
    two_far = pair_z(two_near, 1)

    hidden, grad_gate, grad_up = hidden_units(two_near, two_far, grad_hidden, ffn_full)
    near, far = back_to_rows(grad_gate, grad_up, ffn_full)
    got = pair_z(far, 1)
    rows_turned = turned(after(jnp.concatenate([two_near, two_far]), far))
    grad_a = weight_gradients(rows_turned, grad_gate, cot_turned, hidden, slice(0, SPLIT))
    grad_b = weight_gradients(
        rows_turned, after(grad_up, *grad_a), cot_turned, hidden, slice(SPLIT, HIDDEN)
    )
    keep, sent = split_sum(near, after(got, *grad_b))
    got = pair_z(sent, 0)
    got_a, got_b = swap_core(after(grad_a[1], sent)), swap_core(after(grad_b[1], sent))
    down = nt(after(hidden, sent), down_full)
    grad_normed_two = keep + after(got, down).astype(F32)

    grad_middle = cotangent + norm_backward(middle, inverse_two, grad_normed_two)
    low_grad = grad_middle.astype(BF16)
    got_low = pair_z(low_grad, 0)
    near_a, far_a = fold(after(grad_a[0], low_grad), got_a, True, 4)
    got_line_a = pair_first(far_a, 1, True)
    near_b, far_b = fold(after(grad_b[0], near_a), got_b, False, 4)
    got_line_b = pair_first(far_b, 1, False)
    rows_near = jnp.concatenate([low_grad, after(got_low, near_b)])
    rows_far = pair_z(rows_near, 1)
    rows_middle = jnp.concatenate([rows_near, rows_far])
    grad_attended = nn(rows_middle, output_full).astype(BF16)
    down_far = after(down[half:].astype(BF16), rows_middle)
    got_down = pair_z(down_far, 1)
    grad_output = by_chip(tn(rows_middle, after(attended, grad_attended)).astype(BF16))
    got_output = swap_core(grad_output[1])
    grad_projected = attend_backward(q, kv, lse, after(grad_attended, *grad_output), tables)

    grad = nt(grad_projected, qkv_full)
    near, far = grad[:half], after(grad[half:].astype(BF16), got_down)
    got = pair_z(far, 1)
    rows_one = jnp.concatenate([one_near, one_far])
    grad_qkv = by_chip(tn(rows_one, after(grad_projected, far)).astype(BF16))
    got_qkv = swap_core(grad_qkv[1])
    keep_a, sent_a = split_sum(near_a, after(got_line_a, *grad_qkv))
    got_a = pair_first(sent_a, 0, True)
    keep_b, sent_b = split_sum(near_b, after(got_line_b, *grad_qkv))
    got_b = pair_first(sent_b, 0, False)
    near_output, far_output = fold(after(grad_output[0], sent_a, sent_b), got_output, False, 20)
    got_line_output = pair_first(far_output, 1, False)
    near_qkv, far_qkv = fold(after(grad_qkv[0], near_output), got_qkv, True, 1)
    got_line_qkv = pair_first(far_qkv, 1, True)
    keep, sent = split_sum(near, after(got, near_qkv))
    got = pair_z(sent, 0)

    keep_down, sent_down = split_sum(down[:half], after(got_down, sent))
    got_down = pair_z(sent_down, 0)
    grad_normed_one = keep + got.astype(F32)
    line_a = (keep_a + after(got_a, sent).astype(F32)).astype(BF16)
    line_b = (keep_b + after(got_b, sent).astype(F32)).astype(BF16)
    keep_qkv, sent_qkv = split_sum(near_qkv, after(got_line_qkv, line_a, line_b))
    got_line_qkv = pair_first(sent_qkv, 0, True)
    keep_output, sent_output = split_sum(near_output, after(got_line_output, sent_qkv))
    got_line_output = pair_first(sent_output, 0, False)
    input_gradient = grad_middle + norm_backward(residual, inverse_one, grad_normed_one)
    block_output = middle + (keep_down + got_down.astype(F32))
    grad_ffn_a = scatter_second(line_a, True)
    grad_ffn_b = scatter_second(line_b, False)
    line_qkv = (keep_qkv + got_line_qkv.astype(F32)).astype(BF16)
    line_output = (keep_output + got_line_output.astype(F32)).astype(BF16)
    grad_qkv = scatter_second(line_qkv, True)
    grad_output = scatter_second(line_output, False)

    low_gains = norm_gains.astype(BF16).astype(F32)
    gain_one, gain_two = low_gains[0][:, None], low_gains[1][:, None]
    low_qkv = jnp.concatenate(
        (query_weight, keyvalue_weight[0], keyvalue_weight[1]), axis=1
    ).astype(BF16)
    low_gate, low_up = (w.astype(BF16).astype(F32) for w in (gateup_weight[0], gateup_weight[1]))
    gain_parts = jnp.stack(
        (
            jnp.sum(low_qkv.astype(F32) * grad_qkv, axis=1),
            jnp.sum(low_gate * grad_ffn_a[:, :HIDDEN], axis=1)
            + jnp.sum(low_up * grad_ffn_b[:, :HIDDEN], axis=1),
        )
    )
    gains = gain_parts + shift_z(gain_parts, 1) + shift_z(gain_parts, -1) + shift_z(gain_parts, 2)
    grad_qkv = grad_qkv * gain_one
    reduced = (
        gains,
        grad_qkv[:, :QUERY_COLS],
        jnp.stack((grad_qkv[:, QUERY_COLS : QUERY_COLS + 64], grad_qkv[:, QUERY_COLS + 64 :])),
        grad_output.T,
        jnp.stack((grad_ffn_a[:, :HIDDEN] * gain_two, grad_ffn_b[:, :HIDDEN] * gain_two)),
        jnp.concatenate((grad_ffn_a[:, HIDDEN:], grad_ffn_b[:, HIDDEN:]), axis=1).T,
    )
    masters = (norm_gains, query_weight, keyvalue_weight, output_weight, gateup_weight, down_weight)
    moments = (
        moment_gains, moment_query, moment_keyvalue, moment_output, moment_gateup, moment_down,
    )
    squares = (
        square_gains, square_query, square_keyvalue, square_output, square_gateup, square_down,
    )
    results = [
        adamw(masters[i], reduced[i], moments[i], squares[i], RATES[i], DECAYS[i]) for i in range(6)
    ]
    return (
        block_output[None],
        input_gradient[None],
        *reduced,
        *(r[0] for r in results),
        *(r[1] for r in results),
        *(r[2] for r in results),
    )


def solution(mesh):
    rows = P("dp", "mp", None)
    weights = (
        P(None, "dp"),
        P("dp", "mp"),
        P(None, "dp", "mp"),
        P("mp", "dp"),
        P(None, "dp", "mp"),
        P("mp", "dp"),
    )
    return jax.shard_map(
        on_device,
        mesh=mesh,
        in_specs=(rows, rows, P("dp", None), *weights, *weights, *weights),
        out_specs=(rows, rows, *weights, *weights, *weights, *weights),
        check_vma=False,
    )
```

time: 416 us -> 333 us (0.80)
  waiting for transfers between devices: 174 us -> 93.3 us
  Pallas kernels: 26.1 us -> 68.6 us
  matrix products: 62.1 us -> 28.7 us
  starting transfers between devices: 89.5 us -> 66.5 us
  other arithmetic: 22.8 us -> 29.9 us
  local copies, waits for them, and re-layouts: 17.9 us -> 24.3 us
    ppermute x35 -> x3, waiting for transfers between devices: 88.6 us -> 3.56 us  [shift_z(): return lax.ppermute(x, 'mp', [(i, (i + by) % SIDE) for i in range(SIDE)])]
    ppermute x35 -> x3, starting transfers between devices: 58.4 us -> 5.41 us  [shift_z(): return lax.ppermute(x, 'mp', [(i, (i + by) % SIDE) for i in range(SIDE)])]
    pallas_call x0 -> x12, Pallas kernels: none -> 50 us  [the longest x2 16.7 us: weight_gradients(): pl.pallas_call(functools.partial(weights_kernel, at), out_shape=[jax.Shap...]
    ppermute x28 -> x43, starting transfers between devices: 30.8 us -> 61.1 us  [the longest x16 25.3 us: pair_z(): return lax.ppermute(a, ('dp', 'mp'), pairs)]
    ppermute x28 -> x43, waiting for transfers between devices: 66.8 us -> 89.8 us  [the longest x16 66 us: pair_z(): return lax.ppermute(a, ('dp', 'mp'), pairs)]
    reduce_scatter x2 -> x0, waiting for transfers between devices: 18.4 us -> none  [the longest x1 18.4 us: on_device(): lax.psum_scatter(tn(rows_two, grad_gateup).astype(BF16), 'dp', scatter_di...]
    dot_general x4 -> x2, matrix products: 19.5 us -> 5.44 us  [tn(): lax.dot_general(a, b, (((0,), (0,)), ((), ())), preferred_element_type=F32)]
    dot_general x4, matrix products: 23.5 us -> 12.4 us  [nn(): lax.dot_general(a, b, (((1,), (0,)), ((), ())), preferred_element_type=F32)]
  transfers between devices with their start and end apart: 66 -> 47, of which waited for: 34 -> 22; matrix products, arithmetic and copies ran while one was open for 17% -> 17% of each run, Pallas kernels for 6% -> 14%
where the time goes in v2:
time: 333 us; the launch traced here: 327 us
  waiting for transfers between devices  93.3 us (28%)
  Pallas kernels  68.6 us (21%)
  starting transfers between devices  66.5 us (20%)
  other arithmetic  29.9 us (9%)
  matrix products  28.7 us (9%)
  local copies, waits for them, and re-layouts  24.3 us (7%)
  between operations  15.8 us (5%)
    ppermute x16, waiting for transfers between devices, pair_z(): return lax.ppermute(a, ('dp', 'mp'), pairs)  66 us
    ppermute x16, starting transfers between devices, pair_z(): return lax.ppermute(a, ('dp', 'mp'), pairs)  25.3 us
    unnamed x149, local copies, waits for them, and re-layouts  20.2 us
    pallas_call x2, Pallas kernels, weight_gradients(): pl.pallas_call(functools.partial(weights_kernel, at), out_shape=[jax.Shap...  16.7 us
    ppermute x8, starting transfers between devices, pair_y(): return lax.ppermute(a, 'dp', pairs)  13.5 us
    ppermute x8, waiting for transfers between devices, pair_y(): return lax.ppermute(a, 'dp', pairs)  12.8 us
    dot_general x4, matrix products, nn(): lax.dot_general(a, b, (((1,), (0,)), ((), ())), preferred_element_type=F32)  12.4 us
    pallas_call x1, Pallas kernels, hidden_units(): pl.pallas_call(hidden_kernel, out_shape=[jax.ShapeDtypeStruct((SEQ, HIDDE...  11.4 us
  transfers between devices with their start and end apart: 47, of which 22 were waited for; matrix products, arithmetic and copies ran while one was open for 17% of the time, Pallas kernels for 14%

profile of v2, /device:TPU:0, one launch (start us, length us, event | category | flops | bytes accessed | tf_op | source)
XLA Modules:
  0.0 327.2 jit_solution(5099485817281514722)
XLA Ops:
  12.0 3.2 collective-permute-start.3
  21.3 5.2 %collective-permute-done = bf16[128,2048]{1,0:T(8,128)(2,1)} collective-permute-done((bf16[128,2048]{1,0:T(8,128)(2,1)S(1)}, bf16[128,2048]{1,0:T(8,128)(2,1)}, u32[]{:S(2)}, u32[]{:S(2)}) %collective-permute-start) | collective-permute-done | bytes 524320 | tf_op jit(solution)/shard_map/ppermute | solution.py:57
  27.7 4.1 %collective-permute-start.7 = (bf16[256,2048]{1,0:T(8,128)(2,1)S(1)}, bf16[256,2048]{1,0:T(8,128)(2,1)S(1)}, u32[]{:S(2)}, u32[]{:S(2)}) collective-permute-start(bf16[256,2048]{1,0:T(8,128)(2,1)S(1)} %pad_maximum_fusion.4), channel_id=1, source_target_pairs={{0,3},{1,2},{2,1},{3,0},{4,5},{5,4},{6,7},{7,6},{8,11},{9,10},{10,... | collective-permute-start | bytes 3145736 | tf_op jit(solution)/shard_map/ppermute | solution.py:57
  32.8 3.3 collective-permute-start.6
  39.1 7.6 %collective-permute-done.8 = bf16[128,2048]{1,0:T(8,128)(2,1)S(1)} collective-permute-done((bf16[128,2048]{1,0:T(8,128)(2,1)S(1)}, bf16[128,2048]{1,0:T(8,128)(2,1)S(1)}, u32[]{:S(2)}, u32[]{:S(2)}) %collective-permute-start.8) | collective-permute-done | bytes 524320 | tf_op jit(solution)/shard_map/ppermute | solution.py:57
  47.6 4.1 %collective-permute-done.5 = bf16[4,64,1152]{2,1,0:T(8,128)(2,1)S(1)} collective-permute-done((bf16[4,64,1152]{2,1,0:T(8,128)(2,1)S(1)}, bf16[4,64,1152]{2,1,0:T(8,128)(2,1)S(1)}, u32[]{:S(2)}, u32[]{:S(2)}) %collective-permute-start.5) | collective-permute-done | bytes 589856 | tf_op jit(solution)/shard_map/ppermute | solution.py:87
  55.4 3.2 collective-permute-start.10
  60.3 2.5 shard_map.423
  64.3 2.0 fusion.42
  66.5 8.3 %shard_map.424 = (bf16[512,512]{1,0:T(8,128)(2,1)S(1)}, bf16[512,512]{1,0:T(8,128)(2,1)S(1)}, bf16[512,128]{1,0:T(8,128)(2,1)S(1)}, f32[8,512]{1,0:T(8,128)S(1)}) custom-call(s32[4]{0:T(128)S(1)} %select_reduce_fusion.1.slot_ref, s32[4]{0:T(128)S(1)} %bitcast.144, f32[512,640]{1,0:T(8,128)S(1)} %pad_maximum_fusion.3.qkv_ref, ...), custom_call_target="tpu_custom_call" | custom-call | flops 8800000000 | bytes 24000000 | tf_op jit(solution)/shard_map/pallas_call | solution.py:466
  75.6 2.7 collective-permute-start.11
  80.2 2.3 shard_map.425.c_ref
  83.7 7.9 %collective-permute-done.11 = bf16[256,2048]{1,0:T(8,128)(2,1)S(1)} collective-permute-done((bf16[256,2048]{1,0:T(8,128)(2,1)S(1)}, bf16[256,2048]{1,0:T(8,128)(2,1)S(1)}, u32[]{:S(2)}, u32[]{:S(2)}) %collective-permute-start.11) | collective-permute-done | bytes 1048608 | tf_op jit(solution)/shard_map/ppermute | solution.py:57
  92.3 8.7 %collective-permute-done.12 = bf16[128,2048]{1,0:T(8,128)(2,1)S(1)} collective-permute-done((bf16[128,2048]{1,0:T(8,128)(2,1)S(1)}, bf16[128,2048]{1,0:T(8,128)(2,1)S(1)}, u32[]{:S(2)}, u32[]{:S(2)}) %collective-permute-start.12) | collective-permute-done | bytes 524320 | tf_op jit(solution)/shard_map/ppermute | solution.py:57
  103.8 6.6 %fusion.2.grad_hidden_ref = f32[512,1408]{1,0:T(8,128)S(1)} fusion(bf16[512,2048]{1,0:T(8,128)(2,1)} %constant_dynamic-update-slice_fusion.2.a_ref, bf16[2048,4224]{1,0:T(8,128)(2,1)} %all-gather.2.cloned.1.call-done.gate_w_ref.up_w_ref), kind=kOutput, calls=%fused_computation.2 | convolution fusion | flops 2952790016 | bytes 10747904 | tf_op jit(solution)/shard_map/dot_general | solution.py:200
  110.4 2.4 collective-permute-done.13
  114.1 2.9 collective-permute-start.14
  117.0 13.4 %collective-permute-done.14.far_ref = bf16[256,2048]{1,0:T(8,128)(2,1)S(1)} collective-permute-done((bf16[256,2048]{1,0:T(8,128)(2,1)S(1)}, bf16[256,2048]{1,0:T(8,128)(2,1)S(1)}, u32[]{:S(2)}, u32[]{:S(2)}) %collective-permute-start.14) | collective-permute-done | bytes 1048608 | tf_op jit(solution)/shard_map/ppermute | solution.py:57
  130.4 11.4 %shard_map.426 = (bf16[512,1408]{1,0:T(8,128)(2,1)S(1)}, bf16[512,1408]{1,0:T(8,128)(2,1)S(1)}, bf16[512,1408]{1,0:T(8,128)(2,1)S(1)}) custom-call(bf16[256,2048]{1,0:T(8,128)(2,1)S(1)} %pad_maximum_fusion.5.near_ref, bf16[256,2048]{1,0:T(8,128)(2,1)S(1)} %collective-permute-done.14.far_ref, bf16[2048,4224]{1,0:T(8,128)(2,1)S(1)} %copy-done.17, ...), custom_call_target="tpu_custom_call" | custom-call | flops 11000000512 | bytes 30000000 | tf_op jit(solution)/shard_map/pallas_call | solution.py:332
  141.8 10.3 %shard_map.427 = (f32[256,2048]{1,0:T(8,128)S(1)}, bf16[256,2048]{1,0:T(8,128)(2,1)S(1)}) custom-call(bf16[512,1408]{1,0:T(8,128)(2,1)S(1)} %get-tuple-element.102.gate_ref.b_ref, bf16[512,1408]{1,0:T(8,128)(2,1)S(1)} %get-tuple-element.109.up_ref.b_ref, bf16[2048,4224]{1,0:T(8,128)(2,1)} %all-gather.2.cloned.1.call-done.gate_w_ref.up_w_ref, ...), custom_call_target="tpu_custom_call" | custom-call | flops 11000000512 | bytes 30000000 | tf_op jit(solution)/shard_map/pallas_call | solution.py:247
  152.2 2.7 collective-permute-start.15
  158.6 8.4 %shard_map.429 = (bf16[16,64,2176]{2,1,0:T(8,128)(2,1)S(1)}, bf16[16,64,2176]{2,1,0:T(8,128)(2,1)}) custom-call(s32[1]{0:T(128)} %bitcast.5.core_ref, bf16[2048,512]{1,0:T(8,128)(2,1)S(1)} %shard_map.428.a_ref, bf16[512,1408]{1,0:T(8,128)(2,1)S(1)} %copy-done.26, bf16[2048,512]{1,0:T(8,128)(2,1)S(1)} %copy-done.7, bf16[512,1408]{1,0:T(8,128)(2,1)S(1)} %get-tuple-element.113.d_ref), custom_call_target="tpu_custom_call" | custom-call | flops 8800000000 | bytes 24000000 | tf_op jit(solution)/shard_map/pallas_call | solution.py:292
  167.0 8.3 %shard_map.430 = (bf16[16,64,2048]{2,1,0:T(8,128)(2,1)S(1)}, bf16[16,64,2048]{2,1,0:T(8,128)(2,1)}) custom-call(s32[1]{0:T(128)} %bitcast.5.core_ref, bf16[2048,512]{1,0:T(8,128)(2,1)S(1)} %shard_map.428.a_ref, bf16[512,1408]{1,0:T(8,128)(2,1)S(1)} %copy-done.24, bf16[2048,512]{1,0:T(8,128)(2,1)S(1)} %copy-done.7, bf16[512,1408]{1,0:T(8,128)(2,1)S(1)} %get-tuple-element.113.d_ref), custom_call_target="tpu_custom_call" | custom-call | flops 8800000000 | bytes 24000000 | tf_op jit(solution)/shard_map/pallas_call | solution.py:292
  175.3 2.0 copy-done.27
  179.1 7.6 %fusion = f32[512,2048]{1,0:T(8,128)} fusion(bf16[512,1408]{1,0:T(8,128)(2,1)S(1)} %get-tuple-element.113.d_ref, bf16[2048,4224]{1,0:T(8,128)(2,1)} %all-gather.2.cloned.1.call-done.gate_w_ref.up_w_ref), kind=kOutput, calls=%fused_computation | convolution fusion | flops 2952790016 | bytes 11403264 | tf_op jit(solution)/shard_map/dot_general | solution.py:192
  189.7 2.4 fusion.49
  205.0 2.7 collective-permute-start.21
  209.1 2.4 collective-permute-start.24
  211.5 7.3 %collective-permute-done.20 = bf16[256,2048]{1,0:T(8,128)(2,1)} collective-permute-done((bf16[256,2048]{1,0:T(8,128)(2,1)}, bf16[256,2048]{1,0:T(8,128)(2,1)}, u32[]{:S(2)}, u32[]{:S(2)}) %collective-permute-start.20) | collective-permute-done | bytes 1048608 | tf_op jit(solution)/shard_map/ppermute | solution.py:57
  218.8 2.8 convolution_convert_fusion.3.up_ref
  221.6 2.5 convolution_convert_fusion.1
  225.2 10.3 %shard_map.433 = bf16[512,640]{1,0:T(8,128)(2,1)S(1)} custom-call(s32[4]{0:T(128)S(1)} %select_reduce_fusion.1.slot_ref, s32[4]{0:T(128)S(1)} %bitcast.145, bf16[512,512]{1,0:T(8,128)(2,1)S(1)} %copy-done.30, bf16[512,128]{1,0:T(8,128)(2,1)S(1)} %get-tuple-element.124.kv_ref, f32[8,512]{1,0:T(8,128)S(1)} %get-tuple-element.125.lse_ref, ...), custom_call_target="tpu_custom_call" | custom-call | flops 11000000512 | bytes 30000000 | tf_op jit(solution)/shard_map/pallas_call | solution.py:484
  239.1 2.9 convolution_convert_fusion
  246.6 7.0 %collective-permute-done.22 = bf16[256,2048]{1,0:T(8,128)(2,1)S(1)} collective-permute-done((bf16[256,2048]{1,0:T(8,128)(2,1)S(1)}, bf16[256,2048]{1,0:T(8,128)(2,1)S(1)}, u32[]{:S(2)}, u32[]{:S(2)}) %collective-permute-start.22) | collective-permute-done | bytes 1048608 | tf_op jit(solution)/shard_map/ppermute | solution.py:57
  255.1 2.0 collective-permute-start.42
  257.2 2.1 collective-permute-start.27
  259.3 3.7 %collective-permute-done.28 = bf16[128,2048]{1,0:T(8,128)(2,1)S(1)} collective-permute-done((bf16[128,2048]{1,0:T(8,128)(2,1)S(1)}, bf16[128,2048]{1,0:T(8,128)(2,1)S(1)}, u32[]{:S(2)}, u32[]{:S(2)}) %collective-permute-start.28) | collective-permute-done | bytes 524320 | tf_op jit(solution)/shard_map/ppermute | solution.py:57
  266.0 7.7 %collective-permute-done.31 = bf16[4,64,2048]{2,1,0:T(8,128)(2,1)S(1)} collective-permute-done((bf16[4,64,2048]{2,1,0:T(8,128)(2,1)S(1)}, bf16[4,64,2048]{2,1,0:T(8,128)(2,1)S(1)}, u32[]{:S(2)}, u32[]{:S(2)}) %collective-permute-start.31) | collective-permute-done | bytes 1048608 | tf_op jit(solution)/shard_map/ppermute | solution.py:67
  274.2 2.8 collective-permute-done.30
  282.8 2.4 collective-permute-start.35
  286.1 2.8 collective-permute-start.44
  289.0 2.4 collective-permute-start.33
  295.0 2.1 collective-permute-done.45
  300.5 2.0 collective-permute-done.34
  304.4 2.4 collective-permute-done.36
  309.1 3.3 %collective-permute-start.41 = (f32[2,64]{1,0:T(2,128)S(1)}, f32[2,64]{1,0:T(2,128)S(1)}, u32[]{:S(2)}, u32[]{:S(2)}) collective-permute-start(f32[2,64]{1,0:T(2,128)S(1)} %pad_maximum_fusion.12), channel_id=1, source_target_pairs={{0,2},{1,3},{2,0},{3,1},{4,6},{5,7},{6,4},{7,5},{8,10},{9,11},{10,... | collective-permute-start | bytes 1544 | tf_op jit(solution)/shard_map/ppermute | solution.py:71
  312.4 2.1 collective-permute-start.40
  316.0 3.3 %collective-permute-done.39 = f32[2,64]{1,0:T(2,128)S(1)} collective-permute-done((f32[2,64]{1,0:T(2,128)S(1)}, f32[2,64]{1,0:T(2,128)S(1)}, u32[]{:S(2)}, u32[]{:S(2)}) %collective-permute-start.39) | collective-permute-done | bytes 544 | tf_op jit(solution)/shard_map/ppermute | solution.py:71
  (299 shorter events, 89.0 us)
Async XLA Ops:
  7.3 96.5 %all-gather.2.cloned.1.call-start = ((), (), s32[]{:S(2)}) async-start(), calls=%async_computation | async-start | bytes 17842176 | tf_op jit(solution)/shard_map/all_gather | solution.py:556
  12.0 19.8 %collective-permute-start.3 = (bf16[64,1152]{1,0:T(8,128)(2,1)S(1)}, bf16[64,1152]{1,0:T(8,128)(2,1)S(1)}, u32[]{:S(2)}, u32[]{:S(2)}) collective-permute-start(bf16[64,1152]{1,0:T(8,128)(2,1)S(1)} %get-tuple-element.87), channel_id=1, source_target_pairs={{0,16},{4,68},{8,24},{12,76},{16,0},{20,84},{24,8},{28,92},{32,48}... | collective-permute-start | bytes 442376 | tf_op jit(solution)/shard_map/ppermute | solution.py:79
  15.2 16.6 %collective-permute-start.2 = (bf16[64,1152]{1,0:T(8,128)(2,1)S(1)}, bf16[64,1152]{1,0:T(8,128)(2,1)S(1)}, u32[]{:S(2)}, u32[]{:S(2)}) collective-permute-start(bf16[64,1152]{1,0:T(8,128)(2,1)S(1)} %get-tuple-element.87), channel_id=1, source_target_pairs={{0,24},{4,100},{8,0},{12,108},{16,8},{20,116},{24,16},{28,124},{32... | collective-permute-start | bytes 442376 | tf_op jit(solution)/shard_map/ppermute | solution.py:79
  16.4 15.5 %collective-permute-start.1 = (bf16[64,1152]{1,0:T(8,128)(2,1)S(1)}, bf16[64,1152]{1,0:T(8,128)(2,1)}, u32[]{:S(2)}, u32[]{:S(2)}) collective-permute-start(bf16[64,1152]{1,0:T(8,128)(2,1)S(1)} %get-tuple-element.87), channel_id=1, source_target_pairs={{0,8},{4,36},{8,16},{12,44},{16,24},{20,52},{24,0},{28,60},{32,40}... | collective-permute-start | bytes 442376 | tf_op jit(solution)/shard_map/ppermute | solution.py:79
  17.2 9.3 %collective-permute-start = (bf16[128,2048]{1,0:T(8,128)(2,1)S(1)}, bf16[128,2048]{1,0:T(8,128)(2,1)}, u32[]{:S(2)}, u32[]{:S(2)}) collective-permute-start(bf16[128,2048]{1,0:T(8,128)(2,1)S(1)} %fusion.19), channel_id=1, source_target_pairs={{0,1},{1,0},{2,3},{3,2},{4,7},{5,6},{6,5},{7,4},{8,9},{9,8},{10,11... | collective-permute-start | bytes 1572872 | tf_op jit(solution)/shard_map/ppermute | solution.py:57
  27.7 25.2 %collective-permute-start.7 = (bf16[256,2048]{1,0:T(8,128)(2,1)S(1)}, bf16[256,2048]{1,0:T(8,128)(2,1)S(1)}, u32[]{:S(2)}, u32[]{:S(2)}) collective-permute-start(bf16[256,2048]{1,0:T(8,128)(2,1)S(1)} %pad_maximum_fusion.4), channel_id=1, source_target_pairs={{0,3},{1,2},{2,1},{3,0},{4,5},{5,4},{6,7},{7,6},{8,11},{9,10},{10,... | collective-permute-start | bytes 3145736 | tf_op jit(solution)/shard_map/ppermute | solution.py:57
  31.8 14.9 %collective-permute-start.8 = (bf16[128,2048]{1,0:T(8,128)(2,1)S(1)}, bf16[128,2048]{1,0:T(8,128)(2,1)S(1)}, u32[]{:S(2)}, u32[]{:S(2)}) collective-permute-start(bf16[128,2048]{1,0:T(8,128)(2,1)S(1)} %bitcast_convert_fusion), channel_id=1, source_target_pairs={{0,1},{1,0},{2,3},{3,2},{4,7},{5,6},{6,5},{7,4},{8,9},{9,8},{10,11... | collective-permute-start | bytes 1572872 | tf_op jit(solution)/shard_map/ppermute | solution.py:57
  32.8 14.8 %collective-permute-start.6 = (bf16[4,64,1152]{2,1,0:T(8,128)(2,1)S(1)}, bf16[4,64,1152]{2,1,0:T(8,128)(2,1)S(1)}, u32[]{:S(2)}, u32[]{:S(2)}) collective-permute-start(bf16[4,64,1152]{2,1,0:T(8,128)(2,1)S(1)} %pad_maximum_fusion.8), channel_id=1, source_target_pairs={{0,64},{4,20},{8,72},{12,28},{16,80},{20,4},{24,88},{28,12},{32,96... | collective-permute-start | bytes 1769480 | tf_op jit(solution)/shard_map/ppermute | solution.py:87
  36.1 15.6 %collective-permute-start.5 = (bf16[4,64,1152]{2,1,0:T(8,128)(2,1)S(1)}, bf16[4,64,1152]{2,1,0:T(8,128)(2,1)S(1)}, u32[]{:S(2)}, u32[]{:S(2)}) collective-permute-start(bf16[4,64,1152]{2,1,0:T(8,128)(2,1)S(1)} %pad_maximum_fusion.8), channel_id=1, source_target_pairs={{0,96},{4,28},{8,104},{12,4},{16,112},{20,12},{24,120},{28,20},{32... | collective-permute-start | bytes 1769480 | tf_op jit(solution)/shard_map/ppermute | solution.py:87
  37.2 15.2 %collective-permute-start.4 = (bf16[4,64,1152]{2,1,0:T(8,128)(2,1)S(1)}, bf16[4,64,1152]{2,1,0:T(8,128)(2,1)S(1)}, u32[]{:S(2)}, u32[]{:S(2)}) collective-permute-start(bf16[4,64,1152]{2,1,0:T(8,128)(2,1)S(1)} %pad_maximum_fusion.8), channel_id=1, source_target_pairs={{0,32},{4,12},{8,40},{12,20},{16,48},{20,28},{24,56},{28,4},{32,64... | collective-permute-start | bytes 1769480 | tf_op jit(solution)/shard_map/ppermute | solution.py:87
  53.9 4.7 %collective-permute-start.9 = (bf16[16,64,1152]{2,1,0:T(8,128)(2,1)S(1)}, bf16[16,64,1152]{2,1,0:T(8,128)(2,1)}, u32[]{:S(2)}, u32[]{:S(2)}) collective-permute-start(bf16[16,64,1152]{2,1,0:T(8,128)(2,1)S(1)} %bitcast.135), channel_id=1, source_target_pairs={{0,4},{4,0},{8,12},{12,8},{16,20},{20,16},{24,28},{28,24},{32,36},... | collective-permute-start | bytes 7077896 | tf_op jit(solution)/shard_map/ppermute | solution.py:91
  55.4 19.4 %collective-permute-start.10 = (bf16[256,2048]{1,0:T(8,128)(2,1)}, bf16[256,2048]{1,0:T(8,128)(2,1)S(1)}, u32[]{:S(2)}, u32[]{:S(2)}) collective-permute-start(bf16[256,2048]{1,0:T(8,128)(2,1)} %copy-done.53), channel_id=1, source_target_pairs={{0,3},{1,2},{2,1},{3,0},{4,5},{5,4},{6,7},{7,6},{8,11},{9,10},{10,... | collective-permute-start | bytes 3145736 | tf_op jit(solution)/shard_map/ppermute | solution.py:57
  75.6 16.1 %collective-permute-start.11 = (bf16[256,2048]{1,0:T(8,128)(2,1)S(1)}, bf16[256,2048]{1,0:T(8,128)(2,1)S(1)}, u32[]{:S(2)}, u32[]{:S(2)}) collective-permute-start(bf16[256,2048]{1,0:T(8,128)(2,1)S(1)} %convolution_convert_fusion.2), channel_id=1, source_target_pairs={{0,3},{1,2},{2,1},{3,0},{4,5},{5,4},{6,7},{7,6},{8,11},{9,10},{10,... | collective-permute-start | bytes 3145736 | tf_op jit(solution)/shard_map/ppermute | solution.py:57
  91.8 9.3 %collective-permute-start.12 = (bf16[128,2048]{1,0:T(8,128)(2,1)S(1)}, bf16[128,2048]{1,0:T(8,128)(2,1)S(1)}, u32[]{:S(2)}, u32[]{:S(2)}) collective-permute-start(bf16[128,2048]{1,0:T(8,128)(2,1)S(1)} %fusion.15), channel_id=1, source_target_pairs={{0,1},{1,0},{2,3},{3,2},{4,7},{5,6},{6,5},{7,4},{8,9},{9,8},{10,11... | collective-permute-start | bytes 1572872 | tf_op jit(solution)/shard_map/ppermute | solution.py:57
  103.3 9.5 %collective-permute-start.13 = (bf16[128,2048]{1,0:T(8,128)(2,1)}, bf16[128,2048]{1,0:T(8,128)(2,1)}, u32[]{:S(2)}, u32[]{:S(2)}) collective-permute-start(bf16[128,2048]{1,0:T(8,128)(2,1)} %multiply_convert_fusion), channel_id=1, source_target_pairs={{0,1},{1,0},{2,3},{3,2},{4,7},{5,6},{6,5},{7,4},{8,9},{9,8},{10,11... | collective-permute-start | bytes 1572872 | tf_op jit(solution)/shard_map/ppermute | solution.py:57
  103.8 26.6 %copy-start.17 = (bf16[2048,4224]{1,0:T(8,128)(2,1)S(1)}, bf16[2048,4224]{1,0:T(8,128)(2,1)}, u32[]{:S(2)}) copy-start(bf16[2048,4224]{1,0:T(8,128)(2,1)} %all-gather.2.cloned.1.call-done.gate_w_ref.up_w_ref) | copy-start | bytes 51904516
  114.1 16.3 %collective-permute-start.14 = (bf16[256,2048]{1,0:T(8,128)(2,1)S(1)}, bf16[256,2048]{1,0:T(8,128)(2,1)S(1)}, u32[]{:S(2)}, u32[]{:S(2)}) collective-permute-start(bf16[256,2048]{1,0:T(8,128)(2,1)S(1)} %pad_maximum_fusion.5.near_ref), channel_id=1, source_target_pairs={{0,3},{1,2},{2,1},{3,0},{4,5},{5,4},{6,7},{7,6},{8,11},{9,10},{10,... | collective-permute-start | bytes 3145736 | tf_op jit(solution)/shard_map/ppermute | solution.py:57
  152.2 25.1 %collective-permute-start.15 = (bf16[256,2048]{1,0:T(8,128)(2,1)S(1)}, bf16[256,2048]{1,0:T(8,128)(2,1)}, u32[]{:S(2)}, u32[]{:S(2)}) collective-permute-start(bf16[256,2048]{1,0:T(8,128)(2,1)S(1)} %get-tuple-element.105), channel_id=1, source_target_pairs={{0,3},{1,2},{2,1},{3,0},{4,5},{5,4},{6,7},{7,6},{8,11},{9,10},{10,... | collective-permute-start | bytes 3145736 | tf_op jit(solution)/shard_map/ppermute | solution.py:57
  178.5 14.2 %collective-permute-start.18 = (bf16[16,64,2176]{2,1,0:T(8,128)(2,1)}, bf16[16,64,2176]{2,1,0:T(8,128)(2,1)S(1)}, u32[]{:S(2)}, u32[]{:S(2)}) collective-permute-start(bf16[16,64,2176]{2,1,0:T(8,128)(2,1)} %get-tuple-element.116), channel_id=1, source_target_pairs={{0,4},{4,0},{8,12},{12,8},{16,20},{20,16},{24,28},{28,24},{32,36},... | collective-permute-start | bytes 13369352 | tf_op jit(solution)/shard_map/ppermute | solution.py:91
  178.6 17.1 %collective-permute-start.19 = (bf16[16,64,2048]{2,1,0:T(8,128)(2,1)}, bf16[16,64,2048]{2,1,0:T(8,128)(2,1)S(1)}, u32[]{:S(2)}, u32[]{:S(2)}) collective-permute-start(bf16[16,64,2048]{2,1,0:T(8,128)(2,1)} %get-tuple-element.119), channel_id=1, source_target_pairs={{0,4},{4,0},{8,12},{12,8},{16,20},{20,16},{24,28},{28,24},{32,36},... | collective-permute-start | bytes 12582920 | tf_op jit(solution)/shard_map/ppermute | solution.py:91
  179.1 9.2 %collective-permute-start.16 = (bf16[128,2048]{1,0:T(8,128)(2,1)S(1)}, bf16[128,2048]{1,0:T(8,128)(2,1)S(1)}, u32[]{:S(2)}, u32[]{:S(2)}) collective-permute-start(bf16[128,2048]{1,0:T(8,128)(2,1)S(1)} %add_convert_fusion.4), channel_id=1, source_target_pairs={{0,1},{1,0},{2,3},{3,2},{4,7},{5,6},{6,5},{7,4},{8,9},{9,8},{10,11... | collective-permute-start | bytes 1572872 | tf_op jit(solution)/shard_map/ppermute | solution.py:57
  192.1 9.2 %collective-permute-start.17 = (bf16[128,2048]{1,0:T(8,128)(2,1)S(1)}, bf16[128,2048]{1,0:T(8,128)(2,1)S(1)}, u32[]{:S(2)}, u32[]{:S(2)}) collective-permute-start(bf16[128,2048]{1,0:T(8,128)(2,1)S(1)} %get-tuple-element.172), channel_id=1, source_target_pairs={{0,1},{1,0},{2,3},{3,2},{4,7},{5,6},{6,5},{7,4},{8,9},{9,8},{10,11... | collective-permute-start | bytes 1572872 | tf_op jit(solution)/shard_map/ppermute | solution.py:57
  202.5 16.3 %collective-permute-start.20 = (bf16[256,2048]{1,0:T(8,128)(2,1)}, bf16[256,2048]{1,0:T(8,128)(2,1)}, u32[]{:S(2)}, u32[]{:S(2)}) collective-permute-start(bf16[256,2048]{1,0:T(8,128)(2,1)} %pad_maximum_fusion.6), channel_id=1, source_target_pairs={{0,3},{1,2},{2,1},{3,0},{4,5},{5,4},{6,7},{7,6},{8,11},{9,10},{10,... | collective-permute-start | bytes 3145736 | tf_op jit(solution)/shard_map/ppermute | solution.py:57
  205.0 32.5 %collective-permute-start.21 = (bf16[256,2048]{1,0:T(8,128)(2,1)S(1)}, bf16[256,2048]{1,0:T(8,128)(2,1)S(1)}, u32[]{:S(2)}, u32[]{:S(2)}) collective-permute-start(bf16[256,2048]{1,0:T(8,128)(2,1)S(1)} %slice.457), channel_id=1, source_target_pairs={{0,3},{1,2},{2,1},{3,0},{4,5},{5,4},{6,7},{7,6},{8,11},{9,10},{10,... | collective-permute-start | bytes 3145736 | tf_op jit(solution)/shard_map/ppermute | solution.py:57
  207.7 36.3 %collective-permute-start.23 = (bf16[8,64,2176]{2,1,0:T(8,128)(2,1)}, bf16[8,64,2176]{2,1,0:T(8,128)(2,1)S(1)}, u32[]{:S(2)}, u32[]{:S(2)}) collective-permute-start(bf16[8,64,2176]{2,1,0:T(8,128)(2,1)} %copy-done.18), channel_id=1, source_target_pairs={{0,24},{4,12},{8,16},{12,4},{16,8},{20,28},{24,0},{28,20},{32,56},... | collective-permute-start | bytes 6684680 | tf_op jit(solution)/shard_map/ppermute | solution.py:62
  209.1 33.3 %collective-permute-start.24 = (bf16[8,64,2048]{2,1,0:T(8,128)(2,1)S(1)}, bf16[8,64,2048]{2,1,0:T(8,128)(2,1)S(1)}, u32[]{:S(2)}, u32[]{:S(2)}) collective-permute-start(bf16[8,64,2048]{2,1,0:T(8,128)(2,1)S(1)} %copy-done.20), channel_id=1, source_target_pairs={{0,96},{4,36},{8,104},{12,44},{16,112},{20,52},{24,120},{28,60},{3... | collective-permute-start | bytes 6291464 | tf_op jit(solution)/shard_map/ppermute | solution.py:67
  237.5 16.1 %collective-permute-start.22 = (bf16[256,2048]{1,0:T(8,128)(2,1)S(1)}, bf16[256,2048]{1,0:T(8,128)(2,1)S(1)}, u32[]{:S(2)}, u32[]{:S(2)}) collective-permute-start(bf16[256,2048]{1,0:T(8,128)(2,1)S(1)} %slice.456), channel_id=1, source_target_pairs={{0,3},{1,2},{2,1},{3,0},{4,5},{5,4},{6,7},{7,6},{8,11},{9,10},{10,... | collective-permute-start | bytes 3145736 | tf_op jit(solution)/shard_map/ppermute | solution.py:57
  238.2 6.4 %collective-permute-start.25 = (bf16[16,64,512]{2,1,0:T(8,128)(2,1)S(1)}, bf16[16,64,512]{2,1,0:T(8,128)(2,1)S(1)}, u32[]{:S(2)}, u32[]{:S(2)}) collective-permute-start(bf16[16,64,512]{2,1,0:T(8,128)(2,1)S(1)} %get-tuple-element.180), channel_id=1, source_target_pairs={{0,4},{4,0},{8,12},{12,8},{16,20},{20,16},{24,28},{28,24},{32,36},... | collective-permute-start | bytes 3145736 | tf_op jit(solution)/shard_map/ppermute | solution.py:91
  242.3 3.3 %collective-permute-start.26 = (bf16[16,64,640]{2,1,0:T(8,128)(2,1)S(1)}, bf16[16,64,640]{2,1,0:T(8,128)(2,1)S(1)}, u32[]{:S(2)}, u32[]{:S(2)}) collective-permute-start(bf16[16,64,640]{2,1,0:T(8,128)(2,1)S(1)} %get-tuple-element.178), channel_id=1, source_target_pairs={{0,4},{4,0},{8,12},{12,8},{16,20},{20,16},{24,28},{28,24},{32,36},... | collective-permute-start | bytes 3932168 | tf_op jit(solution)/shard_map/ppermute | solution.py:91
  253.7 9.3 %collective-permute-start.28 = (bf16[128,2048]{1,0:T(8,128)(2,1)S(1)}, bf16[128,2048]{1,0:T(8,128)(2,1)S(1)}, u32[]{:S(2)}, u32[]{:S(2)}) collective-permute-start(bf16[128,2048]{1,0:T(8,128)(2,1)S(1)} %fusion.11), channel_id=1, source_target_pairs={{0,1},{1,0},{2,3},{3,2},{4,7},{5,6},{6,5},{7,4},{8,9},{9,8},{10,11... | collective-permute-start | bytes 1572872 | tf_op jit(solution)/shard_map/ppermute | solution.py:57
  253.8 19.8 %collective-permute-start.31 = (bf16[4,64,2048]{2,1,0:T(8,128)(2,1)S(1)}, bf16[4,64,2048]{2,1,0:T(8,128)(2,1)S(1)}, u32[]{:S(2)}, u32[]{:S(2)}) collective-permute-start(bf16[4,64,2048]{2,1,0:T(8,128)(2,1)S(1)} %add_convert_fusion.3), channel_id=1, source_target_pairs={{0,32},{4,100},{8,40},{12,108},{16,48},{20,116},{24,56},{28,124},{... | collective-permute-start | bytes 3145736 | tf_op jit(solution)/shard_map/ppermute | solution.py:67
  254.5 22.5 %collective-permute-start.30 = (bf16[4,64,2176]{2,1,0:T(8,128)(2,1)S(1)}, bf16[4,64,2176]{2,1,0:T(8,128)(2,1)S(1)}, u32[]{:S(2)}, u32[]{:S(2)}) collective-permute-start(bf16[4,64,2176]{2,1,0:T(8,128)(2,1)S(1)} %add_convert_fusion.1), channel_id=1, source_target_pairs={{0,8},{4,28},{8,0},{12,20},{16,24},{20,12},{24,16},{28,4},{32,40},... | collective-permute-start | bytes 3342344 | tf_op jit(solution)/shard_map/ppermute | solution.py:62
  255.1 23.1 %collective-permute-start.42 = (bf16[8,64,512]{2,1,0:T(8,128)(2,1)S(1)}, bf16[8,64,512]{2,1,0:T(8,128)(2,1)S(1)}, u32[]{:S(2)}, u32[]{:S(2)}) collective-permute-start(bf16[8,64,512]{2,1,0:T(8,128)(2,1)S(1)} %get-tuple-element.144), channel_id=1, source_target_pairs={{0,96},{4,36},{8,104},{12,44},{16,112},{20,52},{24,120},{28,60},{3... | collective-permute-start | bytes 1572872 | tf_op jit(solution)/shard_map/ppermute | solution.py:67
  257.2 22.3 %collective-permute-start.27 = (bf16[128,2048]{1,0:T(8,128)(2,1)S(1)}, bf16[128,2048]{1,0:T(8,128)(2,1)S(1)}, u32[]{:S(2)}, u32[]{:S(2)}) collective-permute-start(bf16[128,2048]{1,0:T(8,128)(2,1)S(1)} %fusion.10), channel_id=1, source_target_pairs={{0,1},{1,0},{2,3},{3,2},{4,7},{5,6},{6,5},{7,4},{8,9},{9,8},{10,11... | collective-permute-start | bytes 1572872 | tf_op jit(solution)/shard_map/ppermute | solution.py:57
  263.0 14.4 %collective-permute-start.29 = (bf16[8,64,640]{2,1,0:T(8,128)(2,1)S(1)}, bf16[8,64,640]{2,1,0:T(8,128)(2,1)S(1)}, u32[]{:S(2)}, u32[]{:S(2)}) collective-permute-start(bf16[8,64,640]{2,1,0:T(8,128)(2,1)S(1)} %get-tuple-element.140), channel_id=1, source_target_pairs={{0,24},{4,12},{8,16},{12,4},{16,8},{20,28},{24,0},{28,20},{32,56},... | collective-permute-start | bytes 1966088 | tf_op jit(solution)/shard_map/ppermute | solution.py:62
  277.5 11.4 %collective-permute-start.32 = (bf16[4,64,640]{2,1,0:T(8,128)(2,1)S(1)}, bf16[4,64,640]{2,1,0:T(8,128)(2,1)S(1)}, u32[]{:S(2)}, u32[]{:S(2)}) collective-permute-start(bf16[4,64,640]{2,1,0:T(8,128)(2,1)S(1)} %add_convert_fusion.6), channel_id=1, source_target_pairs={{0,8},{4,28},{8,0},{12,20},{16,24},{20,12},{24,16},{28,4},{32,40},... | collective-permute-start | bytes 983048 | tf_op jit(solution)/shard_map/ppermute | solution.py:62
  278.3 7.7 %collective-permute-start.43 = (bf16[4,64,512]{2,1,0:T(8,128)(2,1)S(1)}, bf16[4,64,512]{2,1,0:T(8,128)(2,1)S(1)}, u32[]{:S(2)}, u32[]{:S(2)}) collective-permute-start(bf16[4,64,512]{2,1,0:T(8,128)(2,1)S(1)} %add_convert_fusion.9), channel_id=1, source_target_pairs={{0,32},{4,100},{8,40},{12,108},{16,48},{20,116},{24,56},{28,124},{... | collective-permute-start | bytes 786440 | tf_op jit(solution)/shard_map/ppermute | solution.py:67
  280.8 12.5 %collective-permute-start.37 = (bf16[2,64,2048]{2,1,0:T(8,128)(2,1)S(1)}, bf16[2,64,2048]{2,1,0:T(8,128)(2,1)S(1)}, u32[]{:S(2)}, u32[]{:S(2)}) collective-permute-start(bf16[2,64,2048]{2,1,0:T(8,128)(2,1)S(1)} %slice.331), channel_id=1, source_target_pairs={{0,24},{4,12},{8,16},{12,4},{16,8},{20,28},{24,0},{28,20},{32,56},... | collective-permute-start | bytes 1572872 | tf_op jit(solution)/shard_map/ppermute | solution.py:62
  282.8 17.1 %collective-permute-start.35 = (bf16[2,64,2176]{2,1,0:T(8,128)(2,1)S(1)}, bf16[2,64,2176]{2,1,0:T(8,128)(2,1)S(1)}, u32[]{:S(2)}, u32[]{:S(2)}) collective-permute-start(bf16[2,64,2176]{2,1,0:T(8,128)(2,1)S(1)} %slice.324), channel_id=1, source_target_pairs={{0,96},{4,36},{8,104},{12,44},{16,112},{20,52},{24,120},{28,60},{3... | collective-permute-start | bytes 1671176 | tf_op jit(solution)/shard_map/ppermute | solution.py:67
  286.1 6.6 %collective-permute-start.44 = (bf16[2,64,512]{2,1,0:T(8,128)(2,1)S(1)}, bf16[2,64,512]{2,1,0:T(8,128)(2,1)S(1)}, u32[]{:S(2)}, u32[]{:S(2)}) collective-permute-start(bf16[2,64,512]{2,1,0:T(8,128)(2,1)S(1)} %slice.340), channel_id=1, source_target_pairs={{0,24},{4,12},{8,16},{12,4},{16,8},{20,28},{24,0},{28,20},{32,56},... | collective-permute-start | bytes 393224 | tf_op jit(solution)/shard_map/ppermute | solution.py:62
  289.0 8.9 %collective-permute-start.33 = (bf16[2,64,640]{2,1,0:T(8,128)(2,1)S(1)}, bf16[2,64,640]{2,1,0:T(8,128)(2,1)S(1)}, u32[]{:S(2)}, u32[]{:S(2)}) collective-permute-start(bf16[2,64,640]{2,1,0:T(8,128)(2,1)S(1)} %slice.318), channel_id=1, source_target_pairs={{0,96},{4,36},{8,104},{12,44},{16,112},{20,52},{24,120},{28,60},{3... | collective-permute-start | bytes 491528 | tf_op jit(solution)/shard_map/ppermute | solution.py:67
  292.7 4.3 %collective-permute-start.45 = (bf16[1,64,512]{2,1,0:T(8,128)(2,1)S(1)}, bf16[1,64,512]{2,1,0:T(8,128)(2,1)S(1)}, u32[]{:S(2)}, u32[]{:S(2)}) collective-permute-start(bf16[1,64,512]{2,1,0:T(8,128)(2,1)S(1)} %add_convert_fusion.12), channel_id=1, source_target_pairs={{0,8},{4,28},{8,0},{12,20},{16,24},{20,12},{24,16},{28,4},{32,40},... | collective-permute-start | bytes 196616 | tf_op jit(solution)/shard_map/ppermute | solution.py:62
  293.4 10.9 %collective-permute-start.38 = (bf16[1,64,2048]{2,1,0:T(8,128)(2,1)S(1)}, bf16[1,64,2048]{2,1,0:T(8,128)(2,1)S(1)}, u32[]{:S(2)}, u32[]{:S(2)}) collective-permute-start(bf16[1,64,2048]{2,1,0:T(8,128)(2,1)S(1)} %add_convert_fusion.10), channel_id=1, source_target_pairs={{0,8},{4,28},{8,0},{12,20},{16,24},{20,12},{24,16},{28,4},{32,40},... | collective-permute-start | bytes 786440 | tf_op jit(solution)/shard_map/ppermute | solution.py:62
  298.0 4.5 %collective-permute-start.34 = (bf16[1,64,640]{2,1,0:T(8,128)(2,1)S(1)}, bf16[1,64,640]{2,1,0:T(8,128)(2,1)S(1)}, u32[]{:S(2)}, u32[]{:S(2)}) collective-permute-start(bf16[1,64,640]{2,1,0:T(8,128)(2,1)S(1)} %add_convert_fusion.11), channel_id=1, source_target_pairs={{0,32},{4,100},{8,40},{12,108},{16,48},{20,116},{24,56},{28,124},{... | collective-permute-start | bytes 245768 | tf_op jit(solution)/shard_map/ppermute | solution.py:67
  299.9 6.9 %collective-permute-start.36 = (bf16[1,64,2176]{2,1,0:T(8,128)(2,1)S(1)}, bf16[1,64,2176]{2,1,0:T(8,128)(2,1)S(1)}, u32[]{:S(2)}, u32[]{:S(2)}) collective-permute-start(bf16[1,64,2176]{2,1,0:T(8,128)(2,1)S(1)} %add_convert_fusion.7), channel_id=1, source_target_pairs={{0,32},{4,100},{8,40},{12,108},{16,48},{20,116},{24,56},{28,124},{... | collective-permute-start | bytes 835592 | tf_op jit(solution)/shard_map/ppermute | solution.py:67
  309.1 6.6 %collective-permute-start.41 = (f32[2,64]{1,0:T(2,128)S(1)}, f32[2,64]{1,0:T(2,128)S(1)}, u32[]{:S(2)}, u32[]{:S(2)}) collective-permute-start(f32[2,64]{1,0:T(2,128)S(1)} %pad_maximum_fusion.12), channel_id=1, source_target_pairs={{0,2},{1,3},{2,0},{3,1},{4,6},{5,7},{6,4},{7,5},{8,10},{9,11},{10,... | collective-permute-start | bytes 1544 | tf_op jit(solution)/shard_map/ppermute | solution.py:71
  312.4 3.6 %collective-permute-start.40 = (f32[2,64]{1,0:T(2,128)S(1)}, f32[2,64]{1,0:T(2,128)S(1)}, u32[]{:S(2)}, u32[]{:S(2)}) collective-permute-start(f32[2,64]{1,0:T(2,128)S(1)} %pad_maximum_fusion.12), channel_id=1, source_target_pairs={{0,3},{1,0},{2,1},{3,2},{4,7},{5,4},{6,5},{7,6},{8,11},{9,8},{10,9... | collective-permute-start | bytes 1544 | tf_op jit(solution)/shard_map/ppermute | solution.py:71
  314.5 4.8 %collective-permute-start.39 = (f32[2,64]{1,0:T(2,128)S(1)}, f32[2,64]{1,0:T(2,128)S(1)}, u32[]{:S(2)}, u32[]{:S(2)}) collective-permute-start(f32[2,64]{1,0:T(2,128)S(1)} %pad_maximum_fusion.12), channel_id=1, source_target_pairs={{0,1},{1,2},{2,3},{3,0},{4,5},{5,6},{6,7},{7,4},{8,9},{9,10},{10,1... | collective-permute-start | bytes 1544 | tf_op jit(solution)/shard_map/ppermute | solution.py:71
  (72 other events, 447.6 us)
Sparse Core Ops, SparseCore 0:
  12.2 83.5 all-gather.1

commit v3 on v2

--- a/solution.py
+++ b/solution.py
@@ -109,6 +109,10 @@
 
 def pair_steps(core):
     return jnp.where(core == 0, jnp.array([0, 1, 3, 2]), jnp.array([0, 3, 1, 2])).astype(jnp.int32)
+
+
+def send_sum(near, got):
+    return (near[PART:] + got[PART:].astype(F32)).astype(BF16)
 
 
 def split_sum(near, got):
@@ -146,46 +150,12 @@
     return [p.reshape(D, -1) for p in parts]
 
 
-def fold_kernel(x_first, here_ref, mine_ref, got_ref, near_ref, far_ref):
-    y, x, core = here_ref[0], here_ref[1], here_ref[2]
-    steps = lambda k: pick(k, (0, jnp.where(core == 0, 1, 3), jnp.where(core == 0, 3, 1), 2))
-
-    def chip(k):
-        first, second = steps(k // SIDE), steps(k % SIDE)
-        if x_first:
-            return (y ^ second) * SIDE + (x ^ first)
-        return (y ^ first) * SIDE + (x ^ second)
-
-    @pl.loop(0, 2 * SIDE)
-    def _(k):
-        i, j = chip(k), chip(2 * SIDE + k)
-        near_ref[k] = (mine_ref[i].astype(F32) + got_ref[i].astype(F32)).astype(BF16)
-        far_ref[k] = (mine_ref[j].astype(F32) + got_ref[j].astype(F32)).astype(BF16)
-
-
-def fold(mine, got, x_first, us):
-    n = mine.shape[2]
-    return pl.pallas_call(
-        functools.partial(fold_kernel, x_first),
-        out_shape=[jax.ShapeDtypeStruct((2 * SIDE, 64, n), BF16)] * 2,
-        in_specs=[pl.BlockSpec(memory_space=pltpu.SMEM)] + whole(2),
-        out_specs=whole(2),
-        compiler_params=pltpu.CompilerParams(vmem_limit_bytes=32 * 2**20),
-        cost_estimate=cost(us),
-    )(here(), mine, got)
-
-
 def pair_first(a, step, x_first):
     return (pair_x if x_first else pair_y)(a, step)
 
 
 def pair_second(a, step, x_first):
     return (pair_y if x_first else pair_x)(a, step)
-
-
-def scatter_second(line, x_first):
-    keep, sent = split_sum(line[:2], pair_second(line[2:], 1, x_first))
-    return keep[0] + pair_second(sent, 0, x_first)[0].astype(F32)
 
 
 def nt(a, b):
@@ -220,17 +190,18 @@
 
 
 def prepare(norm_gains, query, keyvalue, output, gateup, down):
+    full = lambda v: pl.BlockSpec(v.shape, lambda i: (0,) * len(v.shape))
+    arrays = (norm_gains.T, query, keyvalue, output.T, gateup, down.T)
+    outs = [jax.ShapeDtypeStruct((64, n), BF16) for n in (QKV_COLS + QUERY_COLS, 3 * HIDDEN)]
     return pl.pallas_call(
         prepare_kernel,
-        out_shape=[
-            jax.ShapeDtypeStruct((64, QKV_COLS + QUERY_COLS), BF16),
-            jax.ShapeDtypeStruct((64, 3 * HIDDEN), BF16),
-        ],
-        in_specs=whole(6),
-        out_specs=whole(2),
+        out_shape=outs,
+        grid=(1,),
+        in_specs=[full(v) for v in arrays],
+        out_specs=[full(v) for v in outs],
         compiler_params=pltpu.CompilerParams(vmem_limit_bytes=16 * 2**20),
         cost_estimate=cost(2),
-    )(norm_gains.T, query, keyvalue, output.T, gateup, down.T)
+    )(*arrays)
 
 
 def back_kernel(gate_ref, up_ref, gate_w_ref, up_w_ref, near_ref, far_ref):
@@ -255,55 +226,154 @@
     )(grad_gate, grad_up, weights, weights)
 
 
-def turn_kernel(a_ref, turned_ref):
-    turned_ref[...] = a_ref[...].T
-
-
-def turned(a):
+def turn_kernel(near_ref, far_ref, turned_ref):
+    turned_ref[:, : SEQ // 2] = near_ref[...].T
+    turned_ref[:, SEQ // 2 :] = far_ref[...].T
+
+
+def turned(near, far, us=1):
     return pl.pallas_call(
         turn_kernel,
         out_shape=jax.ShapeDtypeStruct((D, SEQ), BF16),
-        in_specs=whole(1),
+        in_specs=whole(2),
         out_specs=whole(1)[0],
         compiler_params=pltpu.CompilerParams(vmem_limit_bytes=16 * 2**20),
-        cost_estimate=cost(1),
-    )(a)
-
-
-def weights_kernel(at, core_ref, a_ref, b_ref, c_ref, d_ref, mine_ref, other_ref):
-    first = core_ref[0] == 0
-    n = b_ref.shape[1]
-
-    @pl.loop(0, D // 256)
-    def _(chunk):
-        rows = pl.ds(pl.multiple_of(chunk * 256, 256), 256)
-        out = nn(a_ref[rows, :], b_ref[...]).astype(BF16)
-        more = nn(c_ref[rows, :], d_ref[:, at]).astype(BF16)
-        for k in range(2):
-            for cols, full in ((slice(0, n), out), (slice(n, None), more)):
-                low, high = full[k * 128 : k * 128 + 64], full[k * 128 + 64 : k * 128 + 128]
-                mine_ref[chunk * 2 + k, :, cols] = jnp.where(first, low, high)
-                other_ref[chunk * 2 + k, :, cols] = jnp.where(first, high, low)
-
-
-def weight_gradients(a, b, c, d, at):
-    n = b.shape[1] + at.stop - at.start
-    _, _, core = place()
+        cost_estimate=cost(us),
+    )(near, far)
+
+
+def rows_kernel(a_ref, w_ref, near_ref, far_ref):
+    out = nt(a_ref[...], w_ref[...])
+    near_ref[...] = out[: SEQ // 2]
+    far_ref[...] = out[SEQ // 2 :].astype(BF16)
+
+
+def product_rows(a, w, at, us):
+    k, tile = a.shape[1], 512
+    out = pl.BlockSpec((SEQ // 2, tile), lambda i: (0, i))
     return pl.pallas_call(
-        functools.partial(weights_kernel, at),
-        out_shape=[jax.ShapeDtypeStruct((SIDE * SIDE, 64, n), BF16)] * 2,
-        in_specs=[pl.BlockSpec(memory_space=pltpu.SMEM)] + whole(4),
-        out_specs=whole(2),
-        compiler_params=pltpu.CompilerParams(vmem_limit_bytes=40 * 2**20),
-        cost_estimate=cost(8),
-    )(core[None], a, b, c, d)
-
-
-def by_chip(g):
-    _, _, core = place()
-    g = g.reshape(SIDE * SIDE, 2, 64, g.shape[1])
-    pick = lambda c: lax.dynamic_index_in_dim(g, c, 1, keepdims=False)
-    return pick(core), pick(1 - core)
+        rows_kernel,
+        out_shape=[jax.ShapeDtypeStruct((SEQ // 2, D), t) for t in (F32, BF16)],
+        grid=(D // tile,),
+        in_specs=[
+            pl.BlockSpec((SEQ, k), lambda i: (0, 0)),
+            pl.BlockSpec((tile, k), lambda i: (i, at)),
+        ],
+        out_specs=[out, out],
+        compiler_params=pltpu.CompilerParams(vmem_limit_bytes=24 * 2**20),
+        cost_estimate=cost(us),
+    )(a, w)
+
+
+def chip_at(k, here_ref, x_first):
+    y, x, core = here_ref[0], here_ref[1], here_ref[2]
+    steps = lambda i: pick(i, (0, jnp.where(core == 0, 1, 3), jnp.where(core == 0, 3, 1), 2))
+    first, second = steps(k // SIDE), steps(k % SIDE)
+    if x_first:
+        return (y ^ second) * SIDE + (x ^ first)
+    return (y ^ first) * SIDE + (x ^ second)
+
+
+def chip_products(cuts, refs, row):
+    outs = []
+    for i, cut in enumerate(cuts):
+        a_ref, b_ref = refs[2 * i], refs[2 * i + 1]
+        rows = [a_ref[pl.ds(pl.multiple_of(row(j), 64), 64), :] for j in range(SIDE)]
+        outs.append(nn(jnp.concatenate(rows, axis=0), b_ref[:, cut]))
+    return outs
+
+
+def other_kernel(cuts, here_ref, *refs):
+    step, core = pl.program_id(0), here_ref[2]
+    at = 0
+    for out in chip_products(cuts, refs, lambda j: (step * SIDE + j) * 128 + (1 - core) * 64):
+        for j in range(SIDE):
+            refs[-1][j, :, at : at + out.shape[1]] = out[j * 64 : j * 64 + 64].astype(BF16)
+        at += out.shape[1]
+
+
+def mine_kernel(cuts, x_first, here_ref, *refs):
+    step, core = pl.program_id(0), here_ref[2]
+    got = refs[2 * len(cuts) : 2 * len(cuts) + SIDE]
+    row = lambda j: chip_at(step * SIDE + j, here_ref, x_first) * 128 + core * 64
+    outs = chip_products(cuts, refs, row)
+    for half, out_ref in enumerate(refs[-2:]):
+
+        @pl.when(step // 2 == half)
+        def _():
+            at = 0
+            for out in outs:
+                cols = slice(at, at + out.shape[1])
+                for j in range(SIDE):
+                    sums = out[j * 64 : j * 64 + 64] + got[j][0, :, cols].astype(F32)
+                    out_ref[j, :, cols] = sums.astype(BF16)
+                at = cols.stop
+
+
+def weight_products(pairs, got, x_first, us):
+    cuts = [c for _, _, c in pairs]
+    arrays = [v for a, b, _ in pairs for v in (a, b)]
+    n = sum(c.stop - c.start for c in cuts)
+    full = lambda v: pl.BlockSpec(v.shape, lambda i, h: (0, 0))
+    block = (SIDE, 64, n)
+    if got is None:
+        kernel = functools.partial(other_kernel, cuts)
+        specs = [full(v) for v in arrays]
+        outs = jax.ShapeDtypeStruct((SIDE * SIDE, 64, n), BF16)
+        out_specs = pl.BlockSpec(block, lambda i, h: (i, 0, 0))
+    else:
+        kernel = functools.partial(mine_kernel, cuts, x_first)
+        chips = [
+            pl.BlockSpec((1, 64, n), lambda i, h, j=j: (chip_at(i * SIDE + j, h, x_first), 0, 0))
+            for j in range(SIDE)
+        ]
+        specs = [full(v) for v in arrays] + chips
+        arrays = arrays + [got] * SIDE
+        outs = [jax.ShapeDtypeStruct((2 * SIDE, 64, n), BF16)] * 2
+        out_specs = [
+            pl.BlockSpec(block, lambda i, h: (jnp.minimum(i, 1), 0, 0)),
+            pl.BlockSpec(block, lambda i, h: (jnp.maximum(i - 2, 0), 0, 0)),
+        ]
+    return pl.pallas_call(
+        kernel,
+        out_shape=outs,
+        grid_spec=pltpu.PrefetchScalarGridSpec(
+            num_scalar_prefetch=1, grid=(SIDE,), in_specs=specs, out_specs=out_specs
+        ),
+        compiler_params=pltpu.CompilerParams(vmem_limit_bytes=32 * 2**20),
+        cost_estimate=cost(us),
+    )(here(), *arrays)
+
+
+def norm_kernel(near_ref, got_ref, got_own_ref, residual_ref, middle_ref, low_ref):
+    got = got_ref[...].astype(F32) + got_own_ref[...].astype(F32)
+    v = residual_ref[...] + near_ref[...] + got
+    inverse = lax.rsqrt(jnp.mean(v * v, axis=-1, keepdims=True) + EPS)
+    middle_ref[...] = v
+    low_ref[...] = (v * inverse).astype(BF16)
+
+
+def norm_back_kernel(near_ref, got_ref, got_own_ref, v_ref, base_ref, out_ref, low_ref):
+    u = near_ref[...] + (got_ref[...].astype(F32) + got_own_ref[...].astype(F32))
+    v = v_ref[...]
+    inverse = lax.rsqrt(jnp.mean(v * v, axis=-1, keepdims=True) + EPS)
+    inner = jnp.mean(u * v, axis=-1, keepdims=True)
+    out = base_ref[...] + (inverse * u - v * (inverse * inverse * inverse * inner))
+    out_ref[...] = out
+    low_ref[...] = out.astype(BF16)
+
+
+def by_rows(kernel, *arrays):
+    block = pl.BlockSpec((32, D), lambda i: (i, 0))
+    return pl.pallas_call(
+        kernel,
+        out_shape=[jax.ShapeDtypeStruct((PART, D), t) for t in (F32, BF16)],
+        grid=(PART // 32,),
+        in_specs=[block] * len(arrays),
+        out_specs=[block, block],
+        compiler_params=pltpu.CompilerParams(vmem_limit_bytes=12 * 2**20),
+        cost_estimate=cost(1.5),
+    )(*arrays)
 
 
 def hidden_kernel(
@@ -386,23 +456,30 @@
     kv = ordered_ref[...]
     keys_both = halves(kv[:, :HEAD_DIM])
     values_turned = kv.astype(F32).T[HEAD_DIM:].astype(BF16)
+    heads = range(HEADS_LOCAL)
     for block in range(SIDE):
         seen = (block + 1) * PART
         rows = pl.ds(pl.multiple_of(slot_ref[block] * PART, PART), PART)
         bias = mask_bias(ends_ref, block)
-        for pair in range(HEADS_LOCAL // 2):
-            cols = slice(pair * 128, pair * 128 + 128)
-            q = q_ref[rows, cols]
-            outs = []
-            for h in range(2):
-                s = nt(keys_both[h][:seen], q) + bias
-                top = jnp.max(s, axis=0, keepdims=True)
-                e = jnp.exp(s - top)
-                total = jnp.sum(e, axis=0, keepdims=True)
-                p = (e * (1.0 / total)).astype(BF16)
-                outs.append(nn(values_turned[:, :seen], p))
-                lse_ref[2 * pair + h : 2 * pair + h + 1, block * PART : seen] = top + jnp.log(total)
-            att_ref[rows, cols] = jnp.concatenate(outs, axis=0).T.astype(BF16)
+        q = [q_ref[rows, k * 128 : (k + 1) * 128] for k in range(HEADS_LOCAL // 2)]
+        s = [nt(keys_both[h % 2][:seen], q[h // 2]) + bias for h in heads]
+        top = [jnp.max(v, axis=0, keepdims=True) for v in s]
+        e = [jnp.exp(v - t) for v, t in zip(s, top)]
+        total = [jnp.sum(v, axis=0, keepdims=True) for v in e]
+        p = [(v * (1.0 / t)).astype(BF16) for v, t in zip(e, total)]
+        out = [nn(values_turned[:, :seen], v) for v in p]
+        for h in heads:
+            lse_ref[h : h + 1, block * PART : seen] = top[h] + jnp.log(total[h])
+        for k in range(HEADS_LOCAL // 2):
+            both = jnp.concatenate(out[2 * k : 2 * k + 2], axis=0)
+            att_ref[rows, k * 128 : (k + 1) * 128] = both.T.astype(BF16)
+
+
+def apart(x):
+    lane = lax.broadcasted_iota(jnp.int32, x.shape, 1)
+    none = jnp.zeros_like(x)
+    first = lane < HEAD_DIM
+    return jnp.concatenate([jnp.where(first, x, none), jnp.where(first, none, x)], axis=0)
 
 
 def backward_kernel(
@@ -415,36 +492,28 @@
     keys_turned = kv.astype(F32).T[:HEAD_DIM].astype(BF16)
     dk_ref[...] = jnp.zeros_like(dk_ref)
     dv_ref[...] = jnp.zeros_like(dv_ref)
-    lane = lax.broadcasted_iota(jnp.int32, (PART, 128), 1)
+    heads, pairs = range(HEADS_LOCAL), range(HEADS_LOCAL // 2)
     for block in range(SIDE):
         seen = (block + 1) * PART
         rows = pl.ds(pl.multiple_of(slot_ref[block] * PART, PART), PART)
         bias = mask_bias(ends_ref, block)
         cosine, sine = cos_ref[rows, :], -sin_ref[rows, :]
-        for pair in range(HEADS_LOCAL // 2):
-            cols = slice(pair * 128, pair * 128 + 128)
-            q, up = q_ref[rows, cols], up_ref[rows, cols]
-            dqs, ps, dss = [], [], []
-            for h in range(2):
-                s = nt(keys_both[h][:seen], q) + bias
-                p = jnp.exp(s - lse_ref[2 * pair + h : 2 * pair + h + 1, block * PART : seen])
-                dp = nt(values_both[h][:seen], up)
-                inner = jnp.sum(p * dp, axis=0, keepdims=True)
-                ds = (p * (dp - inner)).astype(BF16)
-                dqs.append(nn(keys_turned[:, :seen], ds))
-                ps.append(p.astype(BF16))
-                dss.append(ds)
-            none = jnp.zeros_like(q)
-            q_apart = jnp.concatenate(
-                [jnp.where(lane < HEAD_DIM, q, none), jnp.where(lane < HEAD_DIM, none, q)], axis=0
-            )
-            up_apart = jnp.concatenate(
-                [jnp.where(lane < HEAD_DIM, up, none), jnp.where(lane < HEAD_DIM, none, up)], axis=0
-            )
-            dk_ref[:seen, :] += nn(jnp.concatenate(dss, axis=1), q_apart)
-            dv_ref[:seen, :] += nn(jnp.concatenate(ps, axis=1), up_apart)
-            dq = jnp.concatenate(dqs, axis=0).T * 0.125
-            out_ref[rows, cols] = turn(dq, cosine, sine).astype(BF16)
+        q = [q_ref[rows, k * 128 : (k + 1) * 128] for k in pairs]
+        up = [up_ref[rows, k * 128 : (k + 1) * 128] for k in pairs]
+        s = [nt(keys_both[h % 2][:seen], q[h // 2]) + bias for h in heads]
+        dp = [nt(values_both[h % 2][:seen], up[h // 2]) for h in heads]
+        p = [jnp.exp(s[h] - lse_ref[h : h + 1, block * PART : seen]) for h in heads]
+        inner = [jnp.sum(p[h] * dp[h], axis=0, keepdims=True) for h in heads]
+        ds = [(p[h] * (dp[h] - inner[h])).astype(BF16) for h in heads]
+        p = [v.astype(BF16) for v in p]
+        dq = [nn(keys_turned[:, :seen], v) for v in ds]
+        q_apart = jnp.concatenate([apart(v) for v in q], axis=0)
+        up_apart = jnp.concatenate([apart(v) for v in up], axis=0)
+        dk_ref[:seen, :] += nn(jnp.concatenate(ds, axis=1), q_apart)
+        dv_ref[:seen, :] += nn(jnp.concatenate(p, axis=1), up_apart)
+        for k in pairs:
+            both = jnp.concatenate(dq[2 * k : 2 * k + 2], axis=0).T * 0.125
+            out_ref[rows, k * 128 : (k + 1) * 128] = turn(both, cosine, sine).astype(BF16)
     lane = lax.broadcasted_iota(jnp.int32, (SEQ, 128), 1)
     dk, dv = dk_ref[...], dv_ref[...]
     dk, dv = dk + pltpu.roll(dk, HEAD_DIM, 1), dv + pltpu.roll(dv, HEAD_DIM, 1)
@@ -475,7 +544,7 @@
         out_specs=whole(4),
         scratch_shapes=[pltpu.VMEM((SEQ, 128), BF16)],
         compiler_params=pltpu.CompilerParams(vmem_limit_bytes=24 * 2**20),
-        cost_estimate=cost(8),
+        cost_estimate=cost(5),
     )(slot, ends, qkv, cosine, sine)
 
 
@@ -492,7 +561,7 @@
             pltpu.VMEM((SEQ, 128), F32),
         ],
         compiler_params=pltpu.CompilerParams(vmem_limit_bytes=24 * 2**20),
-        cost_estimate=cost(10),
+        cost_estimate=cost(6),
     )(slot, ends, q, kv, lse, upstream, cosine, sine)
 
 
@@ -527,11 +596,6 @@
     return lax.rsqrt(jnp.mean(v * v, axis=-1, keepdims=True) + EPS)
 
 
-def norm_backward(v, inverse, upstream):
-    inner = jnp.mean(upstream * v, axis=-1, keepdims=True)
-    return inverse * upstream - v * (inverse * inverse * inverse * inner)
-
-
 def after(x, *others):
     return lax.optimization_barrier((x, *others))[0]
 
@@ -547,7 +611,7 @@
 
     inverse_one = inverse_rms(residual)
     normed_one = (residual * inverse_one).astype(BF16)
-    one_near = jnp.concatenate([normed_one, pair_z(normed_one, 0)])
+    got_one = pair_z(normed_one, 0)
     part, ffn_part = prepare(
         norm_gains, after(query_weight, normed_one),
         keyvalue_weight, output_weight, gateup_weight, down_weight,
@@ -555,8 +619,9 @@
     line = jnp.stack([part, shift_first(part, 1), shift_first(part, -1), shift_first(part, 2)])
     ffn_full = lax.all_gather(ffn_part, "dp", axis=0, tiled=True)
     tables = attention_tables(document_lengths[0])
-    line = after(line, one_near, *tables)
+    line = after(line, *tables)
     plane = [line, shift_second(line, 1), shift_second(line, -1), shift_second(line, 2)]
+    one_near = after(jnp.concatenate([normed_one, got_one]), line)
     one_far = pair_z(one_near, 1)
     low_cotangent = after(cotangent.astype(BF16), one_near)
     cot_near = jnp.concatenate([low_cotangent, pair_z(low_cotangent, 0)])
@@ -571,83 +636,107 @@
     far = nt(after(attended, cot_far)[half:], output_full).astype(BF16)
     got = pair_z(far, 1)
     near = nt(after(attended, far)[:half], output_full)
+    cot_turned = turned(after(cot_near, near), cot_far)
+    got = after(got, cot_turned)
+    middle, normed_two = by_rows(norm_kernel, near, got, pair_z(send_sum(near, got), 0), residual)
+    got = pair_z(normed_two, 0)
     cot_rows = jnp.concatenate([cot_near, cot_far])
-    cot_turned = turned(after(cot_rows, near))
-    keep, sent = split_sum(near, after(got, cot_turned))
-    middle = residual + (keep + pair_z(sent, 0).astype(F32))
-    inverse_two = inverse_rms(middle)
-    normed_two = (middle * inverse_two).astype(BF16)
-    got = pair_z(normed_two, 0)
     down_full = ffn_full[:, 2 * HIDDEN :]
     grad_hidden = nn(after(cot_rows, normed_two), down_full)
     two_near = jnp.concatenate([normed_two, after(got, grad_hidden)])
     two_far = pair_z(two_near, 1)
+    one_turned = turned(after(one_near, two_near), one_far)
+    two_far = after(two_far, one_turned)
 
     hidden, grad_gate, grad_up = hidden_units(two_near, two_far, grad_hidden, ffn_full)
     near, far = back_to_rows(grad_gate, grad_up, ffn_full)
     got = pair_z(far, 1)
-    rows_turned = turned(after(jnp.concatenate([two_near, two_far]), far))
-    grad_a = weight_gradients(rows_turned, grad_gate, cot_turned, hidden, slice(0, SPLIT))
-    grad_b = weight_gradients(
-        rows_turned, after(grad_up, *grad_a), cot_turned, hidden, slice(SPLIT, HIDDEN)
-    )
-    keep, sent = split_sum(near, after(got, *grad_b))
-    got = pair_z(sent, 0)
-    got_a, got_b = swap_core(after(grad_a[1], sent)), swap_core(after(grad_b[1], sent))
-    down = nt(after(hidden, sent), down_full)
-    grad_normed_two = keep + after(got, down).astype(F32)
-
-    grad_middle = cotangent + norm_backward(middle, inverse_two, grad_normed_two)
-    low_grad = grad_middle.astype(BF16)
+    rows_turned = turned(after(two_near, far), two_far)
+    all_columns = slice(0, HIDDEN)
+    pairs_a = (
+        (rows_turned, grad_gate, all_columns), (cot_turned, hidden, slice(0, SPLIT))
+    )
+    pairs_b = (
+        (rows_turned, grad_up, all_columns), (cot_turned, hidden, slice(SPLIT, HIDDEN))
+    )
+    other_a = weight_products(pairs_a, None, True, 4)
+    other_b = weight_products(pairs_b, None, False, 4)
+    got = after(got, other_a, other_b)
+    sent = send_sum(near, got)
+    got_own = pair_z(sent, 0)
+    got_a = swap_core(after(other_a, sent))
+    got_b = swap_core(after(other_b, sent))
+    down_near, down_far = product_rows(after(hidden, sent), ffn_full, 2, 5)
+    got_own = after(got_own, down_near)
+
+    grad_middle, low_grad = by_rows(norm_back_kernel, near, got, got_own, middle, cotangent)
     got_low = pair_z(low_grad, 0)
-    near_a, far_a = fold(after(grad_a[0], low_grad), got_a, True, 4)
-    got_line_a = pair_first(far_a, 1, True)
-    near_b, far_b = fold(after(grad_b[0], near_a), got_b, False, 4)
-    got_line_b = pair_first(far_b, 1, False)
-    rows_near = jnp.concatenate([low_grad, after(got_low, near_b)])
+    near_a, far_a = weight_products(pairs_a, after(got_a, low_grad), True, 4)
+    got_a = pair_first(far_a, 1, True)
+    rows_near = jnp.concatenate([low_grad, after(got_low, near_a)])
     rows_far = pair_z(rows_near, 1)
-    rows_middle = jnp.concatenate([rows_near, rows_far])
-    grad_attended = nn(rows_middle, output_full).astype(BF16)
-    down_far = after(down[half:].astype(BF16), rows_middle)
-    got_down = pair_z(down_far, 1)
-    grad_output = by_chip(tn(rows_middle, after(attended, grad_attended)).astype(BF16))
-    got_output = swap_core(grad_output[1])
-    grad_projected = attend_backward(q, kv, lse, after(grad_attended, *grad_output), tables)
-
-    grad = nt(grad_projected, qkv_full)
-    near, far = grad[:half], after(grad[half:].astype(BF16), got_down)
+    near_b, far_b = weight_products(pairs_b, after(got_b, rows_near), False, 0.001)
+    got_b = pair_first(far_b, 1, False)
+    grad_attended = nn(after(rows_near, near_b), output_full).astype(BF16)
+    rows_far = after(rows_far, grad_attended)
+    grad_attended = jnp.concatenate([grad_attended, nn(rows_far, output_full).astype(BF16)])
+    grad_projected = attend_backward(q, kv, lse, grad_attended, tables)
+    pairs_qkv = ((one_turned, grad_projected, slice(0, QKV_COLS)),)
+    other_qkv = weight_products(pairs_qkv, None, True, 1)
+    got_qkv = swap_core(other_qkv)
+    near, far = product_rows(after(grad_projected, other_qkv), qkv_full, 0, 2)
     got = pair_z(far, 1)
-    rows_one = jnp.concatenate([one_near, one_far])
-    grad_qkv = by_chip(tn(rows_one, after(grad_projected, far)).astype(BF16))
-    got_qkv = swap_core(grad_qkv[1])
-    keep_a, sent_a = split_sum(near_a, after(got_line_a, *grad_qkv))
+    keep_a, sent_a = split_sum(near_a, after(got_a, far))
     got_a = pair_first(sent_a, 0, True)
-    keep_b, sent_b = split_sum(near_b, after(got_line_b, *grad_qkv))
+    middle_turned = turned(after(rows_near, sent_a), rows_far, 0.001)
+    pairs_output = ((middle_turned, attended, slice(0, QUERY_COLS)),)
+    other_output = weight_products(pairs_output, None, False, 0.001)
+    got_output = swap_core(other_output)
+    keep_b, sent_b = split_sum(near_b, after(got_b, other_output))
     got_b = pair_first(sent_b, 0, False)
-    near_output, far_output = fold(after(grad_output[0], sent_a, sent_b), got_output, False, 20)
-    got_line_output = pair_first(far_output, 1, False)
-    near_qkv, far_qkv = fold(after(grad_qkv[0], near_output), got_qkv, True, 1)
-    got_line_qkv = pair_first(far_qkv, 1, True)
-    keep, sent = split_sum(near, after(got, near_qkv))
-    got = pair_z(sent, 0)
-
-    keep_down, sent_down = split_sum(down[:half], after(got_down, sent))
-    got_down = pair_z(sent_down, 0)
-    grad_normed_one = keep + got.astype(F32)
-    line_a = (keep_a + after(got_a, sent).astype(F32)).astype(BF16)
-    line_b = (keep_b + after(got_b, sent).astype(F32)).astype(BF16)
-    keep_qkv, sent_qkv = split_sum(near_qkv, after(got_line_qkv, line_a, line_b))
-    got_line_qkv = pair_first(sent_qkv, 0, True)
-    keep_output, sent_output = split_sum(near_output, after(got_line_output, sent_qkv))
-    got_line_output = pair_first(sent_output, 0, False)
-    input_gradient = grad_middle + norm_backward(residual, inverse_one, grad_normed_one)
-    block_output = middle + (keep_down + got_down.astype(F32))
-    grad_ffn_a = scatter_second(line_a, True)
-    grad_ffn_b = scatter_second(line_b, False)
-    line_qkv = (keep_qkv + got_line_qkv.astype(F32)).astype(BF16)
-    line_output = (keep_output + got_line_output.astype(F32)).astype(BF16)
-    grad_qkv = scatter_second(line_qkv, True)
-    grad_output = scatter_second(line_output, False)
+    near_qkv, far_qkv = weight_products(pairs_qkv, after(got_qkv, sent_b), True, 0.001)
+    got_qkv = pair_first(far_qkv, 1, True)
+    near_output, far_output = weight_products(
+        pairs_output, after(got_output, near_qkv), False, 0.001
+    )
+    got_output = pair_first(far_output, 1, False)
+    got = after(got, near_output)
+    sent = send_sum(near, got)
+    got_own = pair_z(sent, 0)
+
+    keep_qkv, sent_qkv = split_sum(near_qkv, after(got_qkv, sent))
+    got_qkv = pair_first(sent_qkv, 0, True)
+    line_a = (keep_a + after(got_a, sent_qkv).astype(F32)).astype(BF16)
+    got_a = pair_second(line_a[2:], 1, True)
+    keep_output, sent_output = split_sum(near_output, after(got_output, line_a))
+    got_output = pair_first(sent_output, 0, False)
+    got_own = after(got_own, sent_output)
+    input_gradient, _ = by_rows(norm_back_kernel, near, got, got_own, residual, grad_middle)
+    got_down = pair_z(after(down_far, got_own), 1)
+    line_b = (keep_b + after(got_b, got_own).astype(F32)).astype(BF16)
+    got_b = pair_second(line_b[2:], 1, False)
+    line_qkv = (keep_qkv + after(got_qkv, line_b).astype(F32)).astype(BF16)
+    got_qkv = pair_second(line_qkv[2:], 1, True)
+    line_output = (keep_output + after(got_output, line_qkv).astype(F32)).astype(BF16)
+    got_output = pair_second(line_output[2:], 1, False)
+    keep_a, sent_a = split_sum(line_a[:2], after(got_a, line_output))
+    got_a = pair_second(sent_a, 0, True)
+    keep_qkv, sent_qkv = split_sum(line_qkv[:2], after(got_qkv, sent_a))
+    got_qkv = pair_second(sent_qkv, 0, True)
+    got_down = after(got_down, sent_qkv)
+    sent_down = send_sum(down_near, got_down)
+    got_down_own = pair_z(sent_down, 0)
+    keep_b, sent_b = split_sum(line_b[:2], after(got_b, sent_down))
+    got_b = pair_second(sent_b, 0, False)
+    keep_output, sent_output = split_sum(line_output[:2], after(got_output, sent_b))
+    got_output = pair_second(sent_output, 0, False)
+    grad_ffn_a = keep_a[0] + got_a[0].astype(F32)
+    grad_qkv = keep_qkv[0] + got_qkv[0].astype(F32)
+    grad_ffn_b = keep_b[0] + got_b[0].astype(F32)
+    grad_output = keep_output[0] + got_output[0].astype(F32)
+    block_output = middle + (
+        down_near[:PART] + (got_down[:PART].astype(F32) + got_down_own.astype(F32))
+    )
 
     low_gains = norm_gains.astype(BF16).astype(F32)
     gain_one, gain_two = low_gains[0][:, None], low_gains[1][:, None]

time: 333 us -> 309 us (0.928)
  matrix products: 28.7 us -> 11.5 us
  Pallas kernels: 68.6 us -> 79.5 us
  waiting for transfers between devices: 93.3 us -> 85.2 us
  other arithmetic: 29.9 us -> 22.7 us
    ppermute x16, waiting for transfers between devices: 66 us -> 36.2 us  [pair_z(): return lax.ppermute(a, ('dp', 'mp'), pairs)]
    pallas_call x7 -> x14, Pallas kernels: 22.9 us -> 42.4 us  [the longest x8 29.6 us: weight_products(): pl.pallas_call(kernel, out_shape=outs, grid_spec=pltpu.PrefetchScalarGrid...]
    ppermute x8, waiting for transfers between devices: 6.12 us -> 21.4 us  [pair_x(): return lax.ppermute(a, 'dp', pairs)]
    ppermute x3, waiting for transfers between devices: 4.74 us -> 15.7 us  [shift_second(): return lax.ppermute(a, 'dp', pairs)]
    dot_general x4 -> x2, matrix products: 10.9 us -> 1.53 us  [nt(): lax.dot_general(a, b, (((1,), (1,)), ((), ())), preferred_element_type=F32)]
    ppermute x16, starting transfers between devices: 25.3 us -> 31.8 us  [pair_z(): return lax.ppermute(a, ('dp', 'mp'), pairs)]
    ppermute x8, waiting for transfers between devices: 12.8 us -> 6.95 us  [pair_y(): return lax.ppermute(a, 'dp', pairs)]
    dot_general x2 -> x0, matrix products: 5.44 us -> none  [tn(): lax.dot_general(a, b, (((0,), (0,)), ((), ())), preferred_element_type=F32)]
  transfers between devices with their start and end apart: 47 -> 47, of which waited for: 22 -> 24; matrix products, arithmetic and copies ran while one was open for 17% -> 11% of each run, Pallas kernels for 14% -> 19%
where the time goes in v3:
time: 309 us; the launch traced here: 304 us
  waiting for transfers between devices  85.2 us (28%)
  Pallas kernels  79.5 us (26%)
  starting transfers between devices  64.6 us (21%)
  local copies, waits for them, and re-layouts  24.6 us (8%)
  other arithmetic  22.7 us (7%)
  between operations  15.7 us (5%)
  matrix products  11.5 us (4%)
    ppermute x16, waiting for transfers between devices, pair_z(): return lax.ppermute(a, ('dp', 'mp'), pairs)  36.2 us
    ppermute x16, starting transfers between devices, pair_z(): return lax.ppermute(a, ('dp', 'mp'), pairs)  31.8 us
    pallas_call x8, Pallas kernels, weight_products(): pl.pallas_call(kernel, out_shape=outs, grid_spec=pltpu.PrefetchScalarGrid...  29.6 us
    ppermute x8, waiting for transfers between devices, pair_x(): return lax.ppermute(a, 'dp', pairs)  21.4 us
    unnamed x160, local copies, waits for them, and re-layouts  21.2 us
    ppermute x3, waiting for transfers between devices, shift_second(): return lax.ppermute(a, 'dp', pairs)  15.7 us
    pallas_call x1, Pallas kernels, hidden_units(): pl.pallas_call(hidden_kernel, out_shape=[jax.ShapeDtypeStruct((SEQ, HIDDE...  11.4 us
    ppermute x8, starting transfers between devices, pair_y(): return lax.ppermute(a, 'dp', pairs)  10.6 us
  transfers between devices with their start and end apart: 47, of which 24 were waited for; matrix products, arithmetic and copies ran while one was open for 11% of the time, Pallas kernels for 19%

profile of v3, /device:TPU:0, one launch (start us, length us, event | category | flops | bytes accessed | tf_op | source)
XLA Modules:
  0.0 303.7 jit_solution(8581685982499763620)
XLA Ops:
  9.6 2.1 multiply_convert_fusion
  12.8 3.2 %collective-permute-start.3 = (bf16[64,1152]{1,0:T(8,128)(2,1)S(1)}, bf16[64,1152]{1,0:T(8,128)(2,1)S(1)}, u32[]{:S(2)}, u32[]{:S(2)}) collective-permute-start(bf16[64,1152]{1,0:T(8,128)(2,1)S(1)} %get-tuple-element.101), channel_id=1, source_target_pairs={{0,16},{4,68},{8,24},{12,76},{16,0},{20,84},{24,8},{28,92},{32,48}... | collective-permute-start | bytes 442376 | tf_op jit(solution)/shard_map/ppermute | solution.py:79
  18.0 1.9 collective-permute-start
  23.5 3.3 %collective-permute-start.6 = (bf16[4,64,1152]{2,1,0:T(8,128)(2,1)S(1)}, bf16[4,64,1152]{2,1,0:T(8,128)(2,1)S(1)}, u32[]{:S(2)}, u32[]{:S(2)}) collective-permute-start(bf16[4,64,1152]{2,1,0:T(8,128)(2,1)S(1)} %pad_maximum_fusion.5), channel_id=1, source_target_pairs={{0,64},{4,20},{8,72},{12,28},{16,80},{20,4},{24,88},{28,12},{32,96... | collective-permute-start | bytes 1769480 | tf_op jit(solution)/shard_map/ppermute | solution.py:87
  30.0 4.1 %collective-permute-start.7 = (bf16[256,2048]{1,0:T(8,128)(2,1)S(1)}, bf16[256,2048]{1,0:T(8,128)(2,1)S(1)}, u32[]{:S(2)}, u32[]{:S(2)}) collective-permute-start(bf16[256,2048]{1,0:T(8,128)(2,1)S(1)} %pad_maximum_fusion.3.near_ref), channel_id=1, source_target_pairs={{0,3},{1,2},{2,1},{3,0},{4,5},{5,4},{6,7},{7,6},{8,11},{9,10},{10,... | collective-permute-start | bytes 3145736 | tf_op jit(solution)/shard_map/ppermute | solution.py:57
  34.3 5.7 %collective-permute-done.6 = bf16[4,64,1152]{2,1,0:T(8,128)(2,1)S(1)} collective-permute-done((bf16[4,64,1152]{2,1,0:T(8,128)(2,1)S(1)}, bf16[4,64,1152]{2,1,0:T(8,128)(2,1)S(1)}, u32[]{:S(2)}, u32[]{:S(2)}) %collective-permute-start.6) | collective-permute-done | bytes 589856 | tf_op jit(solution)/shard_map/ppermute | solution.py:87
  40.0 9.9 %collective-permute-done.5 = bf16[4,64,1152]{2,1,0:T(8,128)(2,1)S(1)} collective-permute-done((bf16[4,64,1152]{2,1,0:T(8,128)(2,1)S(1)}, bf16[4,64,1152]{2,1,0:T(8,128)(2,1)S(1)}, u32[]{:S(2)}, u32[]{:S(2)}) %collective-permute-start.5) | collective-permute-done | bytes 589856 | tf_op jit(solution)/shard_map/ppermute | solution.py:87
  52.9 4.2 %collective-permute-start.10 = (bf16[256,2048]{1,0:T(8,128)(2,1)S(1)}, bf16[256,2048]{1,0:T(8,128)(2,1)S(1)}, u32[]{:S(2)}, u32[]{:S(2)}) collective-permute-start(bf16[256,2048]{1,0:T(8,128)(2,1)S(1)} %constant_dynamic-update-slice_fusion.near_ref), channel_id=1, source_target_pairs={{0,3},{1,2},{2,1},{3,0},{4,5},{5,4},{6,7},{7,6},{8,11},{9,10},{10,... | collective-permute-start | bytes 3145736 | tf_op jit(solution)/shard_map/ppermute | solution.py:57
  57.7 3.1 %shard_map.423 = (bf16[16,2,64,640]{3,2,1,0:T(8,128)(2,1)S(1)}, bf16[16,2,64,512]{3,2,1,0:T(8,128)(2,1)S(1)}) custom-call(s32[3]{0:T(128)S(1)} %pad_add_fusion.here_ref, bf16[16,64,1152]{2,1,0:T(8,128)(2,1)} %bitcast.20.mine_ref, bf16[16,64,1152]{2,1,0:T(8,128)(2,1)} %collective-permute-done.9.other_ref), custom_call_target="tpu_custom_call" | custom-call | flops 3300000000 | bytes 9000000 | tf_op jit(solution)/shard_map/pallas_call | solution.py:139
  65.4 4.3 %shard_map.424 = (bf16[512,512]{1,0:T(8,128)(2,1)S(1)}, bf16[512,512]{1,0:T(8,128)(2,1)S(1)}, bf16[512,128]{1,0:T(8,128)(2,1)S(1)}, f32[8,512]{1,0:T(8,128)S(1)}) custom-call(s32[4]{0:T(128)S(1)} %select_reduce_fusion.1.slot_ref, s32[4]{0:T(128)S(1)} %bitcast.108, f32[512,640]{1,0:T(8,128)S(1)} %pad_maximum_fusion.2.qkv_ref, ...), custom_call_target="tpu_custom_call" | custom-call | flops 5500000256 | bytes 15000000 | tf_op jit(solution)/shard_map/pallas_call | solution.py:535
  70.7 3.9 %collective-permute-start.11 = (bf16[256,2048]{1,0:T(8,128)(2,1)S(1)}, bf16[256,2048]{1,0:T(8,128)(2,1)S(1)}, u32[]{:S(2)}, u32[]{:S(2)}) collective-permute-start(bf16[256,2048]{1,0:T(8,128)(2,1)S(1)} %convolution_convert_fusion), channel_id=1, source_target_pairs={{0,3},{1,2},{2,1},{3,0},{4,5},{5,4},{6,7},{7,6},{8,11},{9,10},{10,... | collective-permute-start | bytes 3145736 | tf_op jit(solution)/shard_map/ppermute | solution.py:57
  76.0 11.3 %collective-permute-done.11.got_ref = bf16[256,2048]{1,0:T(8,128)(2,1)S(1)} collective-permute-done((bf16[256,2048]{1,0:T(8,128)(2,1)S(1)}, bf16[256,2048]{1,0:T(8,128)(2,1)S(1)}, u32[]{:S(2)}, u32[]{:S(2)}) %collective-permute-start.11) | collective-permute-done | bytes 1048608 | tf_op jit(solution)/shard_map/ppermute | solution.py:57
  89.1 7.6 %collective-permute-done.12.got_own_ref = bf16[128,2048]{1,0:T(8,128)(2,1)S(1)} collective-permute-done((bf16[128,2048]{1,0:T(8,128)(2,1)S(1)}, bf16[128,2048]{1,0:T(8,128)(2,1)S(1)}, u32[]{:S(2)}, u32[]{:S(2)}) %collective-permute-start.12) | collective-permute-done | bytes 524320 | tf_op jit(solution)/shard_map/ppermute | solution.py:57
  101.5 6.6 %fusion.grad_hidden_ref = f32[512,1408]{1,0:T(8,128)S(1)} fusion(bf16[512,2048]{1,0:T(8,128)(2,1)} %pad_maximum_fusion.1, bf16[2048,4224]{1,0:T(8,128)(2,1)} %all-gather.2.cloned.1.call-done.gate_w_ref.up_w_ref.w_ref), kind=kOutput, calls=%fused_computation | convolution fusion | flops 2952790016 | bytes 10747904 | tf_op jit(solution)/shard_map/dot_general | solution.py:170
  110.5 3.8 %collective-permute-start.14 = (bf16[256,2048]{1,0:T(8,128)(2,1)S(1)}, bf16[256,2048]{1,0:T(8,128)(2,1)S(1)}, u32[]{:S(2)}, u32[]{:S(2)}) collective-permute-start(bf16[256,2048]{1,0:T(8,128)(2,1)S(1)} %constant_dynamic-update-slice_fusion.2.near_ref), channel_id=1, source_target_pairs={{0,3},{1,2},{2,1},{3,0},{4,5},{5,4},{6,7},{7,6},{8,11},{9,10},{10,... | collective-permute-start | bytes 3145736 | tf_op jit(solution)/shard_map/ppermute | solution.py:57
  116.2 10.9 %collective-permute-done.14.far_ref = bf16[256,2048]{1,0:T(8,128)(2,1)S(1)} collective-permute-done((bf16[256,2048]{1,0:T(8,128)(2,1)S(1)}, bf16[256,2048]{1,0:T(8,128)(2,1)S(1)}, u32[]{:S(2)}, u32[]{:S(2)}) %collective-permute-start.14) | collective-permute-done | bytes 1048608 | tf_op jit(solution)/shard_map/ppermute | solution.py:57
  127.1 11.4 %shard_map.428 = (bf16[512,1408]{1,0:T(8,128)(2,1)S(1)}, bf16[512,1408]{1,0:T(8,128)(2,1)S(1)}, bf16[512,1408]{1,0:T(8,128)(2,1)S(1)}) custom-call(bf16[256,2048]{1,0:T(8,128)(2,1)S(1)} %constant_dynamic-update-slice_fusion.2.near_ref, bf16[256,2048]{1,0:T(8,128)(2,1)S(1)} %collective-permute-done.14.far_ref, bf16[2048,4224]{1,0:T(8,128)(2,1)S(1)} %copy-done.44, ...), custom_call_target="tpu_custom_call" | custom-call | flops 11000000512 | bytes 30000000 | tf_op jit(solution)/shard_map/pallas_call | solution.py:402
  138.5 10.3 %shard_map.429 = (f32[256,2048]{1,0:T(8,128)S(1)}, bf16[256,2048]{1,0:T(8,128)(2,1)S(1)}) custom-call(bf16[512,1408]{1,0:T(8,128)(2,1)S(1)} %get-tuple-element.121.gate_ref.refs_1_, bf16[512,1408]{1,0:T(8,128)(2,1)S(1)} %get-tuple-element.122.up_ref.refs_1_, bf16[2048,4224]{1,0:T(8,128)(2,1)} %all-gather.2.cloned.1.call-done.gate_w_ref.up_w_ref.w_ref, ...), custom_call_target="tpu_custom_call" | custom-call | flops 11000000512 | bytes 30000000 | tf_op jit(solution)/shard_map/pallas_call | solution.py:218
  148.9 3.3 %collective-permute-start.15 = (bf16[256,2048]{1,0:T(8,128)(2,1)S(1)}, bf16[256,2048]{1,0:T(8,128)(2,1)S(1)}, u32[]{:S(2)}, u32[]{:S(2)}) collective-permute-start(bf16[256,2048]{1,0:T(8,128)(2,1)S(1)} %get-tuple-element.124), channel_id=1, source_target_pairs={{0,3},{1,2},{2,1},{3,0},{4,5},{5,4},{6,7},{7,6},{8,11},{9,10},{10,... | collective-permute-start | bytes 3145736 | tf_op jit(solution)/shard_map/ppermute | solution.py:57
  152.8 5.0 %shard_map.431 = bf16[16,64,2176]{2,1,0:T(8,128)(2,1)} custom-call(s32[3]{0:T(128)S(1)} %pad_add_fusion.here_ref, bf16[2048,512]{1,0:T(8,128)(2,1)S(1)} %shard_map.430.refs_0_, bf16[512,1408]{1,0:T(8,128)(2,1)S(1)} %get-tuple-element.121.gate_ref.refs_1_, bf16[2048,512]{1,0:T(8,128)(2,1)S(1)} %shard_map.425.refs_2_, ...), custom_call_target="tpu_custom_call" | custom-call | flops 4400000000 | bytes 12000000 | tf_op jit(solution)/shard_map/pallas_call | solution.py:337
  157.8 4.9 %shard_map.432 = bf16[16,64,2048]{2,1,0:T(8,128)(2,1)} custom-call(s32[3]{0:T(128)S(1)} %pad_add_fusion.here_ref, bf16[2048,512]{1,0:T(8,128)(2,1)S(1)} %shard_map.430.refs_0_, bf16[512,1408]{1,0:T(8,128)(2,1)S(1)} %get-tuple-element.122.up_ref.refs_1_, bf16[2048,512]{1,0:T(8,128)(2,1)S(1)} %shard_map.425.refs_2_, ...), custom_call_target="tpu_custom_call" | custom-call | flops 4400000000 | bytes 12000000 | tf_op jit(solution)/shard_map/pallas_call | solution.py:337
  162.7 2.3 collective-permute-done.15.got_ref
  166.0 6.6 %copy-done.45 = bf16[2048,4224]{1,0:T(8,128)(2,1)S(1)} copy-done((bf16[2048,4224]{1,0:T(8,128)(2,1)S(1)}, bf16[2048,4224]{1,0:T(8,128)(2,1)}, u32[]{:S(2)}) %copy-start.45) | copy-done | bytes 17301528
  172.5 4.7 %shard_map.433 = (f32[256,2048]{1,0:T(8,128)S(1)}, bf16[256,2048]{1,0:T(8,128)(2,1)S(1)}) custom-call(bf16[512,1408]{1,0:T(8,128)(2,1)S(1)} %get-tuple-element.127.refs_3_.a_ref, bf16[2048,4224]{1,0:T(8,128)(2,1)S(1)} %copy-done.45), custom_call_target="tpu_custom_call" | custom-call | flops 5500000256 | bytes 15000000 | tf_op jit(solution)/shard_map/pallas_call | solution.py:254
  178.2 2.0 copy-done.39
  183.4 5.8 %shard_map.435 = (bf16[8,64,2176]{2,1,0:T(8,128)(2,1)S(1)}, bf16[8,64,2176]{2,1,0:T(8,128)(2,1)}) custom-call(s32[3]{0:T(128)S(1)} %pad_add_fusion.here_ref, bf16[2048,512]{1,0:T(8,128)(2,1)S(1)} %shard_map.430.refs_0_, bf16[512,1408]{1,0:T(8,128)(2,1)S(1)} %copy-done.18, bf16[2048,512]{1,0:T(8,128)(2,1)S(1)} %shard_map.425.refs_2_, ...), custom_call_target="tpu_custom_call" | custom-call | flops 4400000000 | bytes 12000000 | tf_op jit(solution)/shard_map/pallas_call | solution.py:337
  191.1 3.3 %collective-permute-start.20 = (bf16[256,2048]{1,0:T(8,128)(2,1)S(1)}, bf16[256,2048]{1,0:T(8,128)(2,1)S(1)}, u32[]{:S(2)}, u32[]{:S(2)}) collective-permute-start(bf16[256,2048]{1,0:T(8,128)(2,1)S(1)} %constant_dynamic-update-slice_fusion.4.near_ref), channel_id=1, source_target_pairs={{0,3},{1,2},{2,1},{3,0},{4,5},{5,4},{6,7},{7,6},{8,11},{9,10},{10,... | collective-permute-start | bytes 3145736 | tf_op jit(solution)/shard_map/ppermute | solution.py:57
  195.5 5.7 %shard_map.436 = (bf16[8,64,2048]{2,1,0:T(8,128)(2,1)S(1)}, bf16[8,64,2048]{2,1,0:T(8,128)(2,1)}) custom-call(s32[3]{0:T(128)S(1)} %pad_add_fusion.here_ref, bf16[2048,512]{1,0:T(8,128)(2,1)S(1)} %shard_map.430.refs_0_, bf16[512,1408]{1,0:T(8,128)(2,1)S(1)} %copy-done.16, bf16[2048,512]{1,0:T(8,128)(2,1)S(1)} %shard_map.425.refs_2_, ...), custom_call_target="tpu_custom_call" | custom-call | flops 1100000 | bytes 3000 | tf_op jit(solution)/shard_map/pallas_call | solution.py:337
  201.2 2.9 collective-permute-start.25
  204.8 2.4 collective-permute-done.20.far_ref
  208.0 5.6 %shard_map.437.refs_1_.a_ref = bf16[512,640]{1,0:T(8,128)(2,1)S(1)} custom-call(s32[4]{0:T(128)S(1)} %select_reduce_fusion.1.slot_ref, s32[4]{0:T(128)S(1)} %bitcast.109, bf16[512,512]{1,0:T(8,128)(2,1)S(1)} %copy-done.53, bf16[512,128]{1,0:T(8,128)(2,1)S(1)} %copy-done.55, f32[8,512]{1,0:T(8,128)S(1)} %copy-done.57, ...), custom_call_target="tpu_custom_call" | custom-call | flops 6600000000 | bytes 18000000 | tf_op jit(solution)/shard_map/pallas_call | solution.py:553
  213.7 2.1 shard_map.438
  216.1 2.6 shard_map.439
  218.7 3.1 %collective-permute-start.21 = (bf16[256,2048]{1,0:T(8,128)(2,1)S(1)}, bf16[256,2048]{1,0:T(8,128)(2,1)S(1)}, u32[]{:S(2)}, u32[]{:S(2)}) collective-permute-start(bf16[256,2048]{1,0:T(8,128)(2,1)S(1)} %get-tuple-element.146), channel_id=1, source_target_pairs={{0,3},{1,2},{2,1},{3,0},{4,5},{5,4},{6,7},{7,6},{8,11},{9,10},{10,... | collective-permute-start | bytes 3145736 | tf_op jit(solution)/shard_map/ppermute | solution.py:57
  229.2 2.4 shard_map.442
  231.6 2.3 collective-permute-start.29
  233.9 2.0 shard_map.443
  238.5 12.0 %collective-permute-done.29 = bf16[8,64,640]{2,1,0:T(8,128)(2,1)S(1)} collective-permute-done((bf16[8,64,640]{2,1,0:T(8,128)(2,1)S(1)}, bf16[8,64,640]{2,1,0:T(8,128)(2,1)S(1)}, u32[]{:S(2)}, u32[]{:S(2)}) %collective-permute-start.29) | collective-permute-done | bytes 655392 | tf_op jit(solution)/shard_map/ppermute | solution.py:62
  252.5 1.9 collective-permute-start.34
  261.3 2.5 collective-permute-done.35
  264.0 2.0 collective-permute-done.34
  267.9 2.1 shard_map.444
  269.9 2.0 collective-permute-start.38
  271.9 2.0 collective-permute-start.44
  276.1 3.0 collective-permute-done.44
  280.2 3.2 %collective-permute-done.45 = bf16[1,64,512]{2,1,0:T(8,128)(2,1)S(1)} collective-permute-done((bf16[1,64,512]{2,1,0:T(8,128)(2,1)S(1)}, bf16[1,64,512]{2,1,0:T(8,128)(2,1)S(1)}, u32[]{:S(2)}, u32[]{:S(2)}) %collective-permute-start.45) | collective-permute-done | bytes 65568 | tf_op jit(solution)/shard_map/ppermute | solution.py:62
  287.5 2.5 collective-permute-start.42
  291.7 3.1 %collective-permute-done.41 = f32[2,64]{1,0:T(2,128)S(1)} collective-permute-done((f32[2,64]{1,0:T(2,128)S(1)}, f32[2,64]{1,0:T(2,128)S(1)}, u32[]{:S(2)}, u32[]{:S(2)}) %collective-permute-start.41) | collective-permute-done | bytes 544 | tf_op jit(solution)/shard_map/ppermute | solution.py:71
  (304 shorter events, 75.3 us)
Async XLA Ops:
  7.3 94.2 %all-gather.2.cloned.1.call-start = ((), (), s32[]{:S(2)}) async-start(), calls=%async_computation | async-start | bytes 17842176 | tf_op jit(solution)/shard_map/all_gather | solution.py:620
  12.8 9.9 %collective-permute-start.3 = (bf16[64,1152]{1,0:T(8,128)(2,1)S(1)}, bf16[64,1152]{1,0:T(8,128)(2,1)S(1)}, u32[]{:S(2)}, u32[]{:S(2)}) collective-permute-start(bf16[64,1152]{1,0:T(8,128)(2,1)S(1)} %get-tuple-element.101), channel_id=1, source_target_pairs={{0,16},{4,68},{8,24},{12,76},{16,0},{20,84},{24,8},{28,92},{32,48}... | collective-permute-start | bytes 442376 | tf_op jit(solution)/shard_map/ppermute | solution.py:79
  16.0 6.7 %collective-permute-start.2 = (bf16[64,1152]{1,0:T(8,128)(2,1)S(1)}, bf16[64,1152]{1,0:T(8,128)(2,1)S(1)}, u32[]{:S(2)}, u32[]{:S(2)}) collective-permute-start(bf16[64,1152]{1,0:T(8,128)(2,1)S(1)} %get-tuple-element.101), channel_id=1, source_target_pairs={{0,24},{4,100},{8,0},{12,108},{16,8},{20,116},{24,16},{28,124},{32... | collective-permute-start | bytes 442376 | tf_op jit(solution)/shard_map/ppermute | solution.py:79
  17.1 6.4 %collective-permute-start.1 = (bf16[64,1152]{1,0:T(8,128)(2,1)S(1)}, bf16[64,1152]{1,0:T(8,128)(2,1)S(1)}, u32[]{:S(2)}, u32[]{:S(2)}) collective-permute-start(bf16[64,1152]{1,0:T(8,128)(2,1)S(1)} %get-tuple-element.101), channel_id=1, source_target_pairs={{0,8},{4,36},{8,16},{12,44},{16,24},{20,52},{24,0},{28,60},{32,40}... | collective-permute-start | bytes 442376 | tf_op jit(solution)/shard_map/ppermute | solution.py:79
  18.0 10.9 %collective-permute-start = (bf16[128,2048]{1,0:T(8,128)(2,1)}, bf16[128,2048]{1,0:T(8,128)(2,1)S(1)}, u32[]{:S(2)}, u32[]{:S(2)}) collective-permute-start(bf16[128,2048]{1,0:T(8,128)(2,1)} %multiply_convert_fusion), channel_id=1, source_target_pairs={{0,1},{1,0},{2,3},{3,2},{4,7},{5,6},{6,5},{7,4},{8,9},{9,8},{10,11... | collective-permute-start | bytes 1572872 | tf_op jit(solution)/shard_map/ppermute | solution.py:57
  22.6 41.9 %copy-start.34 = (f32[512,128]{1,0:T(8,128)}, f32[512,128]{1,0:T(8,128)S(1)}, u32[]{:S(2)}) copy-start(f32[512,128]{1,0:T(8,128)S(1)} %get-tuple-element.216.cos_ref) | copy-start | bytes 786436
  23.5 16.4 %collective-permute-start.6 = (bf16[4,64,1152]{2,1,0:T(8,128)(2,1)S(1)}, bf16[4,64,1152]{2,1,0:T(8,128)(2,1)S(1)}, u32[]{:S(2)}, u32[]{:S(2)}) collective-permute-start(bf16[4,64,1152]{2,1,0:T(8,128)(2,1)S(1)} %pad_maximum_fusion.5), channel_id=1, source_target_pairs={{0,64},{4,20},{8,72},{12,28},{16,80},{20,4},{24,88},{28,12},{32,96... | collective-permute-start | bytes 1769480 | tf_op jit(solution)/shard_map/ppermute | solution.py:87
  26.8 23.1 %collective-permute-start.5 = (bf16[4,64,1152]{2,1,0:T(8,128)(2,1)S(1)}, bf16[4,64,1152]{2,1,0:T(8,128)(2,1)S(1)}, u32[]{:S(2)}, u32[]{:S(2)}) collective-permute-start(bf16[4,64,1152]{2,1,0:T(8,128)(2,1)S(1)} %pad_maximum_fusion.5), channel_id=1, source_target_pairs={{0,96},{4,28},{8,104},{12,4},{16,112},{20,12},{24,120},{28,20},{32... | collective-permute-start | bytes 1769480 | tf_op jit(solution)/shard_map/ppermute | solution.py:87
  27.9 22.1 %collective-permute-start.4 = (bf16[4,64,1152]{2,1,0:T(8,128)(2,1)S(1)}, bf16[4,64,1152]{2,1,0:T(8,128)(2,1)S(1)}, u32[]{:S(2)}, u32[]{:S(2)}) collective-permute-start(bf16[4,64,1152]{2,1,0:T(8,128)(2,1)S(1)} %pad_maximum_fusion.5), channel_id=1, source_target_pairs={{0,32},{4,12},{8,40},{12,20},{16,48},{20,28},{24,56},{28,4},{32,64... | collective-permute-start | bytes 1769480 | tf_op jit(solution)/shard_map/ppermute | solution.py:87
  30.0 22.1 %collective-permute-start.7 = (bf16[256,2048]{1,0:T(8,128)(2,1)S(1)}, bf16[256,2048]{1,0:T(8,128)(2,1)S(1)}, u32[]{:S(2)}, u32[]{:S(2)}) collective-permute-start(bf16[256,2048]{1,0:T(8,128)(2,1)S(1)} %pad_maximum_fusion.3.near_ref), channel_id=1, source_target_pairs={{0,3},{1,2},{2,1},{3,0},{4,5},{5,4},{6,7},{7,6},{8,11},{9,10},{10,... | collective-permute-start | bytes 3145736 | tf_op jit(solution)/shard_map/ppermute | solution.py:57
  34.2 17.9 %collective-permute-start.8 = (bf16[128,2048]{1,0:T(8,128)(2,1)S(1)}, bf16[128,2048]{1,0:T(8,128)(2,1)S(1)}, u32[]{:S(2)}, u32[]{:S(2)}) collective-permute-start(bf16[128,2048]{1,0:T(8,128)(2,1)S(1)} %bitcast_convert_fusion), channel_id=1, source_target_pairs={{0,1},{1,0},{2,3},{3,2},{4,7},{5,6},{6,5},{7,4},{8,9},{9,8},{10,11... | collective-permute-start | bytes 1572872 | tf_op jit(solution)/shard_map/ppermute | solution.py:57
  52.8 4.9 %collective-permute-start.9 = (bf16[16,64,1152]{2,1,0:T(8,128)(2,1)}, bf16[16,64,1152]{2,1,0:T(8,128)(2,1)}, u32[]{:S(2)}, u32[]{:S(2)}) collective-permute-start(bf16[16,64,1152]{2,1,0:T(8,128)(2,1)} %bitcast.20.mine_ref), channel_id=1, source_target_pairs={{0,4},{4,0},{8,12},{12,8},{16,20},{20,16},{24,28},{28,24},{32,36},... | collective-permute-start | bytes 7077896 | tf_op jit(solution)/shard_map/ppermute | solution.py:91
  52.9 17.0 %collective-permute-start.10 = (bf16[256,2048]{1,0:T(8,128)(2,1)S(1)}, bf16[256,2048]{1,0:T(8,128)(2,1)S(1)}, u32[]{:S(2)}, u32[]{:S(2)}) collective-permute-start(bf16[256,2048]{1,0:T(8,128)(2,1)S(1)} %constant_dynamic-update-slice_fusion.near_ref), channel_id=1, source_target_pairs={{0,3},{1,2},{2,1},{3,0},{4,5},{5,4},{6,7},{7,6},{8,11},{9,10},{10,... | collective-permute-start | bytes 3145736 | tf_op jit(solution)/shard_map/ppermute | solution.py:57
  70.7 16.6 %collective-permute-start.11 = (bf16[256,2048]{1,0:T(8,128)(2,1)S(1)}, bf16[256,2048]{1,0:T(8,128)(2,1)S(1)}, u32[]{:S(2)}, u32[]{:S(2)}) collective-permute-start(bf16[256,2048]{1,0:T(8,128)(2,1)S(1)} %convolution_convert_fusion), channel_id=1, source_target_pairs={{0,3},{1,2},{2,1},{3,0},{4,5},{5,4},{6,7},{7,6},{8,11},{9,10},{10,... | collective-permute-start | bytes 3145736 | tf_op jit(solution)/shard_map/ppermute | solution.py:57
  87.5 9.3 %collective-permute-start.12 = (bf16[128,2048]{1,0:T(8,128)(2,1)S(1)}, bf16[128,2048]{1,0:T(8,128)(2,1)S(1)}, u32[]{:S(2)}, u32[]{:S(2)}) collective-permute-start(bf16[128,2048]{1,0:T(8,128)(2,1)S(1)} %fusion.2), channel_id=1, source_target_pairs={{0,1},{1,0},{2,3},{3,2},{4,7},{5,6},{6,5},{7,4},{8,9},{9,8},{10,11... | collective-permute-start | bytes 1572872 | tf_op jit(solution)/shard_map/ppermute | solution.py:57
  99.5 9.5 %collective-permute-start.13 = (bf16[128,2048]{1,0:T(8,128)(2,1)}, bf16[128,2048]{1,0:T(8,128)(2,1)}, u32[]{:S(2)}, u32[]{:S(2)}) collective-permute-start(bf16[128,2048]{1,0:T(8,128)(2,1)} %get-tuple-element.114), channel_id=1, source_target_pairs={{0,1},{1,0},{2,3},{3,2},{4,7},{5,6},{6,5},{7,4},{8,9},{9,8},{10,11... | collective-permute-start | bytes 1572872 | tf_op jit(solution)/shard_map/ppermute | solution.py:57
  110.5 16.6 %collective-permute-start.14 = (bf16[256,2048]{1,0:T(8,128)(2,1)S(1)}, bf16[256,2048]{1,0:T(8,128)(2,1)S(1)}, u32[]{:S(2)}, u32[]{:S(2)}) collective-permute-start(bf16[256,2048]{1,0:T(8,128)(2,1)S(1)} %constant_dynamic-update-slice_fusion.2.near_ref), channel_id=1, source_target_pairs={{0,3},{1,2},{2,1},{3,0},{4,5},{5,4},{6,7},{7,6},{8,11},{9,10},{10,... | collective-permute-start | bytes 3145736 | tf_op jit(solution)/shard_map/ppermute | solution.py:57
  148.9 16.1 %collective-permute-start.15 = (bf16[256,2048]{1,0:T(8,128)(2,1)S(1)}, bf16[256,2048]{1,0:T(8,128)(2,1)S(1)}, u32[]{:S(2)}, u32[]{:S(2)}) collective-permute-start(bf16[256,2048]{1,0:T(8,128)(2,1)S(1)} %get-tuple-element.124), channel_id=1, source_target_pairs={{0,3},{1,2},{2,1},{3,0},{4,5},{5,4},{6,7},{7,6},{8,11},{9,10},{10,... | collective-permute-start | bytes 3145736 | tf_op jit(solution)/shard_map/ppermute | solution.py:57
  165.1 18.2 %collective-permute-start.18 = (bf16[16,64,2176]{2,1,0:T(8,128)(2,1)}, bf16[16,64,2176]{2,1,0:T(8,128)(2,1)S(1)}, u32[]{:S(2)}, u32[]{:S(2)}) collective-permute-start(bf16[16,64,2176]{2,1,0:T(8,128)(2,1)} %shard_map.431), channel_id=1, source_target_pairs={{0,4},{4,0},{8,12},{12,8},{16,20},{20,16},{24,28},{28,24},{32,36},... | collective-permute-start | bytes 13369352 | tf_op jit(solution)/shard_map/ppermute | solution.py:91
  165.2 30.3 %collective-permute-start.19 = (bf16[16,64,2048]{2,1,0:T(8,128)(2,1)}, bf16[16,64,2048]{2,1,0:T(8,128)(2,1)S(1)}, u32[]{:S(2)}, u32[]{:S(2)}) collective-permute-start(bf16[16,64,2048]{2,1,0:T(8,128)(2,1)} %shard_map.432), channel_id=1, source_target_pairs={{0,4},{4,0},{8,12},{12,8},{16,20},{20,16},{24,28},{28,24},{32,36},... | collective-permute-start | bytes 12582920 | tf_op jit(solution)/shard_map/ppermute | solution.py:91
  166.0 12.2 %collective-permute-start.16 = (bf16[128,2048]{1,0:T(8,128)(2,1)S(1)}, bf16[128,2048]{1,0:T(8,128)(2,1)S(1)}, u32[]{:S(2)}, u32[]{:S(2)}) collective-permute-start(bf16[128,2048]{1,0:T(8,128)(2,1)S(1)} %add_convert_fusion.6), channel_id=1, source_target_pairs={{0,1},{1,0},{2,3},{3,2},{4,7},{5,6},{6,5},{7,4},{8,9},{9,8},{10,11... | collective-permute-start | bytes 1572872 | tf_op jit(solution)/shard_map/ppermute | solution.py:57
  181.9 9.2 %collective-permute-start.17 = (bf16[128,2048]{1,0:T(8,128)(2,1)S(1)}, bf16[128,2048]{1,0:T(8,128)(2,1)S(1)}, u32[]{:S(2)}, u32[]{:S(2)}) collective-permute-start(bf16[128,2048]{1,0:T(8,128)(2,1)S(1)} %get-tuple-element.134), channel_id=1, source_target_pairs={{0,1},{1,0},{2,3},{3,2},{4,7},{5,6},{6,5},{7,4},{8,9},{9,8},{10,11... | collective-permute-start | bytes 1572872 | tf_op jit(solution)/shard_map/ppermute | solution.py:57
  191.1 16.1 %collective-permute-start.20 = (bf16[256,2048]{1,0:T(8,128)(2,1)S(1)}, bf16[256,2048]{1,0:T(8,128)(2,1)S(1)}, u32[]{:S(2)}, u32[]{:S(2)}) collective-permute-start(bf16[256,2048]{1,0:T(8,128)(2,1)S(1)} %constant_dynamic-update-slice_fusion.4.near_ref), channel_id=1, source_target_pairs={{0,3},{1,2},{2,1},{3,0},{4,5},{5,4},{6,7},{7,6},{8,11},{9,10},{10,... | collective-permute-start | bytes 3145736 | tf_op jit(solution)/shard_map/ppermute | solution.py:57
  194.5 29.0 %collective-permute-start.22 = (bf16[8,64,2176]{2,1,0:T(8,128)(2,1)}, bf16[8,64,2176]{2,1,0:T(8,128)(2,1)}, u32[]{:S(2)}, u32[]{:S(2)}) collective-permute-start(bf16[8,64,2176]{2,1,0:T(8,128)(2,1)} %get-tuple-element.147), channel_id=1, source_target_pairs={{0,24},{4,12},{8,16},{12,4},{16,8},{20,28},{24,0},{28,20},{32,56},... | collective-permute-start | bytes 6684680 | tf_op jit(solution)/shard_map/ppermute | solution.py:62
  201.2 27.6 %collective-permute-start.25 = (bf16[8,64,2048]{2,1,0:T(8,128)(2,1)}, bf16[8,64,2048]{2,1,0:T(8,128)(2,1)S(1)}, u32[]{:S(2)}, u32[]{:S(2)}) collective-permute-start(bf16[8,64,2048]{2,1,0:T(8,128)(2,1)} %get-tuple-element.150), channel_id=1, source_target_pairs={{0,96},{4,36},{8,104},{12,44},{16,112},{20,52},{24,120},{28,60},{3... | collective-permute-start | bytes 6291464 | tf_op jit(solution)/shard_map/ppermute | solution.py:67
  215.8 13.4 %collective-permute-start.24 = (bf16[16,64,640]{2,1,0:T(8,128)(2,1)S(1)}, bf16[16,64,640]{2,1,0:T(8,128)(2,1)S(1)}, u32[]{:S(2)}, u32[]{:S(2)}) collective-permute-start(bf16[16,64,640]{2,1,0:T(8,128)(2,1)S(1)} %shard_map.438), channel_id=1, source_target_pairs={{0,4},{4,0},{8,12},{12,8},{16,20},{20,16},{24,28},{28,24},{32,36},... | collective-permute-start | bytes 3932168 | tf_op jit(solution)/shard_map/ppermute | solution.py:91
  218.7 17.1 %collective-permute-start.21 = (bf16[256,2048]{1,0:T(8,128)(2,1)S(1)}, bf16[256,2048]{1,0:T(8,128)(2,1)S(1)}, u32[]{:S(2)}, u32[]{:S(2)}) collective-permute-start(bf16[256,2048]{1,0:T(8,128)(2,1)S(1)} %get-tuple-element.146), channel_id=1, source_target_pairs={{0,3},{1,2},{2,1},{3,0},{4,5},{5,4},{6,7},{7,6},{8,11},{9,10},{10,... | collective-permute-start | bytes 3145736 | tf_op jit(solution)/shard_map/ppermute | solution.py:57
  227.8 6.1 %collective-permute-start.23 = (bf16[16,64,512]{2,1,0:T(8,128)(2,1)S(1)}, bf16[16,64,512]{2,1,0:T(8,128)(2,1)S(1)}, u32[]{:S(2)}, u32[]{:S(2)}) collective-permute-start(bf16[16,64,512]{2,1,0:T(8,128)(2,1)S(1)} %shard_map.441), channel_id=1, source_target_pairs={{0,4},{4,0},{8,12},{12,8},{16,20},{20,16},{24,28},{28,24},{32,36},... | collective-permute-start | bytes 3145736 | tf_op jit(solution)/shard_map/ppermute | solution.py:91
  228.0 22.8 %collective-permute-start.28 = (bf16[4,64,2176]{2,1,0:T(8,128)(2,1)S(1)}, bf16[4,64,2176]{2,1,0:T(8,128)(2,1)S(1)}, u32[]{:S(2)}, u32[]{:S(2)}) collective-permute-start(bf16[4,64,2176]{2,1,0:T(8,128)(2,1)S(1)} %add_convert_fusion.1), channel_id=1, source_target_pairs={{0,8},{4,28},{8,0},{12,20},{16,24},{20,12},{24,16},{28,4},{32,40},... | collective-permute-start | bytes 3342344 | tf_op jit(solution)/shard_map/ppermute | solution.py:62
  231.6 19.0 %collective-permute-start.29 = (bf16[8,64,640]{2,1,0:T(8,128)(2,1)S(1)}, bf16[8,64,640]{2,1,0:T(8,128)(2,1)S(1)}, u32[]{:S(2)}, u32[]{:S(2)}) collective-permute-start(bf16[8,64,640]{2,1,0:T(8,128)(2,1)S(1)} %get-tuple-element.158), channel_id=1, source_target_pairs={{0,24},{4,12},{8,16},{12,4},{16,8},{20,28},{24,0},{28,20},{32,56},... | collective-permute-start | bytes 1966088 | tf_op jit(solution)/shard_map/ppermute | solution.py:62
  233.9 21.7 %collective-permute-start.32 = (bf16[4,64,2048]{2,1,0:T(8,128)(2,1)S(1)}, bf16[4,64,2048]{2,1,0:T(8,128)(2,1)S(1)}, u32[]{:S(2)}, u32[]{:S(2)}) collective-permute-start(bf16[4,64,2048]{2,1,0:T(8,128)(2,1)S(1)} %add_convert_fusion.3), channel_id=1, source_target_pairs={{0,32},{4,100},{8,40},{12,108},{16,48},{20,116},{24,56},{28,124},{... | collective-permute-start | bytes 3145736 | tf_op jit(solution)/shard_map/ppermute | solution.py:67
  236.0 18.6 %collective-permute-start.26 = (bf16[128,2048]{1,0:T(8,128)(2,1)S(1)}, bf16[128,2048]{1,0:T(8,128)(2,1)S(1)}, u32[]{:S(2)}, u32[]{:S(2)}) collective-permute-start(bf16[128,2048]{1,0:T(8,128)(2,1)S(1)} %add_convert_fusion.5), channel_id=1, source_target_pairs={{0,1},{1,0},{2,3},{3,2},{4,7},{5,6},{6,5},{7,4},{8,9},{9,8},{10,11... | collective-permute-start | bytes 1572872 | tf_op jit(solution)/shard_map/ppermute | solution.py:57
  236.8 17.6 %collective-permute-start.27 = (bf16[8,64,512]{2,1,0:T(8,128)(2,1)S(1)}, bf16[8,64,512]{2,1,0:T(8,128)(2,1)S(1)}, u32[]{:S(2)}, u32[]{:S(2)}) collective-permute-start(bf16[8,64,512]{2,1,0:T(8,128)(2,1)S(1)} %get-tuple-element.157), channel_id=1, source_target_pairs={{0,96},{4,36},{8,104},{12,44},{16,112},{20,52},{24,120},{28,60},{3... | collective-permute-start | bytes 1572872 | tf_op jit(solution)/shard_map/ppermute | solution.py:67
  250.6 7.2 %collective-permute-start.31 = (bf16[4,64,640]{2,1,0:T(8,128)(2,1)S(1)}, bf16[4,64,640]{2,1,0:T(8,128)(2,1)S(1)}, u32[]{:S(2)}, u32[]{:S(2)}) collective-permute-start(bf16[4,64,640]{2,1,0:T(8,128)(2,1)S(1)} %add_convert_fusion.8), channel_id=1, source_target_pairs={{0,8},{4,28},{8,0},{12,20},{16,24},{20,12},{24,16},{28,4},{32,40},... | collective-permute-start | bytes 983048 | tf_op jit(solution)/shard_map/ppermute | solution.py:62
  252.5 13.4 %collective-permute-start.34 = (bf16[2,64,2176]{2,1,0:T(8,128)(2,1)S(1)}, bf16[2,64,2176]{2,1,0:T(8,128)(2,1)S(1)}, u32[]{:S(2)}, u32[]{:S(2)}) collective-permute-start(bf16[2,64,2176]{2,1,0:T(8,128)(2,1)S(1)} %slice.271), channel_id=1, source_target_pairs={{0,96},{4,36},{8,104},{12,44},{16,112},{20,52},{24,120},{28,60},{3... | collective-permute-start | bytes 1671176 | tf_op jit(solution)/shard_map/ppermute | solution.py:67
  254.5 9.3 %collective-permute-start.35 = (bf16[4,64,512]{2,1,0:T(8,128)(2,1)S(1)}, bf16[4,64,512]{2,1,0:T(8,128)(2,1)S(1)}, u32[]{:S(2)}, u32[]{:S(2)}) collective-permute-start(bf16[4,64,512]{2,1,0:T(8,128)(2,1)S(1)} %add_convert_fusion.12), channel_id=1, source_target_pairs={{0,32},{4,100},{8,40},{12,108},{16,48},{20,116},{24,56},{28,124},{... | collective-permute-start | bytes 786440 | tf_op jit(solution)/shard_map/ppermute | solution.py:67
  254.6 21.2 %collective-permute-start.30 = (bf16[256,2048]{1,0:T(8,128)(2,1)S(1)}, bf16[256,2048]{1,0:T(8,128)(2,1)S(1)}, u32[]{:S(2)}, u32[]{:S(2)}) collective-permute-start(bf16[256,2048]{1,0:T(8,128)(2,1)S(1)} %copy-done.47), channel_id=1, source_target_pairs={{0,3},{1,2},{2,1},{3,0},{4,5},{5,4},{6,7},{7,6},{8,11},{9,10},{10,... | collective-permute-start | bytes 3145736 | tf_op jit(solution)/shard_map/ppermute | solution.py:57
  258.0 9.7 %collective-permute-start.33 = (bf16[2,64,640]{2,1,0:T(8,128)(2,1)S(1)}, bf16[2,64,640]{2,1,0:T(8,128)(2,1)S(1)}, u32[]{:S(2)}, u32[]{:S(2)}) collective-permute-start(bf16[2,64,640]{2,1,0:T(8,128)(2,1)S(1)} %slice.269), channel_id=1, source_target_pairs={{0,96},{4,36},{8,104},{12,44},{16,112},{20,52},{24,120},{28,60},{3... | collective-permute-start | bytes 491528 | tf_op jit(solution)/shard_map/ppermute | solution.py:67
  259.9 16.1 %collective-permute-start.39 = (bf16[2,64,2048]{2,1,0:T(8,128)(2,1)S(1)}, bf16[2,64,2048]{2,1,0:T(8,128)(2,1)S(1)}, u32[]{:S(2)}, u32[]{:S(2)}) collective-permute-start(bf16[2,64,2048]{2,1,0:T(8,128)(2,1)S(1)} %slice.280), channel_id=1, source_target_pairs={{0,24},{4,12},{8,16},{12,4},{16,8},{20,28},{24,0},{28,20},{32,56},... | collective-permute-start | bytes 1572872 | tf_op jit(solution)/shard_map/ppermute | solution.py:62
  267.7 6.2 %collective-permute-start.37 = (bf16[1,64,640]{2,1,0:T(8,128)(2,1)S(1)}, bf16[1,64,640]{2,1,0:T(8,128)(2,1)S(1)}, u32[]{:S(2)}, u32[]{:S(2)}) collective-permute-start(bf16[1,64,640]{2,1,0:T(8,128)(2,1)S(1)} %add_convert_fusion.13), channel_id=1, source_target_pairs={{0,32},{4,100},{8,40},{12,108},{16,48},{20,116},{24,56},{28,124},{... | collective-permute-start | bytes 245768 | tf_op jit(solution)/shard_map/ppermute | solution.py:67
  269.9 9.3 %collective-permute-start.38 = (bf16[1,64,2176]{2,1,0:T(8,128)(2,1)S(1)}, bf16[1,64,2176]{2,1,0:T(8,128)(2,1)S(1)}, u32[]{:S(2)}, u32[]{:S(2)}) collective-permute-start(bf16[1,64,2176]{2,1,0:T(8,128)(2,1)S(1)} %add_convert_fusion.9), channel_id=1, source_target_pairs={{0,32},{4,100},{8,40},{12,108},{16,48},{20,116},{24,56},{28,124},{... | collective-permute-start | bytes 835592 | tf_op jit(solution)/shard_map/ppermute | solution.py:67
  271.9 7.1 %collective-permute-start.44 = (bf16[2,64,512]{2,1,0:T(8,128)(2,1)S(1)}, bf16[2,64,512]{2,1,0:T(8,128)(2,1)S(1)}, u32[]{:S(2)}, u32[]{:S(2)}) collective-permute-start(bf16[2,64,512]{2,1,0:T(8,128)(2,1)S(1)} %slice.287), channel_id=1, source_target_pairs={{0,24},{4,12},{8,16},{12,4},{16,8},{20,28},{24,0},{28,20},{32,56},... | collective-permute-start | bytes 393224 | tf_op jit(solution)/shard_map/ppermute | solution.py:62
  276.0 8.3 %collective-permute-start.40 = (bf16[1,64,2048]{2,1,0:T(8,128)(2,1)S(1)}, bf16[1,64,2048]{2,1,0:T(8,128)(2,1)S(1)}, u32[]{:S(2)}, u32[]{:S(2)}) collective-permute-start(bf16[1,64,2048]{2,1,0:T(8,128)(2,1)S(1)} %add_convert_fusion.10), channel_id=1, source_target_pairs={{0,8},{4,28},{8,0},{12,20},{16,24},{20,12},{24,16},{28,4},{32,40},... | collective-permute-start | bytes 786440 | tf_op jit(solution)/shard_map/ppermute | solution.py:62
  279.1 4.3 %collective-permute-start.45 = (bf16[1,64,512]{2,1,0:T(8,128)(2,1)S(1)}, bf16[1,64,512]{2,1,0:T(8,128)(2,1)S(1)}, u32[]{:S(2)}, u32[]{:S(2)}) collective-permute-start(bf16[1,64,512]{2,1,0:T(8,128)(2,1)S(1)} %add_convert_fusion.14), channel_id=1, source_target_pairs={{0,8},{4,28},{8,0},{12,20},{16,24},{20,12},{24,16},{28,4},{32,40},... | collective-permute-start | bytes 196616 | tf_op jit(solution)/shard_map/ppermute | solution.py:62
  279.4 16.0 %collective-permute-start.36 = (bf16[128,2048]{1,0:T(8,128)(2,1)S(1)}, bf16[128,2048]{1,0:T(8,128)(2,1)S(1)}, u32[]{:S(2)}, u32[]{:S(2)}) collective-permute-start(bf16[128,2048]{1,0:T(8,128)(2,1)S(1)} %add_convert_fusion.4), channel_id=1, source_target_pairs={{0,1},{1,0},{2,3},{3,2},{4,7},{5,6},{6,5},{7,4},{8,9},{9,8},{10,11... | collective-permute-start | bytes 1572872 | tf_op jit(solution)/shard_map/ppermute | solution.py:57
  286.5 5.2 %collective-permute-start.43 = (f32[2,64]{1,0:T(2,128)S(1)}, f32[2,64]{1,0:T(2,128)S(1)}, u32[]{:S(2)}, u32[]{:S(2)}) collective-permute-start(f32[2,64]{1,0:T(2,128)S(1)} %pad_maximum_fusion.10), channel_id=1, source_target_pairs={{0,2},{1,3},{2,0},{3,1},{4,6},{5,7},{6,4},{7,5},{8,10},{9,11},{10,... | collective-permute-start | bytes 1544 | tf_op jit(solution)/shard_map/ppermute | solution.py:71
  287.5 4.2 %collective-permute-start.42 = (f32[2,64]{1,0:T(2,128)S(1)}, f32[2,64]{1,0:T(2,128)S(1)}, u32[]{:S(2)}, u32[]{:S(2)}) collective-permute-start(f32[2,64]{1,0:T(2,128)S(1)} %pad_maximum_fusion.10), channel_id=1, source_target_pairs={{0,3},{1,0},{2,1},{3,2},{4,7},{5,4},{6,5},{7,6},{8,11},{9,8},{10,9... | collective-permute-start | bytes 1544 | tf_op jit(solution)/shard_map/ppermute | solution.py:71
  290.0 4.8 %collective-permute-start.41 = (f32[2,64]{1,0:T(2,128)S(1)}, f32[2,64]{1,0:T(2,128)S(1)}, u32[]{:S(2)}, u32[]{:S(2)}) collective-permute-start(f32[2,64]{1,0:T(2,128)S(1)} %pad_maximum_fusion.10), channel_id=1, source_target_pairs={{0,1},{1,2},{2,3},{3,0},{4,5},{5,6},{6,7},{7,4},{8,9},{9,10},{10,1... | collective-permute-start | bytes 1544 | tf_op jit(solution)/shard_map/ppermute | solution.py:71
  (77 other events, 526.9 us)
Sparse Core Ops, SparseCore 0:
  12.9 83.4 all-gather.1

commit v4 on v3

--- a/solution.py
+++ b/solution.py
@@ -109,6 +109,10 @@
 
 def pair_steps(core):
     return jnp.where(core == 0, jnp.array([0, 1, 3, 2]), jnp.array([0, 3, 1, 2])).astype(jnp.int32)
+
+
+def add_low(near, got):
+    return (near + got.astype(F32)).astype(BF16)
 
 
 def send_sum(near, got):
@@ -177,7 +181,7 @@
 def prepare_kernel(
     gains_ref, query_ref, keyvalue_ref, output_ref, gateup_ref, down_ref, part_ref, ffn_ref
 ):
-    gains = gains_ref[...].astype(BF16).astype(F32)
+    gains = gains_ref[...].astype(BF16).astype(F32).T
     scaled = lambda k, w: (w.astype(BF16).astype(F32) * gains[:, k : k + 1]).astype(BF16)
     part_ref[:, :QUERY_COLS] = scaled(0, query_ref[...])
     part_ref[:, QUERY_COLS:QKV_COLS] = scaled(
@@ -191,7 +195,7 @@
 
 def prepare(norm_gains, query, keyvalue, output, gateup, down):
     full = lambda v: pl.BlockSpec(v.shape, lambda i: (0,) * len(v.shape))
-    arrays = (norm_gains.T, query, keyvalue, output.T, gateup, down.T)
+    arrays = (norm_gains, query, keyvalue, output.T, gateup, down.T)
     outs = [jax.ShapeDtypeStruct((64, n), BF16) for n in (QKV_COLS + QUERY_COLS, 3 * HIDDEN)]
     return pl.pallas_call(
         prepare_kernel,
@@ -199,7 +203,7 @@
         grid=(1,),
         in_specs=[full(v) for v in arrays],
         out_specs=[full(v) for v in outs],
-        compiler_params=pltpu.CompilerParams(vmem_limit_bytes=16 * 2**20),
+        compiler_params=pltpu.CompilerParams(vmem_limit_bytes=60 * 2**20),
         cost_estimate=cost(2),
     )(*arrays)
 
@@ -345,12 +349,80 @@
     )(here(), *arrays)
 
 
-def norm_kernel(near_ref, got_ref, got_own_ref, residual_ref, middle_ref, low_ref):
-    got = got_ref[...].astype(F32) + got_own_ref[...].astype(F32)
-    v = residual_ref[...] + near_ref[...] + got
+def first_norm_kernel(v_ref, _, low_ref, size_ref):
+    v = v_ref[...]
+    square = jnp.mean(v * v, axis=-1, keepdims=True) + EPS
+    low_ref[...] = (v * lax.rsqrt(square)).astype(BF16)
+    size_ref[...] = jnp.broadcast_to(jnp.sqrt(square), size_ref.shape)
+
+
+def first_norm(residual, part):
+    block = pl.BlockSpec((32, D), lambda i: (i, 0))
+    return pl.pallas_call(
+        first_norm_kernel,
+        out_shape=[
+            jax.ShapeDtypeStruct((PART, D), BF16), jax.ShapeDtypeStruct((PART, 128), F32)
+        ],
+        grid=(PART // 32,),
+        in_specs=[block, pl.BlockSpec(memory_space=pl.ANY)],
+        out_specs=[block, pl.BlockSpec((32, 128), lambda i: (i, 0))],
+        compiler_params=pltpu.CompilerParams(vmem_limit_bytes=12 * 2**20),
+        cost_estimate=cost(1),
+    )(residual, part)
+
+
+def pair_norm_kernel(
+    sum_ref, got_ref, residual_ref, normed_ref, size_ref, own_ref, partner_ref, low_ref
+):
+    own = pl.program_id(0) < PART // 64
+    base = jnp.where(own, residual_ref[...], normed_ref[...].astype(F32) * size_ref[:, :1])
+    v = base + (sum_ref[...].astype(F32) + got_ref[...].astype(F32))
     inverse = lax.rsqrt(jnp.mean(v * v, axis=-1, keepdims=True) + EPS)
-    middle_ref[...] = v
     low_ref[...] = (v * inverse).astype(BF16)
+
+    @pl.when(own)
+    def _():
+        own_ref[...] = v
+
+    @pl.when(jnp.logical_not(own))
+    def _():
+        partner_ref[...] = v.astype(BF16)
+
+
+def pair_norm_back_kernel(
+    sum_ref, got_ref, v_ref, partner_ref, cotangent_ref, low_cotangent_ref, out_ref, low_ref
+):
+    own = pl.program_id(0) < PART // 64
+    base = jnp.where(own, cotangent_ref[...], low_cotangent_ref[...].astype(F32))
+    v = jnp.where(own, v_ref[...], partner_ref[...].astype(F32))
+    u = sum_ref[...].astype(F32) + got_ref[...].astype(F32)
+    inverse = lax.rsqrt(jnp.mean(v * v, axis=-1, keepdims=True) + EPS)
+    inner = jnp.mean(u * v, axis=-1, keepdims=True)
+    out = base + (inverse * u - v * (inverse * inverse * inverse * inner))
+    low_ref[...] = out.astype(BF16)
+
+    @pl.when(own)
+    def _():
+        out_ref[...] = out
+
+
+HALF = PART // 64
+EACH, ACROSS = (lambda i: i), (lambda i: (i + HALF) % (2 * HALF))
+OWN, PARTNER = (lambda i: jnp.minimum(i, HALF - 1)), (lambda i: jnp.maximum(i - HALF, 0))
+
+
+def by_pair_rows(kernel, ins, outs):
+    block = lambda n, at: pl.BlockSpec((64, n), lambda i: (at(i), 0))
+    rows = lambda at: 2 * PART if at is EACH else PART
+    return pl.pallas_call(
+        kernel,
+        out_shape=[jax.ShapeDtypeStruct((rows(at), D), t) for t, at in outs],
+        grid=(2 * HALF,),
+        in_specs=[block(a.shape[1], at) for a, at in ins],
+        out_specs=[block(D, at) for _, at in outs],
+        compiler_params=pltpu.CompilerParams(vmem_limit_bytes=24 * 2**20),
+        cost_estimate=cost(2),
+    )(*[a for a, _ in ins])
 
 
 def norm_back_kernel(near_ref, got_ref, got_own_ref, v_ref, base_ref, out_ref, low_ref):
@@ -592,10 +664,6 @@
     return (momentum, variance, updated)
 
 
-def inverse_rms(v):
-    return lax.rsqrt(jnp.mean(v * v, axis=-1, keepdims=True) + EPS)
-
-
 def after(x, *others):
     return lax.optimization_barrier((x, *others))[0]
 
@@ -609,13 +677,12 @@
     residual, cotangent = residual[0], cotangent[0]
     half = SEQ // 2
 
-    inverse_one = inverse_rms(residual)
-    normed_one = (residual * inverse_one).astype(BF16)
+    part, ffn_part = prepare(
+        norm_gains, query_weight, keyvalue_weight, output_weight, gateup_weight, down_weight
+    )
+    normed_one, size = first_norm(residual, part)
     got_one = pair_z(normed_one, 0)
-    part, ffn_part = prepare(
-        norm_gains, after(query_weight, normed_one),
-        keyvalue_weight, output_weight, gateup_weight, down_weight,
-    )
+    got_size = pair_z(size, 0)
     line = jnp.stack([part, shift_first(part, 1), shift_first(part, -1), shift_first(part, 2)])
     ffn_full = lax.all_gather(ffn_part, "dp", axis=0, tiled=True)
     tables = attention_tables(document_lengths[0])
@@ -631,22 +698,27 @@
     cot_far = pair_z(cot_near, 1)
     qkv_full, output_full = place_attention(mine, other)
     qkv = nn(one_near, qkv_full), nn(one_far, qkv_full)
-    attended, q, kv, lse = attend_forward(jnp.concatenate(qkv), tables)
+    attended, q, kv, lse = attend_forward(after(jnp.concatenate(qkv), got_size), tables)
 
     far = nt(after(attended, cot_far)[half:], output_full).astype(BF16)
     got = pair_z(far, 1)
     near = nt(after(attended, far)[:half], output_full)
     cot_turned = turned(after(cot_near, near), cot_far)
     got = after(got, cot_turned)
-    middle, normed_two = by_rows(norm_kernel, near, got, pair_z(send_sum(near, got), 0), residual)
-    got = pair_z(normed_two, 0)
+    sent = add_low(near, got)
+    got_pair = pair_z(sent, 0)
     cot_rows = jnp.concatenate([cot_near, cot_far])
+    got_pair = after(got_pair, cot_rows)
+    middle, partner_middle, two_near = by_pair_rows(
+        pair_norm_kernel,
+        ((sent, EACH), (got_pair, ACROSS), (residual, OWN), (one_near, EACH), (got_size, PARTNER)),
+        ((F32, OWN), (BF16, PARTNER), (BF16, EACH)),
+    )
+    two_far = pair_z(two_near, 1)
     down_full = ffn_full[:, 2 * HIDDEN :]
-    grad_hidden = nn(after(cot_rows, normed_two), down_full)
-    two_near = jnp.concatenate([normed_two, after(got, grad_hidden)])
-    two_far = pair_z(two_near, 1)
     one_turned = turned(after(one_near, two_near), one_far)
-    two_far = after(two_far, one_turned)
+    grad_hidden = nn(after(cot_rows, one_turned), down_full)
+    two_far = after(two_far, grad_hidden)
 
     hidden, grad_gate, grad_up = hidden_units(two_near, two_far, grad_hidden, ffn_full)
     near, far = back_to_rows(grad_gate, grad_up, ffn_full)
@@ -662,18 +734,24 @@
     other_a = weight_products(pairs_a, None, True, 4)
     other_b = weight_products(pairs_b, None, False, 4)
     got = after(got, other_a, other_b)
-    sent = send_sum(near, got)
-    got_own = pair_z(sent, 0)
+    sent = add_low(near, got)
+    got_pair = pair_z(sent, 0)
     got_a = swap_core(after(other_a, sent))
     got_b = swap_core(after(other_b, sent))
-    down_near, down_far = product_rows(after(hidden, sent), ffn_full, 2, 5)
-    got_own = after(got_own, down_near)
-
-    grad_middle, low_grad = by_rows(norm_back_kernel, near, got, got_own, middle, cotangent)
-    got_low = pair_z(low_grad, 0)
-    near_a, far_a = weight_products(pairs_a, after(got_a, low_grad), True, 4)
+    down = nt(after(hidden, sent), down_full)
+    down_near, down_far = down[:half], down[half:].astype(BF16)
+    near_a, far_a = weight_products(pairs_a, after(got_a, down), True, 4)
     got_a = pair_first(far_a, 1, True)
-    rows_near = jnp.concatenate([low_grad, after(got_low, near_a)])
+    got_pair = after(got_pair, near_a)
+
+    grad_middle, rows_near = by_pair_rows(
+        pair_norm_back_kernel,
+        (
+            (sent, EACH), (got_pair, ACROSS), (middle, OWN), (partner_middle, PARTNER),
+            (cotangent, OWN), (cot_near, EACH),
+        ),
+        ((F32, OWN), (BF16, EACH)),
+    )
     rows_far = pair_z(rows_near, 1)
     near_b, far_b = weight_products(pairs_b, after(got_b, rows_near), False, 0.001)
     got_b = pair_first(far_b, 1, False)
@@ -733,7 +811,6 @@
     grad_ffn_a = keep_a[0] + got_a[0].astype(F32)
     grad_qkv = keep_qkv[0] + got_qkv[0].astype(F32)
     grad_ffn_b = keep_b[0] + got_b[0].astype(F32)
-    grad_output = keep_output[0] + got_output[0].astype(F32)
     block_output = middle + (
         down_near[:PART] + (got_down[:PART].astype(F32) + got_down_own.astype(F32))
     )
@@ -751,6 +828,7 @@
             + jnp.sum(low_up * grad_ffn_b[:, :HIDDEN], axis=1),
         )
     )
+    grad_output = keep_output[0] + after(got_output, gain_parts)[0].astype(F32)
     gains = gain_parts + shift_z(gain_parts, 1) + shift_z(gain_parts, -1) + shift_z(gain_parts, 2)
     grad_qkv = grad_qkv * gain_one
     reduced = (

time: 309 us -> 293 us (0.948)
  local copies, waits for them, and re-layouts: 24.6 us -> 12.5 us
  starting transfers between devices: 64.6 us -> 56.5 us
  matrix products: 11.5 us -> 19.1 us
  waiting for transfers between devices: 85.2 us -> 89.9 us
  other arithmetic: 22.7 us -> 18.2 us
  Pallas kernels: 79.5 us -> 75.6 us
    unnamed x160 -> x104, local copies, waits for them, and re-layouts: 21.2 us -> 10.8 us
    dot_general x2 -> x3, matrix products: 1.53 us -> 9.16 us  [nt(): lax.dot_general(a, b, (((1,), (1,)), ((), ())), preferred_element_type=F32)]
    ppermute x16 -> x15, starting transfers between devices: 31.8 us -> 25.2 us  [pair_z(): return lax.ppermute(a, ('dp', 'mp'), pairs)]
    pallas_call x2 -> x1, Pallas kernels: 7.27 us -> 2.62 us  [product_rows(): pl.pallas_call(rows_kernel, out_shape=[jax.ShapeDtypeStruct((SEQ // 2, D)...]
    pallas_call x0 -> x3, Pallas kernels: none -> 4.48 us  [the longest x2 3.96 us: by_pair_rows(): pl.pallas_call(kernel, out_shape=[jax.ShapeDtypeStruct((rows(at), D), t)...]
    ppermute x5, waiting for transfers between devices: 0.58 us -> 5.03 us  [swap_core(): return lax.ppermute(a, 'dp', [(i, i ^ 1) for i in range(2 * SIDE * SIDE)])]
    pallas_call x8, Pallas kernels: 29.6 us -> 25.7 us  [weight_products(): pl.pallas_call(kernel, out_shape=outs, grid_spec=pltpu.PrefetchScalarGrid...]
    ppermute x16 -> x15, waiting for transfers between devices: 36.2 us -> 37.9 us  [pair_z(): return lax.ppermute(a, ('dp', 'mp'), pairs)]
  transfers between devices with their start and end apart: 47 -> 46, of which waited for: 24 -> 23; matrix products, arithmetic and copies ran while one was open for 11% -> 14% of each run, Pallas kernels for 19% -> 18%
where the time goes in v4:
time: 293 us; the launch traced here: 287 us
  waiting for transfers between devices  89.9 us (31%)
  Pallas kernels  75.6 us (26%)
  starting transfers between devices  56.5 us (19%)
  matrix products  19.1 us (7%)
  other arithmetic  18.2 us (6%)
  between operations  15.4 us (5%)
  local copies, waits for them, and re-layouts  12.5 us (4%)
    ppermute x15, waiting for transfers between devices, pair_z(): return lax.ppermute(a, ('dp', 'mp'), pairs)  37.9 us
    pallas_call x8, Pallas kernels, weight_products(): pl.pallas_call(kernel, out_shape=outs, grid_spec=pltpu.PrefetchScalarGrid...  25.7 us
    ppermute x15, starting transfers between devices, pair_z(): return lax.ppermute(a, ('dp', 'mp'), pairs)  25.2 us
    ppermute x8, waiting for transfers between devices, pair_x(): return lax.ppermute(a, 'dp', pairs)  21.2 us
    ppermute x3, waiting for transfers between devices, shift_second(): return lax.ppermute(a, 'dp', pairs)  15.4 us
    pallas_call x1, Pallas kernels, hidden_units(): pl.pallas_call(hidden_kernel, out_shape=[jax.ShapeDtypeStruct((SEQ, HIDDE...  12.9 us
    unnamed x104, local copies, waits for them, and re-layouts  10.8 us
    ppermute x8, starting transfers between devices, pair_y(): return lax.ppermute(a, 'dp', pairs)  10.7 us
  transfers between devices with their start and end apart: 46, of which 23 were waited for; matrix products, arithmetic and copies ran while one was open for 14% of the time, Pallas kernels for 18%

profile of v4, /device:TPU:0, one launch (start us, length us, event | category | flops | bytes accessed | tf_op | source)
XLA Modules:
  0.0 287.2 jit_solution(3295605028216710420)
XLA Ops:
  7.3 2.5 shard_map.422
  9.8 3.2 %collective-permute-start.3 = (bf16[64,1152]{1,0:T(8,128)(2,1)}, bf16[64,1152]{1,0:T(8,128)(2,1)S(1)}, u32[]{:S(2)}, u32[]{:S(2)}) collective-permute-start(bf16[64,1152]{1,0:T(8,128)(2,1)} %get-tuple-element.101._), channel_id=1, source_target_pairs={{0,16},{4,68},{8,24},{12,76},{16,0},{20,84},{24,8},{28,92},{32,48}... | collective-permute-start | bytes 442376 | tf_op jit(solution)/shard_map/ppermute | solution.py:79
  16.5 2.0 collective-permute-start
  21.5 3.3 %collective-permute-start.6 = (bf16[4,64,1152]{2,1,0:T(8,128)(2,1)S(1)}, bf16[4,64,1152]{2,1,0:T(8,128)(2,1)S(1)}, u32[]{:S(2)}, u32[]{:S(2)}) collective-permute-start(bf16[4,64,1152]{2,1,0:T(8,128)(2,1)S(1)} %pad_maximum_fusion.4), channel_id=1, source_target_pairs={{0,64},{4,20},{8,72},{12,28},{16,80},{20,4},{24,88},{28,12},{32,96... | collective-permute-start | bytes 1769480 | tf_op jit(solution)/shard_map/ppermute | solution.py:87
  28.0 3.4 %collective-permute-start.7 = (bf16[256,2048]{1,0:T(8,128)(2,1)S(1)}, bf16[256,2048]{1,0:T(8,128)(2,1)S(1)}, u32[]{:S(2)}, u32[]{:S(2)}) collective-permute-start(bf16[256,2048]{1,0:T(8,128)(2,1)S(1)} %pad_maximum_fusion.2.normed_ref.near_ref), channel_id=1, source_target_pairs={{0,3},{1,2},{2,1},{3,0},{4,5},{5,4},{6,7},{7,6},{8,11},{9,10},{10,... | collective-permute-start | bytes 3145736 | tf_op jit(solution)/shard_map/ppermute | solution.py:57
  32.6 5.3 %collective-permute-done.6 = bf16[4,64,1152]{2,1,0:T(8,128)(2,1)S(1)} collective-permute-done((bf16[4,64,1152]{2,1,0:T(8,128)(2,1)S(1)}, bf16[4,64,1152]{2,1,0:T(8,128)(2,1)S(1)}, u32[]{:S(2)}, u32[]{:S(2)}) %collective-permute-start.6) | collective-permute-done | bytes 589856 | tf_op jit(solution)/shard_map/ppermute | solution.py:87
  37.9 9.9 %collective-permute-done.5 = bf16[4,64,1152]{2,1,0:T(8,128)(2,1)S(1)} collective-permute-done((bf16[4,64,1152]{2,1,0:T(8,128)(2,1)S(1)}, bf16[4,64,1152]{2,1,0:T(8,128)(2,1)S(1)}, u32[]{:S(2)}, u32[]{:S(2)}) %collective-permute-start.5) | collective-permute-done | bytes 589856 | tf_op jit(solution)/shard_map/ppermute | solution.py:87
  52.3 2.9 %collective-permute-start.11 = (bf16[256,2048]{1,0:T(8,128)(2,1)}, bf16[256,2048]{1,0:T(8,128)(2,1)S(1)}, u32[]{:S(2)}, u32[]{:S(2)}) collective-permute-start(bf16[256,2048]{1,0:T(8,128)(2,1)} %copy-done.6), channel_id=1, source_target_pairs={{0,3},{1,2},{2,1},{3,0},{4,5},{5,4},{6,7},{7,6},{8,11},{9,10},{10,... | collective-permute-start | bytes 3145736 | tf_op jit(solution)/shard_map/ppermute | solution.py:57
  55.5 2.4 shard_map.424
  63.4 4.3 %shard_map.425 = (bf16[512,512]{1,0:T(8,128)(2,1)S(1)}, bf16[512,512]{1,0:T(8,128)(2,1)S(1)}, bf16[512,128]{1,0:T(8,128)(2,1)S(1)}, f32[8,512]{1,0:T(8,128)S(1)}) custom-call(s32[4]{0:T(128)S(1)} %select_reduce_fusion.1.slot_ref, s32[4]{0:T(128)S(1)} %bitcast.106, f32[512,640]{1,0:T(8,128)S(1)} %pad_maximum_fusion.1.qkv_ref, f32[512,128]{1,0:T(8,128)S(1)} %copy-done.15, ...), custom_call_target="tpu_custom_call" | custom-call | flops 5500000256 | bytes 15000000 | tf_op jit(solution)/shard_map/pallas_call | solution.py:607
  69.5 2.8 collective-permute-start.12
  73.7 11.9 %collective-permute-done.12 = bf16[256,2048]{1,0:T(8,128)(2,1)S(1)} collective-permute-done((bf16[256,2048]{1,0:T(8,128)(2,1)S(1)}, bf16[256,2048]{1,0:T(8,128)(2,1)S(1)}, u32[]{:S(2)}, u32[]{:S(2)}) %collective-permute-start.12) | collective-permute-done | bytes 1048608 | tf_op jit(solution)/shard_map/ppermute | solution.py:57
  87.1 13.7 %collective-permute-done.13.got_ref = bf16[256,2048]{1,0:T(8,128)(2,1)S(1)} collective-permute-done((bf16[256,2048]{1,0:T(8,128)(2,1)S(1)}, bf16[256,2048]{1,0:T(8,128)(2,1)S(1)}, u32[]{:S(2)}, u32[]{:S(2)}) %collective-permute-start.13) | collective-permute-done | bytes 1048608 | tf_op jit(solution)/shard_map/ppermute | solution.py:57
  100.8 2.3 shard_map.427
  104.9 3.1 %collective-permute-start.14 = (bf16[256,2048]{1,0:T(8,128)(2,1)}, bf16[256,2048]{1,0:T(8,128)(2,1)}, u32[]{:S(2)}, u32[]{:S(2)}) collective-permute-start(bf16[256,2048]{1,0:T(8,128)(2,1)} %get-tuple-element.128.near_ref), channel_id=1, source_target_pairs={{0,3},{1,2},{2,1},{3,0},{4,5},{5,4},{6,7},{7,6},{8,11},{9,10},{10,... | collective-permute-start | bytes 3145736 | tf_op jit(solution)/shard_map/ppermute | solution.py:57
  109.9 6.5 %fusion.2.grad_hidden_ref = f32[512,1408]{1,0:T(8,128)S(1)} fusion(bf16[512,2048]{1,0:T(8,128)(2,1)} %constant_dynamic-update-slice_fusion.2, bf16[2048,4224]{1,0:T(8,128)(2,1)} %all-gather.2.cloned.1.call-done.gate_w_ref.up_w_ref), kind=kOutput, calls=%fused_computation.2 | convolution fusion | flops 2952790016 | bytes 10747904 | tf_op jit(solution)/shard_map/dot_general | solution.py:174
  116.5 5.1 %collective-permute-done.14.far_ref = bf16[256,2048]{1,0:T(8,128)(2,1)} collective-permute-done((bf16[256,2048]{1,0:T(8,128)(2,1)}, bf16[256,2048]{1,0:T(8,128)(2,1)}, u32[]{:S(2)}, u32[]{:S(2)}) %collective-permute-start.14) | collective-permute-done | bytes 1048608 | tf_op jit(solution)/shard_map/ppermute | solution.py:57
  121.6 12.9 %shard_map.429 = (bf16[512,1408]{1,0:T(8,128)(2,1)S(1)}, bf16[512,1408]{1,0:T(8,128)(2,1)S(1)}, bf16[512,1408]{1,0:T(8,128)(2,1)S(1)}) custom-call(bf16[256,2048]{1,0:T(8,128)(2,1)} %get-tuple-element.128.near_ref, bf16[256,2048]{1,0:T(8,128)(2,1)} %collective-permute-done.14.far_ref, bf16[2048,4224]{1,0:T(8,128)(2,1)S(1)} %copy-done.19, ...), custom_call_target="tpu_custom_call" | custom-call | flops 11000000512 | bytes 30000000 | tf_op jit(solution)/shard_map/pallas_call | solution.py:474
  134.5 9.3 %shard_map.430 = (f32[256,2048]{1,0:T(8,128)S(1)}, bf16[256,2048]{1,0:T(8,128)(2,1)S(1)}) custom-call(bf16[512,1408]{1,0:T(8,128)(2,1)S(1)} %get-tuple-element.124.gate_ref.refs_1_, bf16[512,1408]{1,0:T(8,128)(2,1)S(1)} %get-tuple-element.125.up_ref.refs_1_, bf16[2048,4224]{1,0:T(8,128)(2,1)} %all-gather.2.cloned.1.call-done.gate_w_ref.up_w_ref, ...), custom_call_target="tpu_custom_call" | custom-call | flops 11000000512 | bytes 30000000 | tf_op jit(solution)/shard_map/pallas_call | solution.py:222
  143.8 2.8 collective-permute-start.15
  146.6 2.1 shard_map.431.refs_0_
  148.7 3.7 %shard_map.432 = bf16[16,64,2176]{2,1,0:T(8,128)(2,1)S(1)} custom-call(s32[3]{0:T(128)S(1)} %pad_add_fusion.here_ref, bf16[2048,512]{1,0:T(8,128)(2,1)S(1)} %shard_map.431.refs_0_, bf16[512,1408]{1,0:T(8,128)(2,1)S(1)} %get-tuple-element.124.gate_ref.refs_1_, bf16[2048,512]{1,0:T(8,128)(2,1)S(1)} %shard_map.426.refs_2_, ...), custom_call_target="tpu_custom_call" | custom-call | flops 4400000000 | bytes 12000000 | tf_op jit(solution)/shard_map/pallas_call | solution.py:341
  152.5 4.9 %shard_map.433 = bf16[16,64,2048]{2,1,0:T(8,128)(2,1)} custom-call(s32[3]{0:T(128)S(1)} %pad_add_fusion.here_ref, bf16[2048,512]{1,0:T(8,128)(2,1)S(1)} %shard_map.431.refs_0_, bf16[512,1408]{1,0:T(8,128)(2,1)S(1)} %get-tuple-element.125.up_ref.refs_1_, bf16[2048,512]{1,0:T(8,128)(2,1)S(1)} %shard_map.426.refs_2_, ...), custom_call_target="tpu_custom_call" | custom-call | flops 4400000000 | bytes 12000000 | tf_op jit(solution)/shard_map/pallas_call | solution.py:341
  157.4 2.5 collective-permute-done.15
  160.7 7.6 %fusion = f32[512,2048]{1,0:T(8,128)} fusion(bf16[512,1408]{1,0:T(8,128)(2,1)S(1)} %get-tuple-element.130.refs_3_, bf16[2048,4224]{1,0:T(8,128)(2,1)} %all-gather.2.cloned.1.call-done.gate_w_ref.up_w_ref), kind=kOutput, calls=%fused_computation | convolution fusion | flops 2952790016 | bytes 11403264 | tf_op jit(solution)/shard_map/dot_general | solution.py:166
  168.4 4.8 %collective-permute-done.17.refs_4_.refs_5_.refs_6_.refs_7_ = bf16[16,64,2176]{2,1,0:T(8,128)(2,1)S(1)} collective-permute-done((bf16[16,64,2176]{2,1,0:T(8,128)(2,1)S(1)}, bf16[16,64,2176]{2,1,0:T(8,128)(2,1)S(1)}, u32[]{:S(2)}, u32[]{:S(2)}) %collective-permute-start.17) | collective-permute-done | bytes 4456480 | tf_op jit(solution)/shard_map/ppermute | solution.py:91
  173.2 4.5 %shard_map.434 = (bf16[8,64,2176]{2,1,0:T(8,128)(2,1)S(1)}, bf16[8,64,2176]{2,1,0:T(8,128)(2,1)S(1)}) custom-call(s32[3]{0:T(128)S(1)} %pad_add_fusion.here_ref, bf16[2048,512]{1,0:T(8,128)(2,1)S(1)} %shard_map.431.refs_0_, bf16[512,1408]{1,0:T(8,128)(2,1)S(1)} %get-tuple-element.124.gate_ref.refs_1_, bf16[2048,512]{1,0:T(8,128)(2,1)S(1)} %shard_map.426.refs_2_, ...), custom_call_target="tpu_custom_call" | custom-call | flops 4400000000 | bytes 12000000 | tf_op jit(solution)/shard_map/pallas_call | solution.py:341
  179.4 2.8 collective-permute-start.19
  182.2 2.3 collective-permute-start.21
  184.5 4.4 %shard_map.436 = (bf16[8,64,2048]{2,1,0:T(8,128)(2,1)S(1)}, bf16[8,64,2048]{2,1,0:T(8,128)(2,1)S(1)}) custom-call(s32[3]{0:T(128)S(1)} %pad_add_fusion.here_ref, bf16[2048,512]{1,0:T(8,128)(2,1)S(1)} %shard_map.431.refs_0_, bf16[512,1408]{1,0:T(8,128)(2,1)S(1)} %get-tuple-element.125.up_ref.refs_1_, bf16[2048,512]{1,0:T(8,128)(2,1)S(1)} %shard_map.426.refs_2_, ...), custom_call_target="tpu_custom_call" | custom-call | flops 1100000 | bytes 3000 | tf_op jit(solution)/shard_map/pallas_call | solution.py:341
  189.0 2.1 collective-permute-start.24
  191.8 3.7 %collective-permute-done.19.far_ref = bf16[256,2048]{1,0:T(8,128)(2,1)S(1)} collective-permute-done((bf16[256,2048]{1,0:T(8,128)(2,1)S(1)}, bf16[256,2048]{1,0:T(8,128)(2,1)S(1)}, u32[]{:S(2)}, u32[]{:S(2)}) %collective-permute-start.19) | collective-permute-done | bytes 1048608 | tf_op jit(solution)/shard_map/ppermute | solution.py:57
  196.3 5.6 %shard_map.437.refs_1_.a_ref = bf16[512,640]{1,0:T(8,128)(2,1)S(1)} custom-call(s32[4]{0:T(128)S(1)} %select_reduce_fusion.1.slot_ref, s32[4]{0:T(128)S(1)} %bitcast.107, bf16[512,512]{1,0:T(8,128)(2,1)S(1)} %copy-done.28, bf16[512,128]{1,0:T(8,128)(2,1)S(1)} %get-tuple-element.132.kv_ref, f32[8,512]{1,0:T(8,128)S(1)} %get-tuple-element.133.lse_ref, ...), custom_call_target="tpu_custom_call" | custom-call | flops 6600000000 | bytes 18000000 | tf_op jit(solution)/shard_map/pallas_call | solution.py:625
  201.8 2.1 shard_map.438
  204.0 2.6 shard_map.439
  206.6 2.8 collective-permute-start.20
  213.1 1.8 shard_map.441
  216.9 2.3 shard_map.442
  221.9 2.0 shard_map.443
  225.6 12.6 %collective-permute-done.28 = bf16[8,64,640]{2,1,0:T(8,128)(2,1)S(1)} collective-permute-done((bf16[8,64,640]{2,1,0:T(8,128)(2,1)S(1)}, bf16[8,64,640]{2,1,0:T(8,128)(2,1)S(1)}, u32[]{:S(2)}, u32[]{:S(2)}) %collective-permute-start.28) | collective-permute-done | bytes 655392 | tf_op jit(solution)/shard_map/ppermute | solution.py:62
  238.4 2.0 add_convert_fusion
  248.5 3.2 %collective-permute-done.34 = bf16[4,64,512]{2,1,0:T(8,128)(2,1)S(1)} collective-permute-done((bf16[4,64,512]{2,1,0:T(8,128)(2,1)S(1)}, bf16[4,64,512]{2,1,0:T(8,128)(2,1)S(1)}, u32[]{:S(2)}, u32[]{:S(2)}) %collective-permute-start.34) | collective-permute-done | bytes 262176 | tf_op jit(solution)/shard_map/ppermute | solution.py:67
  251.8 2.2 collective-permute-done.33
  256.0 2.0 shard_map.444
  258.0 2.0 collective-permute-start.37
  260.0 1.9 collective-permute-start.43
  264.8 2.9 %collective-permute-done.43 = bf16[2,64,512]{2,1,0:T(8,128)(2,1)S(1)} collective-permute-done((bf16[2,64,512]{2,1,0:T(8,128)(2,1)S(1)}, bf16[2,64,512]{2,1,0:T(8,128)(2,1)S(1)}, u32[]{:S(2)}, u32[]{:S(2)}) %collective-permute-start.43) | collective-permute-done | bytes 131104 | tf_op jit(solution)/shard_map/ppermute | solution.py:62
  267.8 2.6 collective-permute-done.39
  (242 shorter events, 66.2 us)
Async XLA Ops:
  7.2 102.7 %all-gather.2.cloned.1.call-start = ((), (), s32[]{:S(2)}) async-start(), calls=%async_computation | async-start | bytes 17842176 | tf_op jit(solution)/shard_map/all_gather | solution.py:687
  9.8 11.6 %collective-permute-start.3 = (bf16[64,1152]{1,0:T(8,128)(2,1)}, bf16[64,1152]{1,0:T(8,128)(2,1)S(1)}, u32[]{:S(2)}, u32[]{:S(2)}) collective-permute-start(bf16[64,1152]{1,0:T(8,128)(2,1)} %get-tuple-element.101._), channel_id=1, source_target_pairs={{0,16},{4,68},{8,24},{12,76},{16,0},{20,84},{24,8},{28,92},{32,48}... | collective-permute-start | bytes 442376 | tf_op jit(solution)/shard_map/ppermute | solution.py:79
  13.0 8.4 %collective-permute-start.2 = (bf16[64,1152]{1,0:T(8,128)(2,1)}, bf16[64,1152]{1,0:T(8,128)(2,1)S(1)}, u32[]{:S(2)}, u32[]{:S(2)}) collective-permute-start(bf16[64,1152]{1,0:T(8,128)(2,1)} %get-tuple-element.101._), channel_id=1, source_target_pairs={{0,24},{4,100},{8,0},{12,108},{16,8},{20,116},{24,16},{28,124},{32... | collective-permute-start | bytes 442376 | tf_op jit(solution)/shard_map/ppermute | solution.py:79
  14.2 7.2 %collective-permute-start.1 = (bf16[64,1152]{1,0:T(8,128)(2,1)}, bf16[64,1152]{1,0:T(8,128)(2,1)S(1)}, u32[]{:S(2)}, u32[]{:S(2)}) collective-permute-start(bf16[64,1152]{1,0:T(8,128)(2,1)} %get-tuple-element.101._), channel_id=1, source_target_pairs={{0,8},{4,36},{8,16},{12,44},{16,24},{20,52},{24,0},{28,60},{32,40}... | collective-permute-start | bytes 442376 | tf_op jit(solution)/shard_map/ppermute | solution.py:79
  16.5 10.3 %collective-permute-start = (bf16[128,2048]{1,0:T(8,128)(2,1)S(1)}, bf16[128,2048]{1,0:T(8,128)(2,1)}, u32[]{:S(2)}, u32[]{:S(2)}) collective-permute-start(bf16[128,2048]{1,0:T(8,128)(2,1)S(1)} %get-tuple-element.102), channel_id=1, source_target_pairs={{0,1},{1,0},{2,3},{3,2},{4,7},{5,6},{6,5},{7,4},{8,9},{9,8},{10,11... | collective-permute-start | bytes 1572872 | tf_op jit(solution)/shard_map/ppermute | solution.py:57
  21.5 16.4 %collective-permute-start.6 = (bf16[4,64,1152]{2,1,0:T(8,128)(2,1)S(1)}, bf16[4,64,1152]{2,1,0:T(8,128)(2,1)S(1)}, u32[]{:S(2)}, u32[]{:S(2)}) collective-permute-start(bf16[4,64,1152]{2,1,0:T(8,128)(2,1)S(1)} %pad_maximum_fusion.4), channel_id=1, source_target_pairs={{0,64},{4,20},{8,72},{12,28},{16,80},{20,4},{24,88},{28,12},{32,96... | collective-permute-start | bytes 1769480 | tf_op jit(solution)/shard_map/ppermute | solution.py:87
  24.8 23.1 %collective-permute-start.5 = (bf16[4,64,1152]{2,1,0:T(8,128)(2,1)S(1)}, bf16[4,64,1152]{2,1,0:T(8,128)(2,1)S(1)}, u32[]{:S(2)}, u32[]{:S(2)}) collective-permute-start(bf16[4,64,1152]{2,1,0:T(8,128)(2,1)S(1)} %pad_maximum_fusion.4), channel_id=1, source_target_pairs={{0,96},{4,28},{8,104},{12,4},{16,112},{20,12},{24,120},{28,20},{32... | collective-permute-start | bytes 1769480 | tf_op jit(solution)/shard_map/ppermute | solution.py:87
  25.8 22.1 %collective-permute-start.4 = (bf16[4,64,1152]{2,1,0:T(8,128)(2,1)S(1)}, bf16[4,64,1152]{2,1,0:T(8,128)(2,1)S(1)}, u32[]{:S(2)}, u32[]{:S(2)}) collective-permute-start(bf16[4,64,1152]{2,1,0:T(8,128)(2,1)S(1)} %pad_maximum_fusion.4), channel_id=1, source_target_pairs={{0,32},{4,12},{8,40},{12,20},{16,48},{20,28},{24,56},{28,4},{32,64... | collective-permute-start | bytes 1769480 | tf_op jit(solution)/shard_map/ppermute | solution.py:87
  27.9 29.9 %copy-start.4 = (bf16[256,2048]{1,0:T(8,128)(2,1)}, bf16[256,2048]{1,0:T(8,128)(2,1)S(1)}, u32[]{:S(2)}) copy-start(bf16[256,2048]{1,0:T(8,128)(2,1)S(1)} %pad_maximum_fusion.2.normed_ref.near_ref) | copy-start | bytes 3145732
  28.0 21.5 %collective-permute-start.7 = (bf16[256,2048]{1,0:T(8,128)(2,1)S(1)}, bf16[256,2048]{1,0:T(8,128)(2,1)S(1)}, u32[]{:S(2)}, u32[]{:S(2)}) collective-permute-start(bf16[256,2048]{1,0:T(8,128)(2,1)S(1)} %pad_maximum_fusion.2.normed_ref.near_ref), channel_id=1, source_target_pairs={{0,3},{1,2},{2,1},{3,0},{4,5},{5,4},{6,7},{7,6},{8,11},{9,10},{10,... | collective-permute-start | bytes 3145736 | tf_op jit(solution)/shard_map/ppermute | solution.py:57
  31.5 17.1 %collective-permute-start.8 = (bf16[128,2048]{1,0:T(8,128)(2,1)S(1)}, bf16[128,2048]{1,0:T(8,128)(2,1)S(1)}, u32[]{:S(2)}, u32[]{:S(2)}) collective-permute-start(bf16[128,2048]{1,0:T(8,128)(2,1)S(1)} %bitcast_convert_fusion), channel_id=1, source_target_pairs={{0,1},{1,0},{2,3},{3,2},{4,7},{5,6},{6,5},{7,4},{8,9},{9,8},{10,11... | collective-permute-start | bytes 1572872 | tf_op jit(solution)/shard_map/ppermute | solution.py:57
  50.8 4.7 %collective-permute-start.9 = (bf16[16,64,1152]{2,1,0:T(8,128)(2,1)S(1)}, bf16[16,64,1152]{2,1,0:T(8,128)(2,1)}, u32[]{:S(2)}, u32[]{:S(2)}) collective-permute-start(bf16[16,64,1152]{2,1,0:T(8,128)(2,1)S(1)} %bitcast.96), channel_id=1, source_target_pairs={{0,4},{4,0},{8,12},{12,8},{16,20},{20,16},{24,28},{28,24},{32,36},... | collective-permute-start | bytes 7077896 | tf_op jit(solution)/shard_map/ppermute | solution.py:91
  50.9 11.6 %collective-permute-start.10 = (f32[128,128]{1,0:T(8,128)S(1)}, f32[128,128]{1,0:T(8,128)S(1)}, u32[]{:S(2)}, u32[]{:S(2)}) collective-permute-start(f32[128,128]{1,0:T(8,128)S(1)} %get-tuple-element.108), channel_id=1, source_target_pairs={{0,1},{1,0},{2,3},{3,2},{4,7},{5,6},{6,5},{7,4},{8,9},{9,8},{10,11... | collective-permute-start | bytes 196616 | tf_op jit(solution)/shard_map/ppermute | solution.py:57
  52.3 16.4 %collective-permute-start.11 = (bf16[256,2048]{1,0:T(8,128)(2,1)}, bf16[256,2048]{1,0:T(8,128)(2,1)S(1)}, u32[]{:S(2)}, u32[]{:S(2)}) collective-permute-start(bf16[256,2048]{1,0:T(8,128)(2,1)} %copy-done.6), channel_id=1, source_target_pairs={{0,3},{1,2},{2,1},{3,0},{4,5},{5,4},{6,7},{7,6},{8,11},{9,10},{10,... | collective-permute-start | bytes 3145736 | tf_op jit(solution)/shard_map/ppermute | solution.py:57
  69.5 16.1 %collective-permute-start.12 = (bf16[256,2048]{1,0:T(8,128)(2,1)S(1)}, bf16[256,2048]{1,0:T(8,128)(2,1)S(1)}, u32[]{:S(2)}, u32[]{:S(2)}) collective-permute-start(bf16[256,2048]{1,0:T(8,128)(2,1)S(1)} %convolution_convert_fusion), channel_id=1, source_target_pairs={{0,3},{1,2},{2,1},{3,0},{4,5},{5,4},{6,7},{7,6},{8,11},{9,10},{10,... | collective-permute-start | bytes 3145736 | tf_op jit(solution)/shard_map/ppermute | solution.py:57
  85.9 14.9 %copy-start.5 = (bf16[256,2048]{1,0:T(8,128)(2,1)S(1)}, bf16[256,2048]{1,0:T(8,128)(2,1)}, u32[]{:S(2)}) copy-start(bf16[256,2048]{1,0:T(8,128)(2,1)} %copy-done.4) | copy-start | bytes 3145732
  85.9 14.9 %collective-permute-start.13 = (bf16[256,2048]{1,0:T(8,128)(2,1)S(1)}, bf16[256,2048]{1,0:T(8,128)(2,1)S(1)}, u32[]{:S(2)}, u32[]{:S(2)}) collective-permute-start(bf16[256,2048]{1,0:T(8,128)(2,1)S(1)} %add_convert_fusion.5.sum_ref), channel_id=1, source_target_pairs={{0,1},{1,0},{2,3},{3,2},{4,7},{5,6},{6,5},{7,4},{8,9},{9,8},{10,11... | collective-permute-start | bytes 3145736 | tf_op jit(solution)/shard_map/ppermute | solution.py:57
  104.9 16.7 %collective-permute-start.14 = (bf16[256,2048]{1,0:T(8,128)(2,1)}, bf16[256,2048]{1,0:T(8,128)(2,1)}, u32[]{:S(2)}, u32[]{:S(2)}) collective-permute-start(bf16[256,2048]{1,0:T(8,128)(2,1)} %get-tuple-element.128.near_ref), channel_id=1, source_target_pairs={{0,3},{1,2},{2,1},{3,0},{4,5},{5,4},{6,7},{7,6},{8,11},{9,10},{10,... | collective-permute-start | bytes 3145736 | tf_op jit(solution)/shard_map/ppermute | solution.py:57
  143.8 16.1 %collective-permute-start.15 = (bf16[256,2048]{1,0:T(8,128)(2,1)S(1)}, bf16[256,2048]{1,0:T(8,128)(2,1)S(1)}, u32[]{:S(2)}, u32[]{:S(2)}) collective-permute-start(bf16[256,2048]{1,0:T(8,128)(2,1)S(1)} %get-tuple-element.127), channel_id=1, source_target_pairs={{0,3},{1,2},{2,1},{3,0},{4,5},{5,4},{6,7},{7,6},{8,11},{9,10},{10,... | collective-permute-start | bytes 3145736 | tf_op jit(solution)/shard_map/ppermute | solution.py:57
  160.2 13.1 %collective-permute-start.17 = (bf16[16,64,2176]{2,1,0:T(8,128)(2,1)S(1)}, bf16[16,64,2176]{2,1,0:T(8,128)(2,1)S(1)}, u32[]{:S(2)}, u32[]{:S(2)}) collective-permute-start(bf16[16,64,2176]{2,1,0:T(8,128)(2,1)S(1)} %shard_map.432), channel_id=1, source_target_pairs={{0,4},{4,0},{8,12},{12,8},{16,20},{20,16},{24,28},{28,24},{32,36},... | collective-permute-start | bytes 13369352 | tf_op jit(solution)/shard_map/ppermute | solution.py:91
  160.2 24.3 %collective-permute-start.18 = (bf16[16,64,2048]{2,1,0:T(8,128)(2,1)}, bf16[16,64,2048]{2,1,0:T(8,128)(2,1)S(1)}, u32[]{:S(2)}, u32[]{:S(2)}) collective-permute-start(bf16[16,64,2048]{2,1,0:T(8,128)(2,1)} %shard_map.433), channel_id=1, source_target_pairs={{0,4},{4,0},{8,12},{12,8},{16,20},{20,16},{24,28},{28,24},{32,36},... | collective-permute-start | bytes 12582920 | tf_op jit(solution)/shard_map/ppermute | solution.py:91
  160.7 17.0 %collective-permute-start.16 = (bf16[256,2048]{1,0:T(8,128)(2,1)S(1)}, bf16[256,2048]{1,0:T(8,128)(2,1)S(1)}, u32[]{:S(2)}, u32[]{:S(2)}) collective-permute-start(bf16[256,2048]{1,0:T(8,128)(2,1)S(1)} %add_convert_fusion.4.sum_ref), channel_id=1, source_target_pairs={{0,1},{1,0},{2,3},{3,2},{4,7},{5,6},{6,5},{7,4},{8,9},{9,8},{10,11... | collective-permute-start | bytes 3145736 | tf_op jit(solution)/shard_map/ppermute | solution.py:57
  179.4 16.1 %collective-permute-start.19 = (bf16[256,2048]{1,0:T(8,128)(2,1)S(1)}, bf16[256,2048]{1,0:T(8,128)(2,1)S(1)}, u32[]{:S(2)}, u32[]{:S(2)}) collective-permute-start(bf16[256,2048]{1,0:T(8,128)(2,1)S(1)} %get-tuple-element.150.near_ref), channel_id=1, source_target_pairs={{0,3},{1,2},{2,1},{3,0},{4,5},{5,4},{6,7},{7,6},{8,11},{9,10},{10,... | collective-permute-start | bytes 3145736 | tf_op jit(solution)/shard_map/ppermute | solution.py:57
  182.2 28.8 %collective-permute-start.21 = (bf16[8,64,2176]{2,1,0:T(8,128)(2,1)S(1)}, bf16[8,64,2176]{2,1,0:T(8,128)(2,1)}, u32[]{:S(2)}, u32[]{:S(2)}) collective-permute-start(bf16[8,64,2176]{2,1,0:T(8,128)(2,1)S(1)} %get-tuple-element.148), channel_id=1, source_target_pairs={{0,24},{4,12},{8,16},{12,4},{16,8},{20,28},{24,0},{28,20},{32,56},... | collective-permute-start | bytes 6684680 | tf_op jit(solution)/shard_map/ppermute | solution.py:62
  189.0 27.5 %collective-permute-start.24 = (bf16[8,64,2048]{2,1,0:T(8,128)(2,1)S(1)}, bf16[8,64,2048]{2,1,0:T(8,128)(2,1)S(1)}, u32[]{:S(2)}, u32[]{:S(2)}) collective-permute-start(bf16[8,64,2048]{2,1,0:T(8,128)(2,1)S(1)} %get-tuple-element.151), channel_id=1, source_target_pairs={{0,96},{4,36},{8,104},{12,44},{16,112},{20,52},{24,120},{28,60},{3... | collective-permute-start | bytes 6291464 | tf_op jit(solution)/shard_map/ppermute | solution.py:67
  203.9 13.0 %collective-permute-start.23 = (bf16[16,64,640]{2,1,0:T(8,128)(2,1)S(1)}, bf16[16,64,640]{2,1,0:T(8,128)(2,1)S(1)}, u32[]{:S(2)}, u32[]{:S(2)}) collective-permute-start(bf16[16,64,640]{2,1,0:T(8,128)(2,1)S(1)} %shard_map.438), channel_id=1, source_target_pairs={{0,4},{4,0},{8,12},{12,8},{16,20},{20,16},{24,28},{28,24},{32,36},... | collective-permute-start | bytes 3932168 | tf_op jit(solution)/shard_map/ppermute | solution.py:91
  206.6 17.2 %collective-permute-start.20 = (bf16[256,2048]{1,0:T(8,128)(2,1)S(1)}, bf16[256,2048]{1,0:T(8,128)(2,1)S(1)}, u32[]{:S(2)}, u32[]{:S(2)}) collective-permute-start(bf16[256,2048]{1,0:T(8,128)(2,1)S(1)} %get-tuple-element.147), channel_id=1, source_target_pairs={{0,3},{1,2},{2,1},{3,0},{4,5},{5,4},{6,7},{7,6},{8,11},{9,10},{10,... | collective-permute-start | bytes 3145736 | tf_op jit(solution)/shard_map/ppermute | solution.py:57
  214.9 7.0 %collective-permute-start.22 = (bf16[16,64,512]{2,1,0:T(8,128)(2,1)S(1)}, bf16[16,64,512]{2,1,0:T(8,128)(2,1)S(1)}, u32[]{:S(2)}, u32[]{:S(2)}) collective-permute-start(bf16[16,64,512]{2,1,0:T(8,128)(2,1)S(1)} %shard_map.441), channel_id=1, source_target_pairs={{0,4},{4,0},{8,12},{12,8},{16,20},{20,16},{24,28},{28,24},{32,36},... | collective-permute-start | bytes 3145736 | tf_op jit(solution)/shard_map/ppermute | solution.py:91
  215.1 23.3 %collective-permute-start.27 = (bf16[4,64,2176]{2,1,0:T(8,128)(2,1)S(1)}, bf16[4,64,2176]{2,1,0:T(8,128)(2,1)}, u32[]{:S(2)}, u32[]{:S(2)}) collective-permute-start(bf16[4,64,2176]{2,1,0:T(8,128)(2,1)S(1)} %add_convert_fusion.1), channel_id=1, source_target_pairs={{0,8},{4,28},{8,0},{12,20},{16,24},{20,12},{24,16},{28,4},{32,40},... | collective-permute-start | bytes 3342344 | tf_op jit(solution)/shard_map/ppermute | solution.py:62
  219.2 19.0 %collective-permute-start.28 = (bf16[8,64,640]{2,1,0:T(8,128)(2,1)S(1)}, bf16[8,64,640]{2,1,0:T(8,128)(2,1)S(1)}, u32[]{:S(2)}, u32[]{:S(2)}) collective-permute-start(bf16[8,64,640]{2,1,0:T(8,128)(2,1)S(1)} %get-tuple-element.159), channel_id=1, source_target_pairs={{0,24},{4,12},{8,16},{12,4},{16,8},{20,28},{24,0},{28,20},{32,56},... | collective-permute-start | bytes 1966088 | tf_op jit(solution)/shard_map/ppermute | solution.py:62
  220.5 22.7 %collective-permute-start.31 = (bf16[4,64,2048]{2,1,0:T(8,128)(2,1)S(1)}, bf16[4,64,2048]{2,1,0:T(8,128)(2,1)S(1)}, u32[]{:S(2)}, u32[]{:S(2)}) collective-permute-start(bf16[4,64,2048]{2,1,0:T(8,128)(2,1)S(1)} %add_convert_fusion.3), channel_id=1, source_target_pairs={{0,32},{4,100},{8,40},{12,108},{16,48},{20,116},{24,56},{28,124},{... | collective-permute-start | bytes 3145736 | tf_op jit(solution)/shard_map/ppermute | solution.py:67
  224.0 18.5 %collective-permute-start.25 = (bf16[128,2048]{1,0:T(8,128)(2,1)S(1)}, bf16[128,2048]{1,0:T(8,128)(2,1)S(1)}, u32[]{:S(2)}, u32[]{:S(2)}) collective-permute-start(bf16[128,2048]{1,0:T(8,128)(2,1)S(1)} %add_convert_fusion.6), channel_id=1, source_target_pairs={{0,1},{1,0},{2,3},{3,2},{4,7},{5,6},{6,5},{7,4},{8,9},{9,8},{10,11... | collective-permute-start | bytes 1572872 | tf_op jit(solution)/shard_map/ppermute | solution.py:57
  224.1 18.1 %collective-permute-start.26 = (bf16[8,64,512]{2,1,0:T(8,128)(2,1)S(1)}, bf16[8,64,512]{2,1,0:T(8,128)(2,1)S(1)}, u32[]{:S(2)}, u32[]{:S(2)}) collective-permute-start(bf16[8,64,512]{2,1,0:T(8,128)(2,1)S(1)} %get-tuple-element.158), channel_id=1, source_target_pairs={{0,96},{4,36},{8,104},{12,44},{16,112},{20,52},{24,120},{28,60},{3... | collective-permute-start | bytes 1572872 | tf_op jit(solution)/shard_map/ppermute | solution.py:67
  238.3 7.2 %collective-permute-start.30 = (bf16[4,64,640]{2,1,0:T(8,128)(2,1)S(1)}, bf16[4,64,640]{2,1,0:T(8,128)(2,1)S(1)}, u32[]{:S(2)}, u32[]{:S(2)}) collective-permute-start(bf16[4,64,640]{2,1,0:T(8,128)(2,1)S(1)} %add_convert_fusion.8), channel_id=1, source_target_pairs={{0,8},{4,28},{8,0},{12,20},{16,24},{20,12},{24,16},{28,4},{32,40},... | collective-permute-start | bytes 983048 | tf_op jit(solution)/shard_map/ppermute | solution.py:62
  240.4 13.6 %collective-permute-start.33 = (bf16[2,64,2176]{2,1,0:T(8,128)(2,1)S(1)}, bf16[2,64,2176]{2,1,0:T(8,128)(2,1)S(1)}, u32[]{:S(2)}, u32[]{:S(2)}) collective-permute-start(bf16[2,64,2176]{2,1,0:T(8,128)(2,1)S(1)} %slice.264), channel_id=1, source_target_pairs={{0,96},{4,36},{8,104},{12,44},{16,112},{20,52},{24,120},{28,60},{3... | collective-permute-start | bytes 1671176 | tf_op jit(solution)/shard_map/ppermute | solution.py:67
  242.2 9.5 %collective-permute-start.34 = (bf16[4,64,512]{2,1,0:T(8,128)(2,1)S(1)}, bf16[4,64,512]{2,1,0:T(8,128)(2,1)S(1)}, u32[]{:S(2)}, u32[]{:S(2)}) collective-permute-start(bf16[4,64,512]{2,1,0:T(8,128)(2,1)S(1)} %add_convert_fusion.12), channel_id=1, source_target_pairs={{0,32},{4,100},{8,40},{12,108},{16,48},{20,116},{24,56},{28,124},{... | collective-permute-start | bytes 786440 | tf_op jit(solution)/shard_map/ppermute | solution.py:67
  242.5 21.2 %collective-permute-start.29 = (bf16[256,2048]{1,0:T(8,128)(2,1)S(1)}, bf16[256,2048]{1,0:T(8,128)(2,1)S(1)}, u32[]{:S(2)}, u32[]{:S(2)}) collective-permute-start(bf16[256,2048]{1,0:T(8,128)(2,1)S(1)} %slice.356), channel_id=1, source_target_pairs={{0,3},{1,2},{2,1},{3,0},{4,5},{5,4},{6,7},{7,6},{8,11},{9,10},{10,... | collective-permute-start | bytes 3145736 | tf_op jit(solution)/shard_map/ppermute | solution.py:57
  245.6 10.2 %collective-permute-start.32 = (bf16[2,64,640]{2,1,0:T(8,128)(2,1)S(1)}, bf16[2,64,640]{2,1,0:T(8,128)(2,1)S(1)}, u32[]{:S(2)}, u32[]{:S(2)}) collective-permute-start(bf16[2,64,640]{2,1,0:T(8,128)(2,1)S(1)} %slice.262), channel_id=1, source_target_pairs={{0,96},{4,36},{8,104},{12,44},{16,112},{20,52},{24,120},{28,60},{3... | collective-permute-start | bytes 491528 | tf_op jit(solution)/shard_map/ppermute | solution.py:67
  247.3 16.5 %collective-permute-start.38 = (bf16[2,64,2048]{2,1,0:T(8,128)(2,1)S(1)}, bf16[2,64,2048]{2,1,0:T(8,128)(2,1)S(1)}, u32[]{:S(2)}, u32[]{:S(2)}) collective-permute-start(bf16[2,64,2048]{2,1,0:T(8,128)(2,1)S(1)} %slice.274), channel_id=1, source_target_pairs={{0,24},{4,12},{8,16},{12,4},{16,8},{20,28},{24,0},{28,20},{32,56},... | collective-permute-start | bytes 1572872 | tf_op jit(solution)/shard_map/ppermute | solution.py:62
  255.8 6.0 %collective-permute-start.36 = (bf16[1,64,640]{2,1,0:T(8,128)(2,1)S(1)}, bf16[1,64,640]{2,1,0:T(8,128)(2,1)S(1)}, u32[]{:S(2)}, u32[]{:S(2)}) collective-permute-start(bf16[1,64,640]{2,1,0:T(8,128)(2,1)S(1)} %add_convert_fusion.13), channel_id=1, source_target_pairs={{0,32},{4,100},{8,40},{12,108},{16,48},{20,116},{24,56},{28,124},{... | collective-permute-start | bytes 245768 | tf_op jit(solution)/shard_map/ppermute | solution.py:67
  258.0 6.5 %collective-permute-start.37 = (bf16[1,64,2176]{2,1,0:T(8,128)(2,1)S(1)}, bf16[1,64,2176]{2,1,0:T(8,128)(2,1)S(1)}, u32[]{:S(2)}, u32[]{:S(2)}) collective-permute-start(bf16[1,64,2176]{2,1,0:T(8,128)(2,1)S(1)} %add_convert_fusion.9), channel_id=1, source_target_pairs={{0,32},{4,100},{8,40},{12,108},{16,48},{20,116},{24,56},{28,124},{... | collective-permute-start | bytes 835592 | tf_op jit(solution)/shard_map/ppermute | solution.py:67
  260.0 7.7 %collective-permute-start.43 = (bf16[2,64,512]{2,1,0:T(8,128)(2,1)S(1)}, bf16[2,64,512]{2,1,0:T(8,128)(2,1)S(1)}, u32[]{:S(2)}, u32[]{:S(2)}) collective-permute-start(bf16[2,64,512]{2,1,0:T(8,128)(2,1)S(1)} %slice.281), channel_id=1, source_target_pairs={{0,24},{4,12},{8,16},{12,4},{16,8},{20,28},{24,0},{28,20},{32,56},... | collective-permute-start | bytes 393224 | tf_op jit(solution)/shard_map/ppermute | solution.py:62
  263.9 6.5 %collective-permute-start.39 = (bf16[1,64,2048]{2,1,0:T(8,128)(2,1)S(1)}, bf16[1,64,2048]{2,1,0:T(8,128)(2,1)S(1)}, u32[]{:S(2)}, u32[]{:S(2)}) collective-permute-start(bf16[1,64,2048]{2,1,0:T(8,128)(2,1)S(1)} %add_convert_fusion.10), channel_id=1, source_target_pairs={{0,8},{4,28},{8,0},{12,20},{16,24},{20,12},{24,16},{28,4},{32,40},... | collective-permute-start | bytes 786440 | tf_op jit(solution)/shard_map/ppermute | solution.py:62
  264.7 14.3 %collective-permute-start.35 = (bf16[128,2048]{1,0:T(8,128)(2,1)S(1)}, bf16[128,2048]{1,0:T(8,128)(2,1)S(1)}, u32[]{:S(2)}, u32[]{:S(2)}) collective-permute-start(bf16[128,2048]{1,0:T(8,128)(2,1)S(1)} %fusion.4), channel_id=1, source_target_pairs={{0,1},{1,0},{2,3},{3,2},{4,7},{5,6},{6,5},{7,4},{8,9},{9,8},{10,11... | collective-permute-start | bytes 1572872 | tf_op jit(solution)/shard_map/ppermute | solution.py:57
  267.7 8.4 %collective-permute-start.44 = (bf16[1,64,512]{2,1,0:T(8,128)(2,1)S(1)}, bf16[1,64,512]{2,1,0:T(8,128)(2,1)S(1)}, u32[]{:S(2)}, u32[]{:S(2)}) collective-permute-start(bf16[1,64,512]{2,1,0:T(8,128)(2,1)S(1)} %add_convert_fusion.14), channel_id=1, source_target_pairs={{0,8},{4,28},{8,0},{12,20},{16,24},{20,12},{24,16},{28,4},{32,40},... | collective-permute-start | bytes 196616 | tf_op jit(solution)/shard_map/ppermute | solution.py:62
  272.6 5.2 %collective-permute-start.42 = (f32[2,64]{1,0:T(2,128)S(1)}, f32[2,64]{1,0:T(2,128)S(1)}, u32[]{:S(2)}, u32[]{:S(2)}) collective-permute-start(f32[2,64]{1,0:T(2,128)S(1)} %pad_maximum_fusion.9), channel_id=1, source_target_pairs={{0,2},{1,3},{2,0},{3,1},{4,6},{5,7},{6,4},{7,5},{8,10},{9,11},{10,... | collective-permute-start | bytes 1544 | tf_op jit(solution)/shard_map/ppermute | solution.py:71
  272.8 5.0 %collective-permute-start.41 = (f32[2,64]{1,0:T(2,128)S(1)}, f32[2,64]{1,0:T(2,128)S(1)}, u32[]{:S(2)}, u32[]{:S(2)}) collective-permute-start(f32[2,64]{1,0:T(2,128)S(1)} %pad_maximum_fusion.9), channel_id=1, source_target_pairs={{0,3},{1,0},{2,1},{3,2},{4,7},{5,4},{6,5},{7,6},{8,11},{9,8},{10,9... | collective-permute-start | bytes 1544 | tf_op jit(solution)/shard_map/ppermute | solution.py:71
  273.4 5.0 %collective-permute-start.40 = (f32[2,64]{1,0:T(2,128)S(1)}, f32[2,64]{1,0:T(2,128)S(1)}, u32[]{:S(2)}, u32[]{:S(2)}) collective-permute-start(f32[2,64]{1,0:T(2,128)S(1)} %pad_maximum_fusion.9), channel_id=1, source_target_pairs={{0,1},{1,2},{2,3},{3,0},{4,5},{5,6},{6,7},{7,4},{8,9},{9,10},{10,1... | collective-permute-start | bytes 1544 | tf_op jit(solution)/shard_map/ppermute | solution.py:71
  (49 other events, 274.0 us)
Sparse Core Ops, SparseCore 0:
  10.9 83.2 all-gather.1

commit v5 on v4

--- a/solution.py
+++ b/solution.py
@@ -344,7 +344,7 @@
         grid_spec=pltpu.PrefetchScalarGridSpec(
             num_scalar_prefetch=1, grid=(SIDE,), in_specs=specs, out_specs=out_specs
         ),
-        compiler_params=pltpu.CompilerParams(vmem_limit_bytes=32 * 2**20),
+        compiler_params=pltpu.CompilerParams(vmem_limit_bytes=24 * 2**20),
         cost_estimate=cost(us),
     )(here(), *arrays)
 
@@ -475,7 +475,7 @@
         hidden_kernel,
         out_shape=[jax.ShapeDtypeStruct((SEQ, HIDDEN), BF16)] * 3,
         grid=(steps,),
-        in_specs=[pl.BlockSpec((SEQ // 2, D), lambda j: (0, 0))] * 2
+        in_specs=whole(2)
         + [weight(0), weight(1), pl.BlockSpec((SEQ, 128), lambda j: (0, j))],
         out_specs=[pl.BlockSpec((SEQ, 128), lambda j: (0, j))] * 3,
         scratch_shapes=[pltpu.VMEM((SEQ, D), BF16)],

time: 293 us -> 290 us (0.990)
    ppermute x5, waiting for transfers between devices: 5.03 us -> 0.22 us  [swap_core(): return lax.ppermute(a, 'dp', [(i, i ^ 1) for i in range(2 * SIDE * SIDE)])]
    ppermute x15, waiting for transfers between devices: 37.9 us -> 41.8 us  [pair_z(): return lax.ppermute(a, ('dp', 'mp'), pairs)]
    unnamed x104 -> x108, local copies, waits for them, and re-layouts: 10.8 us -> 11.3 us
  transfers between devices with their start and end apart: 46 -> 46, of which waited for: 23 -> 24; matrix products, arithmetic and copies ran while one was open for 14% -> 13% of each run, Pallas kernels for 18% -> 18%
where the time goes in v5:
time: 290 us; the launch traced here: 284 us
  waiting for transfers between devices  90.7 us (31%)
  Pallas kernels  74.4 us (26%)
  starting transfers between devices  55.9 us (19%)
  matrix products  19.1 us (7%)
  other arithmetic  15.4 us (5%)
  between operations  15.4 us (5%)
  local copies, waits for them, and re-layouts  13 us (4%)
    ppermute x15, waiting for transfers between devices, pair_z(): return lax.ppermute(a, ('dp', 'mp'), pairs)  41.8 us
    ppermute x15, starting transfers between devices, pair_z(): return lax.ppermute(a, ('dp', 'mp'), pairs)  25.3 us
    pallas_call x8, Pallas kernels, weight_products(): pl.pallas_call(kernel, out_shape=outs, grid_spec=pltpu.PrefetchScalarGrid...  24.5 us
    ppermute x8, waiting for transfers between devices, pair_x(): return lax.ppermute(a, 'dp', pairs)  22.4 us
    ppermute x3, waiting for transfers between devices, shift_second(): return lax.ppermute(a, 'dp', pairs)  15.4 us
    pallas_call x1, Pallas kernels, hidden_units(): pl.pallas_call(hidden_kernel, out_shape=[jax.ShapeDtypeStruct((SEQ, HIDDE...  12.9 us
    unnamed x108, local copies, waits for them, and re-layouts  11.3 us
    dot_general x5, matrix products, nn(): lax.dot_general(a, b, (((1,), (0,)), ((), ())), preferred_element_type=F32)  9.94 us
  transfers between devices with their start and end apart: 46, of which 24 were waited for; matrix products, arithmetic and copies ran while one was open for 13% of the time, Pallas kernels for 18%

profile of v5, /device:TPU:0, one launch (start us, length us, event | category | flops | bytes accessed | tf_op | source)
XLA Modules:
  0.0 283.9 jit_solution(12928706578713815806)
XLA Ops:
  7.3 2.5 shard_map.422
  9.8 3.2 %collective-permute-start.3 = (bf16[64,1152]{1,0:T(8,128)(2,1)}, bf16[64,1152]{1,0:T(8,128)(2,1)S(1)}, u32[]{:S(2)}, u32[]{:S(2)}) collective-permute-start(bf16[64,1152]{1,0:T(8,128)(2,1)} %get-tuple-element.101._), channel_id=1, source_target_pairs={{0,16},{4,68},{8,24},{12,76},{16,0},{20,84},{24,8},{28,92},{32,48}... | collective-permute-start | bytes 442376 | tf_op jit(solution)/shard_map/ppermute | solution.py:79
  16.5 2.0 collective-permute-start
  21.5 3.3 %collective-permute-start.6 = (bf16[4,64,1152]{2,1,0:T(8,128)(2,1)S(1)}, bf16[4,64,1152]{2,1,0:T(8,128)(2,1)S(1)}, u32[]{:S(2)}, u32[]{:S(2)}) collective-permute-start(bf16[4,64,1152]{2,1,0:T(8,128)(2,1)S(1)} %pad_maximum_fusion.4), channel_id=1, source_target_pairs={{0,64},{4,20},{8,72},{12,28},{16,80},{20,4},{24,88},{28,12},{32,96... | collective-permute-start | bytes 1769480 | tf_op jit(solution)/shard_map/ppermute | solution.py:87
  28.0 3.4 %collective-permute-start.7 = (bf16[256,2048]{1,0:T(8,128)(2,1)S(1)}, bf16[256,2048]{1,0:T(8,128)(2,1)S(1)}, u32[]{:S(2)}, u32[]{:S(2)}) collective-permute-start(bf16[256,2048]{1,0:T(8,128)(2,1)S(1)} %pad_maximum_fusion.2.normed_ref.near_ref), channel_id=1, source_target_pairs={{0,3},{1,2},{2,1},{3,0},{4,5},{5,4},{6,7},{7,6},{8,11},{9,10},{10,... | collective-permute-start | bytes 3145736 | tf_op jit(solution)/shard_map/ppermute | solution.py:57
  32.6 5.3 %collective-permute-done.6 = bf16[4,64,1152]{2,1,0:T(8,128)(2,1)S(1)} collective-permute-done((bf16[4,64,1152]{2,1,0:T(8,128)(2,1)S(1)}, bf16[4,64,1152]{2,1,0:T(8,128)(2,1)S(1)}, u32[]{:S(2)}, u32[]{:S(2)}) %collective-permute-start.6) | collective-permute-done | bytes 589856 | tf_op jit(solution)/shard_map/ppermute | solution.py:87
  37.9 9.9 %collective-permute-done.5 = bf16[4,64,1152]{2,1,0:T(8,128)(2,1)S(1)} collective-permute-done((bf16[4,64,1152]{2,1,0:T(8,128)(2,1)S(1)}, bf16[4,64,1152]{2,1,0:T(8,128)(2,1)S(1)}, u32[]{:S(2)}, u32[]{:S(2)}) %collective-permute-start.5) | collective-permute-done | bytes 589856 | tf_op jit(solution)/shard_map/ppermute | solution.py:87
  52.3 2.9 %collective-permute-start.11 = (bf16[256,2048]{1,0:T(8,128)(2,1)}, bf16[256,2048]{1,0:T(8,128)(2,1)S(1)}, u32[]{:S(2)}, u32[]{:S(2)}) collective-permute-start(bf16[256,2048]{1,0:T(8,128)(2,1)} %copy-done.6), channel_id=1, source_target_pairs={{0,3},{1,2},{2,1},{3,0},{4,5},{5,4},{6,7},{7,6},{8,11},{9,10},{10,... | collective-permute-start | bytes 3145736 | tf_op jit(solution)/shard_map/ppermute | solution.py:57
  55.5 2.4 shard_map.424
  63.4 4.3 %shard_map.425 = (bf16[512,512]{1,0:T(8,128)(2,1)S(1)}, bf16[512,512]{1,0:T(8,128)(2,1)S(1)}, bf16[512,128]{1,0:T(8,128)(2,1)S(1)}, f32[8,512]{1,0:T(8,128)S(1)}) custom-call(s32[4]{0:T(128)S(1)} %select_reduce_fusion.1.slot_ref, s32[4]{0:T(128)S(1)} %bitcast.106, f32[512,640]{1,0:T(8,128)S(1)} %pad_maximum_fusion.1.qkv_ref, f32[512,128]{1,0:T(8,128)S(1)} %copy-done.15, ...), custom_call_target="tpu_custom_call" | custom-call | flops 5500000256 | bytes 15000000 | tf_op jit(solution)/shard_map/pallas_call | solution.py:607
  69.5 2.8 collective-permute-start.12
  73.7 11.9 %collective-permute-done.12 = bf16[256,2048]{1,0:T(8,128)(2,1)S(1)} collective-permute-done((bf16[256,2048]{1,0:T(8,128)(2,1)S(1)}, bf16[256,2048]{1,0:T(8,128)(2,1)S(1)}, u32[]{:S(2)}, u32[]{:S(2)}) %collective-permute-start.12) | collective-permute-done | bytes 1048608 | tf_op jit(solution)/shard_map/ppermute | solution.py:57
  87.1 13.7 %collective-permute-done.13.got_ref = bf16[256,2048]{1,0:T(8,128)(2,1)S(1)} collective-permute-done((bf16[256,2048]{1,0:T(8,128)(2,1)S(1)}, bf16[256,2048]{1,0:T(8,128)(2,1)S(1)}, u32[]{:S(2)}, u32[]{:S(2)}) %collective-permute-start.13) | collective-permute-done | bytes 1048608 | tf_op jit(solution)/shard_map/ppermute | solution.py:57
  100.8 2.3 shard_map.427
  104.9 3.1 %collective-permute-start.14 = (bf16[256,2048]{1,0:T(8,128)(2,1)}, bf16[256,2048]{1,0:T(8,128)(2,1)}, u32[]{:S(2)}, u32[]{:S(2)}) collective-permute-start(bf16[256,2048]{1,0:T(8,128)(2,1)} %get-tuple-element.128.near_ref), channel_id=1, source_target_pairs={{0,3},{1,2},{2,1},{3,0},{4,5},{5,4},{6,7},{7,6},{8,11},{9,10},{10,... | collective-permute-start | bytes 3145736 | tf_op jit(solution)/shard_map/ppermute | solution.py:57
  110.0 6.5 %fusion.2.grad_hidden_ref = f32[512,1408]{1,0:T(8,128)S(1)} fusion(bf16[512,2048]{1,0:T(8,128)(2,1)} %constant_dynamic-update-slice_fusion.2, bf16[2048,4224]{1,0:T(8,128)(2,1)} %all-gather.2.cloned.1.call-done.gate_w_ref.up_w_ref), kind=kOutput, calls=%fused_computation.2 | convolution fusion | flops 2952790016 | bytes 10747904 | tf_op jit(solution)/shard_map/dot_general | solution.py:174
  116.6 5.0 %collective-permute-done.14.far_ref = bf16[256,2048]{1,0:T(8,128)(2,1)} collective-permute-done((bf16[256,2048]{1,0:T(8,128)(2,1)}, bf16[256,2048]{1,0:T(8,128)(2,1)}, u32[]{:S(2)}, u32[]{:S(2)}) %collective-permute-start.14) | collective-permute-done | bytes 1048608 | tf_op jit(solution)/shard_map/ppermute | solution.py:57
  121.6 12.9 %shard_map.429 = (bf16[512,1408]{1,0:T(8,128)(2,1)S(1)}, bf16[512,1408]{1,0:T(8,128)(2,1)S(1)}, bf16[512,1408]{1,0:T(8,128)(2,1)S(1)}) custom-call(bf16[256,2048]{1,0:T(8,128)(2,1)} %get-tuple-element.128.near_ref, bf16[256,2048]{1,0:T(8,128)(2,1)} %collective-permute-done.14.far_ref, bf16[2048,4224]{1,0:T(8,128)(2,1)S(1)} %copy-done.19, ...), custom_call_target="tpu_custom_call" | custom-call | flops 11000000512 | bytes 30000000 | tf_op jit(solution)/shard_map/pallas_call | solution.py:474
  134.5 9.3 %shard_map.430 = (f32[256,2048]{1,0:T(8,128)S(1)}, bf16[256,2048]{1,0:T(8,128)(2,1)S(1)}) custom-call(bf16[512,1408]{1,0:T(8,128)(2,1)S(1)} %get-tuple-element.124.gate_ref.refs_1_, bf16[512,1408]{1,0:T(8,128)(2,1)S(1)} %get-tuple-element.125.up_ref.refs_1_, bf16[2048,4224]{1,0:T(8,128)(2,1)} %all-gather.2.cloned.1.call-done.gate_w_ref.up_w_ref, ...), custom_call_target="tpu_custom_call" | custom-call | flops 11000000512 | bytes 30000000 | tf_op jit(solution)/shard_map/pallas_call | solution.py:222
  143.8 2.8 collective-permute-start.15
  146.6 2.1 shard_map.431.refs_0_
  148.7 3.7 %shard_map.432 = bf16[16,64,2176]{2,1,0:T(8,128)(2,1)S(1)} custom-call(s32[3]{0:T(128)S(1)} %pad_add_fusion.here_ref, bf16[2048,512]{1,0:T(8,128)(2,1)S(1)} %shard_map.431.refs_0_, bf16[512,1408]{1,0:T(8,128)(2,1)S(1)} %get-tuple-element.124.gate_ref.refs_1_, bf16[2048,512]{1,0:T(8,128)(2,1)S(1)} %shard_map.426.refs_2_, ...), custom_call_target="tpu_custom_call" | custom-call | flops 4400000000 | bytes 12000000 | tf_op jit(solution)/shard_map/pallas_call | solution.py:341
  152.5 3.7 %shard_map.433 = bf16[16,64,2048]{2,1,0:T(8,128)(2,1)S(1)} custom-call(s32[3]{0:T(128)S(1)} %pad_add_fusion.here_ref, bf16[2048,512]{1,0:T(8,128)(2,1)S(1)} %shard_map.431.refs_0_, bf16[512,1408]{1,0:T(8,128)(2,1)S(1)} %get-tuple-element.125.up_ref.refs_1_, bf16[2048,512]{1,0:T(8,128)(2,1)S(1)} %shard_map.426.refs_2_, ...), custom_call_target="tpu_custom_call" | custom-call | flops 4400000000 | bytes 12000000 | tf_op jit(solution)/shard_map/pallas_call | solution.py:341
  156.2 3.7 %collective-permute-done.15 = bf16[256,2048]{1,0:T(8,128)(2,1)S(1)} collective-permute-done((bf16[256,2048]{1,0:T(8,128)(2,1)S(1)}, bf16[256,2048]{1,0:T(8,128)(2,1)S(1)}, u32[]{:S(2)}, u32[]{:S(2)}) %collective-permute-start.15) | collective-permute-done | bytes 1048608 | tf_op jit(solution)/shard_map/ppermute | solution.py:57
  160.8 7.7 %fusion = f32[512,2048]{1,0:T(8,128)} fusion(bf16[512,1408]{1,0:T(8,128)(2,1)S(1)} %get-tuple-element.130.refs_3_, bf16[2048,4224]{1,0:T(8,128)(2,1)} %all-gather.2.cloned.1.call-done.gate_w_ref.up_w_ref), kind=kOutput, calls=%fused_computation | convolution fusion | flops 2952790016 | bytes 11403264 | tf_op jit(solution)/shard_map/dot_general | solution.py:166
  168.4 4.5 %shard_map.434 = (bf16[8,64,2176]{2,1,0:T(8,128)(2,1)S(1)}, bf16[8,64,2176]{2,1,0:T(8,128)(2,1)S(1)}) custom-call(s32[3]{0:T(128)S(1)} %pad_add_fusion.here_ref, bf16[2048,512]{1,0:T(8,128)(2,1)S(1)} %shard_map.431.refs_0_, bf16[512,1408]{1,0:T(8,128)(2,1)S(1)} %get-tuple-element.124.gate_ref.refs_1_, bf16[2048,512]{1,0:T(8,128)(2,1)S(1)} %shard_map.426.refs_2_, ...), custom_call_target="tpu_custom_call" | custom-call | flops 4400000000 | bytes 12000000 | tf_op jit(solution)/shard_map/pallas_call | solution.py:341
  172.9 2.6 collective-permute-done.16.got_ref
  177.2 2.8 collective-permute-start.19
  180.0 2.3 collective-permute-start.21
  182.4 4.4 %shard_map.436 = (bf16[8,64,2048]{2,1,0:T(8,128)(2,1)S(1)}, bf16[8,64,2048]{2,1,0:T(8,128)(2,1)S(1)}) custom-call(s32[3]{0:T(128)S(1)} %pad_add_fusion.here_ref, bf16[2048,512]{1,0:T(8,128)(2,1)S(1)} %shard_map.431.refs_0_, bf16[512,1408]{1,0:T(8,128)(2,1)S(1)} %get-tuple-element.125.up_ref.refs_1_, bf16[2048,512]{1,0:T(8,128)(2,1)S(1)} %shard_map.426.refs_2_, ...), custom_call_target="tpu_custom_call" | custom-call | flops 1100000 | bytes 3000 | tf_op jit(solution)/shard_map/pallas_call | solution.py:341
  186.8 2.0 collective-permute-start.24
  189.6 3.7 %collective-permute-done.19.far_ref = bf16[256,2048]{1,0:T(8,128)(2,1)S(1)} collective-permute-done((bf16[256,2048]{1,0:T(8,128)(2,1)S(1)}, bf16[256,2048]{1,0:T(8,128)(2,1)S(1)}, u32[]{:S(2)}, u32[]{:S(2)}) %collective-permute-start.19) | collective-permute-done | bytes 1048608 | tf_op jit(solution)/shard_map/ppermute | solution.py:57
  194.1 5.6 %shard_map.437.refs_1_.a_ref = bf16[512,640]{1,0:T(8,128)(2,1)S(1)} custom-call(s32[4]{0:T(128)S(1)} %select_reduce_fusion.1.slot_ref, s32[4]{0:T(128)S(1)} %bitcast.107, bf16[512,512]{1,0:T(8,128)(2,1)S(1)} %copy-done.28, bf16[512,128]{1,0:T(8,128)(2,1)S(1)} %get-tuple-element.132.kv_ref, f32[8,512]{1,0:T(8,128)S(1)} %get-tuple-element.133.lse_ref, ...), custom_call_target="tpu_custom_call" | custom-call | flops 6600000000 | bytes 18000000 | tf_op jit(solution)/shard_map/pallas_call | solution.py:625
  199.7 2.1 shard_map.438
  201.8 2.6 shard_map.439
  204.5 2.8 collective-permute-start.20
  212.1 2.2 collective-permute-done.24
  214.7 2.3 shard_map.442
  218.8 2.0 shard_map.443
  222.6 12.7 %collective-permute-done.28 = bf16[8,64,640]{2,1,0:T(8,128)(2,1)S(1)} collective-permute-done((bf16[8,64,640]{2,1,0:T(8,128)(2,1)S(1)}, bf16[8,64,640]{2,1,0:T(8,128)(2,1)S(1)}, u32[]{:S(2)}, u32[]{:S(2)}) %collective-permute-start.28) | collective-permute-done | bytes 655392 | tf_op jit(solution)/shard_map/ppermute | solution.py:62
  239.8 2.8 collective-permute-done.30
  247.1 2.3 collective-permute-done.33
  251.4 2.0 shard_map.444
  253.4 2.0 collective-permute-start.37
  255.4 1.9 collective-permute-start.43
  260.2 2.6 collective-permute-done.43
  262.9 2.9 %collective-permute-done.39 = bf16[1,64,2048]{2,1,0:T(8,128)(2,1)S(1)} collective-permute-done((bf16[1,64,2048]{2,1,0:T(8,128)(2,1)S(1)}, bf16[1,64,2048]{2,1,0:T(8,128)(2,1)S(1)}, u32[]{:S(2)}, u32[]{:S(2)}) %collective-permute-start.39) | collective-permute-done | bytes 262176 | tf_op jit(solution)/shard_map/ppermute | solution.py:62
  268.2 2.0 collective-permute-start.41
  (246 shorter events, 64.7 us)
Async XLA Ops:
  7.2 102.8 %all-gather.2.cloned.1.call-start = ((), (), s32[]{:S(2)}) async-start(), calls=%async_computation | async-start | bytes 17842176 | tf_op jit(solution)/shard_map/all_gather | solution.py:687
  9.8 11.6 %collective-permute-start.3 = (bf16[64,1152]{1,0:T(8,128)(2,1)}, bf16[64,1152]{1,0:T(8,128)(2,1)S(1)}, u32[]{:S(2)}, u32[]{:S(2)}) collective-permute-start(bf16[64,1152]{1,0:T(8,128)(2,1)} %get-tuple-element.101._), channel_id=1, source_target_pairs={{0,16},{4,68},{8,24},{12,76},{16,0},{20,84},{24,8},{28,92},{32,48}... | collective-permute-start | bytes 442376 | tf_op jit(solution)/shard_map/ppermute | solution.py:79
  13.0 8.4 %collective-permute-start.2 = (bf16[64,1152]{1,0:T(8,128)(2,1)}, bf16[64,1152]{1,0:T(8,128)(2,1)S(1)}, u32[]{:S(2)}, u32[]{:S(2)}) collective-permute-start(bf16[64,1152]{1,0:T(8,128)(2,1)} %get-tuple-element.101._), channel_id=1, source_target_pairs={{0,24},{4,100},{8,0},{12,108},{16,8},{20,116},{24,16},{28,124},{32... | collective-permute-start | bytes 442376 | tf_op jit(solution)/shard_map/ppermute | solution.py:79
  14.2 7.2 %collective-permute-start.1 = (bf16[64,1152]{1,0:T(8,128)(2,1)}, bf16[64,1152]{1,0:T(8,128)(2,1)S(1)}, u32[]{:S(2)}, u32[]{:S(2)}) collective-permute-start(bf16[64,1152]{1,0:T(8,128)(2,1)} %get-tuple-element.101._), channel_id=1, source_target_pairs={{0,8},{4,36},{8,16},{12,44},{16,24},{20,52},{24,0},{28,60},{32,40}... | collective-permute-start | bytes 442376 | tf_op jit(solution)/shard_map/ppermute | solution.py:79
  16.5 10.3 %collective-permute-start = (bf16[128,2048]{1,0:T(8,128)(2,1)S(1)}, bf16[128,2048]{1,0:T(8,128)(2,1)}, u32[]{:S(2)}, u32[]{:S(2)}) collective-permute-start(bf16[128,2048]{1,0:T(8,128)(2,1)S(1)} %get-tuple-element.102), channel_id=1, source_target_pairs={{0,1},{1,0},{2,3},{3,2},{4,7},{5,6},{6,5},{7,4},{8,9},{9,8},{10,11... | collective-permute-start | bytes 1572872 | tf_op jit(solution)/shard_map/ppermute | solution.py:57
  21.5 16.4 %collective-permute-start.6 = (bf16[4,64,1152]{2,1,0:T(8,128)(2,1)S(1)}, bf16[4,64,1152]{2,1,0:T(8,128)(2,1)S(1)}, u32[]{:S(2)}, u32[]{:S(2)}) collective-permute-start(bf16[4,64,1152]{2,1,0:T(8,128)(2,1)S(1)} %pad_maximum_fusion.4), channel_id=1, source_target_pairs={{0,64},{4,20},{8,72},{12,28},{16,80},{20,4},{24,88},{28,12},{32,96... | collective-permute-start | bytes 1769480 | tf_op jit(solution)/shard_map/ppermute | solution.py:87
  24.8 23.1 %collective-permute-start.5 = (bf16[4,64,1152]{2,1,0:T(8,128)(2,1)S(1)}, bf16[4,64,1152]{2,1,0:T(8,128)(2,1)S(1)}, u32[]{:S(2)}, u32[]{:S(2)}) collective-permute-start(bf16[4,64,1152]{2,1,0:T(8,128)(2,1)S(1)} %pad_maximum_fusion.4), channel_id=1, source_target_pairs={{0,96},{4,28},{8,104},{12,4},{16,112},{20,12},{24,120},{28,20},{32... | collective-permute-start | bytes 1769480 | tf_op jit(solution)/shard_map/ppermute | solution.py:87
  25.8 22.1 %collective-permute-start.4 = (bf16[4,64,1152]{2,1,0:T(8,128)(2,1)S(1)}, bf16[4,64,1152]{2,1,0:T(8,128)(2,1)S(1)}, u32[]{:S(2)}, u32[]{:S(2)}) collective-permute-start(bf16[4,64,1152]{2,1,0:T(8,128)(2,1)S(1)} %pad_maximum_fusion.4), channel_id=1, source_target_pairs={{0,32},{4,12},{8,40},{12,20},{16,48},{20,28},{24,56},{28,4},{32,64... | collective-permute-start | bytes 1769480 | tf_op jit(solution)/shard_map/ppermute | solution.py:87
  27.9 29.9 %copy-start.4 = (bf16[256,2048]{1,0:T(8,128)(2,1)}, bf16[256,2048]{1,0:T(8,128)(2,1)S(1)}, u32[]{:S(2)}) copy-start(bf16[256,2048]{1,0:T(8,128)(2,1)S(1)} %pad_maximum_fusion.2.normed_ref.near_ref) | copy-start | bytes 3145732
  28.0 21.5 %collective-permute-start.7 = (bf16[256,2048]{1,0:T(8,128)(2,1)S(1)}, bf16[256,2048]{1,0:T(8,128)(2,1)S(1)}, u32[]{:S(2)}, u32[]{:S(2)}) collective-permute-start(bf16[256,2048]{1,0:T(8,128)(2,1)S(1)} %pad_maximum_fusion.2.normed_ref.near_ref), channel_id=1, source_target_pairs={{0,3},{1,2},{2,1},{3,0},{4,5},{5,4},{6,7},{7,6},{8,11},{9,10},{10,... | collective-permute-start | bytes 3145736 | tf_op jit(solution)/shard_map/ppermute | solution.py:57
  31.5 17.1 %collective-permute-start.8 = (bf16[128,2048]{1,0:T(8,128)(2,1)S(1)}, bf16[128,2048]{1,0:T(8,128)(2,1)S(1)}, u32[]{:S(2)}, u32[]{:S(2)}) collective-permute-start(bf16[128,2048]{1,0:T(8,128)(2,1)S(1)} %bitcast_convert_fusion), channel_id=1, source_target_pairs={{0,1},{1,0},{2,3},{3,2},{4,7},{5,6},{6,5},{7,4},{8,9},{9,8},{10,11... | collective-permute-start | bytes 1572872 | tf_op jit(solution)/shard_map/ppermute | solution.py:57
  50.8 4.7 %collective-permute-start.9 = (bf16[16,64,1152]{2,1,0:T(8,128)(2,1)S(1)}, bf16[16,64,1152]{2,1,0:T(8,128)(2,1)}, u32[]{:S(2)}, u32[]{:S(2)}) collective-permute-start(bf16[16,64,1152]{2,1,0:T(8,128)(2,1)S(1)} %bitcast.96), channel_id=1, source_target_pairs={{0,4},{4,0},{8,12},{12,8},{16,20},{20,16},{24,28},{28,24},{32,36},... | collective-permute-start | bytes 7077896 | tf_op jit(solution)/shard_map/ppermute | solution.py:91
  51.0 11.5 %collective-permute-start.10 = (f32[128,128]{1,0:T(8,128)S(1)}, f32[128,128]{1,0:T(8,128)S(1)}, u32[]{:S(2)}, u32[]{:S(2)}) collective-permute-start(f32[128,128]{1,0:T(8,128)S(1)} %get-tuple-element.108), channel_id=1, source_target_pairs={{0,1},{1,0},{2,3},{3,2},{4,7},{5,6},{6,5},{7,4},{8,9},{9,8},{10,11... | collective-permute-start | bytes 196616 | tf_op jit(solution)/shard_map/ppermute | solution.py:57
  52.3 16.4 %collective-permute-start.11 = (bf16[256,2048]{1,0:T(8,128)(2,1)}, bf16[256,2048]{1,0:T(8,128)(2,1)S(1)}, u32[]{:S(2)}, u32[]{:S(2)}) collective-permute-start(bf16[256,2048]{1,0:T(8,128)(2,1)} %copy-done.6), channel_id=1, source_target_pairs={{0,3},{1,2},{2,1},{3,0},{4,5},{5,4},{6,7},{7,6},{8,11},{9,10},{10,... | collective-permute-start | bytes 3145736 | tf_op jit(solution)/shard_map/ppermute | solution.py:57
  69.5 16.1 %collective-permute-start.12 = (bf16[256,2048]{1,0:T(8,128)(2,1)S(1)}, bf16[256,2048]{1,0:T(8,128)(2,1)S(1)}, u32[]{:S(2)}, u32[]{:S(2)}) collective-permute-start(bf16[256,2048]{1,0:T(8,128)(2,1)S(1)} %convolution_convert_fusion), channel_id=1, source_target_pairs={{0,3},{1,2},{2,1},{3,0},{4,5},{5,4},{6,7},{7,6},{8,11},{9,10},{10,... | collective-permute-start | bytes 3145736 | tf_op jit(solution)/shard_map/ppermute | solution.py:57
  85.9 14.9 %copy-start.5 = (bf16[256,2048]{1,0:T(8,128)(2,1)S(1)}, bf16[256,2048]{1,0:T(8,128)(2,1)}, u32[]{:S(2)}) copy-start(bf16[256,2048]{1,0:T(8,128)(2,1)} %copy-done.4) | copy-start | bytes 3145732
  86.0 14.9 %collective-permute-start.13 = (bf16[256,2048]{1,0:T(8,128)(2,1)S(1)}, bf16[256,2048]{1,0:T(8,128)(2,1)S(1)}, u32[]{:S(2)}, u32[]{:S(2)}) collective-permute-start(bf16[256,2048]{1,0:T(8,128)(2,1)S(1)} %add_convert_fusion.5.sum_ref), channel_id=1, source_target_pairs={{0,1},{1,0},{2,3},{3,2},{4,7},{5,6},{6,5},{7,4},{8,9},{9,8},{10,11... | collective-permute-start | bytes 3145736 | tf_op jit(solution)/shard_map/ppermute | solution.py:57
  104.9 16.7 %collective-permute-start.14 = (bf16[256,2048]{1,0:T(8,128)(2,1)}, bf16[256,2048]{1,0:T(8,128)(2,1)}, u32[]{:S(2)}, u32[]{:S(2)}) collective-permute-start(bf16[256,2048]{1,0:T(8,128)(2,1)} %get-tuple-element.128.near_ref), channel_id=1, source_target_pairs={{0,3},{1,2},{2,1},{3,0},{4,5},{5,4},{6,7},{7,6},{8,11},{9,10},{10,... | collective-permute-start | bytes 3145736 | tf_op jit(solution)/shard_map/ppermute | solution.py:57
  143.8 16.1 %collective-permute-start.15 = (bf16[256,2048]{1,0:T(8,128)(2,1)S(1)}, bf16[256,2048]{1,0:T(8,128)(2,1)S(1)}, u32[]{:S(2)}, u32[]{:S(2)}) collective-permute-start(bf16[256,2048]{1,0:T(8,128)(2,1)S(1)} %get-tuple-element.127), channel_id=1, source_target_pairs={{0,3},{1,2},{2,1},{3,0},{4,5},{5,4},{6,7},{7,6},{8,11},{9,10},{10,... | collective-permute-start | bytes 3145736 | tf_op jit(solution)/shard_map/ppermute | solution.py:57
  160.2 8.3 %collective-permute-start.17 = (bf16[16,64,2176]{2,1,0:T(8,128)(2,1)S(1)}, bf16[16,64,2176]{2,1,0:T(8,128)(2,1)S(1)}, u32[]{:S(2)}, u32[]{:S(2)}) collective-permute-start(bf16[16,64,2176]{2,1,0:T(8,128)(2,1)S(1)} %shard_map.432), channel_id=1, source_target_pairs={{0,4},{4,0},{8,12},{12,8},{16,20},{20,16},{24,28},{28,24},{32,36},... | collective-permute-start | bytes 13369352 | tf_op jit(solution)/shard_map/ppermute | solution.py:91
  160.3 22.1 %collective-permute-start.18 = (bf16[16,64,2048]{2,1,0:T(8,128)(2,1)S(1)}, bf16[16,64,2048]{2,1,0:T(8,128)(2,1)S(1)}, u32[]{:S(2)}, u32[]{:S(2)}) collective-permute-start(bf16[16,64,2048]{2,1,0:T(8,128)(2,1)S(1)} %shard_map.433), channel_id=1, source_target_pairs={{0,4},{4,0},{8,12},{12,8},{16,20},{20,16},{24,28},{28,24},{32,36},... | collective-permute-start | bytes 12582920 | tf_op jit(solution)/shard_map/ppermute | solution.py:91
  160.8 14.8 %collective-permute-start.16 = (bf16[256,2048]{1,0:T(8,128)(2,1)S(1)}, bf16[256,2048]{1,0:T(8,128)(2,1)S(1)}, u32[]{:S(2)}, u32[]{:S(2)}) collective-permute-start(bf16[256,2048]{1,0:T(8,128)(2,1)S(1)} %add_convert_fusion.4.sum_ref), channel_id=1, source_target_pairs={{0,1},{1,0},{2,3},{3,2},{4,7},{5,6},{6,5},{7,4},{8,9},{9,8},{10,11... | collective-permute-start | bytes 3145736 | tf_op jit(solution)/shard_map/ppermute | solution.py:57
  177.2 16.1 %collective-permute-start.19 = (bf16[256,2048]{1,0:T(8,128)(2,1)S(1)}, bf16[256,2048]{1,0:T(8,128)(2,1)S(1)}, u32[]{:S(2)}, u32[]{:S(2)}) collective-permute-start(bf16[256,2048]{1,0:T(8,128)(2,1)S(1)} %get-tuple-element.150.near_ref), channel_id=1, source_target_pairs={{0,3},{1,2},{2,1},{3,0},{4,5},{5,4},{6,7},{7,6},{8,11},{9,10},{10,... | collective-permute-start | bytes 3145736 | tf_op jit(solution)/shard_map/ppermute | solution.py:57
  180.0 28.6 %collective-permute-start.21 = (bf16[8,64,2176]{2,1,0:T(8,128)(2,1)S(1)}, bf16[8,64,2176]{2,1,0:T(8,128)(2,1)S(1)}, u32[]{:S(2)}, u32[]{:S(2)}) collective-permute-start(bf16[8,64,2176]{2,1,0:T(8,128)(2,1)S(1)} %get-tuple-element.148), channel_id=1, source_target_pairs={{0,24},{4,12},{8,16},{12,4},{16,8},{20,28},{24,0},{28,20},{32,56},... | collective-permute-start | bytes 6684680 | tf_op jit(solution)/shard_map/ppermute | solution.py:62
  186.8 27.5 %collective-permute-start.24 = (bf16[8,64,2048]{2,1,0:T(8,128)(2,1)S(1)}, bf16[8,64,2048]{2,1,0:T(8,128)(2,1)S(1)}, u32[]{:S(2)}, u32[]{:S(2)}) collective-permute-start(bf16[8,64,2048]{2,1,0:T(8,128)(2,1)S(1)} %get-tuple-element.151), channel_id=1, source_target_pairs={{0,96},{4,36},{8,104},{12,44},{16,112},{20,52},{24,120},{28,60},{3... | collective-permute-start | bytes 6291464 | tf_op jit(solution)/shard_map/ppermute | solution.py:67
  201.7 13.0 %collective-permute-start.23 = (bf16[16,64,640]{2,1,0:T(8,128)(2,1)S(1)}, bf16[16,64,640]{2,1,0:T(8,128)(2,1)S(1)}, u32[]{:S(2)}, u32[]{:S(2)}) collective-permute-start(bf16[16,64,640]{2,1,0:T(8,128)(2,1)S(1)} %shard_map.438), channel_id=1, source_target_pairs={{0,4},{4,0},{8,12},{12,8},{16,20},{20,16},{24,28},{28,24},{32,36},... | collective-permute-start | bytes 3932168 | tf_op jit(solution)/shard_map/ppermute | solution.py:91
  204.5 16.3 %collective-permute-start.20 = (bf16[256,2048]{1,0:T(8,128)(2,1)S(1)}, bf16[256,2048]{1,0:T(8,128)(2,1)S(1)}, u32[]{:S(2)}, u32[]{:S(2)}) collective-permute-start(bf16[256,2048]{1,0:T(8,128)(2,1)S(1)} %get-tuple-element.147), channel_id=1, source_target_pairs={{0,3},{1,2},{2,1},{3,0},{4,5},{5,4},{6,7},{7,6},{8,11},{9,10},{10,... | collective-permute-start | bytes 3145736 | tf_op jit(solution)/shard_map/ppermute | solution.py:57
  211.8 7.0 %collective-permute-start.22 = (bf16[16,64,512]{2,1,0:T(8,128)(2,1)S(1)}, bf16[16,64,512]{2,1,0:T(8,128)(2,1)S(1)}, u32[]{:S(2)}, u32[]{:S(2)}) collective-permute-start(bf16[16,64,512]{2,1,0:T(8,128)(2,1)S(1)} %shard_map.441), channel_id=1, source_target_pairs={{0,4},{4,0},{8,12},{12,8},{16,20},{20,16},{24,28},{28,24},{32,36},... | collective-permute-start | bytes 3145736 | tf_op jit(solution)/shard_map/ppermute | solution.py:91
  212.0 23.5 %collective-permute-start.27 = (bf16[4,64,2176]{2,1,0:T(8,128)(2,1)S(1)}, bf16[4,64,2176]{2,1,0:T(8,128)(2,1)S(1)}, u32[]{:S(2)}, u32[]{:S(2)}) collective-permute-start(bf16[4,64,2176]{2,1,0:T(8,128)(2,1)S(1)} %add_convert_fusion.1), channel_id=1, source_target_pairs={{0,8},{4,28},{8,0},{12,20},{16,24},{20,12},{24,16},{28,4},{32,40},... | collective-permute-start | bytes 3342344 | tf_op jit(solution)/shard_map/ppermute | solution.py:62
  217.1 18.2 %collective-permute-start.28 = (bf16[8,64,640]{2,1,0:T(8,128)(2,1)S(1)}, bf16[8,64,640]{2,1,0:T(8,128)(2,1)S(1)}, u32[]{:S(2)}, u32[]{:S(2)}) collective-permute-start(bf16[8,64,640]{2,1,0:T(8,128)(2,1)S(1)} %get-tuple-element.159), channel_id=1, source_target_pairs={{0,24},{4,12},{8,16},{12,4},{16,8},{20,28},{24,0},{28,20},{32,56},... | collective-permute-start | bytes 1966088 | tf_op jit(solution)/shard_map/ppermute | solution.py:62
  218.2 21.0 %collective-permute-start.31 = (bf16[4,64,2048]{2,1,0:T(8,128)(2,1)S(1)}, bf16[4,64,2048]{2,1,0:T(8,128)(2,1)S(1)}, u32[]{:S(2)}, u32[]{:S(2)}) collective-permute-start(bf16[4,64,2048]{2,1,0:T(8,128)(2,1)S(1)} %add_convert_fusion.3), channel_id=1, source_target_pairs={{0,32},{4,100},{8,40},{12,108},{16,48},{20,116},{24,56},{28,124},{... | collective-permute-start | bytes 3145736 | tf_op jit(solution)/shard_map/ppermute | solution.py:67
  220.9 17.2 %collective-permute-start.25 = (bf16[128,2048]{1,0:T(8,128)(2,1)S(1)}, bf16[128,2048]{1,0:T(8,128)(2,1)S(1)}, u32[]{:S(2)}, u32[]{:S(2)}) collective-permute-start(bf16[128,2048]{1,0:T(8,128)(2,1)S(1)} %add_convert_fusion.6), channel_id=1, source_target_pairs={{0,1},{1,0},{2,3},{3,2},{4,7},{5,6},{6,5},{7,4},{8,9},{9,8},{10,11... | collective-permute-start | bytes 1572872 | tf_op jit(solution)/shard_map/ppermute | solution.py:57
  221.0 16.4 %collective-permute-start.26 = (bf16[8,64,512]{2,1,0:T(8,128)(2,1)S(1)}, bf16[8,64,512]{2,1,0:T(8,128)(2,1)S(1)}, u32[]{:S(2)}, u32[]{:S(2)}) collective-permute-start(bf16[8,64,512]{2,1,0:T(8,128)(2,1)S(1)} %get-tuple-element.158), channel_id=1, source_target_pairs={{0,96},{4,36},{8,104},{12,44},{16,112},{20,52},{24,120},{28,60},{3... | collective-permute-start | bytes 1572872 | tf_op jit(solution)/shard_map/ppermute | solution.py:67
  235.4 7.2 %collective-permute-start.30 = (bf16[4,64,640]{2,1,0:T(8,128)(2,1)S(1)}, bf16[4,64,640]{2,1,0:T(8,128)(2,1)S(1)}, u32[]{:S(2)}, u32[]{:S(2)}) collective-permute-start(bf16[4,64,640]{2,1,0:T(8,128)(2,1)S(1)} %add_convert_fusion.8), channel_id=1, source_target_pairs={{0,8},{4,28},{8,0},{12,20},{16,24},{20,12},{24,16},{28,4},{32,40},... | collective-permute-start | bytes 983048 | tf_op jit(solution)/shard_map/ppermute | solution.py:62
  236.0 13.5 %collective-permute-start.33 = (bf16[2,64,2176]{2,1,0:T(8,128)(2,1)S(1)}, bf16[2,64,2176]{2,1,0:T(8,128)(2,1)S(1)}, u32[]{:S(2)}, u32[]{:S(2)}) collective-permute-start(bf16[2,64,2176]{2,1,0:T(8,128)(2,1)S(1)} %slice.264), channel_id=1, source_target_pairs={{0,96},{4,36},{8,104},{12,44},{16,112},{20,52},{24,120},{28,60},{3... | collective-permute-start | bytes 1671176 | tf_op jit(solution)/shard_map/ppermute | solution.py:67
  237.5 9.5 %collective-permute-start.34 = (bf16[4,64,512]{2,1,0:T(8,128)(2,1)S(1)}, bf16[4,64,512]{2,1,0:T(8,128)(2,1)S(1)}, u32[]{:S(2)}, u32[]{:S(2)}) collective-permute-start(bf16[4,64,512]{2,1,0:T(8,128)(2,1)S(1)} %add_convert_fusion.12), channel_id=1, source_target_pairs={{0,32},{4,100},{8,40},{12,108},{16,48},{20,116},{24,56},{28,124},{... | collective-permute-start | bytes 786440 | tf_op jit(solution)/shard_map/ppermute | solution.py:67
  238.1 21.0 %collective-permute-start.29 = (bf16[256,2048]{1,0:T(8,128)(2,1)S(1)}, bf16[256,2048]{1,0:T(8,128)(2,1)S(1)}, u32[]{:S(2)}, u32[]{:S(2)}) collective-permute-start(bf16[256,2048]{1,0:T(8,128)(2,1)S(1)} %slice.356), channel_id=1, source_target_pairs={{0,3},{1,2},{2,1},{3,0},{4,5},{5,4},{6,7},{7,6},{8,11},{9,10},{10,... | collective-permute-start | bytes 3145736 | tf_op jit(solution)/shard_map/ppermute | solution.py:57
  242.7 8.5 %collective-permute-start.32 = (bf16[2,64,640]{2,1,0:T(8,128)(2,1)S(1)}, bf16[2,64,640]{2,1,0:T(8,128)(2,1)S(1)}, u32[]{:S(2)}, u32[]{:S(2)}) collective-permute-start(bf16[2,64,640]{2,1,0:T(8,128)(2,1)S(1)} %slice.262), channel_id=1, source_target_pairs={{0,96},{4,36},{8,104},{12,44},{16,112},{20,52},{24,120},{28,60},{3... | collective-permute-start | bytes 491528 | tf_op jit(solution)/shard_map/ppermute | solution.py:67
  244.2 15.1 %collective-permute-start.38 = (bf16[2,64,2048]{2,1,0:T(8,128)(2,1)S(1)}, bf16[2,64,2048]{2,1,0:T(8,128)(2,1)S(1)}, u32[]{:S(2)}, u32[]{:S(2)}) collective-permute-start(bf16[2,64,2048]{2,1,0:T(8,128)(2,1)S(1)} %slice.274), channel_id=1, source_target_pairs={{0,24},{4,12},{8,16},{12,4},{16,8},{20,28},{24,0},{28,20},{32,56},... | collective-permute-start | bytes 1572872 | tf_op jit(solution)/shard_map/ppermute | solution.py:62
  251.2 6.1 %collective-permute-start.36 = (bf16[1,64,640]{2,1,0:T(8,128)(2,1)S(1)}, bf16[1,64,640]{2,1,0:T(8,128)(2,1)S(1)}, u32[]{:S(2)}, u32[]{:S(2)}) collective-permute-start(bf16[1,64,640]{2,1,0:T(8,128)(2,1)S(1)} %add_convert_fusion.13), channel_id=1, source_target_pairs={{0,32},{4,100},{8,40},{12,108},{16,48},{20,116},{24,56},{28,124},{... | collective-permute-start | bytes 245768 | tf_op jit(solution)/shard_map/ppermute | solution.py:67
  253.4 6.5 %collective-permute-start.37 = (bf16[1,64,2176]{2,1,0:T(8,128)(2,1)S(1)}, bf16[1,64,2176]{2,1,0:T(8,128)(2,1)S(1)}, u32[]{:S(2)}, u32[]{:S(2)}) collective-permute-start(bf16[1,64,2176]{2,1,0:T(8,128)(2,1)S(1)} %add_convert_fusion.9), channel_id=1, source_target_pairs={{0,32},{4,100},{8,40},{12,108},{16,48},{20,116},{24,56},{28,124},{... | collective-permute-start | bytes 835592 | tf_op jit(solution)/shard_map/ppermute | solution.py:67
  255.4 7.4 %collective-permute-start.43 = (bf16[2,64,512]{2,1,0:T(8,128)(2,1)S(1)}, bf16[2,64,512]{2,1,0:T(8,128)(2,1)S(1)}, u32[]{:S(2)}, u32[]{:S(2)}) collective-permute-start(bf16[2,64,512]{2,1,0:T(8,128)(2,1)S(1)} %slice.281), channel_id=1, source_target_pairs={{0,24},{4,12},{8,16},{12,4},{16,8},{20,28},{24,0},{28,20},{32,56},... | collective-permute-start | bytes 393224 | tf_op jit(solution)/shard_map/ppermute | solution.py:62
  259.3 6.5 %collective-permute-start.39 = (bf16[1,64,2048]{2,1,0:T(8,128)(2,1)S(1)}, bf16[1,64,2048]{2,1,0:T(8,128)(2,1)S(1)}, u32[]{:S(2)}, u32[]{:S(2)}) collective-permute-start(bf16[1,64,2048]{2,1,0:T(8,128)(2,1)S(1)} %add_convert_fusion.10), channel_id=1, source_target_pairs={{0,8},{4,28},{8,0},{12,20},{16,24},{20,12},{24,16},{28,4},{32,40},... | collective-permute-start | bytes 786440 | tf_op jit(solution)/shard_map/ppermute | solution.py:62
  260.1 15.5 %collective-permute-start.35 = (bf16[128,2048]{1,0:T(8,128)(2,1)S(1)}, bf16[128,2048]{1,0:T(8,128)(2,1)S(1)}, u32[]{:S(2)}, u32[]{:S(2)}) collective-permute-start(bf16[128,2048]{1,0:T(8,128)(2,1)S(1)} %fusion.4), channel_id=1, source_target_pairs={{0,1},{1,0},{2,3},{3,2},{4,7},{5,6},{6,5},{7,4},{8,9},{9,8},{10,11... | collective-permute-start | bytes 1572872 | tf_op jit(solution)/shard_map/ppermute | solution.py:57
  262.8 8.7 %collective-permute-start.44 = (bf16[1,64,512]{2,1,0:T(8,128)(2,1)S(1)}, bf16[1,64,512]{2,1,0:T(8,128)(2,1)S(1)}, u32[]{:S(2)}, u32[]{:S(2)}) collective-permute-start(bf16[1,64,512]{2,1,0:T(8,128)(2,1)S(1)} %add_convert_fusion.14), channel_id=1, source_target_pairs={{0,8},{4,28},{8,0},{12,20},{16,24},{20,12},{24,16},{28,4},{32,40},... | collective-permute-start | bytes 196616 | tf_op jit(solution)/shard_map/ppermute | solution.py:62
  268.1 5.2 %collective-permute-start.42 = (f32[2,64]{1,0:T(2,128)S(1)}, f32[2,64]{1,0:T(2,128)S(1)}, u32[]{:S(2)}, u32[]{:S(2)}) collective-permute-start(f32[2,64]{1,0:T(2,128)S(1)} %pad_maximum_fusion.9), channel_id=1, source_target_pairs={{0,2},{1,3},{2,0},{3,1},{4,6},{5,7},{6,4},{7,5},{8,10},{9,11},{10,... | collective-permute-start | bytes 1544 | tf_op jit(solution)/shard_map/ppermute | solution.py:71
  268.2 5.0 %collective-permute-start.41 = (f32[2,64]{1,0:T(2,128)S(1)}, f32[2,64]{1,0:T(2,128)S(1)}, u32[]{:S(2)}, u32[]{:S(2)}) collective-permute-start(f32[2,64]{1,0:T(2,128)S(1)} %pad_maximum_fusion.9), channel_id=1, source_target_pairs={{0,3},{1,0},{2,1},{3,2},{4,7},{5,4},{6,5},{7,6},{8,11},{9,8},{10,9... | collective-permute-start | bytes 1544 | tf_op jit(solution)/shard_map/ppermute | solution.py:71
  270.2 4.8 %collective-permute-start.40 = (f32[2,64]{1,0:T(2,128)S(1)}, f32[2,64]{1,0:T(2,128)S(1)}, u32[]{:S(2)}, u32[]{:S(2)}) collective-permute-start(f32[2,64]{1,0:T(2,128)S(1)} %pad_maximum_fusion.9), channel_id=1, source_target_pairs={{0,1},{1,2},{2,3},{3,0},{4,5},{5,6},{6,7},{7,4},{8,9},{9,10},{10,1... | collective-permute-start | bytes 1544 | tf_op jit(solution)/shard_map/ppermute | solution.py:71
  (51 other events, 282.9 us)
Sparse Core Ops, SparseCore 0:
  10.9 83.2 all-gather.1

commit v6 on v5

--- a/solution.py
+++ b/solution.py
@@ -225,7 +225,7 @@
         grid=(D // tile,),
         in_specs=[grad, grad, weight(0), weight(1)],
         out_specs=[out, out],
-        compiler_params=pltpu.CompilerParams(vmem_limit_bytes=32 * 2**20),
+        compiler_params=pltpu.CompilerParams(vmem_limit_bytes=24 * 2**20),
         cost_estimate=cost(10),
     )(grad_gate, grad_up, weights, weights)
 
@@ -264,7 +264,7 @@
             pl.BlockSpec((tile, k), lambda i: (i, at)),
         ],
         out_specs=[out, out],
-        compiler_params=pltpu.CompilerParams(vmem_limit_bytes=24 * 2**20),
+        compiler_params=pltpu.CompilerParams(vmem_limit_bytes=16 * 2**20),
         cost_estimate=cost(us),
     )(a, w)
 
@@ -344,7 +344,7 @@
         grid_spec=pltpu.PrefetchScalarGridSpec(
             num_scalar_prefetch=1, grid=(SIDE,), in_specs=specs, out_specs=out_specs
         ),
-        compiler_params=pltpu.CompilerParams(vmem_limit_bytes=24 * 2**20),
+        compiler_params=pltpu.CompilerParams(vmem_limit_bytes=20 * 2**20),
         cost_estimate=cost(us),
     )(here(), *arrays)
 

time: 290 us -> 297 us (1.024)
  local copies, waits for them, and re-layouts: 13 us -> 18.4 us
    unnamed x108 -> x104, local copies, waits for them, and re-layouts: 11.3 us -> 16.7 us
  transfers between devices with their start and end apart: 46 -> 46, of which waited for: 24 -> 24; matrix products, arithmetic and copies ran while one was open for 13% -> 13% of each run, Pallas kernels for 18% -> 17%
where the time goes in v6:
time: 297 us; the launch traced here: 291 us
  waiting for transfers between devices  92.4 us (31%)
  Pallas kernels  73.9 us (25%)
  starting transfers between devices  55.9 us (19%)
  local copies, waits for them, and re-layouts  18.4 us (6%)
  other arithmetic  17.9 us (6%)
  matrix products  16.9 us (6%)
  between operations  15.4 us (5%)
    ppermute x15, waiting for transfers between devices, pair_z(): return lax.ppermute(a, ('dp', 'mp'), pairs)  42.2 us
    ppermute x15, starting transfers between devices, pair_z(): return lax.ppermute(a, ('dp', 'mp'), pairs)  25.4 us
    pallas_call x8, Pallas kernels, weight_products(): pl.pallas_call(kernel, out_shape=outs, grid_spec=pltpu.PrefetchScalarGrid...  24.9 us
    ppermute x8, waiting for transfers between devices, pair_x(): return lax.ppermute(a, 'dp', pairs)  21.7 us
    unnamed x104, local copies, waits for them, and re-layouts  16.7 us
    ppermute x3, waiting for transfers between devices, shift_second(): return lax.ppermute(a, 'dp', pairs)  15.4 us
    pallas_call x1, Pallas kernels, hidden_units(): pl.pallas_call(hidden_kernel, out_shape=[jax.ShapeDtypeStruct((SEQ, HIDDE...  12.9 us
    ppermute x8, starting transfers between devices, pair_y(): return lax.ppermute(a, 'dp', pairs)  10.1 us
  transfers between devices with their start and end apart: 46, of which 24 were waited for; matrix products, arithmetic and copies ran while one was open for 13% of the time, Pallas kernels for 17%

profile of v6, /device:TPU:0, one launch (start us, length us, event | category | flops | bytes accessed | tf_op | source)
XLA Modules:
  0.0 290.9 jit_solution(14149493305117973114)
XLA Ops:
  7.3 2.5 shard_map.422
  9.8 3.2 %collective-permute-start.3 = (bf16[64,1152]{1,0:T(8,128)(2,1)}, bf16[64,1152]{1,0:T(8,128)(2,1)S(1)}, u32[]{:S(2)}, u32[]{:S(2)}) collective-permute-start(bf16[64,1152]{1,0:T(8,128)(2,1)} %get-tuple-element.101._), channel_id=1, source_target_pairs={{0,16},{4,68},{8,24},{12,76},{16,0},{20,84},{24,8},{28,92},{32,48}... | collective-permute-start | bytes 442376 | tf_op jit(solution)/shard_map/ppermute | solution.py:79
  16.5 2.0 collective-permute-start
  21.5 3.3 %collective-permute-start.6 = (bf16[4,64,1152]{2,1,0:T(8,128)(2,1)S(1)}, bf16[4,64,1152]{2,1,0:T(8,128)(2,1)S(1)}, u32[]{:S(2)}, u32[]{:S(2)}) collective-permute-start(bf16[4,64,1152]{2,1,0:T(8,128)(2,1)S(1)} %pad_maximum_fusion.4), channel_id=1, source_target_pairs={{0,64},{4,20},{8,72},{12,28},{16,80},{20,4},{24,88},{28,12},{32,96... | collective-permute-start | bytes 1769480 | tf_op jit(solution)/shard_map/ppermute | solution.py:87
  28.0 3.4 %collective-permute-start.7 = (bf16[256,2048]{1,0:T(8,128)(2,1)S(1)}, bf16[256,2048]{1,0:T(8,128)(2,1)S(1)}, u32[]{:S(2)}, u32[]{:S(2)}) collective-permute-start(bf16[256,2048]{1,0:T(8,128)(2,1)S(1)} %pad_maximum_fusion.2.normed_ref.near_ref), channel_id=1, source_target_pairs={{0,3},{1,2},{2,1},{3,0},{4,5},{5,4},{6,7},{7,6},{8,11},{9,10},{10,... | collective-permute-start | bytes 3145736 | tf_op jit(solution)/shard_map/ppermute | solution.py:57
  32.6 5.3 %collective-permute-done.6 = bf16[4,64,1152]{2,1,0:T(8,128)(2,1)S(1)} collective-permute-done((bf16[4,64,1152]{2,1,0:T(8,128)(2,1)S(1)}, bf16[4,64,1152]{2,1,0:T(8,128)(2,1)S(1)}, u32[]{:S(2)}, u32[]{:S(2)}) %collective-permute-start.6) | collective-permute-done | bytes 589856 | tf_op jit(solution)/shard_map/ppermute | solution.py:87
  37.9 9.9 %collective-permute-done.5 = bf16[4,64,1152]{2,1,0:T(8,128)(2,1)S(1)} collective-permute-done((bf16[4,64,1152]{2,1,0:T(8,128)(2,1)S(1)}, bf16[4,64,1152]{2,1,0:T(8,128)(2,1)S(1)}, u32[]{:S(2)}, u32[]{:S(2)}) %collective-permute-start.5) | collective-permute-done | bytes 589856 | tf_op jit(solution)/shard_map/ppermute | solution.py:87
  52.3 2.9 %collective-permute-start.11 = (bf16[256,2048]{1,0:T(8,128)(2,1)}, bf16[256,2048]{1,0:T(8,128)(2,1)S(1)}, u32[]{:S(2)}, u32[]{:S(2)}) collective-permute-start(bf16[256,2048]{1,0:T(8,128)(2,1)} %copy-done.6), channel_id=1, source_target_pairs={{0,3},{1,2},{2,1},{3,0},{4,5},{5,4},{6,7},{7,6},{8,11},{9,10},{10,... | collective-permute-start | bytes 3145736 | tf_op jit(solution)/shard_map/ppermute | solution.py:57
  55.5 2.4 shard_map.424
  63.4 4.3 %shard_map.425 = (bf16[512,512]{1,0:T(8,128)(2,1)S(1)}, bf16[512,512]{1,0:T(8,128)(2,1)S(1)}, bf16[512,128]{1,0:T(8,128)(2,1)S(1)}, f32[8,512]{1,0:T(8,128)S(1)}) custom-call(s32[4]{0:T(128)S(1)} %select_reduce_fusion.1.slot_ref, s32[4]{0:T(128)S(1)} %bitcast.106, f32[512,640]{1,0:T(8,128)S(1)} %pad_maximum_fusion.1.qkv_ref, f32[512,128]{1,0:T(8,128)S(1)} %copy-done.15, ...), custom_call_target="tpu_custom_call" | custom-call | flops 5500000256 | bytes 15000000 | tf_op jit(solution)/shard_map/pallas_call | solution.py:607
  69.5 2.8 collective-permute-start.12
  73.7 11.9 %collective-permute-done.12 = bf16[256,2048]{1,0:T(8,128)(2,1)S(1)} collective-permute-done((bf16[256,2048]{1,0:T(8,128)(2,1)S(1)}, bf16[256,2048]{1,0:T(8,128)(2,1)S(1)}, u32[]{:S(2)}, u32[]{:S(2)}) %collective-permute-start.12) | collective-permute-done | bytes 1048608 | tf_op jit(solution)/shard_map/ppermute | solution.py:57
  87.1 13.7 %collective-permute-done.13.got_ref = bf16[256,2048]{1,0:T(8,128)(2,1)S(1)} collective-permute-done((bf16[256,2048]{1,0:T(8,128)(2,1)S(1)}, bf16[256,2048]{1,0:T(8,128)(2,1)S(1)}, u32[]{:S(2)}, u32[]{:S(2)}) %collective-permute-start.13) | collective-permute-done | bytes 1048608 | tf_op jit(solution)/shard_map/ppermute | solution.py:57
  100.8 2.3 shard_map.427
  104.9 3.1 %collective-permute-start.14 = (bf16[256,2048]{1,0:T(8,128)(2,1)}, bf16[256,2048]{1,0:T(8,128)(2,1)}, u32[]{:S(2)}, u32[]{:S(2)}) collective-permute-start(bf16[256,2048]{1,0:T(8,128)(2,1)} %get-tuple-element.128.near_ref), channel_id=1, source_target_pairs={{0,3},{1,2},{2,1},{3,0},{4,5},{5,4},{6,7},{7,6},{8,11},{9,10},{10,... | collective-permute-start | bytes 3145736 | tf_op jit(solution)/shard_map/ppermute | solution.py:57
  110.0 6.5 %fusion.2.grad_hidden_ref = f32[512,1408]{1,0:T(8,128)S(1)} fusion(bf16[512,2048]{1,0:T(8,128)(2,1)} %constant_dynamic-update-slice_fusion.2, bf16[2048,4224]{1,0:T(8,128)(2,1)} %all-gather.2.cloned.1.call-done.gate_w_ref.up_w_ref), kind=kOutput, calls=%fused_computation.2 | convolution fusion | flops 2952790016 | bytes 10747904 | tf_op jit(solution)/shard_map/dot_general | solution.py:174
  116.6 5.1 %collective-permute-done.14.far_ref = bf16[256,2048]{1,0:T(8,128)(2,1)} collective-permute-done((bf16[256,2048]{1,0:T(8,128)(2,1)}, bf16[256,2048]{1,0:T(8,128)(2,1)}, u32[]{:S(2)}, u32[]{:S(2)}) %collective-permute-start.14) | collective-permute-done | bytes 1048608 | tf_op jit(solution)/shard_map/ppermute | solution.py:57
  121.6 12.9 %shard_map.429 = (bf16[512,1408]{1,0:T(8,128)(2,1)S(1)}, bf16[512,1408]{1,0:T(8,128)(2,1)S(1)}, bf16[512,1408]{1,0:T(8,128)(2,1)S(1)}) custom-call(bf16[256,2048]{1,0:T(8,128)(2,1)} %get-tuple-element.128.near_ref, bf16[256,2048]{1,0:T(8,128)(2,1)} %collective-permute-done.14.far_ref, bf16[2048,4224]{1,0:T(8,128)(2,1)S(1)} %copy-done.19, ...), custom_call_target="tpu_custom_call" | custom-call | flops 11000000512 | bytes 30000000 | tf_op jit(solution)/shard_map/pallas_call | solution.py:474
  134.5 5.9 %copy-done.20 = bf16[2048,4224]{1,0:T(8,128)(2,1)S(1)} copy-done((bf16[2048,4224]{1,0:T(8,128)(2,1)S(1)}, bf16[2048,4224]{1,0:T(8,128)(2,1)}, u32[]{:S(2)}) %copy-start.20) | copy-done | bytes 17301528
  140.4 8.3 %shard_map.430 = (f32[256,2048]{1,0:T(8,128)S(1)}, bf16[256,2048]{1,0:T(8,128)(2,1)S(1)}) custom-call(bf16[512,1408]{1,0:T(8,128)(2,1)S(1)} %get-tuple-element.124.gate_ref.refs_1_, bf16[512,1408]{1,0:T(8,128)(2,1)S(1)} %get-tuple-element.125.up_ref.refs_1_, bf16[2048,4224]{1,0:T(8,128)(2,1)S(1)} %copy-done.20, bf16[2048,4224]{1,0:T(8,128)(2,1)S(1)} %copy-done.20), custom_call_target="tpu_custom_call" | custom-call | flops 11000000512 | bytes 30000000 | tf_op jit(solution)/shard_map/pallas_call | solution.py:222
  148.8 2.8 collective-permute-start.15
  151.6 2.1 shard_map.431.refs_0_
  153.7 3.7 %shard_map.432 = bf16[16,64,2176]{2,1,0:T(8,128)(2,1)S(1)} custom-call(s32[3]{0:T(128)S(1)} %pad_add_fusion.here_ref, bf16[2048,512]{1,0:T(8,128)(2,1)S(1)} %shard_map.431.refs_0_, bf16[512,1408]{1,0:T(8,128)(2,1)S(1)} %get-tuple-element.124.gate_ref.refs_1_, bf16[2048,512]{1,0:T(8,128)(2,1)S(1)} %shard_map.426.refs_2_, ...), custom_call_target="tpu_custom_call" | custom-call | flops 4400000000 | bytes 12000000 | tf_op jit(solution)/shard_map/pallas_call | solution.py:341
  157.4 3.7 %shard_map.433 = bf16[16,64,2048]{2,1,0:T(8,128)(2,1)S(1)} custom-call(s32[3]{0:T(128)S(1)} %pad_add_fusion.here_ref, bf16[2048,512]{1,0:T(8,128)(2,1)S(1)} %shard_map.431.refs_0_, bf16[512,1408]{1,0:T(8,128)(2,1)S(1)} %get-tuple-element.125.up_ref.refs_1_, bf16[2048,512]{1,0:T(8,128)(2,1)S(1)} %shard_map.426.refs_2_, ...), custom_call_target="tpu_custom_call" | custom-call | flops 4400000000 | bytes 12000000 | tf_op jit(solution)/shard_map/pallas_call | solution.py:341
  161.1 3.7 %collective-permute-done.15 = bf16[256,2048]{1,0:T(8,128)(2,1)S(1)} collective-permute-done((bf16[256,2048]{1,0:T(8,128)(2,1)S(1)}, bf16[256,2048]{1,0:T(8,128)(2,1)S(1)}, u32[]{:S(2)}, u32[]{:S(2)}) %collective-permute-start.15) | collective-permute-done | bytes 1048608 | tf_op jit(solution)/shard_map/ppermute | solution.py:57
  165.7 5.5 %fusion = f32[512,2048]{1,0:T(8,128)S(1)} fusion(bf16[512,1408]{1,0:T(8,128)(2,1)S(1)} %get-tuple-element.130.refs_3_, bf16[2048,4224]{1,0:T(8,128)(2,1)} %all-gather.2.cloned.1.call-done.gate_w_ref.up_w_ref), kind=kOutput, calls=%fused_computation | convolution fusion | flops 2952790016 | bytes 11403264 | tf_op jit(solution)/shard_map/dot_general | solution.py:166
  172.8 4.7 %shard_map.434 = (bf16[8,64,2176]{2,1,0:T(8,128)(2,1)S(1)}, bf16[8,64,2176]{2,1,0:T(8,128)(2,1)S(1)}) custom-call(s32[3]{0:T(128)S(1)} %pad_add_fusion.here_ref, bf16[2048,512]{1,0:T(8,128)(2,1)S(1)} %shard_map.431.refs_0_, bf16[512,1408]{1,0:T(8,128)(2,1)S(1)} %get-tuple-element.124.gate_ref.refs_1_, bf16[2048,512]{1,0:T(8,128)(2,1)S(1)} %shard_map.426.refs_2_, ...), custom_call_target="tpu_custom_call" | custom-call | flops 4400000000 | bytes 12000000 | tf_op jit(solution)/shard_map/pallas_call | solution.py:341
  177.5 3.1 %collective-permute-done.16.got_ref = bf16[256,2048]{1,0:T(8,128)(2,1)S(1)} collective-permute-done((bf16[256,2048]{1,0:T(8,128)(2,1)S(1)}, bf16[256,2048]{1,0:T(8,128)(2,1)S(1)}, u32[]{:S(2)}, u32[]{:S(2)}) %collective-permute-start.16) | collective-permute-done | bytes 1048608 | tf_op jit(solution)/shard_map/ppermute | solution.py:57
  182.3 2.8 collective-permute-start.19
  185.0 2.4 collective-permute-start.21
  187.4 4.6 %shard_map.436 = (bf16[8,64,2048]{2,1,0:T(8,128)(2,1)S(1)}, bf16[8,64,2048]{2,1,0:T(8,128)(2,1)S(1)}) custom-call(s32[3]{0:T(128)S(1)} %pad_add_fusion.here_ref, bf16[2048,512]{1,0:T(8,128)(2,1)S(1)} %shard_map.431.refs_0_, bf16[512,1408]{1,0:T(8,128)(2,1)S(1)} %get-tuple-element.125.up_ref.refs_1_, bf16[2048,512]{1,0:T(8,128)(2,1)S(1)} %shard_map.426.refs_2_, ...), custom_call_target="tpu_custom_call" | custom-call | flops 1100000 | bytes 3000 | tf_op jit(solution)/shard_map/pallas_call | solution.py:341
  192.0 1.9 collective-permute-start.24
  194.7 3.6 %collective-permute-done.19.far_ref = bf16[256,2048]{1,0:T(8,128)(2,1)S(1)} collective-permute-done((bf16[256,2048]{1,0:T(8,128)(2,1)S(1)}, bf16[256,2048]{1,0:T(8,128)(2,1)S(1)}, u32[]{:S(2)}, u32[]{:S(2)}) %collective-permute-start.19) | collective-permute-done | bytes 1048608 | tf_op jit(solution)/shard_map/ppermute | solution.py:57
  199.1 5.6 %shard_map.437.refs_1_.a_ref = bf16[512,640]{1,0:T(8,128)(2,1)S(1)} custom-call(s32[4]{0:T(128)S(1)} %select_reduce_fusion.1.slot_ref, s32[4]{0:T(128)S(1)} %bitcast.107, bf16[512,512]{1,0:T(8,128)(2,1)S(1)} %copy-done.29, bf16[512,128]{1,0:T(8,128)(2,1)S(1)} %get-tuple-element.132.kv_ref, f32[8,512]{1,0:T(8,128)S(1)} %get-tuple-element.133.lse_ref, ...), custom_call_target="tpu_custom_call" | custom-call | flops 6600000000 | bytes 18000000 | tf_op jit(solution)/shard_map/pallas_call | solution.py:625
  204.7 2.1 shard_map.438
  206.9 2.6 shard_map.439
  209.5 2.8 collective-permute-start.20
  219.9 2.4 shard_map.442
  224.7 2.0 shard_map.443
  228.5 12.7 %collective-permute-done.28 = bf16[8,64,640]{2,1,0:T(8,128)(2,1)S(1)} collective-permute-done((bf16[8,64,640]{2,1,0:T(8,128)(2,1)S(1)}, bf16[8,64,640]{2,1,0:T(8,128)(2,1)S(1)}, u32[]{:S(2)}, u32[]{:S(2)}) %collective-permute-start.28) | collective-permute-done | bytes 655392 | tf_op jit(solution)/shard_map/ppermute | solution.py:62
  246.5 2.0 collective-permute-done.30
  251.3 2.9 collective-permute-done.34
  254.3 2.1 collective-permute-done.33
  258.4 2.0 shard_map.444
  260.4 2.0 collective-permute-start.37
  267.2 2.9 collective-permute-done.43
  270.2 2.6 collective-permute-done.39
  275.2 2.0 collective-permute-start.41
  (242 shorter events, 70.5 us)
Async XLA Ops:
  7.2 102.8 %all-gather.2.cloned.1.call-start = ((), (), s32[]{:S(2)}) async-start(), calls=%async_computation | async-start | bytes 17842176 | tf_op jit(solution)/shard_map/all_gather | solution.py:687
  9.8 11.6 %collective-permute-start.3 = (bf16[64,1152]{1,0:T(8,128)(2,1)}, bf16[64,1152]{1,0:T(8,128)(2,1)S(1)}, u32[]{:S(2)}, u32[]{:S(2)}) collective-permute-start(bf16[64,1152]{1,0:T(8,128)(2,1)} %get-tuple-element.101._), channel_id=1, source_target_pairs={{0,16},{4,68},{8,24},{12,76},{16,0},{20,84},{24,8},{28,92},{32,48}... | collective-permute-start | bytes 442376 | tf_op jit(solution)/shard_map/ppermute | solution.py:79
  13.0 8.4 %collective-permute-start.2 = (bf16[64,1152]{1,0:T(8,128)(2,1)}, bf16[64,1152]{1,0:T(8,128)(2,1)S(1)}, u32[]{:S(2)}, u32[]{:S(2)}) collective-permute-start(bf16[64,1152]{1,0:T(8,128)(2,1)} %get-tuple-element.101._), channel_id=1, source_target_pairs={{0,24},{4,100},{8,0},{12,108},{16,8},{20,116},{24,16},{28,124},{32... | collective-permute-start | bytes 442376 | tf_op jit(solution)/shard_map/ppermute | solution.py:79
  14.2 7.2 %collective-permute-start.1 = (bf16[64,1152]{1,0:T(8,128)(2,1)}, bf16[64,1152]{1,0:T(8,128)(2,1)S(1)}, u32[]{:S(2)}, u32[]{:S(2)}) collective-permute-start(bf16[64,1152]{1,0:T(8,128)(2,1)} %get-tuple-element.101._), channel_id=1, source_target_pairs={{0,8},{4,36},{8,16},{12,44},{16,24},{20,52},{24,0},{28,60},{32,40}... | collective-permute-start | bytes 442376 | tf_op jit(solution)/shard_map/ppermute | solution.py:79
  16.5 10.3 %collective-permute-start = (bf16[128,2048]{1,0:T(8,128)(2,1)S(1)}, bf16[128,2048]{1,0:T(8,128)(2,1)}, u32[]{:S(2)}, u32[]{:S(2)}) collective-permute-start(bf16[128,2048]{1,0:T(8,128)(2,1)S(1)} %get-tuple-element.102), channel_id=1, source_target_pairs={{0,1},{1,0},{2,3},{3,2},{4,7},{5,6},{6,5},{7,4},{8,9},{9,8},{10,11... | collective-permute-start | bytes 1572872 | tf_op jit(solution)/shard_map/ppermute | solution.py:57
  21.5 16.4 %collective-permute-start.6 = (bf16[4,64,1152]{2,1,0:T(8,128)(2,1)S(1)}, bf16[4,64,1152]{2,1,0:T(8,128)(2,1)S(1)}, u32[]{:S(2)}, u32[]{:S(2)}) collective-permute-start(bf16[4,64,1152]{2,1,0:T(8,128)(2,1)S(1)} %pad_maximum_fusion.4), channel_id=1, source_target_pairs={{0,64},{4,20},{8,72},{12,28},{16,80},{20,4},{24,88},{28,12},{32,96... | collective-permute-start | bytes 1769480 | tf_op jit(solution)/shard_map/ppermute | solution.py:87
  24.8 23.1 %collective-permute-start.5 = (bf16[4,64,1152]{2,1,0:T(8,128)(2,1)S(1)}, bf16[4,64,1152]{2,1,0:T(8,128)(2,1)S(1)}, u32[]{:S(2)}, u32[]{:S(2)}) collective-permute-start(bf16[4,64,1152]{2,1,0:T(8,128)(2,1)S(1)} %pad_maximum_fusion.4), channel_id=1, source_target_pairs={{0,96},{4,28},{8,104},{12,4},{16,112},{20,12},{24,120},{28,20},{32... | collective-permute-start | bytes 1769480 | tf_op jit(solution)/shard_map/ppermute | solution.py:87
  25.8 22.1 %collective-permute-start.4 = (bf16[4,64,1152]{2,1,0:T(8,128)(2,1)S(1)}, bf16[4,64,1152]{2,1,0:T(8,128)(2,1)S(1)}, u32[]{:S(2)}, u32[]{:S(2)}) collective-permute-start(bf16[4,64,1152]{2,1,0:T(8,128)(2,1)S(1)} %pad_maximum_fusion.4), channel_id=1, source_target_pairs={{0,32},{4,12},{8,40},{12,20},{16,48},{20,28},{24,56},{28,4},{32,64... | collective-permute-start | bytes 1769480 | tf_op jit(solution)/shard_map/ppermute | solution.py:87
  27.9 29.9 %copy-start.4 = (bf16[256,2048]{1,0:T(8,128)(2,1)}, bf16[256,2048]{1,0:T(8,128)(2,1)S(1)}, u32[]{:S(2)}) copy-start(bf16[256,2048]{1,0:T(8,128)(2,1)S(1)} %pad_maximum_fusion.2.normed_ref.near_ref) | copy-start | bytes 3145732
  28.0 21.5 %collective-permute-start.7 = (bf16[256,2048]{1,0:T(8,128)(2,1)S(1)}, bf16[256,2048]{1,0:T(8,128)(2,1)S(1)}, u32[]{:S(2)}, u32[]{:S(2)}) collective-permute-start(bf16[256,2048]{1,0:T(8,128)(2,1)S(1)} %pad_maximum_fusion.2.normed_ref.near_ref), channel_id=1, source_target_pairs={{0,3},{1,2},{2,1},{3,0},{4,5},{5,4},{6,7},{7,6},{8,11},{9,10},{10,... | collective-permute-start | bytes 3145736 | tf_op jit(solution)/shard_map/ppermute | solution.py:57
  31.5 17.1 %collective-permute-start.8 = (bf16[128,2048]{1,0:T(8,128)(2,1)S(1)}, bf16[128,2048]{1,0:T(8,128)(2,1)S(1)}, u32[]{:S(2)}, u32[]{:S(2)}) collective-permute-start(bf16[128,2048]{1,0:T(8,128)(2,1)S(1)} %bitcast_convert_fusion), channel_id=1, source_target_pairs={{0,1},{1,0},{2,3},{3,2},{4,7},{5,6},{6,5},{7,4},{8,9},{9,8},{10,11... | collective-permute-start | bytes 1572872 | tf_op jit(solution)/shard_map/ppermute | solution.py:57
  50.8 4.7 %collective-permute-start.9 = (bf16[16,64,1152]{2,1,0:T(8,128)(2,1)S(1)}, bf16[16,64,1152]{2,1,0:T(8,128)(2,1)}, u32[]{:S(2)}, u32[]{:S(2)}) collective-permute-start(bf16[16,64,1152]{2,1,0:T(8,128)(2,1)S(1)} %bitcast.96), channel_id=1, source_target_pairs={{0,4},{4,0},{8,12},{12,8},{16,20},{20,16},{24,28},{28,24},{32,36},... | collective-permute-start | bytes 7077896 | tf_op jit(solution)/shard_map/ppermute | solution.py:91
  50.9 11.5 %collective-permute-start.10 = (f32[128,128]{1,0:T(8,128)S(1)}, f32[128,128]{1,0:T(8,128)S(1)}, u32[]{:S(2)}, u32[]{:S(2)}) collective-permute-start(f32[128,128]{1,0:T(8,128)S(1)} %get-tuple-element.108), channel_id=1, source_target_pairs={{0,1},{1,0},{2,3},{3,2},{4,7},{5,6},{6,5},{7,4},{8,9},{9,8},{10,11... | collective-permute-start | bytes 196616 | tf_op jit(solution)/shard_map/ppermute | solution.py:57
  52.3 16.4 %collective-permute-start.11 = (bf16[256,2048]{1,0:T(8,128)(2,1)}, bf16[256,2048]{1,0:T(8,128)(2,1)S(1)}, u32[]{:S(2)}, u32[]{:S(2)}) collective-permute-start(bf16[256,2048]{1,0:T(8,128)(2,1)} %copy-done.6), channel_id=1, source_target_pairs={{0,3},{1,2},{2,1},{3,0},{4,5},{5,4},{6,7},{7,6},{8,11},{9,10},{10,... | collective-permute-start | bytes 3145736 | tf_op jit(solution)/shard_map/ppermute | solution.py:57
  69.5 16.1 %collective-permute-start.12 = (bf16[256,2048]{1,0:T(8,128)(2,1)S(1)}, bf16[256,2048]{1,0:T(8,128)(2,1)S(1)}, u32[]{:S(2)}, u32[]{:S(2)}) collective-permute-start(bf16[256,2048]{1,0:T(8,128)(2,1)S(1)} %convolution_convert_fusion), channel_id=1, source_target_pairs={{0,3},{1,2},{2,1},{3,0},{4,5},{5,4},{6,7},{7,6},{8,11},{9,10},{10,... | collective-permute-start | bytes 3145736 | tf_op jit(solution)/shard_map/ppermute | solution.py:57
  85.9 14.9 %copy-start.5 = (bf16[256,2048]{1,0:T(8,128)(2,1)S(1)}, bf16[256,2048]{1,0:T(8,128)(2,1)}, u32[]{:S(2)}) copy-start(bf16[256,2048]{1,0:T(8,128)(2,1)} %copy-done.4) | copy-start | bytes 3145732
  86.0 14.9 %collective-permute-start.13 = (bf16[256,2048]{1,0:T(8,128)(2,1)S(1)}, bf16[256,2048]{1,0:T(8,128)(2,1)S(1)}, u32[]{:S(2)}, u32[]{:S(2)}) collective-permute-start(bf16[256,2048]{1,0:T(8,128)(2,1)S(1)} %add_convert_fusion.5.sum_ref), channel_id=1, source_target_pairs={{0,1},{1,0},{2,3},{3,2},{4,7},{5,6},{6,5},{7,4},{8,9},{9,8},{10,11... | collective-permute-start | bytes 3145736 | tf_op jit(solution)/shard_map/ppermute | solution.py:57
  104.9 16.7 %collective-permute-start.14 = (bf16[256,2048]{1,0:T(8,128)(2,1)}, bf16[256,2048]{1,0:T(8,128)(2,1)}, u32[]{:S(2)}, u32[]{:S(2)}) collective-permute-start(bf16[256,2048]{1,0:T(8,128)(2,1)} %get-tuple-element.128.near_ref), channel_id=1, source_target_pairs={{0,3},{1,2},{2,1},{3,0},{4,5},{5,4},{6,7},{7,6},{8,11},{9,10},{10,... | collective-permute-start | bytes 3145736 | tf_op jit(solution)/shard_map/ppermute | solution.py:57
  148.8 16.1 %collective-permute-start.15 = (bf16[256,2048]{1,0:T(8,128)(2,1)S(1)}, bf16[256,2048]{1,0:T(8,128)(2,1)S(1)}, u32[]{:S(2)}, u32[]{:S(2)}) collective-permute-start(bf16[256,2048]{1,0:T(8,128)(2,1)S(1)} %get-tuple-element.127), channel_id=1, source_target_pairs={{0,3},{1,2},{2,1},{3,0},{4,5},{5,4},{6,7},{7,6},{8,11},{9,10},{10,... | collective-permute-start | bytes 3145736 | tf_op jit(solution)/shard_map/ppermute | solution.py:57
  165.1 7.6 %collective-permute-start.17 = (bf16[16,64,2176]{2,1,0:T(8,128)(2,1)S(1)}, bf16[16,64,2176]{2,1,0:T(8,128)(2,1)S(1)}, u32[]{:S(2)}, u32[]{:S(2)}) collective-permute-start(bf16[16,64,2176]{2,1,0:T(8,128)(2,1)S(1)} %shard_map.432), channel_id=1, source_target_pairs={{0,4},{4,0},{8,12},{12,8},{16,20},{20,16},{24,28},{28,24},{32,36},... | collective-permute-start | bytes 13369352 | tf_op jit(solution)/shard_map/ppermute | solution.py:91
  165.2 22.2 %collective-permute-start.18 = (bf16[16,64,2048]{2,1,0:T(8,128)(2,1)S(1)}, bf16[16,64,2048]{2,1,0:T(8,128)(2,1)S(1)}, u32[]{:S(2)}, u32[]{:S(2)}) collective-permute-start(bf16[16,64,2048]{2,1,0:T(8,128)(2,1)S(1)} %shard_map.433), channel_id=1, source_target_pairs={{0,4},{4,0},{8,12},{12,8},{16,20},{20,16},{24,28},{28,24},{32,36},... | collective-permute-start | bytes 12582920 | tf_op jit(solution)/shard_map/ppermute | solution.py:91
  165.7 14.8 %collective-permute-start.16 = (bf16[256,2048]{1,0:T(8,128)(2,1)S(1)}, bf16[256,2048]{1,0:T(8,128)(2,1)S(1)}, u32[]{:S(2)}, u32[]{:S(2)}) collective-permute-start(bf16[256,2048]{1,0:T(8,128)(2,1)S(1)} %add_convert_fusion.4.sum_ref), channel_id=1, source_target_pairs={{0,1},{1,0},{2,3},{3,2},{4,7},{5,6},{6,5},{7,4},{8,9},{9,8},{10,11... | collective-permute-start | bytes 3145736 | tf_op jit(solution)/shard_map/ppermute | solution.py:57
  182.3 16.1 %collective-permute-start.19 = (bf16[256,2048]{1,0:T(8,128)(2,1)S(1)}, bf16[256,2048]{1,0:T(8,128)(2,1)S(1)}, u32[]{:S(2)}, u32[]{:S(2)}) collective-permute-start(bf16[256,2048]{1,0:T(8,128)(2,1)S(1)} %get-tuple-element.150.near_ref), channel_id=1, source_target_pairs={{0,3},{1,2},{2,1},{3,0},{4,5},{5,4},{6,7},{7,6},{8,11},{9,10},{10,... | collective-permute-start | bytes 3145736 | tf_op jit(solution)/shard_map/ppermute | solution.py:57
  185.0 28.8 %collective-permute-start.21 = (bf16[8,64,2176]{2,1,0:T(8,128)(2,1)S(1)}, bf16[8,64,2176]{2,1,0:T(8,128)(2,1)}, u32[]{:S(2)}, u32[]{:S(2)}) collective-permute-start(bf16[8,64,2176]{2,1,0:T(8,128)(2,1)S(1)} %get-tuple-element.148), channel_id=1, source_target_pairs={{0,24},{4,12},{8,16},{12,4},{16,8},{20,28},{24,0},{28,20},{32,56},... | collective-permute-start | bytes 6684680 | tf_op jit(solution)/shard_map/ppermute | solution.py:62
  192.0 27.5 %collective-permute-start.24 = (bf16[8,64,2048]{2,1,0:T(8,128)(2,1)S(1)}, bf16[8,64,2048]{2,1,0:T(8,128)(2,1)S(1)}, u32[]{:S(2)}, u32[]{:S(2)}) collective-permute-start(bf16[8,64,2048]{2,1,0:T(8,128)(2,1)S(1)} %get-tuple-element.151), channel_id=1, source_target_pairs={{0,96},{4,36},{8,104},{12,44},{16,112},{20,52},{24,120},{28,60},{3... | collective-permute-start | bytes 6291464 | tf_op jit(solution)/shard_map/ppermute | solution.py:67
  206.8 13.2 %collective-permute-start.23 = (bf16[16,64,640]{2,1,0:T(8,128)(2,1)S(1)}, bf16[16,64,640]{2,1,0:T(8,128)(2,1)S(1)}, u32[]{:S(2)}, u32[]{:S(2)}) collective-permute-start(bf16[16,64,640]{2,1,0:T(8,128)(2,1)S(1)} %shard_map.438), channel_id=1, source_target_pairs={{0,4},{4,0},{8,12},{12,8},{16,20},{20,16},{24,28},{28,24},{32,36},... | collective-permute-start | bytes 3932168 | tf_op jit(solution)/shard_map/ppermute | solution.py:91
  209.5 17.2 %collective-permute-start.20 = (bf16[256,2048]{1,0:T(8,128)(2,1)S(1)}, bf16[256,2048]{1,0:T(8,128)(2,1)S(1)}, u32[]{:S(2)}, u32[]{:S(2)}) collective-permute-start(bf16[256,2048]{1,0:T(8,128)(2,1)S(1)} %get-tuple-element.147), channel_id=1, source_target_pairs={{0,3},{1,2},{2,1},{3,0},{4,5},{5,4},{6,7},{7,6},{8,11},{9,10},{10,... | collective-permute-start | bytes 3145736 | tf_op jit(solution)/shard_map/ppermute | solution.py:57
  217.8 7.0 %collective-permute-start.22 = (bf16[16,64,512]{2,1,0:T(8,128)(2,1)S(1)}, bf16[16,64,512]{2,1,0:T(8,128)(2,1)S(1)}, u32[]{:S(2)}, u32[]{:S(2)}) collective-permute-start(bf16[16,64,512]{2,1,0:T(8,128)(2,1)S(1)} %shard_map.441), channel_id=1, source_target_pairs={{0,4},{4,0},{8,12},{12,8},{16,20},{20,16},{24,28},{28,24},{32,36},... | collective-permute-start | bytes 3145736 | tf_op jit(solution)/shard_map/ppermute | solution.py:91
  217.9 23.5 %collective-permute-start.27 = (bf16[4,64,2176]{2,1,0:T(8,128)(2,1)S(1)}, bf16[4,64,2176]{2,1,0:T(8,128)(2,1)S(1)}, u32[]{:S(2)}, u32[]{:S(2)}) collective-permute-start(bf16[4,64,2176]{2,1,0:T(8,128)(2,1)S(1)} %add_convert_fusion.1), channel_id=1, source_target_pairs={{0,8},{4,28},{8,0},{12,20},{16,24},{20,12},{24,16},{28,4},{32,40},... | collective-permute-start | bytes 3342344 | tf_op jit(solution)/shard_map/ppermute | solution.py:62
  222.3 19.0 %collective-permute-start.28 = (bf16[8,64,640]{2,1,0:T(8,128)(2,1)S(1)}, bf16[8,64,640]{2,1,0:T(8,128)(2,1)S(1)}, u32[]{:S(2)}, u32[]{:S(2)}) collective-permute-start(bf16[8,64,640]{2,1,0:T(8,128)(2,1)S(1)} %get-tuple-element.159), channel_id=1, source_target_pairs={{0,24},{4,12},{8,16},{12,4},{16,8},{20,28},{24,0},{28,20},{32,56},... | collective-permute-start | bytes 1966088 | tf_op jit(solution)/shard_map/ppermute | solution.py:62
  223.4 22.5 %collective-permute-start.31 = (bf16[4,64,2048]{2,1,0:T(8,128)(2,1)S(1)}, bf16[4,64,2048]{2,1,0:T(8,128)(2,1)S(1)}, u32[]{:S(2)}, u32[]{:S(2)}) collective-permute-start(bf16[4,64,2048]{2,1,0:T(8,128)(2,1)S(1)} %add_convert_fusion.3), channel_id=1, source_target_pairs={{0,32},{4,100},{8,40},{12,108},{16,48},{20,116},{24,56},{28,124},{... | collective-permute-start | bytes 3145736 | tf_op jit(solution)/shard_map/ppermute | solution.py:67
  226.9 18.1 %collective-permute-start.25 = (bf16[128,2048]{1,0:T(8,128)(2,1)S(1)}, bf16[128,2048]{1,0:T(8,128)(2,1)S(1)}, u32[]{:S(2)}, u32[]{:S(2)}) collective-permute-start(bf16[128,2048]{1,0:T(8,128)(2,1)S(1)} %add_convert_fusion.6), channel_id=1, source_target_pairs={{0,1},{1,0},{2,3},{3,2},{4,7},{5,6},{6,5},{7,4},{8,9},{9,8},{10,11... | collective-permute-start | bytes 1572872 | tf_op jit(solution)/shard_map/ppermute | solution.py:57
  227.0 17.6 %collective-permute-start.26 = (bf16[8,64,512]{2,1,0:T(8,128)(2,1)S(1)}, bf16[8,64,512]{2,1,0:T(8,128)(2,1)S(1)}, u32[]{:S(2)}, u32[]{:S(2)}) collective-permute-start(bf16[8,64,512]{2,1,0:T(8,128)(2,1)S(1)} %get-tuple-element.158), channel_id=1, source_target_pairs={{0,96},{4,36},{8,104},{12,44},{16,112},{20,52},{24,120},{28,60},{3... | collective-permute-start | bytes 1572872 | tf_op jit(solution)/shard_map/ppermute | solution.py:67
  241.3 7.2 %collective-permute-start.30 = (bf16[4,64,640]{2,1,0:T(8,128)(2,1)S(1)}, bf16[4,64,640]{2,1,0:T(8,128)(2,1)S(1)}, u32[]{:S(2)}, u32[]{:S(2)}) collective-permute-start(bf16[4,64,640]{2,1,0:T(8,128)(2,1)S(1)} %add_convert_fusion.8), channel_id=1, source_target_pairs={{0,8},{4,28},{8,0},{12,20},{16,24},{20,12},{24,16},{28,4},{32,40},... | collective-permute-start | bytes 983048 | tf_op jit(solution)/shard_map/ppermute | solution.py:62
  243.1 13.3 %collective-permute-start.33 = (bf16[2,64,2176]{2,1,0:T(8,128)(2,1)S(1)}, bf16[2,64,2176]{2,1,0:T(8,128)(2,1)S(1)}, u32[]{:S(2)}, u32[]{:S(2)}) collective-permute-start(bf16[2,64,2176]{2,1,0:T(8,128)(2,1)S(1)} %slice.264), channel_id=1, source_target_pairs={{0,96},{4,36},{8,104},{12,44},{16,112},{20,52},{24,120},{28,60},{3... | collective-permute-start | bytes 1671176 | tf_op jit(solution)/shard_map/ppermute | solution.py:67
  244.7 9.5 %collective-permute-start.34 = (bf16[4,64,512]{2,1,0:T(8,128)(2,1)S(1)}, bf16[4,64,512]{2,1,0:T(8,128)(2,1)S(1)}, u32[]{:S(2)}, u32[]{:S(2)}) collective-permute-start(bf16[4,64,512]{2,1,0:T(8,128)(2,1)S(1)} %add_convert_fusion.12), channel_id=1, source_target_pairs={{0,32},{4,100},{8,40},{12,108},{16,48},{20,116},{24,56},{28,124},{... | collective-permute-start | bytes 786440 | tf_op jit(solution)/shard_map/ppermute | solution.py:67
  245.0 21.1 %collective-permute-start.29 = (bf16[256,2048]{1,0:T(8,128)(2,1)S(1)}, bf16[256,2048]{1,0:T(8,128)(2,1)S(1)}, u32[]{:S(2)}, u32[]{:S(2)}) collective-permute-start(bf16[256,2048]{1,0:T(8,128)(2,1)S(1)} %slice.356), channel_id=1, source_target_pairs={{0,3},{1,2},{2,1},{3,0},{4,5},{5,4},{6,7},{7,6},{8,11},{9,10},{10,... | collective-permute-start | bytes 3145736 | tf_op jit(solution)/shard_map/ppermute | solution.py:57
  248.6 9.6 %collective-permute-start.32 = (bf16[2,64,640]{2,1,0:T(8,128)(2,1)S(1)}, bf16[2,64,640]{2,1,0:T(8,128)(2,1)S(1)}, u32[]{:S(2)}, u32[]{:S(2)}) collective-permute-start(bf16[2,64,640]{2,1,0:T(8,128)(2,1)S(1)} %slice.262), channel_id=1, source_target_pairs={{0,96},{4,36},{8,104},{12,44},{16,112},{20,52},{24,120},{28,60},{3... | collective-permute-start | bytes 491528 | tf_op jit(solution)/shard_map/ppermute | solution.py:67
  250.1 16.1 %collective-permute-start.38 = (bf16[2,64,2048]{2,1,0:T(8,128)(2,1)S(1)}, bf16[2,64,2048]{2,1,0:T(8,128)(2,1)S(1)}, u32[]{:S(2)}, u32[]{:S(2)}) collective-permute-start(bf16[2,64,2048]{2,1,0:T(8,128)(2,1)S(1)} %slice.274), channel_id=1, source_target_pairs={{0,24},{4,12},{8,16},{12,4},{16,8},{20,28},{24,0},{28,20},{32,56},... | collective-permute-start | bytes 1572872 | tf_op jit(solution)/shard_map/ppermute | solution.py:62
  258.2 6.1 %collective-permute-start.36 = (bf16[1,64,640]{2,1,0:T(8,128)(2,1)S(1)}, bf16[1,64,640]{2,1,0:T(8,128)(2,1)S(1)}, u32[]{:S(2)}, u32[]{:S(2)}) collective-permute-start(bf16[1,64,640]{2,1,0:T(8,128)(2,1)S(1)} %add_convert_fusion.13), channel_id=1, source_target_pairs={{0,32},{4,100},{8,40},{12,108},{16,48},{20,116},{24,56},{28,124},{... | collective-permute-start | bytes 245768 | tf_op jit(solution)/shard_map/ppermute | solution.py:67
  260.4 6.5 %collective-permute-start.37 = (bf16[1,64,2176]{2,1,0:T(8,128)(2,1)S(1)}, bf16[1,64,2176]{2,1,0:T(8,128)(2,1)S(1)}, u32[]{:S(2)}, u32[]{:S(2)}) collective-permute-start(bf16[1,64,2176]{2,1,0:T(8,128)(2,1)S(1)} %add_convert_fusion.9), channel_id=1, source_target_pairs={{0,32},{4,100},{8,40},{12,108},{16,48},{20,116},{24,56},{28,124},{... | collective-permute-start | bytes 835592 | tf_op jit(solution)/shard_map/ppermute | solution.py:67
  262.4 7.6 %collective-permute-start.43 = (bf16[2,64,512]{2,1,0:T(8,128)(2,1)S(1)}, bf16[2,64,512]{2,1,0:T(8,128)(2,1)S(1)}, u32[]{:S(2)}, u32[]{:S(2)}) collective-permute-start(bf16[2,64,512]{2,1,0:T(8,128)(2,1)S(1)} %slice.281), channel_id=1, source_target_pairs={{0,24},{4,12},{8,16},{12,4},{16,8},{20,28},{24,0},{28,20},{32,56},... | collective-permute-start | bytes 393224 | tf_op jit(solution)/shard_map/ppermute | solution.py:62
  266.3 6.5 %collective-permute-start.39 = (bf16[1,64,2048]{2,1,0:T(8,128)(2,1)S(1)}, bf16[1,64,2048]{2,1,0:T(8,128)(2,1)S(1)}, u32[]{:S(2)}, u32[]{:S(2)}) collective-permute-start(bf16[1,64,2048]{2,1,0:T(8,128)(2,1)S(1)} %add_convert_fusion.10), channel_id=1, source_target_pairs={{0,8},{4,28},{8,0},{12,20},{16,24},{20,12},{24,16},{28,4},{32,40},... | collective-permute-start | bytes 786440 | tf_op jit(solution)/shard_map/ppermute | solution.py:62
  267.1 15.5 %collective-permute-start.35 = (bf16[128,2048]{1,0:T(8,128)(2,1)S(1)}, bf16[128,2048]{1,0:T(8,128)(2,1)S(1)}, u32[]{:S(2)}, u32[]{:S(2)}) collective-permute-start(bf16[128,2048]{1,0:T(8,128)(2,1)S(1)} %fusion.4), channel_id=1, source_target_pairs={{0,1},{1,0},{2,3},{3,2},{4,7},{5,6},{6,5},{7,4},{8,9},{9,8},{10,11... | collective-permute-start | bytes 1572872 | tf_op jit(solution)/shard_map/ppermute | solution.py:57
  270.1 8.4 %collective-permute-start.44 = (bf16[1,64,512]{2,1,0:T(8,128)(2,1)S(1)}, bf16[1,64,512]{2,1,0:T(8,128)(2,1)S(1)}, u32[]{:S(2)}, u32[]{:S(2)}) collective-permute-start(bf16[1,64,512]{2,1,0:T(8,128)(2,1)S(1)} %add_convert_fusion.14), channel_id=1, source_target_pairs={{0,8},{4,28},{8,0},{12,20},{16,24},{20,12},{24,16},{28,4},{32,40},... | collective-permute-start | bytes 196616 | tf_op jit(solution)/shard_map/ppermute | solution.py:62
  275.0 5.2 %collective-permute-start.42 = (f32[2,64]{1,0:T(2,128)S(1)}, f32[2,64]{1,0:T(2,128)S(1)}, u32[]{:S(2)}, u32[]{:S(2)}) collective-permute-start(f32[2,64]{1,0:T(2,128)S(1)} %pad_maximum_fusion.9), channel_id=1, source_target_pairs={{0,2},{1,3},{2,0},{3,1},{4,6},{5,7},{6,4},{7,5},{8,10},{9,11},{10,... | collective-permute-start | bytes 1544 | tf_op jit(solution)/shard_map/ppermute | solution.py:71
  275.2 5.0 %collective-permute-start.41 = (f32[2,64]{1,0:T(2,128)S(1)}, f32[2,64]{1,0:T(2,128)S(1)}, u32[]{:S(2)}, u32[]{:S(2)}) collective-permute-start(f32[2,64]{1,0:T(2,128)S(1)} %pad_maximum_fusion.9), channel_id=1, source_target_pairs={{0,3},{1,0},{2,1},{3,2},{4,7},{5,4},{6,5},{7,6},{8,11},{9,8},{10,9... | collective-permute-start | bytes 1544 | tf_op jit(solution)/shard_map/ppermute | solution.py:71
  277.2 4.8 %collective-permute-start.40 = (f32[2,64]{1,0:T(2,128)S(1)}, f32[2,64]{1,0:T(2,128)S(1)}, u32[]{:S(2)}, u32[]{:S(2)}) collective-permute-start(f32[2,64]{1,0:T(2,128)S(1)} %pad_maximum_fusion.9), channel_id=1, source_target_pairs={{0,1},{1,2},{2,3},{3,0},{4,5},{5,6},{6,7},{7,4},{8,9},{9,10},{10,1... | collective-permute-start | bytes 1544 | tf_op jit(solution)/shard_map/ppermute | solution.py:71
  (49 other events, 278.4 us)
Sparse Core Ops, SparseCore 0:
  10.9 83.2 all-gather.1
